TPU v7x, 32 devices: a whole 2x2x4 slice. The times are simulated.
32 devices in a mesh: tm: 4 (over z), chan: 8 (over y, x, core).
Axes of the slice: x: 2, y: 2, z: 4, core: 2. Of those that a mesh axis runs over, the one named last changes fastest.
Arguments:
- phase_step: float32 [8, 256, 32768], P(None, 'tm', 'chan'), may hold values from -3.1416 to 3.1416, as said below
- wrap_count: int32 [8, 256, 32768], P(None, 'tm', 'chan'), may hold values from -1 to 1
- coupling: float32 [8], replicated, may hold values from 0.5 to 2
- filter_taps: float32 [8, 128], replicated, may hold values from -0.06 to 0.06
Outputs:
- strain: float32 [8, 256, 32768], P(None, 'tm', 'chan')
Inputs may be any that keep to these rules, and one draw needn't show every extreme that they name: `phase_step`: wrapped phase differences, within -pi to pi.
All inputs are finite; a program needn't handle non-finite values.
Results may differ from a plain program's by a relative error of at most 0.00007.
Values sent between devices are 32-bit elements; how exact they have to be, the bound alone decides.
No kernel may reach another device: no remote copies, remote signals or barrier semaphores. Data moves between devices by JAX's collectives and lax.ppermute only.
A program may use at most 128 MiB of HBM per device.

v0:
```python
import math

import jax
import jax.numpy as jnp
from jax import lax
from jax.sharding import PartitionSpec as P

two_pi = 2.0 * math.pi


def extended(block, sides, width):
    for axis, dim in sides:
        count = lax.axis_size(axis)
        forward = [(i, i + 1) for i in range(count - 1)]
        backward = [(target, source) for source, target in forward]
        low = lax.ppermute(
            lax.slice_in_dim(block, block.shape[dim] - width, None, axis=dim), axis, forward
        )
        high = lax.ppermute(lax.slice_in_dim(block, 0, width, axis=dim), axis, backward)
        block = jnp.concatenate([low, block, high], axis=dim)
    return block


def spatial_filter(padded, filter_taps):
    stacked = jnp.transpose(padded, (1, 0, 2))
    kernel = filter_taps[:, None, :]
    result = lax.conv_general_dilated(
        stacked,
        kernel,
        (1,),
        "VALID",
        feature_group_count=filter_taps.shape[0],
        precision=lax.Precision.HIGHEST,
    )
    return jnp.transpose(result, (1, 0, 2))


def earlier_blocks(totals, position):
    gathered = lax.all_gather(totals[None], "tm", axis=0, tiled=True)
    earlier_mask = (jnp.arange(gathered.shape[0]) < position).astype(jnp.float32)
    return jnp.sum(gathered * earlier_mask[:, None, None], axis=0)


def shards(phase_step, wrap_count, coupling, filter_taps):
    increment = phase_step + two_pi * wrap_count.astype(jnp.float32)
    partial_value = jnp.cumsum(increment, axis=1)
    block_total = partial_value[:, -1, :]
    position = lax.axis_index("tm")
    width = phase_step.shape[2]
    half = filter_taps.shape[1] // 2
    offset = earlier_blocks(block_total, position)
    unwrapped = partial_value + offset[:, None, :]
    population = phase_step.shape[0] * width * lax.axis_size("chan")
    mode_sums = lax.psum(jnp.sum(unwrapped, axis=(0, 2)), "chan")
    common = mode_sums / population
    shifted = coupling[:, None, None] * common[None, :, None]
    leveled = unwrapped - shifted
    padded = extended(leveled, (("chan", 2),), half)
    filtered = spatial_filter(padded, filter_taps)[:, :, :width]
    return (leveled - filtered) * (1.0 / (4.0 * two_pi))


def solution(mesh):
    placed = (P(None, "tm", "chan"), P(None, "tm", "chan"), P(), P())
    return jax.shard_map(
        shards, mesh=mesh, in_specs=placed, out_specs=P(None, "tm", "chan"), check_vma=False
    )
```

profile of v0, /device:TPU:0, one launch (start us, length us, event | category | flops | bytes accessed | tf_op | source)
XLA Modules:
  0.0 706.3 jit_solution(13516921844181531626)
XLA Ops:
  0.0 11.7 %multiply_add_fusion = f32[8,64,4096]{2,1,0:T(8,128)} fusion(f32[8,64,4096]{2,1,0:T(8,128)} %param.4, s32[8,64,4096]{2,1,0:T(8,128)} %param.5), kind=kLoop, calls=%fused_computation.11 | loop fusion | flops 6291456 | bytes 25165824 | tf_op jit(solution)/shard_map/add | solution.py:45
  11.7 11.5 %fusion.8 = f32[8,64,4096]{2,0,1:T(8,128)} fusion(f32[8,64,4096]{2,1,0:T(8,128)} %multiply_add_fusion), kind=kOutput, calls=%fused_computation.9 | output fusion | flops 132120576 | bytes 16777216 | tf_op jit(solution)/shard_map/jit(cumsum)/reduce_window_sum | solution.py:46
  23.2 0.0 slice-start
  23.2 13.4 %copy.11 = f32[8,64,4096]{1,0,2:T(8,128)} copy(f32[8,64,4096]{2,0,1:T(8,128)} %fusion.8) | data formatting | bytes 16777216 | tf_op jit(solution)/shard_map/jit(cumsum)/reduce_window_sum | solution.py:46
  36.7 0.0 slice-done
  36.7 17.5 %all-gather = f32[32,1,4096]{2,0,1:T(8,128)S(1)} all-gather(f32[8,1,4096]{2,0,1:T(8,128)S(1)} %slice-done), channel_id=2, replica_groups=mesh['tm'=4,'chan'=8] {'tm'}, dimensions={0}, use_global_device_ids=true | all-gather | bytes 655360 | tf_op jit(solution)/shard_map/all_gather | solution.py:39
  54.1 0.1 fusion.10
  54.2 0.6 copy.10
  54.8 7.7 %add_reduce_fusion = f32[64]{0:T(128)S(1)} fusion(f32[8,64,4096]{1,0,2:T(8,128)} %copy.11, f32[8,4096]{0,1:T(8,128)S(1)} %copy.10), kind=kLoop, calls=%fused_computation.8 | loop fusion | flops 4194240 | bytes 8519936 | tf_op jit(solution)/shard_map/reduce_sum | solution.py:54
  62.5 12.2 %psum.7 = f32[64]{0:T(128)S(1)} all-reduce(f32[64]{0:T(128)S(1)} %add_reduce_fusion), channel_id=1, replica_groups=mesh['tm'=4,'chan'=8] {'chan'}, use_global_device_ids=true, to_apply=%region_3.4 | all-reduce | flops 64 | bytes 512 | tf_op jit(solution)/shard_map/psum | solution.py:54
  74.8 0.0 copy-done.2
  74.8 0.1 broadcast_multiply_fusion
  74.9 11.1 %add_subtract_fusion = f32[8,64,4096]{1,0,2:T(8,128)S(1)} fusion(f32[8,64,4096]{1,0,2:T(8,128)} %copy.11, f32[8,64]{1,0:T(8,128)S(1)} %broadcast_multiply_fusion, f32[8,4096]{0,1:T(8,128)S(1)} %copy.10), kind=kLoop, calls=%fused_computation.7 | loop fusion | flops 4194304 | bytes 16910336 | tf_op jit(solution)/shard_map/sub | solution.py:57
  85.9 0.0 copy-start
  85.9 5.7 copy-done
  91.7 1.3 collective-permute-start
  93.0 1.5 collective-permute-start.1
  94.5 0.0 copy-done.1
  94.5 0.1 copy.12
  94.6 0.0 collective-permute-done
  94.6 1.8 collective-permute-done.1
  96.5 11.0 %fusion.17 = f32[8,64,4224]{1,0,2:T(8,128)S(1)} fusion(f32[8,64,64]{1,0,2:T(8,128)S(1)} %collective-permute-done.1, f32[8,64,4096]{1,0,2:T(8,128)} %copy-done, f32[8,64,64]{1,0,2:T(8,128)S(1)} %collective-permute-done), kind=kLoop, calls=%fused_computation.1.clone.clone.clone.1 | loop fusion | flops 4325376 | bytes 17301504 | tf_op jit(solution)/shard_map/slice | solution.py:59
  107.5 586.0 %subtract_multiply_fusion = f32[8,64,4096]{1,0,2:T(8,128)} fusion(f32[8,64,4096]{1,0,2:T(8,128)} %copy-done, f32[8,1,128]{0,1,2:T(1,128)S(1)} %copy.12, f32[8,64,4224]{1,0,2:T(8,128)S(1)} %fusion.17), kind=kOutput, calls=%fused_computation.6 | convolution fusion | flops 3225419776 | bytes 25432064 | tf_op jit(solution)/shard_map/slice | solution.py:59
  693.6 12.7 %copy.13 = f32[8,64,4096]{2,1,0:T(8,128)} copy(f32[8,64,4096]{1,0,2:T(8,128)} %subtract_multiply_fusion) | data formatting | bytes 16777216 | tf_op jit(solution)/shard_map/mul | solution.py:60
  (5 shorter events, 0.0 us)
Async XLA Ops:
  23.2 13.5 %slice-start = ((f32[8,64,4096]{2,0,1:T(8,128)}), f32[8,1,4096]{2,0,1:T(8,128)S(1)}, s32[]{:S(2)}) async-start(f32[8,64,4096]{2,0,1:T(8,128)} %fusion.8), calls=%async_computation | async-start | bytes 262144 | tf_op jit(solution)/shard_map/slice | solution.py:47
  36.6 38.1 %copy-start.2 = (f32[8]{0:T(128)S(1)}, f32[8]{0:T(128)}, u32[]{:S(2)}) copy-start(f32[8]{0:T(128)} %param.6) | copy-start | bytes 100
  74.9 19.7 %copy-start.1 = (f32[8,128]{1,0:T(8,128)S(1)}, f32[8,128]{1,0:T(8,128)}, u32[]{:S(2)}) copy-start(f32[8,128]{1,0:T(8,128)} %param.7) | copy-start | bytes 12292
  85.9 5.7 copy-start
  91.7 3.0 collective-permute-start
  93.0 3.4 collective-permute-start.1
where the time goes:
time: 713 us; the launch traced here: 706 us
  matrix products  586 us (82%)
  other arithmetic  53.2 us (7%)
  local copies, waits for them, and re-layouts  32.6 us (5%)
  blocking collectives  29.7 us (4%)
    slice x1, matrix products, shards(): filtered = spatial_filter(padded, filter_taps)[:, :, :width]  586 us
    all_gather x1, blocking collectives, earlier_blocks(): gathered = lax.all_gather(totals[None], 'tm', axis=0, tiled=True)  17.5 us
  transfers between devices with their start and end apart: 2, of which 1 were waited for; matrix products, arithmetic and copies ran while one was open for 0% of the time, Pallas kernels for 0%

commit v1 on v0

v1 whole, which is shorter than its diff:
```python
import functools
import math

import jax
import jax.numpy as jnp
from jax import lax
from jax.experimental import pallas as pl
from jax.experimental.pallas import tpu as pltpu
from jax.sharding import PartitionSpec as P

two_pi = 2.0 * math.pi
LANES = 128
SUBLANES = 8


def shifted_down(value, amount):
    rows = lax.broadcasted_iota(jnp.int32, value.shape, 0)
    return jnp.where(rows >= amount, pltpu.roll(value, amount, 0), 0.0)


def scanned(pieces):
    sums, carry = [], None
    for value in pieces:
        amount = 1
        while amount < SUBLANES:
            value = value + shifted_down(value, amount)
            amount *= 2
        if carry is not None:
            value = value + carry
        carry = jnp.broadcast_to(value[SUBLANES - 1 :, :], value.shape)
        sums.append(value)
    return sums


def store_split(high_ref, low_ref, cable, block, sums):
    for pair in range(0, len(sums), 2):
        both = jnp.concatenate(sums[pair : pair + 2], axis=0)
        high = both.astype(jnp.bfloat16)
        low = (both - high.astype(jnp.float32)).astype(jnp.bfloat16)
        rows = pl.ds(pair * SUBLANES, 2 * SUBLANES)
        high_ref[cable, block, rows, :] = high
        low_ref[cable, block, rows, :] = low


def unwrap_kernel(
    phase_hbm, wrap_hbm, left_ref, right_ref, taps_ref,
    high_ref, low_ref, totals_ref, sums_ref, weight_ref,
    phase_ref, wrap_ref, sem,
):
    cables, time, width = phase_hbm.shape
    blocks = width // LANES
    groups = time // SUBLANES

    def copies(cable):
        return (
            pltpu.make_async_copy(phase_hbm.at[cable], phase_ref.at[cable], sem.at[0, cable]),
            pltpu.make_async_copy(wrap_hbm.at[cable], wrap_ref.at[cable], sem.at[1, cable]),
        )

    for cable in range(cables):
        for copy in copies(cable):
            copy.start()

    outputs = lax.broadcasted_iota(jnp.int32, (LANES, LANES), 0)
    inputs = lax.broadcasted_iota(jnp.int32, (LANES, LANES), 1)
    centre = (lax.broadcasted_iota(jnp.int32, (1, LANES), 1) == LANES // 2).astype(jnp.float32)

    @pl.loop(0, cables)
    def _(cable):
        row = (centre - taps_ref[pl.ds(cable, 1), :]) * (1.0 / (4.0 * two_pi))
        circulant = pltpu.roll(
            jnp.broadcast_to(row, (LANES, LANES)), 0, 1, stride=1, stride_axis=0
        )
        first = jnp.where(inputs >= outputs, circulant, 0.0).T
        second = jnp.where(inputs < outputs, circulant, 0.0).T
        band = jnp.concatenate([first, second], axis=1)
        high = band.astype(jnp.bfloat16)
        low = (band - high.astype(jnp.float32)).astype(jnp.bfloat16)
        for place, part in enumerate((high, high, low, low)):
            weight_ref[cable, pl.ds(place * LANES, LANES), :] = part
        for edge_ref, block in ((left_ref, 0), (right_ref, blocks + 1)):
            sums = scanned(
                [edge_ref[cable, pl.ds(i * SUBLANES, SUBLANES), :] for i in range(groups)]
            )
            store_split(high_ref, low_ref, cable, block, sums)
            totals_ref[pl.ds(block * cables + cable, 1), :] = sums[-1][SUBLANES - 1 :, :]

    def cable_step(cable, accumulated):
        for copy in copies(cable):
            copy.wait()

        def block_step(block, accumulated):
            lanes = pl.ds(pl.multiple_of(block * LANES, LANES), LANES)
            pieces = []
            for i in range(groups):
                rows = pl.ds(i * SUBLANES, SUBLANES)
                turns = wrap_ref[cable, rows, lanes].astype(jnp.float32)
                pieces.append(phase_ref[cable, rows, lanes] + two_pi * turns)
            sums = scanned(pieces)
            store_split(high_ref, low_ref, cable, block + 1, sums)
            totals_ref[pl.ds((block + 1) * cables + cable, 1), :] = sums[-1][SUBLANES - 1 :, :]
            return tuple(a + b for a, b in zip(accumulated, sums))

        return lax.fori_loop(0, blocks, block_step, accumulated, unroll=4)

    zeros = tuple(jnp.zeros((SUBLANES, LANES), jnp.float32) for _ in range(groups))
    accumulated = lax.fori_loop(0, cables, cable_step, zeros)
    lane = lax.broadcasted_iota(jnp.int32, (SUBLANES, LANES), 1)
    tile = jnp.zeros((SUBLANES, LANES), jnp.float32)
    for i, value in enumerate(accumulated):
        tile = jnp.where(lane == i, jnp.sum(value, axis=1, keepdims=True), tile)
    sums_ref[...] = tile


def filter_kernel(high_ref, low_ref, weight_ref, local_ref):
    cables, extended, time, _ = high_ref.shape
    half = LANES // 2
    lane = lax.broadcasted_iota(jnp.int32, (time, LANES), 1)

    @pl.loop(0, cables)
    def _(cable):
        weight = weight_ref[cable]
        high = high_ref[cable].reshape(extended * time, LANES)
        low = low_ref[cable].reshape(extended * time, LANES)
        product = jnp.dot(
            jnp.concatenate([high, low, high, low], axis=1),
            weight,
            preferred_element_type=jnp.float32,
        )
        previous = None
        for block in range(extended - 1):
            here = product[block * time : (block + 1) * time, :LANES]
            there = product[(block + 1) * time : (block + 2) * time, LANES:]
            rolled = pltpu.roll(here + there, half, 1)
            if block > 0:
                local_ref[cable, block - 1] = jnp.where(lane < half, previous, rolled)
            previous = rolled


def level_kernel(
    population, local_ref, weight_ref, offsets_refs, sums_ref, coupling_ref, place_ref, out_hbm,
    stage_ref, bias_ref, slope_ref, sem,
):
    cables, blocks, time, _ = local_ref.shape
    groups = time // SUBLANES
    extended = blocks + 2
    half = LANES // 2
    position, steps = place_ref[0], sums_ref.shape[0]
    is_first, is_last = place_ref[1], place_ref[2]

    own = jnp.zeros((SUBLANES, LANES), jnp.float32)
    before = jnp.zeros((SUBLANES, LANES), jnp.float32)
    for step in range(steps):
        gathered = jnp.sum(sums_ref[step], axis=0)
        own = own + jnp.where(position == step, gathered, 0.0)
        before = before + jnp.where(position > step, gathered, 0.0)
    earlier = before[SUBLANES - 1 :, groups - 1 : groups]
    common = (own + earlier) * (1.0 / population)
    columns = [
        jnp.broadcast_to(common[:, i : i + 1], (SUBLANES, LANES)) for i in range(groups)
    ]
    padded = -(-(extended + 1) // SUBLANES) * SUBLANES
    row = lax.broadcasted_iota(jnp.int32, (padded, LANES), 0)
    lane = lax.broadcasted_iota(jnp.int32, (padded, LANES), 1)
    inside_first = jnp.where((row == 0) & (is_first == 1), 0.0, 1.0)
    inside_last = jnp.where((row == extended - 2) & (is_last == 1), 0.0, 1.0)

    def merged(value):
        rolled = pltpu.roll(value, half, 1)
        return jnp.where(lane < half, rolled, pltpu.roll(rolled, padded - 1, 0))

    def cable_step(cable, carry):
        offset = None
        for ref in offsets_refs:
            value = ref[pl.ds(cable, extended, stride=cables), :]
            offset = value if offset is None else offset + value
        offset = jnp.concatenate(
            [offset, jnp.ones((padded - extended, LANES), jnp.float32)], axis=0
        )
        high = offset.astype(jnp.bfloat16)
        low = (offset - high.astype(jnp.float32)).astype(jnp.bfloat16)
        product = jnp.dot(
            jnp.concatenate([high, low, high, low], axis=1),
            weight_ref[cable],
            preferred_element_type=jnp.float32,
        )
        here, there = product[:, :LANES], product[:, LANES:]
        bias_ref[...] = merged(here + pltpu.roll(there, padded - 1, 0))
        ones_here = here[extended : extended + 1, :]
        ones_there = there[extended : extended + 1, :]
        slope_ref[...] = merged(ones_here * inside_first + ones_there * inside_last)
        scale = coupling_ref[cable]
        shifts = [scale * column for column in columns]

        def block_step(block, carry):
            lanes = pl.ds(pl.multiple_of(block * LANES, LANES), LANES)
            bias = jnp.broadcast_to(bias_ref[pl.ds(block, 1), :], (SUBLANES, LANES))
            slope = jnp.broadcast_to(slope_ref[pl.ds(block, 1), :], (SUBLANES, LANES))
            for i in range(groups):
                value = local_ref[cable, block, pl.ds(i * SUBLANES, SUBLANES), :]
                stage_ref[cable, pl.ds(i * SUBLANES, SUBLANES), lanes] = value + (
                    bias - shifts[i] * slope
                )
            return carry

        lax.fori_loop(0, blocks, block_step, 0, unroll=4)
        pltpu.make_async_copy(stage_ref.at[cable], out_hbm.at[cable], sem.at[cable]).start()
        return carry

    lax.fori_loop(0, cables, cable_step, 0)
    for cable in range(cables):
        pltpu.make_async_copy(stage_ref.at[cable], out_hbm.at[cable], sem.at[cable]).wait()


def edge_increment(phase_step, wrap_count, start):
    phase = lax.slice_in_dim(phase_step, start, start + LANES, axis=2)
    turns = lax.slice_in_dim(wrap_count, start, start + LANES, axis=2)
    return phase + two_pi * turns.astype(jnp.float32)


def shards(phase_step, wrap_count, coupling, filter_taps):
    cables, time, width = phase_step.shape
    blocks = width // LANES
    extended = blocks + 2
    groups = time // SUBLANES
    steps, places = lax.axis_size("tm"), lax.axis_size("chan")
    step, place = lax.axis_index("tm"), lax.axis_index("chan")

    forward = [(i, i + 1) for i in range(places - 1)]
    backward = [(target, source) for source, target in forward]
    left = lax.ppermute(
        edge_increment(phase_step, wrap_count, width - LANES), "chan", forward
    )
    right = lax.ppermute(edge_increment(phase_step, wrap_count, 0), "chan", backward)

    whole = pl.BlockSpec(memory_space=pltpu.VMEM)
    outside = pl.BlockSpec(memory_space=pl.ANY)
    scalars = pl.BlockSpec(memory_space=pltpu.SMEM)
    high, low, totals, sums, weight = pl.pallas_call(
        unwrap_kernel,
        out_shape=(
            pltpu.VMEM((cables, extended, time, LANES), jnp.bfloat16),
            pltpu.VMEM((cables, extended, time, LANES), jnp.bfloat16),
            jax.ShapeDtypeStruct((extended * cables, LANES), jnp.float32),
            jax.ShapeDtypeStruct((SUBLANES, LANES), jnp.float32),
            pltpu.VMEM((cables, 4 * LANES, 2 * LANES), jnp.bfloat16),
        ),
        in_specs=[outside, outside, whole, whole, whole],
        out_specs=[whole] * 5,
        scratch_shapes=[
            pltpu.VMEM((cables, time, width), jnp.float32),
            pltpu.VMEM((cables, time, width), jnp.int32),
            pltpu.SemaphoreType.DMA((2, cables)),
        ],
        compiler_params=pltpu.CompilerParams(vmem_limit_bytes=40 << 20),
        name="unwrap",
    )(phase_step, wrap_count, left, right, filter_taps)

    received = []
    running = totals
    reach = 1
    while reach < steps:
        later = [(i, i + reach) for i in range(steps - reach)]
        received.append(lax.ppermute(running, "tm", later))
        running = running + received[-1]
        reach *= 2

    copies = jnp.broadcast_to(sums[None], (steps * places, SUBLANES, LANES))
    gathered = lax.all_to_all(copies, ("tm", "chan"), 0, 0, tiled=True)
    gathered = gathered.reshape(steps, places, SUBLANES, LANES)

    local = pl.pallas_call(
        filter_kernel,
        out_shape=pltpu.VMEM((cables, blocks, time, LANES), jnp.float32),
        in_specs=[whole] * 3,
        out_specs=whole,
        compiler_params=pltpu.CompilerParams(vmem_limit_bytes=24 << 20),
        cost_estimate=pl.CostEstimate(
            flops=2 * cables * extended * time * 512 * 256, bytes_accessed=1 << 20, transcendentals=0
        ),
        name="filter",
    )(high, low, weight)

    marks = jnp.stack([step, (place == 0).astype(jnp.int32), (place == places - 1).astype(jnp.int32)])
    population = cables * width * places
    return pl.pallas_call(
        functools.partial(level_kernel, population),
        out_shape=jax.ShapeDtypeStruct(phase_step.shape, jnp.float32),
        in_specs=[whole, whole, [whole] * len(received), whole, scalars, scalars],
        out_specs=outside,
        scratch_shapes=[
            pltpu.VMEM((cables, time, width), jnp.float32),
            pltpu.VMEM((-(-(extended + 1) // SUBLANES) * SUBLANES, LANES), jnp.float32),
            pltpu.VMEM((-(-(extended + 1) // SUBLANES) * SUBLANES, LANES), jnp.float32),
            pltpu.SemaphoreType.DMA((cables,)),
        ],
        compiler_params=pltpu.CompilerParams(vmem_limit_bytes=24 << 20),
        name="level",
    )(local, weight, received, gathered, coupling, marks)


def solution(mesh):
    placed = (P(None, "tm", "chan"), P(None, "tm", "chan"), P(), P())
    return jax.shard_map(
        shards, mesh=mesh, in_specs=placed, out_specs=P(None, "tm", "chan"), check_vma=False
    )
```

time: 713 us -> 62.6 us (0.09)
  matrix products: 586 us -> 0 us
  other arithmetic: 53.2 us -> 1.37 us
  blocking collectives: 29.7 us -> 0 us
  Pallas kernels: 0 us -> 19.1 us
  starting transfers between devices: 2.82 us -> 20.6 us
  local copies, waits for them, and re-layouts: 32.6 us -> 16.8 us
    slice x1 -> x0, matrix products: 586 us -> none  [shards(): filtered = spatial_filter(padded, filter_taps)[:, :, :width]]
    pallas_call x0 -> x3, Pallas kernels: none -> 19.1 us  [the longest x1 7.46 us: shards(): pl.pallas_call(unwrap_kernel, out_shape=(pltpu.VMEM((cables, extended, ti...]
    all_gather x1 -> x0, blocking collectives: 17.5 us -> none  [earlier_blocks(): gathered = lax.all_gather(totals[None], 'tm', axis=0, tiled=True)]
    another operation x1 -> x0, local copies, waits for them, and re-layouts: 13.4 us -> none  [shards(): partial_value = jnp.cumsum(increment, axis=1)]
    mul x1 -> x0, local copies, waits for them, and re-layouts: 12.7 us -> none  [shards(): return (leveled - filtered) * (1.0 / (4.0 * two_pi))]
    psum x1 -> x0, blocking collectives: 12.2 us -> none  [shards(): mode_sums = lax.psum(jnp.sum(unwrapped, axis=(0, 2)), 'chan')]
    another operation x1, other arithmetic: 11.5 us -> 0.08 us  [shards(): jnp.stack([step, (place == 0).astype(jnp.int32), (place == places - 1).as...]
    sub x1 -> x0, other arithmetic: 11.1 us -> none  [shards(): leveled = unwrapped - shifted]
  transfers between devices with their start and end apart: 2 -> 5, of which waited for: 1 -> 1; matrix products, arithmetic and copies ran while one was open for 0% -> 1% of each run, Pallas kernels for 0% -> 10%
where the time goes in v1:
time: 62.6 us; the launch traced here: 62.2 us
  starting transfers between devices  20.6 us (33%)
  Pallas kernels  19.1 us (31%)
  local copies, waits for them, and re-layouts  16.8 us (27%)
  waiting for transfers between devices  4.22 us (7%)
  other arithmetic  1.37 us (2%)
    unnamed x16, local copies, waits for them, and re-layouts  16.1 us
    all_to_all x1, starting transfers between devices, shards(): gathered = lax.all_to_all(copies, ('tm', 'chan'), 0, 0, tiled=True)  8.86 us
    ppermute x2, starting transfers between devices, shards(): received.append(lax.ppermute(running, 'tm', later))  8.06 us
    pallas_call x1, Pallas kernels, shards(): pl.pallas_call(unwrap_kernel, out_shape=(pltpu.VMEM((cables, extended, ti...  7.46 us
    pallas_call x1, Pallas kernels, shards(): pl.pallas_call(filter_kernel, out_shape=pltpu.VMEM((cables, blocks, time,...  6.46 us
    pallas_call x1, Pallas kernels, shards(): pl.pallas_call(functools.partial(level_kernel, population), out_shape=jax...  5.19 us
    ppermute x1, waiting for transfers between devices, shards(): lax.ppermute(edge_increment(phase_step, wrap_count, 0), 'chan', backward)  4.21 us
    ppermute x1, starting transfers between devices, shards(): lax.ppermute(edge_increment(phase_step, wrap_count, width - LANES), 'chan...  2.37 us
  transfers between devices with their start and end apart: 5, of which 1 were waited for; matrix products, arithmetic and copies ran while one was open for 1% of the time, Pallas kernels for 10%

profile of v1, /device:TPU:0, one launch (start us, length us, event | category | flops | bytes accessed | tf_op | source)
XLA Modules:
  0.0 62.2 jit_solution(18278529282749093004)
XLA Ops:
  0.0 1.3 %multiply_add_fusion = (f32[8,64,128]{2,1,0:T(8,128)S(1)}, f32[8,64,128]{2,1,0:T(8,128)S(1)}) fusion(s32[8,64,4096]{2,1,0:T(8,128)} %wrap_hbm.1, f32[8,64,4096]{2,1,0:T(8,128)} %phase_hbm.1), kind=kLoop, calls=%fused_computation | loop fusion | flops 393216 | bytes 1572864 | tf_op jit(solution)/shard_map/add | solution.py:218
  1.3 2.4 %collective-permute-start = (f32[8,64,128]{2,1,0:T(8,128)S(1)}, f32[8,64,128]{2,1,0:T(8,128)S(1)}, u32[]{:S(2)}, u32[]{:S(2)}) collective-permute-start(f32[8,64,128]{2,1,0:T(8,128)S(1)} %get-tuple-element.16), channel_id=1, source_target_pairs={{0,1},{1,2},{2,3},{3,4},{4,5},{5,6},{6,7},{8,9},{9,10},{10,11},{11... | collective-permute-start | bytes 786440 | tf_op jit(solution)/shard_map/ppermute | solution.py:231
  3.7 1.3 %collective-permute-start.1 = (f32[8,64,128]{2,1,0:T(8,128)S(1)}, f32[8,64,128]{2,1,0:T(8,128)S(1)}, u32[]{:S(2)}, u32[]{:S(2)}) collective-permute-start(f32[8,64,128]{2,1,0:T(8,128)S(1)} %get-tuple-element.15), channel_id=1, source_target_pairs={{1,0},{2,1},{3,2},{4,3},{5,4},{6,5},{7,6},{9,8},{10,9},{11,10},{12... | collective-permute-start | bytes 786440 | tf_op jit(solution)/shard_map/ppermute | solution.py:234
  5.0 0.0 collective-permute-done.left_ref
  5.0 4.2 %collective-permute-done.1.right_ref = f32[8,64,128]{2,1,0:T(8,128)S(1)} collective-permute-done((f32[8,64,128]{2,1,0:T(8,128)S(1)}, f32[8,64,128]{2,1,0:T(8,128)S(1)}, u32[]{:S(2)}, u32[]{:S(2)}) %collective-permute-start.1) | collective-permute-done | bytes 262176 | tf_op jit(solution)/shard_map/ppermute | solution.py:234
  9.2 0.7 %copy-done.6 = f32[8,128]{1,0:T(8,128)S(1)} copy-done((f32[8,128]{1,0:T(8,128)S(1)}, f32[8,128]{1,0:T(8,128)}, u32[]{:S(2)}) %copy-start.6) | copy-done | bytes 4120
  9.9 7.5 %unwrap.1 = (bf16[8,34,64,128]{3,2,1,0:T(8,128)(2,1)S(1)}, bf16[8,34,64,128]{3,2,1,0:T(8,128)(2,1)S(1)}, f32[272,128]{1,0:T(8,128)S(1)}, f32[8,128]{1,0:T(8,128)S(1)}, bf16[8,512,256]{2,1,0:T(8,128)(2,1)S(1)}) custom-call(f32[8,64,4096]{2,1,0:T(8,128)} %phase_hbm.1, s32[8,64,4096]{2,1,0:T(8,128)} %wrap_hbm.1, ...), custom_call_target="tpu_custom_call" | custom-call | tf_op jit(solution)/shard_map/unwrap/pallas_call | solution.py:239
  17.3 0.0 copy-start.2
  17.4 2.1 %copy-done.2 = bf16[8,34,64,128]{3,2,1,0:T(8,128)(2,1)} copy-done((bf16[8,34,64,128]{3,2,1,0:T(8,128)(2,1)}, bf16[8,34,64,128]{3,2,1,0:T(8,128)(2,1)S(1)}, u32[]{:S(2)}) %copy-start.2) | copy-done | bytes 4456472
  19.4 2.0 %copy-done.4 = bf16[8,34,64,128]{3,2,1,0:T(8,128)(2,1)} copy-done((bf16[8,34,64,128]{3,2,1,0:T(8,128)(2,1)}, bf16[8,34,64,128]{3,2,1,0:T(8,128)(2,1)S(1)}, u32[]{:S(2)}) %copy-start.4) | copy-done | bytes 4456472
  21.5 3.5 %collective-permute-start.2 = (f32[272,128]{1,0:T(8,128)S(1)}, f32[272,128]{1,0:T(8,128)S(1)}, u32[]{:S(2)}, u32[]{:S(2)}) collective-permute-start(f32[272,128]{1,0:T(8,128)S(1)} %get-tuple-element.13), channel_id=1, source_target_pairs={{0,8},{8,16},{16,24},{1,9},{9,17},{17,25},{2,10},{10,18},{18,26},{... | collective-permute-start | bytes 417800 | tf_op jit(solution)/shard_map/ppermute | solution.py:264
  25.0 0.1 pad_add_fusion.place_ref
  25.1 0.7 %broadcast_in_dim.2 = f32[32,8,128]{2,1,0:T(8,128)} broadcast(f32[8,128]{1,0:T(8,128)S(1)} %get-tuple-element.14), dimensions={1,2} | broadcast | bytes 135168 | tf_op jit(solution)/shard_map/broadcast_in_dim | solution.py:268
  25.7 8.9 %all-to-all-start = ((f32[32,8,128]{2,1,0:T(8,128)}), f32[32,8,128]{2,1,0:T(8,128)S(1)}, u32[]{:S(2)}, u32[]{:S(2)}) async-start(f32[32,8,128]{2,1,0:T(8,128)} %broadcast_in_dim.2), calls=%async_computation | async-start | bytes 262144 | tf_op jit(solution)/shard_map/all_to_all | solution.py:269
  34.6 0.0 collective-permute-done.2.offsets_refs_0_
  34.6 4.6 %collective-permute-start.3 = (f32[272,128]{1,0:T(8,128)S(1)}, f32[272,128]{1,0:T(8,128)S(1)}, u32[]{:S(2)}, u32[]{:S(2)}) collective-permute-start(f32[272,128]{1,0:T(8,128)S(1)} %add.11), channel_id=1, source_target_pairs={{0,16},{8,24},{1,17},{9,25},{2,18},{10,26},{3,19},{11,27},{4,20},{... | collective-permute-start | bytes 417800 | tf_op jit(solution)/shard_map/ppermute | solution.py:264
  39.2 0.0 copy-start.3
  39.2 2.3 %copy-done.3 = bf16[8,34,64,128]{3,2,1,0:T(8,128)(2,1)S(1)} copy-done((bf16[8,34,64,128]{3,2,1,0:T(8,128)(2,1)S(1)}, bf16[8,34,64,128]{3,2,1,0:T(8,128)(2,1)}, u32[]{:S(2)}) %copy-start.3) | copy-done | bytes 4456472
  41.5 2.3 %copy-done.5 = bf16[8,34,64,128]{3,2,1,0:T(8,128)(2,1)S(1)} copy-done((bf16[8,34,64,128]{3,2,1,0:T(8,128)(2,1)S(1)}, bf16[8,34,64,128]{3,2,1,0:T(8,128)(2,1)}, u32[]{:S(2)}) %copy-start.5) | copy-done | bytes 4456472
  43.8 6.5 %filter.1.local_ref = f32[8,32,64,128]{3,2,1,0:T(8,128)S(1)} custom-call(bf16[8,34,64,128]{3,2,1,0:T(8,128)(2,1)S(1)} %copy-done.3, bf16[8,34,64,128]{3,2,1,0:T(8,128)(2,1)S(1)} %copy-done.5, bf16[8,512,256]{2,1,0:T(8,128)(2,1)S(1)} %get-tuple-element.12.weight_ref), custom_call_target="tpu_custom_call" | custom-call | flops 4563402752 | bytes 1048576 | tf_op jit(solution)/shard_map/filter/pallas_call | solution.py:272
  50.2 0.0 copy-start
  50.2 3.4 %copy-done = f32[8,32,64,128]{3,2,1,0:T(8,128)} copy-done((f32[8,32,64,128]{3,2,1,0:T(8,128)}, f32[8,32,64,128]{3,2,1,0:T(8,128)S(1)}, u32[]{:S(2)}) %copy-start) | copy-done | bytes 8388632
  53.6 3.4 %copy-done.1 = f32[8,32,64,128]{3,2,1,0:T(8,128)S(1)} copy-done((f32[8,32,64,128]{3,2,1,0:T(8,128)S(1)}, f32[8,32,64,128]{3,2,1,0:T(8,128)}, u32[]{:S(2)}) %copy-start.1) | copy-done | bytes 8388632
  57.0 5.2 %level.1 = f32[8,64,4096]{2,1,0:T(8,128)} custom-call(f32[8,32,64,128]{3,2,1,0:T(8,128)S(1)} %copy-done.1, bf16[8,512,256]{2,1,0:T(8,128)(2,1)S(1)} %get-tuple-element.12.weight_ref, f32[272,128]{1,0:T(8,128)S(1)} %collective-permute-done.2.offsets_refs_0_, f32[272,128]{1,0:T(8,128)S(1)} %collective-permute-done.3.offsets_refs_1_, ...), custom_call_target="tpu_custom_call" | custom-call | tf_op jit(solution)/shard_map/level/pallas_call | solution.py:286
  (9 shorter events, 0.0 us)
Async XLA Ops:
  1.3 3.7 %collective-permute-start = (f32[8,64,128]{2,1,0:T(8,128)S(1)}, f32[8,64,128]{2,1,0:T(8,128)S(1)}, u32[]{:S(2)}, u32[]{:S(2)}) collective-permute-start(f32[8,64,128]{2,1,0:T(8,128)S(1)} %get-tuple-element.16), channel_id=1, source_target_pairs={{0,1},{1,2},{2,3},{3,4},{4,5},{5,6},{6,7},{8,9},{9,10},{10,11},{11... | collective-permute-start | bytes 786440 | tf_op jit(solution)/shard_map/ppermute | solution.py:231
  3.7 5.5 %collective-permute-start.1 = (f32[8,64,128]{2,1,0:T(8,128)S(1)}, f32[8,64,128]{2,1,0:T(8,128)S(1)}, u32[]{:S(2)}, u32[]{:S(2)}) collective-permute-start(f32[8,64,128]{2,1,0:T(8,128)S(1)} %get-tuple-element.15), channel_id=1, source_target_pairs={{1,0},{2,1},{3,2},{4,3},{5,4},{6,5},{7,6},{9,8},{10,9},{11,10},{12... | collective-permute-start | bytes 786440 | tf_op jit(solution)/shard_map/ppermute | solution.py:234
  9.2 0.7 %copy-start.6 = (f32[8,128]{1,0:T(8,128)S(1)}, f32[8,128]{1,0:T(8,128)}, u32[]{:S(2)}) copy-start(f32[8,128]{1,0:T(8,128)} %taps_ref.1) | copy-start | bytes 12292
  17.3 2.1 %copy-start.2 = (bf16[8,34,64,128]{3,2,1,0:T(8,128)(2,1)}, bf16[8,34,64,128]{3,2,1,0:T(8,128)(2,1)S(1)}, u32[]{:S(2)}) copy-start(bf16[8,34,64,128]{3,2,1,0:T(8,128)(2,1)S(1)} %get-tuple-element.10.high_ref) | copy-start | bytes 13369348
  19.4 2.0 %copy-start.4 = (bf16[8,34,64,128]{3,2,1,0:T(8,128)(2,1)}, bf16[8,34,64,128]{3,2,1,0:T(8,128)(2,1)S(1)}, u32[]{:S(2)}) copy-start(bf16[8,34,64,128]{3,2,1,0:T(8,128)(2,1)S(1)} %get-tuple-element.11.low_ref) | copy-start | bytes 13369348
  21.5 13.1 %collective-permute-start.2 = (f32[272,128]{1,0:T(8,128)S(1)}, f32[272,128]{1,0:T(8,128)S(1)}, u32[]{:S(2)}, u32[]{:S(2)}) collective-permute-start(f32[272,128]{1,0:T(8,128)S(1)} %get-tuple-element.13), channel_id=1, source_target_pairs={{0,8},{8,16},{16,24},{1,9},{9,17},{17,25},{2,10},{10,18},{18,26},{... | collective-permute-start | bytes 417800 | tf_op jit(solution)/shard_map/ppermute | solution.py:264
  25.7 27.9 %all-to-all-start = ((f32[32,8,128]{2,1,0:T(8,128)}), f32[32,8,128]{2,1,0:T(8,128)S(1)}, u32[]{:S(2)}, u32[]{:S(2)}) async-start(f32[32,8,128]{2,1,0:T(8,128)} %broadcast_in_dim.2), calls=%async_computation | async-start | bytes 262144 | tf_op jit(solution)/shard_map/all_to_all | solution.py:269
  34.6 19.0 %collective-permute-start.3 = (f32[272,128]{1,0:T(8,128)S(1)}, f32[272,128]{1,0:T(8,128)S(1)}, u32[]{:S(2)}, u32[]{:S(2)}) collective-permute-start(f32[272,128]{1,0:T(8,128)S(1)} %add.11), channel_id=1, source_target_pairs={{0,16},{8,24},{1,17},{9,25},{2,18},{10,26},{3,19},{11,27},{4,20},{... | collective-permute-start | bytes 417800 | tf_op jit(solution)/shard_map/ppermute | solution.py:264
  39.2 2.3 %copy-start.3 = (bf16[8,34,64,128]{3,2,1,0:T(8,128)(2,1)S(1)}, bf16[8,34,64,128]{3,2,1,0:T(8,128)(2,1)}, u32[]{:S(2)}) copy-start(bf16[8,34,64,128]{3,2,1,0:T(8,128)(2,1)} %copy-done.2) | copy-start | bytes 13369348
  41.5 2.3 %copy-start.5 = (bf16[8,34,64,128]{3,2,1,0:T(8,128)(2,1)S(1)}, bf16[8,34,64,128]{3,2,1,0:T(8,128)(2,1)}, u32[]{:S(2)}) copy-start(bf16[8,34,64,128]{3,2,1,0:T(8,128)(2,1)} %copy-done.4) | copy-start | bytes 13369348
  43.8 9.9 %copy-start.7 = (f32[8]{0:T(128)S(1)}, f32[8]{0:T(128)}, u32[]{:S(2)}) copy-start(f32[8]{0:T(128)} %coupling_ref.1) | copy-start | bytes 100
  50.2 3.4 %copy-start = (f32[8,32,64,128]{3,2,1,0:T(8,128)}, f32[8,32,64,128]{3,2,1,0:T(8,128)S(1)}, u32[]{:S(2)}) copy-start(f32[8,32,64,128]{3,2,1,0:T(8,128)S(1)} %filter.1.local_ref) | copy-start | bytes 25165828
  53.6 3.4 %copy-start.1 = (f32[8,32,64,128]{3,2,1,0:T(8,128)S(1)}, f32[8,32,64,128]{3,2,1,0:T(8,128)}, u32[]{:S(2)}) copy-start(f32[8,32,64,128]{3,2,1,0:T(8,128)} %copy-done) | copy-start | bytes 25165828

commit v2 on v1

--- a/solution.py
+++ b/solution.py
@@ -42,8 +42,29 @@
         low_ref[cable, block, rows, :] = low
 
 
+def edges_kernel(phase_hbm, wrap_hbm, inner_ref, outer_ref, phase_ref, wrap_ref, sem):
+    width = phase_hbm.shape[2]
+    is_even = lax.rem(lax.axis_index("chan"), 2) == 0
+    lowest = 0
+    highest = width - LANES
+    starts = (jnp.where(is_even, highest, lowest), jnp.where(is_even, lowest, highest))
+    copies = []
+    for side, start in enumerate(starts):
+        lanes = pl.ds(pl.multiple_of(start, LANES), LANES)
+        for kind, (source, target) in enumerate(((phase_hbm, phase_ref), (wrap_hbm, wrap_ref))):
+            copies.append(
+                pltpu.make_async_copy(source.at[:, :, lanes], target.at[side], sem.at[kind, side])
+            )
+    for copy in copies:
+        copy.start()
+    for copy in copies:
+        copy.wait()
+    for side, target in enumerate((inner_ref, outer_ref)):
+        target[...] = phase_ref[side] + two_pi * wrap_ref[side].astype(jnp.float32)
+
+
 def unwrap_kernel(
-    phase_hbm, wrap_hbm, left_ref, right_ref, taps_ref,
+    phase_hbm, wrap_hbm, inner_ref, outer_ref, taps_ref,
     high_ref, low_ref, totals_ref, sums_ref, weight_ref,
     phase_ref, wrap_ref, sem,
 ):
@@ -61,6 +82,7 @@
         for copy in copies(cable):
             copy.start()
 
+    is_even = lax.rem(lax.axis_index("chan"), 2) == 0
     outputs = lax.broadcasted_iota(jnp.int32, (LANES, LANES), 0)
     inputs = lax.broadcasted_iota(jnp.int32, (LANES, LANES), 1)
     centre = (lax.broadcasted_iota(jnp.int32, (1, LANES), 1) == LANES // 2).astype(jnp.float32)
@@ -78,10 +100,14 @@
         low = (band - high.astype(jnp.float32)).astype(jnp.bfloat16)
         for place, part in enumerate((high, high, low, low)):
             weight_ref[cable, pl.ds(place * LANES, LANES), :] = part
-        for edge_ref, block in ((left_ref, 0), (right_ref, blocks + 1)):
-            sums = scanned(
-                [edge_ref[cable, pl.ds(i * SUBLANES, SUBLANES), :] for i in range(groups)]
-            )
+        for flip, block in ((is_even, 0), (jnp.logical_not(is_even), blocks + 1)):
+            pieces = []
+            for i in range(groups):
+                rows = pl.ds(i * SUBLANES, SUBLANES)
+                pieces.append(
+                    jnp.where(flip, outer_ref[cable, rows, :], inner_ref[cable, rows, :])
+                )
+            sums = scanned(pieces)
             store_split(high_ref, low_ref, cable, block, sums)
             totals_ref[pl.ds(block * cables + cable, 1), :] = sums[-1][SUBLANES - 1 :, :]
 
@@ -138,42 +164,38 @@
 
 
 def level_kernel(
-    population, local_ref, weight_ref, offsets_refs, sums_ref, coupling_ref, place_ref, out_hbm,
-    stage_ref, bias_ref, slope_ref, sem,
+    population, local_ref, weight_ref, swapped_refs, sums_ref, coupling_ref,
+    out_hbm, stage_ref, offset_ref, bias_ref, slope_ref, sem,
 ):
     cables, blocks, time, _ = local_ref.shape
     groups = time // SUBLANES
     extended = blocks + 2
     half = LANES // 2
-    position, steps = place_ref[0], sums_ref.shape[0]
-    is_first, is_last = place_ref[1], place_ref[2]
-
-    own = jnp.zeros((SUBLANES, LANES), jnp.float32)
-    before = jnp.zeros((SUBLANES, LANES), jnp.float32)
-    for step in range(steps):
-        gathered = jnp.sum(sums_ref[step], axis=0)
-        own = own + jnp.where(position == step, gathered, 0.0)
-        before = before + jnp.where(position > step, gathered, 0.0)
-    earlier = before[SUBLANES - 1 :, groups - 1 : groups]
-    common = (own + earlier) * (1.0 / population)
+    step, place = lax.axis_index("tm"), lax.axis_index("chan")
+    is_first = place == 0
+    is_last = place == lax.axis_size("chan") - 1
+
+    offset = jnp.zeros(offset_ref.shape, jnp.float32)
+    for bit, ref in enumerate(swapped_refs):
+        offset = offset + jnp.where((step & (1 << bit)) != 0, ref[...], 0.0)
+    offset_ref[...] = offset
+    earlier = offset[extended * cables + SUBLANES - 1 :, groups - 1 : groups]
+    common = (sums_ref[...] + earlier) * (1.0 / population)
     columns = [
         jnp.broadcast_to(common[:, i : i + 1], (SUBLANES, LANES)) for i in range(groups)
     ]
     padded = -(-(extended + 1) // SUBLANES) * SUBLANES
     row = lax.broadcasted_iota(jnp.int32, (padded, LANES), 0)
     lane = lax.broadcasted_iota(jnp.int32, (padded, LANES), 1)
-    inside_first = jnp.where((row == 0) & (is_first == 1), 0.0, 1.0)
-    inside_last = jnp.where((row == extended - 2) & (is_last == 1), 0.0, 1.0)
+    inside_first = jnp.where((row == 0) & is_first, 0.0, 1.0)
+    inside_last = jnp.where((row == extended - 2) & is_last, 0.0, 1.0)
 
     def merged(value):
         rolled = pltpu.roll(value, half, 1)
         return jnp.where(lane < half, rolled, pltpu.roll(rolled, padded - 1, 0))
 
     def cable_step(cable, carry):
-        offset = None
-        for ref in offsets_refs:
-            value = ref[pl.ds(cable, extended, stride=cables), :]
-            offset = value if offset is None else offset + value
+        offset = offset_ref[pl.ds(cable, extended, stride=cables), :]
         offset = jnp.concatenate(
             [offset, jnp.ones((padded - extended, LANES), jnp.float32)], axis=0
         )
@@ -212,30 +234,41 @@
         pltpu.make_async_copy(stage_ref.at[cable], out_hbm.at[cable], sem.at[cable]).wait()
 
 
-def edge_increment(phase_step, wrap_count, start):
-    phase = lax.slice_in_dim(phase_step, start, start + LANES, axis=2)
-    turns = lax.slice_in_dim(wrap_count, start, start + LANES, axis=2)
-    return phase + two_pi * turns.astype(jnp.float32)
+def swapped(value, axis, bit):
+    return lax.ppermute(value, axis, [(i, i ^ bit) for i in range(lax.axis_size(axis))])
 
 
 def shards(phase_step, wrap_count, coupling, filter_taps):
     cables, time, width = phase_step.shape
     blocks = width // LANES
     extended = blocks + 2
-    groups = time // SUBLANES
+    phase_step = pltpu.with_memory_space_constraint(phase_step, pltpu.HBM)
+    wrap_count = pltpu.with_memory_space_constraint(wrap_count, pltpu.HBM)
     steps, places = lax.axis_size("tm"), lax.axis_size("chan")
-    step, place = lax.axis_index("tm"), lax.axis_index("chan")
-
-    forward = [(i, i + 1) for i in range(places - 1)]
-    backward = [(target, source) for source, target in forward]
-    left = lax.ppermute(
-        edge_increment(phase_step, wrap_count, width - LANES), "chan", forward
-    )
-    right = lax.ppermute(edge_increment(phase_step, wrap_count, 0), "chan", backward)
 
     whole = pl.BlockSpec(memory_space=pltpu.VMEM)
     outside = pl.BlockSpec(memory_space=pl.ANY)
     scalars = pl.BlockSpec(memory_space=pltpu.SMEM)
+    inner, outer = pl.pallas_call(
+        edges_kernel,
+        out_shape=[pltpu.VMEM((cables, time, LANES), jnp.float32)] * 2,
+        in_specs=[outside] * 2,
+        out_specs=[whole] * 2,
+        scratch_shapes=[
+            pltpu.VMEM((2, cables, time, LANES), jnp.float32),
+            pltpu.VMEM((2, cables, time, LANES), jnp.int32),
+            pltpu.SemaphoreType.DMA((2, 2)),
+        ],
+        compiler_params=pltpu.CompilerParams(vmem_limit_bytes=8 << 20),
+        name="edges",
+    )(phase_step, wrap_count)
+    inner = swapped(inner, "chan", 1)
+    outer = lax.ppermute(
+        outer,
+        "chan",
+        [(i, i + 1) for i in range(1, places - 1, 2)] + [(i + 1, i) for i in range(1, places - 1, 2)],
+    )
+
     high, low, totals, sums, weight = pl.pallas_call(
         unwrap_kernel,
         out_shape=(
@@ -254,20 +287,15 @@
         ],
         compiler_params=pltpu.CompilerParams(vmem_limit_bytes=40 << 20),
         name="unwrap",
-    )(phase_step, wrap_count, left, right, filter_taps)
-
+    )(phase_step, wrap_count, inner, outer, filter_taps)
+
+    for bit in range(places.bit_length() - 1):
+        sums = sums + swapped(sums, "chan", 1 << bit)
     received = []
-    running = totals
-    reach = 1
-    while reach < steps:
-        later = [(i, i + reach) for i in range(steps - reach)]
-        received.append(lax.ppermute(running, "tm", later))
+    running = jnp.concatenate([totals, sums], axis=0)
+    for bit in range(steps.bit_length() - 1):
+        received.append(swapped(running, "tm", 1 << bit))
         running = running + received[-1]
-        reach *= 2
-
-    copies = jnp.broadcast_to(sums[None], (steps * places, SUBLANES, LANES))
-    gathered = lax.all_to_all(copies, ("tm", "chan"), 0, 0, tiled=True)
-    gathered = gathered.reshape(steps, places, SUBLANES, LANES)
 
     local = pl.pallas_call(
         filter_kernel,
@@ -281,22 +309,22 @@
         name="filter",
     )(high, low, weight)
 
-    marks = jnp.stack([step, (place == 0).astype(jnp.int32), (place == places - 1).astype(jnp.int32)])
     population = cables * width * places
     return pl.pallas_call(
         functools.partial(level_kernel, population),
         out_shape=jax.ShapeDtypeStruct(phase_step.shape, jnp.float32),
-        in_specs=[whole, whole, [whole] * len(received), whole, scalars, scalars],
+        in_specs=[whole, whole, [whole] * len(received), whole, scalars],
         out_specs=outside,
         scratch_shapes=[
             pltpu.VMEM((cables, time, width), jnp.float32),
+            pltpu.VMEM((extended * cables + SUBLANES, LANES), jnp.float32),
             pltpu.VMEM((-(-(extended + 1) // SUBLANES) * SUBLANES, LANES), jnp.float32),
             pltpu.VMEM((-(-(extended + 1) // SUBLANES) * SUBLANES, LANES), jnp.float32),
             pltpu.SemaphoreType.DMA((cables,)),
         ],
         compiler_params=pltpu.CompilerParams(vmem_limit_bytes=24 << 20),
         name="level",
-    )(local, weight, received, gathered, coupling, marks)
+    )(local, weight, received, sums, coupling)
 
 
 def solution(mesh):

time: 62.6 us -> 49.5 us (0.79)
  local copies, waits for them, and re-layouts: 16.8 us -> 0.01 us
  waiting for transfers between devices: 4.22 us -> 8.22 us
  other arithmetic: 1.37 us -> 0.04 us
  Pallas kernels: 19.1 us -> 20.4 us
    unnamed x16 -> x4, local copies, waits for them, and re-layouts: 16.1 us -> 0.01 us
    ppermute x4 -> x7, starting transfers between devices: 11.7 us -> 20.6 us  [the longest x6 19.9 us: swapped(): lax.ppermute(value, axis, [(i, i ^ bit) for i in range(lax.axis_size(axis...]
    all_to_all x1 -> x0, starting transfers between devices: 8.86 us -> none  [shards(): gathered = lax.all_to_all(copies, ('tm', 'chan'), 0, 0, tiled=True)]
    ppermute x4 -> x7, waiting for transfers between devices: 4.22 us -> 8.22 us  [the longest x6 8.21 us: swapped(): lax.ppermute(value, axis, [(i, i ^ bit) for i in range(lax.axis_size(axis...]
    pallas_call x0 -> x1, Pallas kernels: none -> 1.31 us  [shards(): pl.pallas_call(edges_kernel, out_shape=[pltpu.VMEM((cables, time, LANES),...]
    add x1 -> x3, other arithmetic: 1.28 us -> 0.01 us  [shards(): sums = sums + swapped(sums, 'chan', 1 << bit)]
    broadcast_in_dim x1 -> x0, local copies, waits for them, and re-layouts: 0.66 us -> none  [shards(): copies = jnp.broadcast_to(sums[None], (steps * places, SUBLANES, LANES))]
  transfers between devices with their start and end apart: 5 -> 7, of which waited for: 1 -> 5; matrix products, arithmetic and copies ran while one was open for 1% -> 0% of each run, Pallas kernels for 10% -> 13%
where the time goes in v2:
time: 49.5 us; the launch traced here: 49.4 us
  starting transfers between devices  20.6 us (42%)
  Pallas kernels  20.4 us (41%)
  waiting for transfers between devices  8.22 us (17%)
    ppermute x6, starting transfers between devices, swapped(): lax.ppermute(value, axis, [(i, i ^ bit) for i in range(lax.axis_size(axis...  19.9 us
    ppermute x6, waiting for transfers between devices, swapped(): lax.ppermute(value, axis, [(i, i ^ bit) for i in range(lax.axis_size(axis...  8.21 us
    pallas_call x1, Pallas kernels, shards(): pl.pallas_call(unwrap_kernel, out_shape=(pltpu.VMEM((cables, extended, ti...  7.46 us
    pallas_call x1, Pallas kernels, shards(): pl.pallas_call(filter_kernel, out_shape=pltpu.VMEM((cables, blocks, time,...  6.47 us
    pallas_call x1, Pallas kernels, shards(): pl.pallas_call(functools.partial(level_kernel, population), out_shape=jax...  5.2 us
    pallas_call x1, Pallas kernels, shards(): pl.pallas_call(edges_kernel, out_shape=[pltpu.VMEM((cables, time, LANES),...  1.31 us
  transfers between devices with their start and end apart: 7, of which 5 were waited for; matrix products, arithmetic and copies ran while one was open for 0% of the time, Pallas kernels for 13%

profile of v2, /device:TPU:0, one launch (start us, length us, event | category | flops | bytes accessed | tf_op | source)
XLA Modules:
  0.0 49.4 jit_solution(2172268805603070374)
XLA Ops:
  0.0 0.0 copy-start
  0.0 1.3 %edges.1 = (f32[8,64,128]{2,1,0:T(8,128)S(1)}, f32[8,64,128]{2,1,0:T(8,128)S(1)}) custom-call(f32[8,64,4096]{2,1,0:T(8,128)} %phase_hbm.3, s32[8,64,4096]{2,1,0:T(8,128)} %wrap_hbm.3), custom_call_target="tpu_custom_call" | custom-call | tf_op jit(solution)/shard_map/edges/pallas_call | solution.py:252
  1.3 0.5 %collective-permute-start = (f32[8,64,128]{2,1,0:T(8,128)S(1)}, f32[8,64,128]{2,1,0:T(8,128)S(1)}, u32[]{:S(2)}, u32[]{:S(2)}) collective-permute-start(f32[8,64,128]{2,1,0:T(8,128)S(1)} %get-tuple-element.12), channel_id=1, source_target_pairs={{0,1},{1,0},{2,3},{3,2},{4,5},{5,4},{6,7},{7,6},{8,9},{9,8},{10,11... | collective-permute-start | bytes 786440 | tf_op jit(solution)/shard_map/ppermute | solution.py:238
  1.8 0.7 %collective-permute-start.1 = (f32[8,64,128]{2,1,0:T(8,128)S(1)}, f32[8,64,128]{2,1,0:T(8,128)S(1)}, u32[]{:S(2)}, u32[]{:S(2)}) collective-permute-start(f32[8,64,128]{2,1,0:T(8,128)S(1)} %get-tuple-element.13), channel_id=1, source_target_pairs={{1,2},{3,4},{5,6},{2,1},{4,3},{6,5},{9,10},{11,12},{13,14},{10,9},... | collective-permute-start | bytes 786440 | tf_op jit(solution)/shard_map/ppermute | solution.py:266
  2.5 0.5 collective-permute-done.inner_ref
  3.0 0.0 collective-permute-done.1.outer_ref
  3.0 0.0 copy-done
  3.0 7.5 %unwrap.1 = (bf16[8,34,64,128]{3,2,1,0:T(8,128)(2,1)S(1)}, bf16[8,34,64,128]{3,2,1,0:T(8,128)(2,1)S(1)}, f32[272,128]{1,0:T(8,128)S(1)}, f32[8,128]{1,0:T(8,128)S(1)}, bf16[8,512,256]{2,1,0:T(8,128)(2,1)S(1)}) custom-call(f32[8,64,4096]{2,1,0:T(8,128)} %phase_hbm.3, s32[8,64,4096]{2,1,0:T(8,128)} %wrap_hbm.3, ...), custom_call_target="tpu_custom_call" | custom-call | tf_op jit(solution)/shard_map/unwrap/pallas_call | solution.py:272
  10.5 9.4 %collective-permute-start.2 = (f32[8,128]{1,0:T(8,128)S(1)}, f32[8,128]{1,0:T(8,128)S(1)}, u32[]{:S(2)}, u32[]{:S(2)}) collective-permute-start(f32[8,128]{1,0:T(8,128)S(1)} %get-tuple-element.18), channel_id=1, source_target_pairs={{0,1},{1,0},{2,3},{3,2},{4,5},{5,4},{6,7},{7,6},{8,9},{9,8},{10,11... | collective-permute-start | bytes 12296 | tf_op jit(solution)/shard_map/ppermute | solution.py:238
  19.9 0.8 %collective-permute-done.2 = f32[8,128]{1,0:T(8,128)S(1)} collective-permute-done((f32[8,128]{1,0:T(8,128)S(1)}, f32[8,128]{1,0:T(8,128)S(1)}, u32[]{:S(2)}, u32[]{:S(2)}) %collective-permute-start.2) | collective-permute-done | bytes 4128 | tf_op jit(solution)/shard_map/ppermute | solution.py:238
  20.7 3.3 %collective-permute-start.3 = (f32[8,128]{1,0:T(8,128)S(1)}, f32[8,128]{1,0:T(8,128)S(1)}, u32[]{:S(2)}, u32[]{:S(2)}) collective-permute-start(f32[8,128]{1,0:T(8,128)S(1)} %add.12), channel_id=1, source_target_pairs={{0,2},{1,3},{2,0},{3,1},{4,6},{5,7},{6,4},{7,5},{8,10},{9,11},{10,... | collective-permute-start | bytes 12296 | tf_op jit(solution)/shard_map/ppermute | solution.py:238
  24.0 1.6 %collective-permute-done.3 = f32[8,128]{1,0:T(8,128)S(1)} collective-permute-done((f32[8,128]{1,0:T(8,128)S(1)}, f32[8,128]{1,0:T(8,128)S(1)}, u32[]{:S(2)}, u32[]{:S(2)}) %collective-permute-start.3) | collective-permute-done | bytes 4128 | tf_op jit(solution)/shard_map/ppermute | solution.py:238
  25.6 1.6 %collective-permute-start.4 = (f32[8,128]{1,0:T(8,128)S(1)}, f32[8,128]{1,0:T(8,128)S(1)}, u32[]{:S(2)}, u32[]{:S(2)}) collective-permute-start(f32[8,128]{1,0:T(8,128)S(1)} %add.13), channel_id=1, source_target_pairs={{0,4},{1,5},{2,6},{3,7},{4,0},{5,1},{6,2},{7,3},{8,12},{9,13},{10,... | collective-permute-start | bytes 12296 | tf_op jit(solution)/shard_map/ppermute | solution.py:238
  27.2 2.0 %collective-permute-done.4 = f32[8,128]{1,0:T(8,128)S(1)} collective-permute-done((f32[8,128]{1,0:T(8,128)S(1)}, f32[8,128]{1,0:T(8,128)S(1)}, u32[]{:S(2)}, u32[]{:S(2)}) %collective-permute-start.4) | collective-permute-done | bytes 4128 | tf_op jit(solution)/shard_map/ppermute | solution.py:238
  29.2 1.8 %collective-permute-start.5 = (f32[280,128]{1,0:T(8,128)S(1)}, f32[280,128]{1,0:T(8,128)S(1)}, u32[]{:S(2)}, u32[]{:S(2)}) collective-permute-start(f32[280,128]{1,0:T(8,128)S(1)} %pad_maximum_fusion), channel_id=1, source_target_pairs={{0,8},{8,0},{16,24},{24,16},{1,9},{9,1},{17,25},{25,17},{2,10},{10... | collective-permute-start | bytes 430088 | tf_op jit(solution)/shard_map/ppermute | solution.py:238
  31.0 3.3 %collective-permute-done.5.swapped_refs_0_ = f32[280,128]{1,0:T(8,128)S(1)} collective-permute-done((f32[280,128]{1,0:T(8,128)S(1)}, f32[280,128]{1,0:T(8,128)S(1)}, u32[]{:S(2)}, u32[]{:S(2)}) %collective-permute-start.5) | collective-permute-done | bytes 143392 | tf_op jit(solution)/shard_map/ppermute | solution.py:238
  34.4 3.3 %collective-permute-start.6 = (f32[280,128]{1,0:T(8,128)S(1)}, f32[280,128]{1,0:T(8,128)S(1)}, u32[]{:S(2)}, u32[]{:S(2)}) collective-permute-start(f32[280,128]{1,0:T(8,128)S(1)} %fusion), channel_id=1, source_target_pairs={{0,16},{8,24},{16,0},{24,8},{1,17},{9,25},{17,1},{25,9},{2,18},{10... | collective-permute-start | bytes 430088 | tf_op jit(solution)/shard_map/ppermute | solution.py:238
  37.7 0.0 copy-start.1
  37.7 6.5 %filter.1.local_ref = f32[8,32,64,128]{3,2,1,0:T(8,128)S(1)} custom-call(bf16[8,34,64,128]{3,2,1,0:T(8,128)(2,1)S(1)} %get-tuple-element.14.high_ref, bf16[8,34,64,128]{3,2,1,0:T(8,128)(2,1)S(1)} %get-tuple-element.15.low_ref, bf16[8,512,256]{2,1,0:T(8,128)(2,1)S(1)} %get-tuple-element.16.weight_ref), custom_call_target="tpu_custom_call" | custom-call | flops 4563402752 | bytes 1048576 | tf_op jit(solution)/shard_map/filter/pallas_call | solution.py:300
  44.1 0.0 collective-permute-done.6.swapped_refs_1_
  44.1 0.0 copy-done.1
  44.2 5.2 %level.1 = f32[8,64,4096]{2,1,0:T(8,128)} custom-call(f32[8,32,64,128]{3,2,1,0:T(8,128)S(1)} %filter.1.local_ref, bf16[8,512,256]{2,1,0:T(8,128)(2,1)S(1)} %get-tuple-element.16.weight_ref, f32[280,128]{1,0:T(8,128)S(1)} %collective-permute-done.5.swapped_refs_0_, f32[280,128]{1,0:T(8,128)S(1)} %collective-permute-done.6.swapped_refs_1_, ...), custom_call_target="tpu_custom_call" | custom-call | tf_op jit(solution)/shard_map/level/pallas_call | solution.py:313
  (5 shorter events, 0.0 us)
Async XLA Ops:
  0.0 3.0 %copy-start = (f32[8,128]{1,0:T(8,128)S(1)}, f32[8,128]{1,0:T(8,128)}, u32[]{:S(2)}) copy-start(f32[8,128]{1,0:T(8,128)} %taps_ref.1) | copy-start | bytes 12292
  1.3 1.7 %collective-permute-start = (f32[8,64,128]{2,1,0:T(8,128)S(1)}, f32[8,64,128]{2,1,0:T(8,128)S(1)}, u32[]{:S(2)}, u32[]{:S(2)}) collective-permute-start(f32[8,64,128]{2,1,0:T(8,128)S(1)} %get-tuple-element.12), channel_id=1, source_target_pairs={{0,1},{1,0},{2,3},{3,2},{4,5},{5,4},{6,7},{7,6},{8,9},{9,8},{10,11... | collective-permute-start | bytes 786440 | tf_op jit(solution)/shard_map/ppermute | solution.py:238
  1.8 1.2 %collective-permute-start.1 = (f32[8,64,128]{2,1,0:T(8,128)S(1)}, f32[8,64,128]{2,1,0:T(8,128)S(1)}, u32[]{:S(2)}, u32[]{:S(2)}) collective-permute-start(f32[8,64,128]{2,1,0:T(8,128)S(1)} %get-tuple-element.13), channel_id=1, source_target_pairs={{1,2},{3,4},{5,6},{2,1},{4,3},{6,5},{9,10},{11,12},{13,14},{10,9},... | collective-permute-start | bytes 786440 | tf_op jit(solution)/shard_map/ppermute | solution.py:266
  10.5 10.2 %collective-permute-start.2 = (f32[8,128]{1,0:T(8,128)S(1)}, f32[8,128]{1,0:T(8,128)S(1)}, u32[]{:S(2)}, u32[]{:S(2)}) collective-permute-start(f32[8,128]{1,0:T(8,128)S(1)} %get-tuple-element.18), channel_id=1, source_target_pairs={{0,1},{1,0},{2,3},{3,2},{4,5},{5,4},{6,7},{7,6},{8,9},{9,8},{10,11... | collective-permute-start | bytes 12296 | tf_op jit(solution)/shard_map/ppermute | solution.py:238
  20.7 4.9 %collective-permute-start.3 = (f32[8,128]{1,0:T(8,128)S(1)}, f32[8,128]{1,0:T(8,128)S(1)}, u32[]{:S(2)}, u32[]{:S(2)}) collective-permute-start(f32[8,128]{1,0:T(8,128)S(1)} %add.12), channel_id=1, source_target_pairs={{0,2},{1,3},{2,0},{3,1},{4,6},{5,7},{6,4},{7,5},{8,10},{9,11},{10,... | collective-permute-start | bytes 12296 | tf_op jit(solution)/shard_map/ppermute | solution.py:238
  25.6 3.6 %collective-permute-start.4 = (f32[8,128]{1,0:T(8,128)S(1)}, f32[8,128]{1,0:T(8,128)S(1)}, u32[]{:S(2)}, u32[]{:S(2)}) collective-permute-start(f32[8,128]{1,0:T(8,128)S(1)} %add.13), channel_id=1, source_target_pairs={{0,4},{1,5},{2,6},{3,7},{4,0},{5,1},{6,2},{7,3},{8,12},{9,13},{10,... | collective-permute-start | bytes 12296 | tf_op jit(solution)/shard_map/ppermute | solution.py:238
  29.2 5.2 %collective-permute-start.5 = (f32[280,128]{1,0:T(8,128)S(1)}, f32[280,128]{1,0:T(8,128)S(1)}, u32[]{:S(2)}, u32[]{:S(2)}) collective-permute-start(f32[280,128]{1,0:T(8,128)S(1)} %pad_maximum_fusion), channel_id=1, source_target_pairs={{0,8},{8,0},{16,24},{24,16},{1,9},{9,1},{17,25},{25,17},{2,10},{10... | collective-permute-start | bytes 430088 | tf_op jit(solution)/shard_map/ppermute | solution.py:238
  34.4 9.8 %collective-permute-start.6 = (f32[280,128]{1,0:T(8,128)S(1)}, f32[280,128]{1,0:T(8,128)S(1)}, u32[]{:S(2)}, u32[]{:S(2)}) collective-permute-start(f32[280,128]{1,0:T(8,128)S(1)} %fusion), channel_id=1, source_target_pairs={{0,16},{8,24},{16,0},{24,8},{1,17},{9,25},{17,1},{25,9},{2,18},{10... | collective-permute-start | bytes 430088 | tf_op jit(solution)/shard_map/ppermute | solution.py:238
  37.7 6.5 %copy-start.1 = (f32[8]{0:T(128)S(1)}, f32[8]{0:T(128)}, u32[]{:S(2)}) copy-start(f32[8]{0:T(128)} %coupling_ref.1) | copy-start | bytes 100

commit v3 on v2

v3 whole, which is shorter than its diff:
```python
import functools
import math

import jax
import jax.numpy as jnp
from jax import lax
from jax.experimental import pallas as pl
from jax.experimental.pallas import tpu as pltpu
from jax.sharding import PartitionSpec as P

two_pi = 2.0 * math.pi
LANES = 128
HALF = LANES // 2
SUBLANES = 8


def shifted_down(value, amount):
    rows = lax.broadcasted_iota(jnp.int32, value.shape, 0)
    return jnp.where(rows >= amount, pltpu.roll(value, amount, 0), 0.0)


def scanned(pieces):
    sums, carry = [], None
    for value in pieces:
        amount = 1
        while amount < SUBLANES:
            value = value + shifted_down(value, amount)
            amount *= 2
        if carry is not None:
            value = value + carry
        carry = jnp.broadcast_to(value[SUBLANES - 1 :, :], value.shape)
        sums.append(value)
    return sums


def split(value):
    high = value.astype(jnp.bfloat16)
    return high, (value - high.astype(jnp.float32)).astype(jnp.bfloat16)


def store_split(high_ref, low_ref, cable, block, sums):
    for pair in range(0, len(sums), 2):
        rows = pl.ds(pair * SUBLANES, 2 * SUBLANES)
        high, low = split(jnp.concatenate(sums[pair : pair + 2], axis=0))
        high_ref[cable, block, rows, :] = high
        low_ref[cable, block, rows, :] = low


def edges_kernel(phase_hbm, wrap_hbm, inner_ref, outer_ref, phase_ref, wrap_ref, sem):
    cables, time, width = phase_hbm.shape
    is_even = lax.rem(lax.axis_index("chan"), 2) == 0
    sends_last = (is_even, jnp.logical_not(is_even))
    copies = []
    for side, last in enumerate(sends_last):
        lanes = pl.ds(pl.multiple_of(jnp.where(last, width - LANES, 0), LANES), LANES)
        for kind, (source, target) in enumerate(((phase_hbm, phase_ref), (wrap_hbm, wrap_ref))):
            copies.append(
                pltpu.make_async_copy(source.at[:, :, lanes], target.at[side], sem.at[kind, side])
            )
    for copy in copies:
        copy.start()
    for copy in copies:
        copy.wait()
    lane = lax.broadcasted_iota(jnp.int32, (time, LANES), 1)
    for side, (last, target) in enumerate(zip(sends_last, (inner_ref, outer_ref))):
        for cable in range(cables // 2):
            low, high = (
                phase_ref[side, c] + two_pi * wrap_ref[side, c].astype(jnp.float32)
                for c in (cable, cable + cables // 2)
            )
            low = jnp.where(last, pltpu.roll(low, HALF, 1), low)
            high = jnp.where(last, high, pltpu.roll(high, HALF, 1))
            target[cable] = jnp.where(lane < HALF, low, high)


def unwrap_kernel(
    phase_hbm, wrap_hbm, taps_ref,
    high_ref, low_ref, totals_ref, sums_ref, weight_ref,
    phase_ref, wrap_ref, sem,
):
    cables, time, width = phase_hbm.shape
    blocks = width // LANES
    groups = time // SUBLANES

    def copies(cable):
        return (
            pltpu.make_async_copy(phase_hbm.at[cable], phase_ref.at[cable], sem.at[0, cable]),
            pltpu.make_async_copy(wrap_hbm.at[cable], wrap_ref.at[cable], sem.at[1, cable]),
        )

    for cable in range(cables):
        for copy in copies(cable):
            copy.start()

    outputs = lax.broadcasted_iota(jnp.int32, (LANES, LANES), 0)
    inputs = lax.broadcasted_iota(jnp.int32, (LANES, LANES), 1)
    centre = (lax.broadcasted_iota(jnp.int32, (1, LANES), 1) == HALF).astype(jnp.float32)

    @pl.loop(0, cables)
    def _(cable):
        row = (centre - taps_ref[pl.ds(cable, 1), :]) * (1.0 / (4.0 * two_pi))
        circulant = pltpu.roll(
            jnp.broadcast_to(row, (LANES, LANES)), 0, 1, stride=1, stride_axis=0
        )
        first = jnp.where(inputs >= outputs, circulant, 0.0).T
        second = jnp.where(inputs < outputs, circulant, 0.0).T
        high, low = split(jnp.concatenate([first, second], axis=1))
        for place, part in enumerate((high, high, low, low)):
            weight_ref[cable, pl.ds(place * LANES, LANES), :] = part

    def cable_step(cable, accumulated):
        for copy in copies(cable):
            copy.wait()

        def block_step(block, accumulated):
            lanes = pl.ds(pl.multiple_of(block * LANES, LANES), LANES)
            pieces = []
            for i in range(groups):
                rows = pl.ds(i * SUBLANES, SUBLANES)
                turns = wrap_ref[cable, rows, lanes].astype(jnp.float32)
                pieces.append(phase_ref[cable, rows, lanes] + two_pi * turns)
            sums = scanned(pieces)
            store_split(high_ref, low_ref, cable, block, sums)
            totals_ref[pl.ds(block * cables + cable, 1), :] = sums[-1][SUBLANES - 1 :, :]
            return tuple(a + b for a, b in zip(accumulated, sums))

        return lax.fori_loop(0, blocks, block_step, accumulated, unroll=4)

    zeros = tuple(jnp.zeros((SUBLANES, LANES), jnp.float32) for _ in range(groups))
    accumulated = lax.fori_loop(0, cables, cable_step, zeros)
    lane = lax.broadcasted_iota(jnp.int32, (SUBLANES, LANES), 1)
    tile = jnp.zeros((SUBLANES, LANES), jnp.float32)
    for i, value in enumerate(accumulated):
        tile = jnp.where(lane == i, jnp.sum(value, axis=1, keepdims=True), tile)
    sums_ref[...] = tile


def halo_kernel(inner_ref, outer_ref, high_ref, low_ref, totals_ref):
    pairs, time, _ = inner_ref.shape
    cables = 2 * pairs
    groups = time // SUBLANES
    is_even = lax.rem(lax.axis_index("chan"), 2) == 0
    for pair in range(pairs):
        inner, outer = (
            scanned([ref[pair, pl.ds(i * SUBLANES, SUBLANES), :] for i in range(groups)])
            for ref in (inner_ref, outer_ref)
        )
        right = [jnp.where(is_even, a, b) for a, b in zip(inner, outer)]
        left = [jnp.where(is_even, b, a) for a, b in zip(inner, outer)]
        for block, sums, moved in ((0, right, pair + pairs), (1, left, pair)):
            for cable in (pair, pair + pairs):
                placed = [pltpu.roll(v, HALF, 1) for v in sums] if cable == moved else sums
                store_split(high_ref, low_ref, cable, block, placed)
                totals_ref[pl.ds(block * cables + cable, 1), :] = placed[-1][SUBLANES - 1 :, :]


def filter_kernel(first, high_ref, low_ref, halo_high_ref, halo_low_ref, weight_ref, local_ref):
    _, blocks, time, _ = high_ref.shape
    lane = lax.broadcasted_iota(jnp.int32, (time, LANES), 1)

    @pl.loop(0, local_ref.shape[0])
    def _(index):
        cable = first + index
        high, low = (
            jnp.concatenate(
                [main[cable].reshape(blocks * time, LANES), halo[cable].reshape(2 * time, LANES)],
                axis=0,
            )
            for main, halo in ((high_ref, halo_high_ref), (low_ref, halo_low_ref))
        )
        product = jnp.dot(
            jnp.concatenate([high, low, high, low], axis=1),
            weight_ref[cable],
            preferred_element_type=jnp.float32,
        )

        def rolled(block):
            here = block if block >= 0 else blocks + 1
            there = block + 1
            return pltpu.roll(
                product[here * time : (here + 1) * time, :LANES]
                + product[there * time : (there + 1) * time, LANES:],
                HALF,
                1,
            )

        previous = rolled(-1)
        for block in range(blocks):
            following = rolled(block)
            local_ref[index, block] = jnp.where(lane < HALF, previous, following)
            previous = following


def level_kernel(
    population, local_refs, weight_ref, totals_refs, sums_ref, earlier_refs, coupling_ref,
    out_hbm, stage_ref, offset_ref, sem,
):
    share, blocks, time, _ = local_refs[0].shape
    cables = out_hbm.shape[0]
    groups = time // SUBLANES
    step, place = lax.axis_index("tm"), lax.axis_index("chan")
    inside_left = jnp.where(place == 0, 0.0, 1.0)
    inside_right = jnp.where(place == lax.axis_size("chan") - 1, 0.0, 1.0)

    def from_earlier(refs):
        value = jnp.zeros(refs[0].shape, jnp.float32)
        for bit, ref in enumerate(refs):
            value = value + jnp.where((step & (1 << bit)) != 0, ref[...], 0.0)
        return value

    offset_ref[...] = from_earlier(totals_refs)
    earlier = from_earlier(earlier_refs)[SUBLANES - 1 :, groups - 1 : groups]
    common = (sums_ref[...] + earlier) * (1.0 / population)
    columns = [
        jnp.broadcast_to(common[:, i : i + 1], (SUBLANES, LANES)) for i in range(groups)
    ]
    used = blocks + 2
    padded = -(-(used + 1) // SUBLANES) * SUBLANES
    row = lax.broadcasted_iota(jnp.int32, (padded, LANES), 0)
    lane = lax.broadcasted_iota(jnp.int32, (padded, LANES), 1)

    def filtered_offset(cable):
        offset = jnp.concatenate(
            [
                offset_ref[pl.ds(cable, used, stride=cables), :],
                jnp.ones((padded - used, LANES), jnp.float32),
            ],
            axis=0,
        )
        high, low = split(offset)
        product = jnp.dot(
            jnp.concatenate([high, low, high, low], axis=1),
            weight_ref[cable],
            preferred_element_type=jnp.float32,
        )
        here, there = product[:, :LANES], product[:, LANES:]
        left = pltpu.roll(here[used - 1 : used] + there[:1], HALF, 1)
        following = pltpu.roll(here + pltpu.roll(there, padded - 1, 0), HALF, 1)
        previous = jnp.where(row == 0, left, pltpu.roll(following, 1, 0))
        bias = jnp.where(lane < HALF, previous, following)
        here, there = here[used : used + 1], there[used : used + 1]
        middle = pltpu.roll(here + there, HALF, 1)
        first = pltpu.roll(here * inside_left + there, HALF, 1)
        last = pltpu.roll(here + there * inside_right, HALF, 1)
        first = jnp.where(lane[:1] < HALF, first, middle)
        last = jnp.where(lane[:1] < HALF, middle, last)
        return bias, first, middle, last

    carry = filtered_offset(0)
    for part, local_ref in enumerate(local_refs):

        def cable_step(index, carry, part=part, local_ref=local_ref):
            cable = part * share + index
            following = filtered_offset(jnp.minimum(cable + 1, cables - 1))
            bias, first, middle, last = carry
            shifts = [coupling_ref[cable] * column for column in columns]
            inner = [shift * middle for shift in shifts]
            for block in range(blocks):
                lanes = pl.ds(block * LANES, LANES)
                added = jnp.broadcast_to(bias[block : block + 1, :], (SUBLANES, LANES))
                if block == 0:
                    slopes = [shift * first for shift in shifts]
                elif block == blocks - 1:
                    slopes = [shift * last for shift in shifts]
                else:
                    slopes = inner
                for i in range(groups):
                    rows = pl.ds(i * SUBLANES, SUBLANES)
                    stage_ref[cable, rows, lanes] = local_ref[index, block, rows, :] + (
                        added - slopes[i]
                    )
            pltpu.make_async_copy(stage_ref.at[cable], out_hbm.at[cable], sem.at[cable]).start()
            return following

        carry = lax.fori_loop(0, share, cable_step, carry)
    for cable in range(cables):
        pltpu.make_async_copy(stage_ref.at[cable], out_hbm.at[cable], sem.at[cable]).wait()


def swapped(value, axis, bit):
    return lax.ppermute(value, axis, [(i, i ^ bit) for i in range(lax.axis_size(axis))])


def shards(phase_step, wrap_count, coupling, filter_taps):
    cables, time, width = phase_step.shape
    blocks = width // LANES
    steps, places = lax.axis_size("tm"), lax.axis_size("chan")
    population = cables * width * places
    parts = 4
    share = cables // parts
    phase_step = pltpu.with_memory_space_constraint(phase_step, pltpu.HBM)
    wrap_count = pltpu.with_memory_space_constraint(wrap_count, pltpu.HBM)
    whole = pl.BlockSpec(memory_space=pltpu.VMEM)
    outside = pl.BlockSpec(memory_space=pl.ANY)
    scalars = pl.BlockSpec(memory_space=pltpu.SMEM)

    inner, outer = pl.pallas_call(
        edges_kernel,
        out_shape=[pltpu.VMEM((cables // 2, time, LANES), jnp.float32)] * 2,
        in_specs=[outside] * 2,
        out_specs=[whole] * 2,
        scratch_shapes=[
            pltpu.VMEM((2, cables, time, LANES), jnp.float32),
            pltpu.VMEM((2, cables, time, LANES), jnp.int32),
            pltpu.SemaphoreType.DMA((2, 2)),
        ],
        compiler_params=pltpu.CompilerParams(vmem_limit_bytes=8 << 20),
        name="edges",
    )(phase_step, wrap_count)
    odd_pairs = [(i, i + 1) for i in range(1, places - 1, 2)]
    outer = lax.ppermute(outer, "chan", odd_pairs + [(b, a) for a, b in odd_pairs])
    inner = swapped(inner, "chan", 1)

    high, low, totals, sums, weight = pl.pallas_call(
        unwrap_kernel,
        out_shape=(
            pltpu.VMEM((cables, blocks, time, LANES), jnp.bfloat16),
            pltpu.VMEM((cables, blocks, time, LANES), jnp.bfloat16),
            pltpu.VMEM((blocks * cables, LANES), jnp.float32),
            pltpu.VMEM((SUBLANES, LANES), jnp.float32),
            pltpu.VMEM((cables, 4 * LANES, 2 * LANES), jnp.bfloat16),
        ),
        in_specs=[outside, outside, whole],
        out_specs=[whole] * 5,
        scratch_shapes=[
            pltpu.VMEM((cables, time, width), jnp.float32),
            pltpu.VMEM((cables, time, width), jnp.int32),
            pltpu.SemaphoreType.DMA((2, cables)),
        ],
        compiler_params=pltpu.CompilerParams(vmem_limit_bytes=40 << 20),
        cost_estimate=pl.CostEstimate(
            flops=0, bytes_accessed=2 * phase_step.size * 4, transcendentals=0
        ),
        name="unwrap",
    )(phase_step, wrap_count, filter_taps)

    halo_high, halo_low, halo_totals = pl.pallas_call(
        halo_kernel,
        out_shape=(
            pltpu.VMEM((cables, 2, time, LANES), jnp.bfloat16),
            pltpu.VMEM((cables, 2, time, LANES), jnp.bfloat16),
            pltpu.VMEM((2 * cables, LANES), jnp.float32),
        ),
        in_specs=[whole] * 2,
        out_specs=[whole] * 3,
        compiler_params=pltpu.CompilerParams(vmem_limit_bytes=8 << 20),
        name="halo",
    )(inner, outer)

    def filtered(part, weight):
        return pl.pallas_call(
            functools.partial(filter_kernel, part * share),
            out_shape=pltpu.VMEM((share, blocks, time, LANES), jnp.float32),
            in_specs=[whole] * 5,
            out_specs=whole,
            compiler_params=pltpu.CompilerParams(vmem_limit_bytes=16 << 20),
            cost_estimate=pl.CostEstimate(
                flops=2 * share * (blocks + 2) * time * 8 * LANES * LANES,
                bytes_accessed=1 << 20,
                transcendentals=0,
            ),
            name="filter",
        )(high, low, halo_high, halo_low, weight)

    running = jnp.concatenate([totals, halo_totals], axis=0)
    received = [swapped(running, "tm", 1)]
    sums, halo_totals = lax.optimization_barrier((sums, halo_totals))
    rounds = [("chan", 1 << bit) for bit in range(places.bit_length() - 1)]
    rounds += [("tm", 1 << bit) for bit in range(steps.bit_length() - 1)]
    local, received_sums, chan_sums, mark = [], [], sums, sums
    for number, (axis, bit) in enumerate(rounds):
        incoming = swapped(sums, axis, bit)
        if len(local) < parts:
            tied, mark = lax.optimization_barrier((weight, mark))
            part = filtered(len(local), tied)
            incoming, part = lax.optimization_barrier((incoming, part))
            local.append(part)
        if number % 2 == 1 and 1 << len(received) < steps:
            running = running + received[-1]
            running, incoming = lax.optimization_barrier((running, incoming))
            received.append(swapped(running, "tm", 1 << len(received)))
        if axis == "tm":
            received_sums.append(incoming)
        sums = mark = sums + incoming
        if axis == "chan":
            chan_sums = sums
    while len(local) < parts:
        local.append(filtered(len(local), weight))

    return pl.pallas_call(
        functools.partial(level_kernel, population),
        out_shape=jax.ShapeDtypeStruct(phase_step.shape, jnp.float32),
        in_specs=[
            [whole] * parts, whole, [whole] * len(received), whole, [whole] * len(received), scalars
        ],
        out_specs=outside,
        scratch_shapes=[
            pltpu.VMEM((cables, time, width), jnp.float32),
            pltpu.VMEM(((blocks + 2) * cables, LANES), jnp.float32),
            pltpu.SemaphoreType.DMA((cables,)),
        ],
        compiler_params=pltpu.CompilerParams(vmem_limit_bytes=24 << 20),
        name="level",
    )(local, weight, received, chan_sums, received_sums, coupling)


def solution(mesh):
    placed = (P(None, "tm", "chan"), P(None, "tm", "chan"), P(), P())
    return jax.shard_map(
        shards, mesh=mesh, in_specs=placed, out_specs=P(None, "tm", "chan"), check_vma=False
    )
```

time: 49.5 us -> 40.1 us (0.81)
  starting transfers between devices: 20.6 us -> 13.2 us
  waiting for transfers between devices: 8.22 us -> 6.71 us
  Pallas kernels: 20.4 us -> 19.9 us
    ppermute x6 -> x8, starting transfers between devices: 19.9 us -> 12.5 us  [swapped(): lax.ppermute(value, axis, [(i, i ^ bit) for i in range(lax.axis_size(axis...]
    ppermute x6 -> x8, waiting for transfers between devices: 8.21 us -> 6.71 us  [swapped(): lax.ppermute(value, axis, [(i, i ^ bit) for i in range(lax.axis_size(axis...]
    pallas_call x1, Pallas kernels: 5.2 us -> 4.26 us  [shards(): pl.pallas_call(functools.partial(level_kernel, population), out_shape=jax...]
    pallas_call x3 -> x7, Pallas kernels: 15.2 us -> 15.6 us  [the longest x1 7.47 us: shards(): pl.pallas_call(unwrap_kernel, out_shape=(pltpu.VMEM((cables, blocks, time...]
  transfers between devices with their start and end apart: 7 -> 9, of which waited for: 5 -> 3; matrix products, arithmetic and copies ran while one was open for 0% -> 0% of each run, Pallas kernels for 13% -> 35%
where the time goes in v3:
time: 40.1 us; the launch traced here: 39.9 us
  Pallas kernels  19.9 us (50%)
  starting transfers between devices  13.2 us (33%)
  waiting for transfers between devices  6.71 us (17%)
    ppermute x8, starting transfers between devices, swapped(): lax.ppermute(value, axis, [(i, i ^ bit) for i in range(lax.axis_size(axis...  12.5 us
    pallas_call x1, Pallas kernels, shards(): pl.pallas_call(unwrap_kernel, out_shape=(pltpu.VMEM((cables, blocks, time...  7.47 us
    ppermute x8, waiting for transfers between devices, swapped(): lax.ppermute(value, axis, [(i, i ^ bit) for i in range(lax.axis_size(axis...  6.71 us
    pallas_call x4, Pallas kernels, filtered(): pl.pallas_call(functools.partial(filter_kernel, part * share), out_shape=...  6.49 us
    pallas_call x1, Pallas kernels, shards(): pl.pallas_call(functools.partial(level_kernel, population), out_shape=jax...  4.26 us
    pallas_call x1, Pallas kernels, shards(): pl.pallas_call(edges_kernel, out_shape=[pltpu.VMEM((cables // 2, time, LA...  1.45 us
  transfers between devices with their start and end apart: 9, of which 3 were waited for; matrix products, arithmetic and copies ran while one was open for 0% of the time, Pallas kernels for 35%

profile of v3, /device:TPU:0, one launch (start us, length us, event | category | flops | bytes accessed | tf_op | source)
XLA Modules:
  0.0 39.9 jit_solution(16661027238326260225)
XLA Ops:
  0.0 1.5 %edges.1 = (f32[4,64,128]{2,1,0:T(8,128)S(1)}, f32[4,64,128]{2,1,0:T(8,128)S(1)}) custom-call(f32[8,64,4096]{2,1,0:T(8,128)} %phase_hbm.3, s32[8,64,4096]{2,1,0:T(8,128)} %wrap_hbm.3), custom_call_target="tpu_custom_call" | custom-call | tf_op jit(solution)/shard_map/edges/pallas_call | solution.py:297
  1.5 0.5 %collective-permute-start = (f32[4,64,128]{2,1,0:T(8,128)S(1)}, f32[4,64,128]{2,1,0:T(8,128)S(1)}, u32[]{:S(2)}, u32[]{:S(2)}) collective-permute-start(f32[4,64,128]{2,1,0:T(8,128)S(1)} %get-tuple-element.31), channel_id=1, source_target_pairs={{0,1},{1,0},{2,3},{3,2},{4,5},{5,4},{6,7},{7,6},{8,9},{9,8},{10,11... | collective-permute-start | bytes 393224 | tf_op jit(solution)/shard_map/ppermute | solution.py:281
  2.0 0.7 %collective-permute-start.1 = (f32[4,64,128]{2,1,0:T(8,128)S(1)}, f32[4,64,128]{2,1,0:T(8,128)S(1)}, u32[]{:S(2)}, u32[]{:S(2)}) collective-permute-start(f32[4,64,128]{2,1,0:T(8,128)S(1)} %get-tuple-element.32), channel_id=1, source_target_pairs={{1,2},{3,4},{5,6},{2,1},{4,3},{6,5},{9,10},{11,12},{13,14},{10,9},... | collective-permute-start | bytes 393224 | tf_op jit(solution)/shard_map/ppermute | solution.py:311
  2.7 7.5 %unwrap.1 = (bf16[8,32,64,128]{3,2,1,0:T(8,128)(2,1)S(1)}, bf16[8,32,64,128]{3,2,1,0:T(8,128)(2,1)S(1)}, f32[256,128]{1,0:T(8,128)S(1)}, f32[8,128]{1,0:T(8,128)S(1)}, bf16[8,512,256]{2,1,0:T(8,128)(2,1)S(1)}) custom-call(f32[8,64,4096]{2,1,0:T(8,128)} %phase_hbm.3, s32[8,64,4096]{2,1,0:T(8,128)} %wrap_hbm.3, f32[8,128]{1,0:T(8,128)S(1)} %copy-done), custom_call_target="tpu_custom_call" | custom-call | bytes 16777216 | tf_op jit(solution)/shard_map/unwrap/pallas_call | solution.py:314
  10.1 0.0 collective-permute-done.inner_ref
  10.2 0.2 halo.1
  10.4 3.9 %collective-permute-start.2 = (f32[8,128]{1,0:T(8,128)S(1)}, f32[8,128]{1,0:T(8,128)S(1)}, u32[]{:S(2)}, u32[]{:S(2)}) collective-permute-start(f32[8,128]{1,0:T(8,128)S(1)} %get-tuple-element.34), channel_id=1, source_target_pairs={{0,1},{1,0},{2,3},{3,2},{4,5},{5,4},{6,7},{7,6},{8,9},{9,8},{10,11... | collective-permute-start | bytes 12296 | tf_op jit(solution)/shard_map/ppermute | solution.py:281
  14.3 1.6 %collective-permute-start.4 = (f32[272,128]{1,0:T(8,128)S(1)}, f32[272,128]{1,0:T(8,128)S(1)}, u32[]{:S(2)}, u32[]{:S(2)}) collective-permute-start(f32[272,128]{1,0:T(8,128)S(1)} %constant_dynamic-update-slice_fusion), channel_id=1, source_target_pairs={{0,8},{8,0},{16,24},{24,16},{1,9},{9,1},{17,25},{25,17},{2,10},{10... | collective-permute-start | bytes 417800 | tf_op jit(solution)/shard_map/ppermute | solution.py:281
  15.9 1.6 %filter.4.local_refs_0_ = f32[2,32,64,128]{3,2,1,0:T(8,128)S(1)} custom-call(bf16[8,32,64,128]{3,2,1,0:T(8,128)(2,1)S(1)} %get-tuple-element.35.high_ref, bf16[8,32,64,128]{3,2,1,0:T(8,128)(2,1)S(1)} %get-tuple-element.36.low_ref, bf16[8,2,64,128]{3,2,1,0:T(8,128)(2,1)S(1)} %get-tuple-element.37.halo_high_ref, ...), custom_call_target="tpu_custom_call" | custom-call | flops 1140850688 | bytes 1048576 | tf_op jit(solution)/shard_map/filter/pallas_call | solution.py:351
  17.5 0.0 collective-permute-done.2
  17.5 1.6 %collective-permute-start.3 = (f32[8,128]{1,0:T(8,128)S(1)}, f32[8,128]{1,0:T(8,128)S(1)}, u32[]{:S(2)}, u32[]{:S(2)}) collective-permute-start(f32[8,128]{1,0:T(8,128)S(1)} %add.15), channel_id=1, source_target_pairs={{0,2},{1,3},{2,0},{3,1},{4,6},{5,7},{6,4},{7,5},{8,10},{9,11},{10,... | collective-permute-start | bytes 12296 | tf_op jit(solution)/shard_map/ppermute | solution.py:281
  19.1 1.6 %filter.5.local_refs_1_ = f32[2,32,64,128]{3,2,1,0:T(8,128)S(1)} custom-call(bf16[8,32,64,128]{3,2,1,0:T(8,128)(2,1)S(1)} %get-tuple-element.35.high_ref, bf16[8,32,64,128]{3,2,1,0:T(8,128)(2,1)S(1)} %get-tuple-element.36.low_ref, bf16[8,2,64,128]{3,2,1,0:T(8,128)(2,1)S(1)} %get-tuple-element.37.halo_high_ref, ...), custom_call_target="tpu_custom_call" | custom-call | flops 1140850688 | bytes 1048576 | tf_op jit(solution)/shard_map/filter/pallas_call | solution.py:351
  20.7 0.5 %collective-permute-done.3 = f32[8,128]{1,0:T(8,128)S(1)} collective-permute-done((f32[8,128]{1,0:T(8,128)S(1)}, f32[8,128]{1,0:T(8,128)S(1)}, u32[]{:S(2)}, u32[]{:S(2)}) %collective-permute-start.3) | collective-permute-done | bytes 4128 | tf_op jit(solution)/shard_map/ppermute | solution.py:281
  21.3 1.6 %collective-permute-start.5 = (f32[8,128]{1,0:T(8,128)S(1)}, f32[8,128]{1,0:T(8,128)S(1)}, u32[]{:S(2)}, u32[]{:S(2)}) collective-permute-start(f32[8,128]{1,0:T(8,128)S(1)} %add.17), channel_id=1, source_target_pairs={{0,4},{1,5},{2,6},{3,7},{4,0},{5,1},{6,2},{7,3},{8,12},{9,13},{10,... | collective-permute-start | bytes 12296 | tf_op jit(solution)/shard_map/ppermute | solution.py:281
  22.8 2.6 %collective-permute-start.7 = (f32[272,128]{1,0:T(8,128)S(1)}, f32[272,128]{1,0:T(8,128)S(1)}, u32[]{:S(2)}, u32[]{:S(2)}) collective-permute-start(f32[272,128]{1,0:T(8,128)S(1)} %add.16), channel_id=1, source_target_pairs={{0,16},{8,24},{16,0},{24,8},{1,17},{9,25},{17,1},{25,9},{2,18},{10... | collective-permute-start | bytes 417800 | tf_op jit(solution)/shard_map/ppermute | solution.py:281
  25.4 1.6 %filter.6.local_refs_2_ = f32[2,32,64,128]{3,2,1,0:T(8,128)S(1)} custom-call(bf16[8,32,64,128]{3,2,1,0:T(8,128)(2,1)S(1)} %get-tuple-element.35.high_ref, bf16[8,32,64,128]{3,2,1,0:T(8,128)(2,1)S(1)} %get-tuple-element.36.low_ref, bf16[8,2,64,128]{3,2,1,0:T(8,128)(2,1)S(1)} %get-tuple-element.37.halo_high_ref, ...), custom_call_target="tpu_custom_call" | custom-call | flops 1140850688 | bytes 1048576 | tf_op jit(solution)/shard_map/filter/pallas_call | solution.py:351
  27.1 0.0 collective-permute-done.5
  27.1 0.0 copy-start.1
  27.1 0.8 %collective-permute-start.6 = (f32[8,128]{1,0:T(8,128)S(1)}, f32[8,128]{1,0:T(8,128)S(1)}, u32[]{:S(2)}, u32[]{:S(2)}) collective-permute-start(f32[8,128]{1,0:T(8,128)S(1)} %add.18.sums_ref), channel_id=1, source_target_pairs={{0,8},{8,0},{16,24},{24,16},{1,9},{9,1},{17,25},{25,17},{2,10},{10... | collective-permute-start | bytes 12296 | tf_op jit(solution)/shard_map/ppermute | solution.py:281
  27.8 1.6 %filter.7.local_refs_3_ = f32[2,32,64,128]{3,2,1,0:T(8,128)S(1)} custom-call(bf16[8,32,64,128]{3,2,1,0:T(8,128)(2,1)S(1)} %get-tuple-element.35.high_ref, bf16[8,32,64,128]{3,2,1,0:T(8,128)(2,1)S(1)} %get-tuple-element.36.low_ref, bf16[8,2,64,128]{3,2,1,0:T(8,128)(2,1)S(1)} %get-tuple-element.37.halo_high_ref, ...), custom_call_target="tpu_custom_call" | custom-call | flops 1140850688 | bytes 1048576 | tf_op jit(solution)/shard_map/filter/pallas_call | solution.py:351
  29.5 1.7 %collective-permute-done.6.earlier_refs_0_ = f32[8,128]{1,0:T(8,128)S(1)} collective-permute-done((f32[8,128]{1,0:T(8,128)S(1)}, f32[8,128]{1,0:T(8,128)S(1)}, u32[]{:S(2)}, u32[]{:S(2)}) %collective-permute-start.6) | collective-permute-done | bytes 4128 | tf_op jit(solution)/shard_map/ppermute | solution.py:281
  31.2 4.5 %collective-permute-done.8.earlier_refs_1_ = f32[8,128]{1,0:T(8,128)S(1)} collective-permute-done((f32[8,128]{1,0:T(8,128)S(1)}, f32[8,128]{1,0:T(8,128)S(1)}, u32[]{:S(2)}, u32[]{:S(2)}) %collective-permute-start.8) | collective-permute-done | bytes 4128 | tf_op jit(solution)/shard_map/ppermute | solution.py:281
  35.7 0.0 collective-permute-done.7.totals_refs_1_
  35.7 4.3 %level.1 = f32[8,64,4096]{2,1,0:T(8,128)} custom-call(f32[2,32,64,128]{3,2,1,0:T(8,128)S(1)} %filter.4.local_refs_0_, f32[2,32,64,128]{3,2,1,0:T(8,128)S(1)} %filter.5.local_refs_1_, f32[2,32,64,128]{3,2,1,0:T(8,128)S(1)} %filter.6.local_refs_2_, f32[2,32,64,128]{3,2,1,0:T(8,128)S(1)} %filter.7.local_refs_3_, ...), custom_call_target="tpu_custom_call" | custom-call | tf_op jit(solution)/shard_map/level/pallas_call | solution.py:390
  (13 shorter events, 0.1 us)
Async XLA Ops:
  0.0 2.6 %copy-start = (f32[8,128]{1,0:T(8,128)S(1)}, f32[8,128]{1,0:T(8,128)}, u32[]{:S(2)}) copy-start(f32[8,128]{1,0:T(8,128)} %taps_ref.1) | copy-start | bytes 12292
  1.5 8.7 %collective-permute-start = (f32[4,64,128]{2,1,0:T(8,128)S(1)}, f32[4,64,128]{2,1,0:T(8,128)S(1)}, u32[]{:S(2)}, u32[]{:S(2)}) collective-permute-start(f32[4,64,128]{2,1,0:T(8,128)S(1)} %get-tuple-element.31), channel_id=1, source_target_pairs={{0,1},{1,0},{2,3},{3,2},{4,5},{5,4},{6,7},{7,6},{8,9},{9,8},{10,11... | collective-permute-start | bytes 393224 | tf_op jit(solution)/shard_map/ppermute | solution.py:281
  2.0 8.2 %collective-permute-start.1 = (f32[4,64,128]{2,1,0:T(8,128)S(1)}, f32[4,64,128]{2,1,0:T(8,128)S(1)}, u32[]{:S(2)}, u32[]{:S(2)}) collective-permute-start(f32[4,64,128]{2,1,0:T(8,128)S(1)} %get-tuple-element.32), channel_id=1, source_target_pairs={{1,2},{3,4},{5,6},{2,1},{4,3},{6,5},{9,10},{11,12},{13,14},{10,9},... | collective-permute-start | bytes 393224 | tf_op jit(solution)/shard_map/ppermute | solution.py:311
  10.4 7.1 %collective-permute-start.2 = (f32[8,128]{1,0:T(8,128)S(1)}, f32[8,128]{1,0:T(8,128)S(1)}, u32[]{:S(2)}, u32[]{:S(2)}) collective-permute-start(f32[8,128]{1,0:T(8,128)S(1)} %get-tuple-element.34), channel_id=1, source_target_pairs={{0,1},{1,0},{2,3},{3,2},{4,5},{5,4},{6,7},{7,6},{8,9},{9,8},{10,11... | collective-permute-start | bytes 12296 | tf_op jit(solution)/shard_map/ppermute | solution.py:281
  14.3 6.9 %collective-permute-start.4 = (f32[272,128]{1,0:T(8,128)S(1)}, f32[272,128]{1,0:T(8,128)S(1)}, u32[]{:S(2)}, u32[]{:S(2)}) collective-permute-start(f32[272,128]{1,0:T(8,128)S(1)} %constant_dynamic-update-slice_fusion), channel_id=1, source_target_pairs={{0,8},{8,0},{16,24},{24,16},{1,9},{9,1},{17,25},{25,17},{2,10},{10... | collective-permute-start | bytes 417800 | tf_op jit(solution)/shard_map/ppermute | solution.py:281
  17.5 3.7 %collective-permute-start.3 = (f32[8,128]{1,0:T(8,128)S(1)}, f32[8,128]{1,0:T(8,128)S(1)}, u32[]{:S(2)}, u32[]{:S(2)}) collective-permute-start(f32[8,128]{1,0:T(8,128)S(1)} %add.15), channel_id=1, source_target_pairs={{0,2},{1,3},{2,0},{3,1},{4,6},{5,7},{6,4},{7,5},{8,10},{9,11},{10,... | collective-permute-start | bytes 12296 | tf_op jit(solution)/shard_map/ppermute | solution.py:281
  21.3 5.8 %collective-permute-start.5 = (f32[8,128]{1,0:T(8,128)S(1)}, f32[8,128]{1,0:T(8,128)S(1)}, u32[]{:S(2)}, u32[]{:S(2)}) collective-permute-start(f32[8,128]{1,0:T(8,128)S(1)} %add.17), channel_id=1, source_target_pairs={{0,4},{1,5},{2,6},{3,7},{4,0},{5,1},{6,2},{7,3},{8,12},{9,13},{10,... | collective-permute-start | bytes 12296 | tf_op jit(solution)/shard_map/ppermute | solution.py:281
  22.8 12.8 %collective-permute-start.7 = (f32[272,128]{1,0:T(8,128)S(1)}, f32[272,128]{1,0:T(8,128)S(1)}, u32[]{:S(2)}, u32[]{:S(2)}) collective-permute-start(f32[272,128]{1,0:T(8,128)S(1)} %add.16), channel_id=1, source_target_pairs={{0,16},{8,24},{16,0},{24,8},{1,17},{9,25},{17,1},{25,9},{2,18},{10... | collective-permute-start | bytes 417800 | tf_op jit(solution)/shard_map/ppermute | solution.py:281
  27.1 8.6 %copy-start.1 = (f32[8]{0:T(128)S(1)}, f32[8]{0:T(128)}, u32[]{:S(2)}) copy-start(f32[8]{0:T(128)} %coupling_ref.1) | copy-start | bytes 100
  27.1 4.1 %collective-permute-start.6 = (f32[8,128]{1,0:T(8,128)S(1)}, f32[8,128]{1,0:T(8,128)S(1)}, u32[]{:S(2)}, u32[]{:S(2)}) collective-permute-start(f32[8,128]{1,0:T(8,128)S(1)} %add.18.sums_ref), channel_id=1, source_target_pairs={{0,8},{8,0},{16,24},{24,16},{1,9},{9,1},{17,25},{25,17},{2,10},{10... | collective-permute-start | bytes 12296 | tf_op jit(solution)/shard_map/ppermute | solution.py:281
  31.2 4.5 %collective-permute-start.8 = (f32[8,128]{1,0:T(8,128)S(1)}, f32[8,128]{1,0:T(8,128)S(1)}, u32[]{:S(2)}, u32[]{:S(2)}) collective-permute-start(f32[8,128]{1,0:T(8,128)S(1)} %add.19), channel_id=1, source_target_pairs={{0,16},{8,24},{16,0},{24,8},{1,17},{9,25},{17,1},{25,9},{2,18},{10... | collective-permute-start | bytes 12296 | tf_op jit(solution)/shard_map/ppermute | solution.py:281

commit v4 on v3

--- a/solution.py
+++ b/solution.py
@@ -281,6 +281,14 @@
     return lax.ppermute(value, axis, [(i, i ^ bit) for i in range(lax.axis_size(axis))])
 
 
+def passed_on(value, bit):
+    steps = lax.axis_size("tm")
+    pairs = [
+        (i, i ^ bit) for i in range(steps) if i & bit == 0 or (i ^ bit) | (2 * bit - 1) < steps - 1
+    ]
+    return lax.ppermute(value, "tm", pairs)
+
+
 def shards(phase_step, wrap_count, coupling, filter_taps):
     cables, time, width = phase_step.shape
     blocks = width // LANES
@@ -363,13 +371,13 @@
         )(high, low, halo_high, halo_low, weight)
 
     running = jnp.concatenate([totals, halo_totals], axis=0)
-    received = [swapped(running, "tm", 1)]
+    received = [passed_on(running, 1)]
     sums, halo_totals = lax.optimization_barrier((sums, halo_totals))
     rounds = [("chan", 1 << bit) for bit in range(places.bit_length() - 1)]
     rounds += [("tm", 1 << bit) for bit in range(steps.bit_length() - 1)]
     local, received_sums, chan_sums, mark = [], [], sums, sums
     for number, (axis, bit) in enumerate(rounds):
-        incoming = swapped(sums, axis, bit)
+        incoming = passed_on(sums, bit) if axis == "tm" else swapped(sums, axis, bit)
         if len(local) < parts:
             tied, mark = lax.optimization_barrier((weight, mark))
             part = filtered(len(local), tied)
@@ -378,7 +386,7 @@
         if number % 2 == 1 and 1 << len(received) < steps:
             running = running + received[-1]
             running, incoming = lax.optimization_barrier((running, incoming))
-            received.append(swapped(running, "tm", 1 << len(received)))
+            received.append(passed_on(running, 1 << len(received)))
         if axis == "tm":
             received_sums.append(incoming)
         sums = mark = sums + incoming

time: 40.1 us -> 43.5 us (1.085)
  starting transfers between devices: 13.2 us -> 20 us
  waiting for transfers between devices: 6.71 us -> 3.11 us
    ppermute x0 -> x4, starting transfers between devices: none -> 11.8 us  [passed_on(): return lax.ppermute(value, 'tm', pairs)]
    ppermute x8 -> x4, waiting for transfers between devices: 6.71 us -> 0.5 us  [swapped(): lax.ppermute(value, axis, [(i, i ^ bit) for i in range(lax.axis_size(axis...]
    ppermute x8 -> x4, starting transfers between devices: 12.5 us -> 7.57 us  [swapped(): lax.ppermute(value, axis, [(i, i ^ bit) for i in range(lax.axis_size(axis...]
    ppermute x0 -> x4, waiting for transfers between devices: none -> 2.62 us  [passed_on(): return lax.ppermute(value, 'tm', pairs)]
  transfers between devices with their start and end apart: 9 -> 9, of which waited for: 3 -> 3; matrix products, arithmetic and copies ran while one was open for 0% -> 0% of each run, Pallas kernels for 35% -> 32%
where the time goes in v4:
time: 43.5 us; the launch traced here: 43.3 us
  starting transfers between devices  20 us (46%)
  Pallas kernels  19.9 us (46%)
  waiting for transfers between devices  3.11 us (7%)
    ppermute x4, starting transfers between devices, passed_on(): return lax.ppermute(value, 'tm', pairs)  11.8 us
    ppermute x4, starting transfers between devices, swapped(): lax.ppermute(value, axis, [(i, i ^ bit) for i in range(lax.axis_size(axis...  7.57 us
    pallas_call x1, Pallas kernels, shards(): pl.pallas_call(unwrap_kernel, out_shape=(pltpu.VMEM((cables, blocks, time...  7.47 us
    pallas_call x4, Pallas kernels, filtered(): pl.pallas_call(functools.partial(filter_kernel, part * share), out_shape=...  6.51 us
    pallas_call x1, Pallas kernels, shards(): pl.pallas_call(functools.partial(level_kernel, population), out_shape=jax...  4.26 us
    ppermute x4, waiting for transfers between devices, passed_on(): return lax.ppermute(value, 'tm', pairs)  2.62 us
    pallas_call x1, Pallas kernels, shards(): pl.pallas_call(edges_kernel, out_shape=[pltpu.VMEM((cables // 2, time, LA...  1.45 us
  transfers between devices with their start and end apart: 9, of which 3 were waited for; matrix products, arithmetic and copies ran while one was open for 0% of the time, Pallas kernels for 32%

profile of v4, /device:TPU:0, one launch (start us, length us, event | category | flops | bytes accessed | tf_op | source)
XLA Modules:
  0.0 43.3 jit_solution(13528841993120578979)
XLA Ops:
  0.0 1.5 %edges.1 = (f32[4,64,128]{2,1,0:T(8,128)S(1)}, f32[4,64,128]{2,1,0:T(8,128)S(1)}) custom-call(f32[8,64,4096]{2,1,0:T(8,128)} %phase_hbm.3, s32[8,64,4096]{2,1,0:T(8,128)} %wrap_hbm.3), custom_call_target="tpu_custom_call" | custom-call | tf_op jit(solution)/shard_map/edges/pallas_call | solution.py:305
  1.5 0.5 %collective-permute-start = (f32[4,64,128]{2,1,0:T(8,128)S(1)}, f32[4,64,128]{2,1,0:T(8,128)S(1)}, u32[]{:S(2)}, u32[]{:S(2)}) collective-permute-start(f32[4,64,128]{2,1,0:T(8,128)S(1)} %get-tuple-element.31), channel_id=1, source_target_pairs={{0,1},{1,0},{2,3},{3,2},{4,5},{5,4},{6,7},{7,6},{8,9},{9,8},{10,11... | collective-permute-start | bytes 393224 | tf_op jit(solution)/shard_map/ppermute | solution.py:281
  2.0 0.7 %collective-permute-start.1 = (f32[4,64,128]{2,1,0:T(8,128)S(1)}, f32[4,64,128]{2,1,0:T(8,128)S(1)}, u32[]{:S(2)}, u32[]{:S(2)}) collective-permute-start(f32[4,64,128]{2,1,0:T(8,128)S(1)} %get-tuple-element.32), channel_id=1, source_target_pairs={{1,2},{3,4},{5,6},{2,1},{4,3},{6,5},{9,10},{11,12},{13,14},{10,9},... | collective-permute-start | bytes 393224 | tf_op jit(solution)/shard_map/ppermute | solution.py:319
  2.7 7.5 %unwrap.1 = (bf16[8,32,64,128]{3,2,1,0:T(8,128)(2,1)S(1)}, bf16[8,32,64,128]{3,2,1,0:T(8,128)(2,1)S(1)}, f32[256,128]{1,0:T(8,128)S(1)}, f32[8,128]{1,0:T(8,128)S(1)}, bf16[8,512,256]{2,1,0:T(8,128)(2,1)S(1)}) custom-call(f32[8,64,4096]{2,1,0:T(8,128)} %phase_hbm.3, s32[8,64,4096]{2,1,0:T(8,128)} %wrap_hbm.3, f32[8,128]{1,0:T(8,128)S(1)} %copy-done), custom_call_target="tpu_custom_call" | custom-call | bytes 16777216 | tf_op jit(solution)/shard_map/unwrap/pallas_call | solution.py:322
  10.2 0.0 collective-permute-done.1.outer_ref
  10.2 0.2 halo.1
  10.4 3.9 %collective-permute-start.2 = (f32[8,128]{1,0:T(8,128)S(1)}, f32[8,128]{1,0:T(8,128)S(1)}, u32[]{:S(2)}, u32[]{:S(2)}) collective-permute-start(f32[8,128]{1,0:T(8,128)S(1)} %get-tuple-element.34), channel_id=1, source_target_pairs={{0,1},{1,0},{2,3},{3,2},{4,5},{5,4},{6,7},{7,6},{8,9},{9,8},{10,11... | collective-permute-start | bytes 12296 | tf_op jit(solution)/shard_map/ppermute | solution.py:281
  14.3 3.5 %collective-permute-start.4 = (f32[272,128]{1,0:T(8,128)S(1)}, f32[272,128]{1,0:T(8,128)S(1)}, u32[]{:S(2)}, u32[]{:S(2)}) collective-permute-start(f32[272,128]{1,0:T(8,128)S(1)} %constant_dynamic-update-slice_fusion), channel_id=1, source_target_pairs={{0,8},{8,0},{16,24},{1,9},{9,1},{17,25},{2,10},{10,2},{18,26},{3,1... | collective-permute-start | bytes 417800 | tf_op jit(solution)/shard_map/ppermute | solution.py:289
  17.8 1.6 %filter.4.local_refs_0_ = f32[2,32,64,128]{3,2,1,0:T(8,128)S(1)} custom-call(bf16[8,32,64,128]{3,2,1,0:T(8,128)(2,1)S(1)} %get-tuple-element.35.high_ref, bf16[8,32,64,128]{3,2,1,0:T(8,128)(2,1)S(1)} %get-tuple-element.36.low_ref, bf16[8,2,64,128]{3,2,1,0:T(8,128)(2,1)S(1)} %get-tuple-element.37.halo_high_ref, ...), custom_call_target="tpu_custom_call" | custom-call | flops 1140850688 | bytes 1048576 | tf_op jit(solution)/shard_map/filter/pallas_call | solution.py:359
  19.4 1.5 %collective-permute-start.3 = (f32[8,128]{1,0:T(8,128)S(1)}, f32[8,128]{1,0:T(8,128)S(1)}, u32[]{:S(2)}, u32[]{:S(2)}) collective-permute-start(f32[8,128]{1,0:T(8,128)S(1)} %add.15), channel_id=1, source_target_pairs={{0,2},{1,3},{2,0},{3,1},{4,6},{5,7},{6,4},{7,5},{8,10},{9,11},{10,... | collective-permute-start | bytes 12296 | tf_op jit(solution)/shard_map/ppermute | solution.py:281
  21.0 1.6 %filter.5.local_refs_1_ = f32[2,32,64,128]{3,2,1,0:T(8,128)S(1)} custom-call(bf16[8,32,64,128]{3,2,1,0:T(8,128)(2,1)S(1)} %get-tuple-element.35.high_ref, bf16[8,32,64,128]{3,2,1,0:T(8,128)(2,1)S(1)} %get-tuple-element.36.low_ref, bf16[8,2,64,128]{3,2,1,0:T(8,128)(2,1)S(1)} %get-tuple-element.37.halo_high_ref, ...), custom_call_target="tpu_custom_call" | custom-call | flops 1140850688 | bytes 1048576 | tf_op jit(solution)/shard_map/filter/pallas_call | solution.py:359
  22.6 0.5 %collective-permute-done.3 = f32[8,128]{1,0:T(8,128)S(1)} collective-permute-done((f32[8,128]{1,0:T(8,128)S(1)}, f32[8,128]{1,0:T(8,128)S(1)}, u32[]{:S(2)}, u32[]{:S(2)}) %collective-permute-start.3) | collective-permute-done | bytes 4128 | tf_op jit(solution)/shard_map/ppermute | solution.py:281
  23.1 0.0 collective-permute-done.4.totals_refs_0_
  23.2 1.6 %collective-permute-start.5 = (f32[8,128]{1,0:T(8,128)S(1)}, f32[8,128]{1,0:T(8,128)S(1)}, u32[]{:S(2)}, u32[]{:S(2)}) collective-permute-start(f32[8,128]{1,0:T(8,128)S(1)} %add.17), channel_id=1, source_target_pairs={{0,4},{1,5},{2,6},{3,7},{4,0},{5,1},{6,2},{7,3},{8,12},{9,13},{10,... | collective-permute-start | bytes 12296 | tf_op jit(solution)/shard_map/ppermute | solution.py:281
  24.7 4.5 %collective-permute-start.7 = (f32[272,128]{1,0:T(8,128)S(1)}, f32[272,128]{1,0:T(8,128)S(1)}, u32[]{:S(2)}, u32[]{:S(2)}) collective-permute-start(f32[272,128]{1,0:T(8,128)S(1)} %add.16), channel_id=1, source_target_pairs={{0,16},{8,24},{1,17},{9,25},{2,18},{10,26},{3,19},{11,27},{4,20},{... | collective-permute-start | bytes 417800 | tf_op jit(solution)/shard_map/ppermute | solution.py:289
  29.2 1.6 %filter.6.local_refs_2_ = f32[2,32,64,128]{3,2,1,0:T(8,128)S(1)} custom-call(bf16[8,32,64,128]{3,2,1,0:T(8,128)(2,1)S(1)} %get-tuple-element.35.high_ref, bf16[8,32,64,128]{3,2,1,0:T(8,128)(2,1)S(1)} %get-tuple-element.36.low_ref, bf16[8,2,64,128]{3,2,1,0:T(8,128)(2,1)S(1)} %get-tuple-element.37.halo_high_ref, ...), custom_call_target="tpu_custom_call" | custom-call | flops 1140850688 | bytes 1048576 | tf_op jit(solution)/shard_map/filter/pallas_call | solution.py:359
  30.9 0.0 collective-permute-done.5
  30.9 0.0 copy-start.1
  30.9 2.6 %collective-permute-start.6 = (f32[8,128]{1,0:T(8,128)S(1)}, f32[8,128]{1,0:T(8,128)S(1)}, u32[]{:S(2)}, u32[]{:S(2)}) collective-permute-start(f32[8,128]{1,0:T(8,128)S(1)} %add.18.sums_ref), channel_id=1, source_target_pairs={{0,8},{8,0},{16,24},{1,9},{9,1},{17,25},{2,10},{10,2},{18,26},{3,1... | collective-permute-start | bytes 12296 | tf_op jit(solution)/shard_map/ppermute | solution.py:289
  33.5 1.6 %filter.7.local_refs_3_ = f32[2,32,64,128]{3,2,1,0:T(8,128)S(1)} custom-call(bf16[8,32,64,128]{3,2,1,0:T(8,128)(2,1)S(1)} %get-tuple-element.35.high_ref, bf16[8,32,64,128]{3,2,1,0:T(8,128)(2,1)S(1)} %get-tuple-element.36.low_ref, bf16[8,2,64,128]{3,2,1,0:T(8,128)(2,1)S(1)} %get-tuple-element.37.halo_high_ref, ...), custom_call_target="tpu_custom_call" | custom-call | flops 1140850688 | bytes 1048576 | tf_op jit(solution)/shard_map/filter/pallas_call | solution.py:359
  35.1 1.3 %collective-permute-done.6.earlier_refs_0_ = f32[8,128]{1,0:T(8,128)S(1)} collective-permute-done((f32[8,128]{1,0:T(8,128)S(1)}, f32[8,128]{1,0:T(8,128)S(1)}, u32[]{:S(2)}, u32[]{:S(2)}) %collective-permute-start.6) | collective-permute-done | bytes 4128 | tf_op jit(solution)/shard_map/ppermute | solution.py:289
  36.4 1.3 %collective-permute-start.8 = (f32[8,128]{1,0:T(8,128)S(1)}, f32[8,128]{1,0:T(8,128)S(1)}, u32[]{:S(2)}, u32[]{:S(2)}) collective-permute-start(f32[8,128]{1,0:T(8,128)S(1)} %add.19), channel_id=1, source_target_pairs={{0,16},{8,24},{1,17},{9,25},{2,18},{10,26},{3,19},{11,27},{4,20},{... | collective-permute-start | bytes 12296 | tf_op jit(solution)/shard_map/ppermute | solution.py:289
  37.7 1.3 %collective-permute-done.8.earlier_refs_1_ = f32[8,128]{1,0:T(8,128)S(1)} collective-permute-done((f32[8,128]{1,0:T(8,128)S(1)}, f32[8,128]{1,0:T(8,128)S(1)}, u32[]{:S(2)}, u32[]{:S(2)}) %collective-permute-start.8) | collective-permute-done | bytes 4128 | tf_op jit(solution)/shard_map/ppermute | solution.py:289
  39.0 4.3 %level.1 = f32[8,64,4096]{2,1,0:T(8,128)} custom-call(f32[2,32,64,128]{3,2,1,0:T(8,128)S(1)} %filter.4.local_refs_0_, f32[2,32,64,128]{3,2,1,0:T(8,128)S(1)} %filter.5.local_refs_1_, f32[2,32,64,128]{3,2,1,0:T(8,128)S(1)} %filter.6.local_refs_2_, f32[2,32,64,128]{3,2,1,0:T(8,128)S(1)} %filter.7.local_refs_3_, ...), custom_call_target="tpu_custom_call" | custom-call | tf_op jit(solution)/shard_map/level/pallas_call | solution.py:398
  (13 shorter events, 0.1 us)
Async XLA Ops:
  0.0 2.6 %copy-start = (f32[8,128]{1,0:T(8,128)S(1)}, f32[8,128]{1,0:T(8,128)}, u32[]{:S(2)}) copy-start(f32[8,128]{1,0:T(8,128)} %taps_ref.1) | copy-start | bytes 12292
  1.5 8.7 %collective-permute-start = (f32[4,64,128]{2,1,0:T(8,128)S(1)}, f32[4,64,128]{2,1,0:T(8,128)S(1)}, u32[]{:S(2)}, u32[]{:S(2)}) collective-permute-start(f32[4,64,128]{2,1,0:T(8,128)S(1)} %get-tuple-element.31), channel_id=1, source_target_pairs={{0,1},{1,0},{2,3},{3,2},{4,5},{5,4},{6,7},{7,6},{8,9},{9,8},{10,11... | collective-permute-start | bytes 393224 | tf_op jit(solution)/shard_map/ppermute | solution.py:281
  2.0 8.2 %collective-permute-start.1 = (f32[4,64,128]{2,1,0:T(8,128)S(1)}, f32[4,64,128]{2,1,0:T(8,128)S(1)}, u32[]{:S(2)}, u32[]{:S(2)}) collective-permute-start(f32[4,64,128]{2,1,0:T(8,128)S(1)} %get-tuple-element.32), channel_id=1, source_target_pairs={{1,2},{3,4},{5,6},{2,1},{4,3},{6,5},{9,10},{11,12},{13,14},{10,9},... | collective-permute-start | bytes 393224 | tf_op jit(solution)/shard_map/ppermute | solution.py:319
  10.4 9.1 %collective-permute-start.2 = (f32[8,128]{1,0:T(8,128)S(1)}, f32[8,128]{1,0:T(8,128)S(1)}, u32[]{:S(2)}, u32[]{:S(2)}) collective-permute-start(f32[8,128]{1,0:T(8,128)S(1)} %get-tuple-element.34), channel_id=1, source_target_pairs={{0,1},{1,0},{2,3},{3,2},{4,5},{5,4},{6,7},{7,6},{8,9},{9,8},{10,11... | collective-permute-start | bytes 12296 | tf_op jit(solution)/shard_map/ppermute | solution.py:281
  14.3 8.8 %collective-permute-start.4 = (f32[272,128]{1,0:T(8,128)S(1)}, f32[272,128]{1,0:T(8,128)S(1)}, u32[]{:S(2)}, u32[]{:S(2)}) collective-permute-start(f32[272,128]{1,0:T(8,128)S(1)} %constant_dynamic-update-slice_fusion), channel_id=1, source_target_pairs={{0,8},{8,0},{16,24},{1,9},{9,1},{17,25},{2,10},{10,2},{18,26},{3,1... | collective-permute-start | bytes 417800 | tf_op jit(solution)/shard_map/ppermute | solution.py:289
  19.4 3.7 %collective-permute-start.3 = (f32[8,128]{1,0:T(8,128)S(1)}, f32[8,128]{1,0:T(8,128)S(1)}, u32[]{:S(2)}, u32[]{:S(2)}) collective-permute-start(f32[8,128]{1,0:T(8,128)S(1)} %add.15), channel_id=1, source_target_pairs={{0,2},{1,3},{2,0},{3,1},{4,6},{5,7},{6,4},{7,5},{8,10},{9,11},{10,... | collective-permute-start | bytes 12296 | tf_op jit(solution)/shard_map/ppermute | solution.py:281
  23.2 7.7 %collective-permute-start.5 = (f32[8,128]{1,0:T(8,128)S(1)}, f32[8,128]{1,0:T(8,128)S(1)}, u32[]{:S(2)}, u32[]{:S(2)}) collective-permute-start(f32[8,128]{1,0:T(8,128)S(1)} %add.17), channel_id=1, source_target_pairs={{0,4},{1,5},{2,6},{3,7},{4,0},{5,1},{6,2},{7,3},{8,12},{9,13},{10,... | collective-permute-start | bytes 12296 | tf_op jit(solution)/shard_map/ppermute | solution.py:281
  24.7 14.3 %collective-permute-start.7 = (f32[272,128]{1,0:T(8,128)S(1)}, f32[272,128]{1,0:T(8,128)S(1)}, u32[]{:S(2)}, u32[]{:S(2)}) collective-permute-start(f32[272,128]{1,0:T(8,128)S(1)} %add.16), channel_id=1, source_target_pairs={{0,16},{8,24},{1,17},{9,25},{2,18},{10,26},{3,19},{11,27},{4,20},{... | collective-permute-start | bytes 417800 | tf_op jit(solution)/shard_map/ppermute | solution.py:289
  30.9 8.1 %copy-start.1 = (f32[8]{0:T(128)S(1)}, f32[8]{0:T(128)}, u32[]{:S(2)}) copy-start(f32[8]{0:T(128)} %coupling_ref.1) | copy-start | bytes 100
  30.9 5.5 %collective-permute-start.6 = (f32[8,128]{1,0:T(8,128)S(1)}, f32[8,128]{1,0:T(8,128)S(1)}, u32[]{:S(2)}, u32[]{:S(2)}) collective-permute-start(f32[8,128]{1,0:T(8,128)S(1)} %add.18.sums_ref), channel_id=1, source_target_pairs={{0,8},{8,0},{16,24},{1,9},{9,1},{17,25},{2,10},{10,2},{18,26},{3,1... | collective-permute-start | bytes 12296 | tf_op jit(solution)/shard_map/ppermute | solution.py:289
  36.4 2.6 %collective-permute-start.8 = (f32[8,128]{1,0:T(8,128)S(1)}, f32[8,128]{1,0:T(8,128)S(1)}, u32[]{:S(2)}, u32[]{:S(2)}) collective-permute-start(f32[8,128]{1,0:T(8,128)S(1)} %add.19), channel_id=1, source_target_pairs={{0,16},{8,24},{1,17},{9,25},{2,18},{10,26},{3,19},{11,27},{4,20},{... | collective-permute-start | bytes 12296 | tf_op jit(solution)/shard_map/ppermute | solution.py:289

commit v5 on v3

--- a/solution.py
+++ b/solution.py
@@ -139,12 +139,15 @@
     pairs, time, _ = inner_ref.shape
     cables = 2 * pairs
     groups = time // SUBLANES
-    is_even = lax.rem(lax.axis_index("chan"), 2) == 0
+    place = lax.axis_index("chan")
+    is_even = lax.rem(place, 2) == 0
+    at_end = (place == 0) | (place == lax.axis_size("chan") - 1)
     for pair in range(pairs):
         inner, outer = (
             scanned([ref[pair, pl.ds(i * SUBLANES, SUBLANES), :] for i in range(groups)])
             for ref in (inner_ref, outer_ref)
         )
+        outer = [jnp.where(at_end, 0.0, value) for value in outer]
         right = [jnp.where(is_even, a, b) for a, b in zip(inner, outer)]
         left = [jnp.where(is_even, b, a) for a, b in zip(inner, outer)]
         for block, sums, moved in ((0, right, pair + pairs), (1, left, pair)):
@@ -307,8 +310,8 @@
         compiler_params=pltpu.CompilerParams(vmem_limit_bytes=8 << 20),
         name="edges",
     )(phase_step, wrap_count)
-    odd_pairs = [(i, i + 1) for i in range(1, places - 1, 2)]
-    outer = lax.ppermute(outer, "chan", odd_pairs + [(b, a) for a, b in odd_pairs])
+    outer_pairs = [(i, (i + (1 if i % 2 else -1)) % places) for i in range(places)]
+    outer = lax.ppermute(outer, "chan", outer_pairs)
     inner = swapped(inner, "chan", 1)
 
     high, low, totals, sums, weight = pl.pallas_call(
@@ -369,21 +372,24 @@
     rounds += [("tm", 1 << bit) for bit in range(steps.bit_length() - 1)]
     local, received_sums, chan_sums, mark = [], [], sums, sums
     for number, (axis, bit) in enumerate(rounds):
+        if number > 1 and number % 2 == 0 and 1 << len(received) < steps:
+            running = running + received[-1]
+            received.append(swapped(running, "tm", 1 << len(received)))
+            sums, running = lax.optimization_barrier((sums, running))
         incoming = swapped(sums, axis, bit)
         if len(local) < parts:
             tied, mark = lax.optimization_barrier((weight, mark))
             part = filtered(len(local), tied)
             incoming, part = lax.optimization_barrier((incoming, part))
             local.append(part)
-        if number % 2 == 1 and 1 << len(received) < steps:
-            running = running + received[-1]
-            running, incoming = lax.optimization_barrier((running, incoming))
-            received.append(swapped(running, "tm", 1 << len(received)))
         if axis == "tm":
             received_sums.append(incoming)
         sums = mark = sums + incoming
         if axis == "chan":
             chan_sums = sums
+    while 1 << len(received) < steps:
+        running = running + received[-1]
+        received.append(swapped(running, "tm", 1 << len(received)))
     while len(local) < parts:
         local.append(filtered(len(local), weight))
 

time: 40.1 us -> 39.2 us (0.978)
  starting transfers between devices: 13.2 us -> 10.6 us
  waiting for transfers between devices: 6.71 us -> 8.34 us
    ppermute x8, starting transfers between devices: 12.5 us -> 7.06 us  [swapped(): lax.ppermute(value, axis, [(i, i ^ bit) for i in range(lax.axis_size(axis...]
    ppermute x1, starting transfers between devices: 0.66 us -> 3.56 us  [shards(): outer = lax.ppermute(outer, 'chan', outer_pairs)]
    ppermute x8, waiting for transfers between devices: 6.71 us -> 8.34 us  [swapped(): lax.ppermute(value, axis, [(i, i ^ bit) for i in range(lax.axis_size(axis...]
  transfers between devices with their start and end apart: 9 -> 9, of which waited for: 3 -> 4; matrix products, arithmetic and copies ran while one was open for 0% -> 0% of each run, Pallas kernels for 35% -> 36%
where the time goes in v5:
time: 39.2 us; the launch traced here: 39 us
  Pallas kernels  19.9 us (51%)
  starting transfers between devices  10.6 us (27%)
  waiting for transfers between devices  8.34 us (21%)
    ppermute x8, waiting for transfers between devices, swapped(): lax.ppermute(value, axis, [(i, i ^ bit) for i in range(lax.axis_size(axis...  8.34 us
    pallas_call x1, Pallas kernels, shards(): pl.pallas_call(unwrap_kernel, out_shape=(pltpu.VMEM((cables, blocks, time...  7.46 us
    ppermute x8, starting transfers between devices, swapped(): lax.ppermute(value, axis, [(i, i ^ bit) for i in range(lax.axis_size(axis...  7.06 us
    pallas_call x4, Pallas kernels, filtered(): pl.pallas_call(functools.partial(filter_kernel, part * share), out_shape=...  6.5 us
    pallas_call x1, Pallas kernels, shards(): pl.pallas_call(functools.partial(level_kernel, population), out_shape=jax...  4.26 us
    ppermute x1, starting transfers between devices, shards(): outer = lax.ppermute(outer, 'chan', outer_pairs)  3.56 us
    pallas_call x1, Pallas kernels, shards(): pl.pallas_call(edges_kernel, out_shape=[pltpu.VMEM((cables // 2, time, LA...  1.45 us
  transfers between devices with their start and end apart: 9, of which 4 were waited for; matrix products, arithmetic and copies ran while one was open for 0% of the time, Pallas kernels for 36%

profile of v5, /device:TPU:0, one launch (start us, length us, event | category | flops | bytes accessed | tf_op | source)
XLA Modules:
  0.0 39.0 jit_solution(7248663214058722913)
XLA Ops:
  0.0 1.5 %edges.1 = (f32[4,64,128]{2,1,0:T(8,128)S(1)}, f32[4,64,128]{2,1,0:T(8,128)S(1)}) custom-call(f32[8,64,4096]{2,1,0:T(8,128)} %phase_hbm.3, s32[8,64,4096]{2,1,0:T(8,128)} %wrap_hbm.3), custom_call_target="tpu_custom_call" | custom-call | tf_op jit(solution)/shard_map/edges/pallas_call | solution.py:300
  1.5 0.5 %collective-permute-start = (f32[4,64,128]{2,1,0:T(8,128)S(1)}, f32[4,64,128]{2,1,0:T(8,128)S(1)}, u32[]{:S(2)}, u32[]{:S(2)}) collective-permute-start(f32[4,64,128]{2,1,0:T(8,128)S(1)} %get-tuple-element.30), channel_id=1, source_target_pairs={{0,1},{1,0},{2,3},{3,2},{4,5},{5,4},{6,7},{7,6},{8,9},{9,8},{10,11... | collective-permute-start | bytes 393224 | tf_op jit(solution)/shard_map/ppermute | solution.py:284
  2.0 3.6 %collective-permute-start.1 = (f32[4,64,128]{2,1,0:T(8,128)S(1)}, f32[4,64,128]{2,1,0:T(8,128)S(1)}, u32[]{:S(2)}, u32[]{:S(2)}) collective-permute-start(f32[4,64,128]{2,1,0:T(8,128)S(1)} %get-tuple-element.31), channel_id=1, source_target_pairs={{0,7},{1,2},{2,1},{3,4},{4,3},{5,6},{6,5},{7,0},{8,15},{9,10},{10,... | collective-permute-start | bytes 393224 | tf_op jit(solution)/shard_map/ppermute | solution.py:314
  5.5 7.5 %unwrap.1 = (bf16[8,32,64,128]{3,2,1,0:T(8,128)(2,1)S(1)}, bf16[8,32,64,128]{3,2,1,0:T(8,128)(2,1)S(1)}, f32[256,128]{1,0:T(8,128)S(1)}, f32[8,128]{1,0:T(8,128)S(1)}, bf16[8,512,256]{2,1,0:T(8,128)(2,1)S(1)}) custom-call(f32[8,64,4096]{2,1,0:T(8,128)} %phase_hbm.3, s32[8,64,4096]{2,1,0:T(8,128)} %wrap_hbm.3, f32[8,128]{1,0:T(8,128)S(1)} %copy-done), custom_call_target="tpu_custom_call" | custom-call | bytes 16777216 | tf_op jit(solution)/shard_map/unwrap/pallas_call | solution.py:317
  13.0 0.0 collective-permute-done.inner_ref
  13.0 0.0 collective-permute-done.1.outer_ref
  13.0 0.2 halo.1
  13.3 0.1 collective-permute-start.2
  13.4 1.6 %collective-permute-start.4 = (f32[272,128]{1,0:T(8,128)S(1)}, f32[272,128]{1,0:T(8,128)S(1)}, u32[]{:S(2)}, u32[]{:S(2)}) collective-permute-start(f32[272,128]{1,0:T(8,128)S(1)} %constant_dynamic-update-slice_fusion), channel_id=1, source_target_pairs={{0,8},{8,0},{16,24},{24,16},{1,9},{9,1},{17,25},{25,17},{2,10},{10... | collective-permute-start | bytes 417800 | tf_op jit(solution)/shard_map/ppermute | solution.py:284
  15.0 1.6 %filter.4.local_refs_0_ = f32[2,32,64,128]{3,2,1,0:T(8,128)S(1)} custom-call(bf16[8,32,64,128]{3,2,1,0:T(8,128)(2,1)S(1)} %get-tuple-element.34.high_ref, bf16[8,32,64,128]{3,2,1,0:T(8,128)(2,1)S(1)} %get-tuple-element.35.low_ref, bf16[8,2,64,128]{3,2,1,0:T(8,128)(2,1)S(1)} %get-tuple-element.36.halo_high_ref, ...), custom_call_target="tpu_custom_call" | custom-call | flops 1140850688 | bytes 1048576 | tf_op jit(solution)/shard_map/filter/pallas_call | solution.py:354
  16.7 0.6 %collective-permute-start.3 = (f32[8,128]{1,0:T(8,128)S(1)}, f32[8,128]{1,0:T(8,128)S(1)}, u32[]{:S(2)}, u32[]{:S(2)}) collective-permute-start(f32[8,128]{1,0:T(8,128)S(1)} %add.15), channel_id=1, source_target_pairs={{0,2},{1,3},{2,0},{3,1},{4,6},{5,7},{6,4},{7,5},{8,10},{9,11},{10,... | collective-permute-start | bytes 12296 | tf_op jit(solution)/shard_map/ppermute | solution.py:284
  17.2 1.6 %filter.5.local_refs_1_ = f32[2,32,64,128]{3,2,1,0:T(8,128)S(1)} custom-call(bf16[8,32,64,128]{3,2,1,0:T(8,128)(2,1)S(1)} %get-tuple-element.34.high_ref, bf16[8,32,64,128]{3,2,1,0:T(8,128)(2,1)S(1)} %get-tuple-element.35.low_ref, bf16[8,2,64,128]{3,2,1,0:T(8,128)(2,1)S(1)} %get-tuple-element.36.halo_high_ref, ...), custom_call_target="tpu_custom_call" | custom-call | flops 1140850688 | bytes 1048576 | tf_op jit(solution)/shard_map/filter/pallas_call | solution.py:354
  18.9 1.5 %collective-permute-done.3 = f32[8,128]{1,0:T(8,128)S(1)} collective-permute-done((f32[8,128]{1,0:T(8,128)S(1)}, f32[8,128]{1,0:T(8,128)S(1)}, u32[]{:S(2)}, u32[]{:S(2)}) %collective-permute-start.3) | collective-permute-done | bytes 4128 | tf_op jit(solution)/shard_map/ppermute | solution.py:284
  20.4 2.7 %collective-permute-start.7 = (f32[272,128]{1,0:T(8,128)S(1)}, f32[272,128]{1,0:T(8,128)S(1)}, u32[]{:S(2)}, u32[]{:S(2)}) collective-permute-start(f32[272,128]{1,0:T(8,128)S(1)} %add.17), channel_id=1, source_target_pairs={{0,16},{8,24},{16,0},{24,8},{1,17},{9,25},{17,1},{25,9},{2,18},{10... | collective-permute-start | bytes 417800 | tf_op jit(solution)/shard_map/ppermute | solution.py:284
  23.0 0.6 %collective-permute-start.5 = (f32[8,128]{1,0:T(8,128)S(1)}, f32[8,128]{1,0:T(8,128)S(1)}, u32[]{:S(2)}, u32[]{:S(2)}) collective-permute-start(f32[8,128]{1,0:T(8,128)S(1)} %add.16), channel_id=1, source_target_pairs={{0,4},{1,5},{2,6},{3,7},{4,0},{5,1},{6,2},{7,3},{8,12},{9,13},{10,... | collective-permute-start | bytes 12296 | tf_op jit(solution)/shard_map/ppermute | solution.py:284
  23.6 1.6 %filter.6.local_refs_2_ = f32[2,32,64,128]{3,2,1,0:T(8,128)S(1)} custom-call(bf16[8,32,64,128]{3,2,1,0:T(8,128)(2,1)S(1)} %get-tuple-element.34.high_ref, bf16[8,32,64,128]{3,2,1,0:T(8,128)(2,1)S(1)} %get-tuple-element.35.low_ref, bf16[8,2,64,128]{3,2,1,0:T(8,128)(2,1)S(1)} %get-tuple-element.36.halo_high_ref, ...), custom_call_target="tpu_custom_call" | custom-call | flops 1140850688 | bytes 1048576 | tf_op jit(solution)/shard_map/filter/pallas_call | solution.py:354
  25.2 1.4 %collective-permute-done.5 = f32[8,128]{1,0:T(8,128)S(1)} collective-permute-done((f32[8,128]{1,0:T(8,128)S(1)}, f32[8,128]{1,0:T(8,128)S(1)}, u32[]{:S(2)}, u32[]{:S(2)}) %collective-permute-start.5) | collective-permute-done | bytes 4128 | tf_op jit(solution)/shard_map/ppermute | solution.py:284
  26.6 0.7 %collective-permute-start.6 = (f32[8,128]{1,0:T(8,128)S(1)}, f32[8,128]{1,0:T(8,128)S(1)}, u32[]{:S(2)}, u32[]{:S(2)}) collective-permute-start(f32[8,128]{1,0:T(8,128)S(1)} %add.18.sums_ref), channel_id=1, source_target_pairs={{0,8},{8,0},{16,24},{24,16},{1,9},{9,1},{17,25},{25,17},{2,10},{10... | collective-permute-start | bytes 12296 | tf_op jit(solution)/shard_map/ppermute | solution.py:284
  27.3 1.6 %filter.7.local_refs_3_ = f32[2,32,64,128]{3,2,1,0:T(8,128)S(1)} custom-call(bf16[8,32,64,128]{3,2,1,0:T(8,128)(2,1)S(1)} %get-tuple-element.34.high_ref, bf16[8,32,64,128]{3,2,1,0:T(8,128)(2,1)S(1)} %get-tuple-element.35.low_ref, bf16[8,2,64,128]{3,2,1,0:T(8,128)(2,1)S(1)} %get-tuple-element.36.halo_high_ref, ...), custom_call_target="tpu_custom_call" | custom-call | flops 1140850688 | bytes 1048576 | tf_op jit(solution)/shard_map/filter/pallas_call | solution.py:354
  28.9 1.3 %collective-permute-done.6.earlier_refs_0_ = f32[8,128]{1,0:T(8,128)S(1)} collective-permute-done((f32[8,128]{1,0:T(8,128)S(1)}, f32[8,128]{1,0:T(8,128)S(1)}, u32[]{:S(2)}, u32[]{:S(2)}) %collective-permute-start.6) | collective-permute-done | bytes 4128 | tf_op jit(solution)/shard_map/ppermute | solution.py:284
  30.2 0.3 collective-permute-start.8
  30.6 4.2 %collective-permute-done.8.earlier_refs_1_ = f32[8,128]{1,0:T(8,128)S(1)} collective-permute-done((f32[8,128]{1,0:T(8,128)S(1)}, f32[8,128]{1,0:T(8,128)S(1)}, u32[]{:S(2)}, u32[]{:S(2)}) %collective-permute-start.8) | collective-permute-done | bytes 4128 | tf_op jit(solution)/shard_map/ppermute | solution.py:284
  34.7 0.0 collective-permute-done.7.totals_refs_1_
  34.7 4.3 %level.1 = f32[8,64,4096]{2,1,0:T(8,128)} custom-call(f32[2,32,64,128]{3,2,1,0:T(8,128)S(1)} %filter.4.local_refs_0_, f32[2,32,64,128]{3,2,1,0:T(8,128)S(1)} %filter.5.local_refs_1_, f32[2,32,64,128]{3,2,1,0:T(8,128)S(1)} %filter.6.local_refs_2_, f32[2,32,64,128]{3,2,1,0:T(8,128)S(1)} %filter.7.local_refs_3_, ...), custom_call_target="tpu_custom_call" | custom-call | tf_op jit(solution)/shard_map/level/pallas_call | solution.py:396
  (13 shorter events, 0.1 us)
Async XLA Ops:
  0.0 5.5 %copy-start = (f32[8,128]{1,0:T(8,128)S(1)}, f32[8,128]{1,0:T(8,128)}, u32[]{:S(2)}) copy-start(f32[8,128]{1,0:T(8,128)} %taps_ref.1) | copy-start | bytes 12292
  1.5 11.6 %collective-permute-start = (f32[4,64,128]{2,1,0:T(8,128)S(1)}, f32[4,64,128]{2,1,0:T(8,128)S(1)}, u32[]{:S(2)}, u32[]{:S(2)}) collective-permute-start(f32[4,64,128]{2,1,0:T(8,128)S(1)} %get-tuple-element.30), channel_id=1, source_target_pairs={{0,1},{1,0},{2,3},{3,2},{4,5},{5,4},{6,7},{7,6},{8,9},{9,8},{10,11... | collective-permute-start | bytes 393224 | tf_op jit(solution)/shard_map/ppermute | solution.py:284
  2.0 11.1 %collective-permute-start.1 = (f32[4,64,128]{2,1,0:T(8,128)S(1)}, f32[4,64,128]{2,1,0:T(8,128)S(1)}, u32[]{:S(2)}, u32[]{:S(2)}) collective-permute-start(f32[4,64,128]{2,1,0:T(8,128)S(1)} %get-tuple-element.31), channel_id=1, source_target_pairs={{0,7},{1,2},{2,1},{3,4},{4,3},{5,6},{6,5},{7,0},{8,15},{9,10},{10,... | collective-permute-start | bytes 393224 | tf_op jit(solution)/shard_map/ppermute | solution.py:314
  13.3 3.4 %collective-permute-start.2 = (f32[8,128]{1,0:T(8,128)S(1)}, f32[8,128]{1,0:T(8,128)S(1)}, u32[]{:S(2)}, u32[]{:S(2)}) collective-permute-start(f32[8,128]{1,0:T(8,128)S(1)} %get-tuple-element.33), channel_id=1, source_target_pairs={{0,1},{1,0},{2,3},{3,2},{4,5},{5,4},{6,7},{7,6},{8,9},{9,8},{10,11... | collective-permute-start | bytes 12296 | tf_op jit(solution)/shard_map/ppermute | solution.py:284
  13.4 7.0 %collective-permute-start.4 = (f32[272,128]{1,0:T(8,128)S(1)}, f32[272,128]{1,0:T(8,128)S(1)}, u32[]{:S(2)}, u32[]{:S(2)}) collective-permute-start(f32[272,128]{1,0:T(8,128)S(1)} %constant_dynamic-update-slice_fusion), channel_id=1, source_target_pairs={{0,8},{8,0},{16,24},{24,16},{1,9},{9,1},{17,25},{25,17},{2,10},{10... | collective-permute-start | bytes 417800 | tf_op jit(solution)/shard_map/ppermute | solution.py:284
  16.7 3.7 %collective-permute-start.3 = (f32[8,128]{1,0:T(8,128)S(1)}, f32[8,128]{1,0:T(8,128)S(1)}, u32[]{:S(2)}, u32[]{:S(2)}) collective-permute-start(f32[8,128]{1,0:T(8,128)S(1)} %add.15), channel_id=1, source_target_pairs={{0,2},{1,3},{2,0},{3,1},{4,6},{5,7},{6,4},{7,5},{8,10},{9,11},{10,... | collective-permute-start | bytes 12296 | tf_op jit(solution)/shard_map/ppermute | solution.py:284
  20.4 14.4 %collective-permute-start.7 = (f32[272,128]{1,0:T(8,128)S(1)}, f32[272,128]{1,0:T(8,128)S(1)}, u32[]{:S(2)}, u32[]{:S(2)}) collective-permute-start(f32[272,128]{1,0:T(8,128)S(1)} %add.17), channel_id=1, source_target_pairs={{0,16},{8,24},{16,0},{24,8},{1,17},{9,25},{17,1},{25,9},{2,18},{10... | collective-permute-start | bytes 417800 | tf_op jit(solution)/shard_map/ppermute | solution.py:284
  23.0 3.6 %collective-permute-start.5 = (f32[8,128]{1,0:T(8,128)S(1)}, f32[8,128]{1,0:T(8,128)S(1)}, u32[]{:S(2)}, u32[]{:S(2)}) collective-permute-start(f32[8,128]{1,0:T(8,128)S(1)} %add.16), channel_id=1, source_target_pairs={{0,4},{1,5},{2,6},{3,7},{4,0},{5,1},{6,2},{7,3},{8,12},{9,13},{10,... | collective-permute-start | bytes 12296 | tf_op jit(solution)/shard_map/ppermute | solution.py:284
  26.6 8.1 %copy-start.1 = (f32[8]{0:T(128)S(1)}, f32[8]{0:T(128)}, u32[]{:S(2)}) copy-start(f32[8]{0:T(128)} %coupling_ref.1) | copy-start | bytes 100
  26.6 3.6 %collective-permute-start.6 = (f32[8,128]{1,0:T(8,128)S(1)}, f32[8,128]{1,0:T(8,128)S(1)}, u32[]{:S(2)}, u32[]{:S(2)}) collective-permute-start(f32[8,128]{1,0:T(8,128)S(1)} %add.18.sums_ref), channel_id=1, source_target_pairs={{0,8},{8,0},{16,24},{24,16},{1,9},{9,1},{17,25},{25,17},{2,10},{10... | collective-permute-start | bytes 12296 | tf_op jit(solution)/shard_map/ppermute | solution.py:284
  30.2 4.5 %collective-permute-start.8 = (f32[8,128]{1,0:T(8,128)S(1)}, f32[8,128]{1,0:T(8,128)S(1)}, u32[]{:S(2)}, u32[]{:S(2)}) collective-permute-start(f32[8,128]{1,0:T(8,128)S(1)} %add.19), channel_id=1, source_target_pairs={{0,16},{8,24},{16,0},{24,8},{1,17},{9,25},{17,1},{25,9},{2,18},{10... | collective-permute-start | bytes 12296 | tf_op jit(solution)/shard_map/ppermute | solution.py:284

commit v6 on v5

--- a/solution.py
+++ b/solution.py
@@ -12,6 +12,7 @@
 LANES = 128
 HALF = LANES // 2
 SUBLANES = 8
+CHUNKS = 2
 
 
 def shifted_down(value, amount):
@@ -82,14 +83,21 @@
     blocks = width // LANES
     groups = time // SUBLANES
 
-    def copies(cable):
+    span = width // CHUNKS
+
+    def copies(chunk):
+        cable, lanes = chunk // CHUNKS, pl.ds(pl.multiple_of(chunk % CHUNKS * span, span), span)
         return (
-            pltpu.make_async_copy(phase_hbm.at[cable], phase_ref.at[cable], sem.at[0, cable]),
-            pltpu.make_async_copy(wrap_hbm.at[cable], wrap_ref.at[cable], sem.at[1, cable]),
-        )
-
-    for cable in range(cables):
-        for copy in copies(cable):
+            pltpu.make_async_copy(
+                phase_hbm.at[cable, :, lanes], phase_ref.at[cable, :, lanes], sem.at[0, chunk]
+            ),
+            pltpu.make_async_copy(
+                wrap_hbm.at[cable, :, lanes], wrap_ref.at[cable, :, lanes], sem.at[1, chunk]
+            ),
+        )
+
+    for chunk in range(cables * CHUNKS):
+        for copy in copies(chunk):
             copy.start()
 
     outputs = lax.broadcasted_iota(jnp.int32, (LANES, LANES), 0)
@@ -108,11 +116,14 @@
         for place, part in enumerate((high, high, low, low)):
             weight_ref[cable, pl.ds(place * LANES, LANES), :] = part
 
-    def cable_step(cable, accumulated):
-        for copy in copies(cable):
+    def chunk_step(chunk, accumulated):
+        for copy in copies(chunk):
             copy.wait()
-
-        def block_step(block, accumulated):
+        cable = chunk // CHUNKS
+        start = chunk % CHUNKS * (blocks // CHUNKS)
+
+        def block_step(index, accumulated):
+            block = start + index
             lanes = pl.ds(pl.multiple_of(block * LANES, LANES), LANES)
             pieces = []
             for i in range(groups):
@@ -124,10 +135,10 @@
             totals_ref[pl.ds(block * cables + cable, 1), :] = sums[-1][SUBLANES - 1 :, :]
             return tuple(a + b for a, b in zip(accumulated, sums))
 
-        return lax.fori_loop(0, blocks, block_step, accumulated, unroll=4)
+        return lax.fori_loop(0, blocks // CHUNKS, block_step, accumulated, unroll=4)
 
     zeros = tuple(jnp.zeros((SUBLANES, LANES), jnp.float32) for _ in range(groups))
-    accumulated = lax.fori_loop(0, cables, cable_step, zeros)
+    accumulated = lax.fori_loop(0, cables * CHUNKS, chunk_step, zeros)
     lane = lax.broadcasted_iota(jnp.int32, (SUBLANES, LANES), 1)
     tile = jnp.zeros((SUBLANES, LANES), jnp.float32)
     for i, value in enumerate(accumulated):
@@ -198,7 +209,8 @@
     population, local_refs, weight_ref, totals_refs, sums_ref, earlier_refs, coupling_ref,
     out_hbm, stage_ref, offset_ref, sem,
 ):
-    share, blocks, time, _ = local_refs[0].shape
+    _, blocks, time, _ = local_refs[0].shape
+    span = blocks * LANES // CHUNKS
     cables = out_hbm.shape[0]
     groups = time // SUBLANES
     step, place = lax.axis_index("tm"), lax.axis_index("chan")
@@ -249,11 +261,18 @@
         last = jnp.where(lane[:1] < HALF, middle, last)
         return bias, first, middle, last
 
+    def written(cable, chunk):
+        lanes = pl.ds(chunk * span, span)
+        return pltpu.make_async_copy(
+            stage_ref.at[cable, :, lanes], out_hbm.at[cable, :, lanes], sem.at[cable, chunk]
+        )
+
     carry = filtered_offset(0)
-    for part, local_ref in enumerate(local_refs):
-
-        def cable_step(index, carry, part=part, local_ref=local_ref):
-            cable = part * share + index
+    first_cable = 0
+    for local_ref in local_refs:
+
+        def cable_step(index, carry, first_cable=first_cable, local_ref=local_ref):
+            cable = first_cable + index
             following = filtered_offset(jnp.minimum(cable + 1, cables - 1))
             bias, first, middle, last = carry
             shifts = [coupling_ref[cable] * column for column in columns]
@@ -272,12 +291,15 @@
                     stage_ref[cable, rows, lanes] = local_ref[index, block, rows, :] + (
                         added - slopes[i]
                     )
-            pltpu.make_async_copy(stage_ref.at[cable], out_hbm.at[cable], sem.at[cable]).start()
+                if (block + 1) % (blocks // CHUNKS) == 0:
+                    written(cable, block // (blocks // CHUNKS)).start()
             return following
 
-        carry = lax.fori_loop(0, share, cable_step, carry)
+        carry = lax.fori_loop(0, local_ref.shape[0], cable_step, carry)
+        first_cable += local_ref.shape[0]
     for cable in range(cables):
-        pltpu.make_async_copy(stage_ref.at[cable], out_hbm.at[cable], sem.at[cable]).wait()
+        for chunk in range(CHUNKS):
+            written(cable, chunk).wait()
 
 
 def swapped(value, axis, bit):
@@ -289,8 +311,8 @@
     blocks = width // LANES
     steps, places = lax.axis_size("tm"), lax.axis_size("chan")
     population = cables * width * places
-    parts = 4
-    share = cables // parts
+    bounds = [0, 3 * cables // 8, 5 * cables // 8, cables]
+    parts = len(bounds) - 1
     phase_step = pltpu.with_memory_space_constraint(phase_step, pltpu.HBM)
     wrap_count = pltpu.with_memory_space_constraint(wrap_count, pltpu.HBM)
     whole = pl.BlockSpec(memory_space=pltpu.VMEM)
@@ -328,7 +350,7 @@
         scratch_shapes=[
             pltpu.VMEM((cables, time, width), jnp.float32),
             pltpu.VMEM((cables, time, width), jnp.int32),
-            pltpu.SemaphoreType.DMA((2, cables)),
+            pltpu.SemaphoreType.DMA((2, cables * CHUNKS)),
         ],
         compiler_params=pltpu.CompilerParams(vmem_limit_bytes=40 << 20),
         cost_estimate=pl.CostEstimate(
@@ -351,8 +373,9 @@
     )(inner, outer)
 
     def filtered(part, weight):
+        share = bounds[part + 1] - bounds[part]
         return pl.pallas_call(
-            functools.partial(filter_kernel, part * share),
+            functools.partial(filter_kernel, bounds[part]),
             out_shape=pltpu.VMEM((share, blocks, time, LANES), jnp.float32),
             in_specs=[whole] * 5,
             out_specs=whole,
@@ -370,25 +393,28 @@
     sums, halo_totals = lax.optimization_barrier((sums, halo_totals))
     rounds = [("chan", 1 << bit) for bit in range(places.bit_length() - 1)]
     rounds += [("tm", 1 << bit) for bit in range(steps.bit_length() - 1)]
-    local, received_sums, chan_sums, mark = [], [], sums, sums
+    local, received_sums, chan_sums, ready = [], [], sums, None
     for number, (axis, bit) in enumerate(rounds):
-        if number > 1 and number % 2 == 0 and 1 << len(received) < steps:
-            running = running + received[-1]
-            received.append(swapped(running, "tm", 1 << len(received)))
-            sums, running = lax.optimization_barrier((sums, running))
         incoming = swapped(sums, axis, bit)
-        if len(local) < parts:
-            tied, mark = lax.optimization_barrier((weight, mark))
+        if number % 2 == 0 and number > 0 and ready is not None:
+            received.append(swapped(ready, "tm", 1 << len(received)))
+            ready = None
+        elif number > 0 and len(local) < parts:
+            tied, sums = lax.optimization_barrier((weight, sums))
             part = filtered(len(local), tied)
             incoming, part = lax.optimization_barrier((incoming, part))
             local.append(part)
+        if number % 2 == 1 and 1 << len(received) < steps:
+            running = running + received[-1]
+            ready, incoming = lax.optimization_barrier((running, incoming))
         if axis == "tm":
             received_sums.append(incoming)
-        sums = mark = sums + incoming
+        sums = sums + incoming
         if axis == "chan":
             chan_sums = sums
     while 1 << len(received) < steps:
-        running = running + received[-1]
+        running = running + received[-1] if ready is None else ready
+        ready = None
         received.append(swapped(running, "tm", 1 << len(received)))
     while len(local) < parts:
         local.append(filtered(len(local), weight))
@@ -403,7 +429,7 @@
         scratch_shapes=[
             pltpu.VMEM((cables, time, width), jnp.float32),
             pltpu.VMEM(((blocks + 2) * cables, LANES), jnp.float32),
-            pltpu.SemaphoreType.DMA((cables,)),
+            pltpu.SemaphoreType.DMA((cables, CHUNKS)),
         ],
         compiler_params=pltpu.CompilerParams(vmem_limit_bytes=24 << 20),
         name="level",

time: 39.2 us -> 36.5 us (0.931)
  waiting for transfers between devices: 8.34 us -> 2.39 us
  starting transfers between devices: 10.6 us -> 13.6 us
    ppermute x8, waiting for transfers between devices: 8.34 us -> 2.39 us  [swapped(): lax.ppermute(value, axis, [(i, i ^ bit) for i in range(lax.axis_size(axis...]
    ppermute x8, starting transfers between devices: 7.06 us -> 10.1 us  [swapped(): lax.ppermute(value, axis, [(i, i ^ bit) for i in range(lax.axis_size(axis...]
    pallas_call x4 -> x3, Pallas kernels: 6.5 us -> 6.51 us  [filtered(): pl.pallas_call(functools.partial(filter_kernel, bounds[part]), out_shape=...]
  transfers between devices with their start and end apart: 9 -> 9, of which waited for: 4 -> 4; matrix products, arithmetic and copies ran while one was open for 0% -> 0% of each run, Pallas kernels for 36% -> 39%
where the time goes in v6:
time: 36.5 us; the launch traced here: 36.4 us
  Pallas kernels  20.2 us (55%)
  starting transfers between devices  13.6 us (37%)
  waiting for transfers between devices  2.39 us (7%)
    ppermute x8, starting transfers between devices, swapped(): lax.ppermute(value, axis, [(i, i ^ bit) for i in range(lax.axis_size(axis...  10.1 us
    pallas_call x1, Pallas kernels, shards(): pl.pallas_call(unwrap_kernel, out_shape=(pltpu.VMEM((cables, blocks, time...  7.73 us
    pallas_call x3, Pallas kernels, filtered(): pl.pallas_call(functools.partial(filter_kernel, bounds[part]), out_shape=...  6.51 us
    pallas_call x1, Pallas kernels, shards(): pl.pallas_call(functools.partial(level_kernel, population), out_shape=jax...  4.27 us
    ppermute x1, starting transfers between devices, shards(): outer = lax.ppermute(outer, 'chan', outer_pairs)  3.56 us
    ppermute x8, waiting for transfers between devices, swapped(): lax.ppermute(value, axis, [(i, i ^ bit) for i in range(lax.axis_size(axis...  2.39 us
    pallas_call x1, Pallas kernels, shards(): pl.pallas_call(edges_kernel, out_shape=[pltpu.VMEM((cables // 2, time, LA...  1.45 us
  transfers between devices with their start and end apart: 9, of which 4 were waited for; matrix products, arithmetic and copies ran while one was open for 0% of the time, Pallas kernels for 39%

profile of v6, /device:TPU:0, one launch (start us, length us, event | category | flops | bytes accessed | tf_op | source)
XLA Modules:
  0.0 36.4 jit_solution(9313023611658536971)
XLA Ops:
  0.0 1.5 %edges.1 = (f32[4,64,128]{2,1,0:T(8,128)S(1)}, f32[4,64,128]{2,1,0:T(8,128)S(1)}) custom-call(f32[8,64,4096]{2,1,0:T(8,128)} %phase_hbm.3, s32[8,64,4096]{2,1,0:T(8,128)} %wrap_hbm.3), custom_call_target="tpu_custom_call" | custom-call | tf_op jit(solution)/shard_map/edges/pallas_call | solution.py:322
  1.5 0.5 %collective-permute-start = (f32[4,64,128]{2,1,0:T(8,128)S(1)}, f32[4,64,128]{2,1,0:T(8,128)S(1)}, u32[]{:S(2)}, u32[]{:S(2)}) collective-permute-start(f32[4,64,128]{2,1,0:T(8,128)S(1)} %get-tuple-element.30), channel_id=1, source_target_pairs={{0,1},{1,0},{2,3},{3,2},{4,5},{5,4},{6,7},{7,6},{8,9},{9,8},{10,11... | collective-permute-start | bytes 393224 | tf_op jit(solution)/shard_map/ppermute | solution.py:306
  2.0 3.6 %collective-permute-start.1 = (f32[4,64,128]{2,1,0:T(8,128)S(1)}, f32[4,64,128]{2,1,0:T(8,128)S(1)}, u32[]{:S(2)}, u32[]{:S(2)}) collective-permute-start(f32[4,64,128]{2,1,0:T(8,128)S(1)} %get-tuple-element.31), channel_id=1, source_target_pairs={{0,7},{1,2},{2,1},{3,4},{4,3},{5,6},{6,5},{7,0},{8,15},{9,10},{10,... | collective-permute-start | bytes 393224 | tf_op jit(solution)/shard_map/ppermute | solution.py:336
  5.5 7.7 %unwrap.1 = (bf16[8,32,64,128]{3,2,1,0:T(8,128)(2,1)S(1)}, bf16[8,32,64,128]{3,2,1,0:T(8,128)(2,1)S(1)}, f32[256,128]{1,0:T(8,128)S(1)}, f32[8,128]{1,0:T(8,128)S(1)}, bf16[8,512,256]{2,1,0:T(8,128)(2,1)S(1)}) custom-call(f32[8,64,4096]{2,1,0:T(8,128)} %phase_hbm.3, s32[8,64,4096]{2,1,0:T(8,128)} %wrap_hbm.3, f32[8,128]{1,0:T(8,128)S(1)} %copy-done), custom_call_target="tpu_custom_call" | custom-call | bytes 16777216 | tf_op jit(solution)/shard_map/unwrap/pallas_call | solution.py:339
  13.3 0.0 collective-permute-done.inner_ref
  13.3 0.0 collective-permute-done.1.outer_ref
  13.3 0.2 halo.1
  13.5 0.1 collective-permute-start.2
  13.6 1.6 %collective-permute-start.4 = (f32[272,128]{1,0:T(8,128)S(1)}, f32[272,128]{1,0:T(8,128)S(1)}, u32[]{:S(2)}, u32[]{:S(2)}) collective-permute-start(f32[272,128]{1,0:T(8,128)S(1)} %constant_dynamic-update-slice_fusion), channel_id=1, source_target_pairs={{0,8},{8,0},{16,24},{24,16},{1,9},{9,1},{17,25},{25,17},{2,10},{10... | collective-permute-start | bytes 417800 | tf_op jit(solution)/shard_map/ppermute | solution.py:306
  15.3 0.0 collective-permute-done.2
  15.3 0.5 %collective-permute-start.3 = (f32[8,128]{1,0:T(8,128)S(1)}, f32[8,128]{1,0:T(8,128)S(1)}, u32[]{:S(2)}, u32[]{:S(2)}) collective-permute-start(f32[8,128]{1,0:T(8,128)S(1)} %add.15), channel_id=1, source_target_pairs={{0,2},{1,3},{2,0},{3,1},{4,6},{5,7},{6,4},{7,5},{8,10},{9,11},{10,... | collective-permute-start | bytes 12296 | tf_op jit(solution)/shard_map/ppermute | solution.py:306
  15.8 2.4 %filter.3.local_refs_0_ = f32[3,32,64,128]{3,2,1,0:T(8,128)S(1)} custom-call(bf16[8,32,64,128]{3,2,1,0:T(8,128)(2,1)S(1)} %get-tuple-element.34.high_ref, bf16[8,32,64,128]{3,2,1,0:T(8,128)(2,1)S(1)} %get-tuple-element.35.low_ref, bf16[8,2,64,128]{3,2,1,0:T(8,128)(2,1)S(1)} %get-tuple-element.36.halo_high_ref, ...), custom_call_target="tpu_custom_call" | custom-call | flops 1711276032 | bytes 1048576 | tf_op jit(solution)/shard_map/filter/pallas_call | solution.py:377
  18.2 0.6 %collective-permute-done.3 = f32[8,128]{1,0:T(8,128)S(1)} collective-permute-done((f32[8,128]{1,0:T(8,128)S(1)}, f32[8,128]{1,0:T(8,128)S(1)}, u32[]{:S(2)}, u32[]{:S(2)}) %collective-permute-start.3) | collective-permute-done | bytes 4128 | tf_op jit(solution)/shard_map/ppermute | solution.py:306
  18.9 0.8 %collective-permute-done.4.totals_refs_0_ = f32[272,128]{1,0:T(8,128)S(1)} collective-permute-done((f32[272,128]{1,0:T(8,128)S(1)}, f32[272,128]{1,0:T(8,128)S(1)}, u32[]{:S(2)}, u32[]{:S(2)}) %collective-permute-start.4) | collective-permute-done | bytes 139296 | tf_op jit(solution)/shard_map/ppermute | solution.py:306
  19.7 0.6 %collective-permute-start.5 = (f32[8,128]{1,0:T(8,128)S(1)}, f32[8,128]{1,0:T(8,128)S(1)}, u32[]{:S(2)}, u32[]{:S(2)}) collective-permute-start(f32[8,128]{1,0:T(8,128)S(1)} %add.17), channel_id=1, source_target_pairs={{0,4},{1,5},{2,6},{3,7},{4,0},{5,1},{6,2},{7,3},{8,12},{9,13},{10,... | collective-permute-start | bytes 12296 | tf_op jit(solution)/shard_map/ppermute | solution.py:306
  20.3 2.6 %collective-permute-start.8 = (f32[272,128]{1,0:T(8,128)S(1)}, f32[272,128]{1,0:T(8,128)S(1)}, u32[]{:S(2)}, u32[]{:S(2)}) collective-permute-start(f32[272,128]{1,0:T(8,128)S(1)} %add.16), channel_id=1, source_target_pairs={{0,16},{8,24},{16,0},{24,8},{1,17},{9,25},{17,1},{25,9},{2,18},{10... | collective-permute-start | bytes 417800 | tf_op jit(solution)/shard_map/ppermute | solution.py:306
  22.9 0.5 %collective-permute-done.5 = f32[8,128]{1,0:T(8,128)S(1)} collective-permute-done((f32[8,128]{1,0:T(8,128)S(1)}, f32[8,128]{1,0:T(8,128)S(1)}, u32[]{:S(2)}, u32[]{:S(2)}) %collective-permute-start.5) | collective-permute-done | bytes 4128 | tf_op jit(solution)/shard_map/ppermute | solution.py:306
  23.4 1.6 %collective-permute-start.6 = (f32[8,128]{1,0:T(8,128)S(1)}, f32[8,128]{1,0:T(8,128)S(1)}, u32[]{:S(2)}, u32[]{:S(2)}) collective-permute-start(f32[8,128]{1,0:T(8,128)S(1)} %add.18.sums_ref), channel_id=1, source_target_pairs={{0,8},{8,0},{16,24},{24,16},{1,9},{9,1},{17,25},{25,17},{2,10},{10... | collective-permute-start | bytes 12296 | tf_op jit(solution)/shard_map/ppermute | solution.py:306
  25.0 1.6 %filter.4.local_refs_1_ = f32[2,32,64,128]{3,2,1,0:T(8,128)S(1)} custom-call(bf16[8,32,64,128]{3,2,1,0:T(8,128)(2,1)S(1)} %get-tuple-element.34.high_ref, bf16[8,32,64,128]{3,2,1,0:T(8,128)(2,1)S(1)} %get-tuple-element.35.low_ref, bf16[8,2,64,128]{3,2,1,0:T(8,128)(2,1)S(1)} %get-tuple-element.36.halo_high_ref, ...), custom_call_target="tpu_custom_call" | custom-call | flops 1140850688 | bytes 1048576 | tf_op jit(solution)/shard_map/filter/pallas_call | solution.py:377
  26.6 0.4 %collective-permute-done.6.earlier_refs_0_ = f32[8,128]{1,0:T(8,128)S(1)} collective-permute-done((f32[8,128]{1,0:T(8,128)S(1)}, f32[8,128]{1,0:T(8,128)S(1)}, u32[]{:S(2)}, u32[]{:S(2)}) %collective-permute-start.6) | collective-permute-done | bytes 4128 | tf_op jit(solution)/shard_map/ppermute | solution.py:306
  27.0 2.6 %collective-permute-start.7 = (f32[8,128]{1,0:T(8,128)S(1)}, f32[8,128]{1,0:T(8,128)S(1)}, u32[]{:S(2)}, u32[]{:S(2)}) collective-permute-start(f32[8,128]{1,0:T(8,128)S(1)} %add.19), channel_id=1, source_target_pairs={{0,16},{8,24},{16,0},{24,8},{1,17},{9,25},{17,1},{25,9},{2,18},{10... | collective-permute-start | bytes 12296 | tf_op jit(solution)/shard_map/ppermute | solution.py:306
  29.6 2.4 %filter.5.local_refs_2_ = f32[3,32,64,128]{3,2,1,0:T(8,128)S(1)} custom-call(bf16[8,32,64,128]{3,2,1,0:T(8,128)(2,1)S(1)} %get-tuple-element.34.high_ref, bf16[8,32,64,128]{3,2,1,0:T(8,128)(2,1)S(1)} %get-tuple-element.35.low_ref, bf16[8,2,64,128]{3,2,1,0:T(8,128)(2,1)S(1)} %get-tuple-element.36.halo_high_ref, ...), custom_call_target="tpu_custom_call" | custom-call | flops 1711276032 | bytes 1048576 | tf_op jit(solution)/shard_map/filter/pallas_call | solution.py:377
  32.1 0.0 collective-permute-done.8.totals_refs_1_
  32.1 4.3 %level.1 = f32[8,64,4096]{2,1,0:T(8,128)} custom-call(f32[3,32,64,128]{3,2,1,0:T(8,128)S(1)} %filter.3.local_refs_0_, f32[2,32,64,128]{3,2,1,0:T(8,128)S(1)} %filter.4.local_refs_1_, f32[3,32,64,128]{3,2,1,0:T(8,128)S(1)} %filter.5.local_refs_2_, bf16[8,512,256]{2,1,0:T(8,128)(2,1)S(1)} %get-tuple-element.49.weight_ref, ...), custom_call_target="tpu_custom_call" | custom-call | tf_op jit(solution)/shard_map/level/pallas_call | solution.py:422
  (12 shorter events, 0.1 us)
Async XLA Ops:
  0.0 5.5 %copy-start = (f32[8,128]{1,0:T(8,128)S(1)}, f32[8,128]{1,0:T(8,128)}, u32[]{:S(2)}) copy-start(f32[8,128]{1,0:T(8,128)} %taps_ref.1) | copy-start | bytes 12292
  1.5 11.8 %collective-permute-start = (f32[4,64,128]{2,1,0:T(8,128)S(1)}, f32[4,64,128]{2,1,0:T(8,128)S(1)}, u32[]{:S(2)}, u32[]{:S(2)}) collective-permute-start(f32[4,64,128]{2,1,0:T(8,128)S(1)} %get-tuple-element.30), channel_id=1, source_target_pairs={{0,1},{1,0},{2,3},{3,2},{4,5},{5,4},{6,7},{7,6},{8,9},{9,8},{10,11... | collective-permute-start | bytes 393224 | tf_op jit(solution)/shard_map/ppermute | solution.py:306
  2.0 11.3 %collective-permute-start.1 = (f32[4,64,128]{2,1,0:T(8,128)S(1)}, f32[4,64,128]{2,1,0:T(8,128)S(1)}, u32[]{:S(2)}, u32[]{:S(2)}) collective-permute-start(f32[4,64,128]{2,1,0:T(8,128)S(1)} %get-tuple-element.31), channel_id=1, source_target_pairs={{0,7},{1,2},{2,1},{3,4},{4,3},{5,6},{6,5},{7,0},{8,15},{9,10},{10,... | collective-permute-start | bytes 393224 | tf_op jit(solution)/shard_map/ppermute | solution.py:336
  13.5 1.7 %collective-permute-start.2 = (f32[8,128]{1,0:T(8,128)S(1)}, f32[8,128]{1,0:T(8,128)S(1)}, u32[]{:S(2)}, u32[]{:S(2)}) collective-permute-start(f32[8,128]{1,0:T(8,128)S(1)} %get-tuple-element.33), channel_id=1, source_target_pairs={{0,1},{1,0},{2,3},{3,2},{4,5},{5,4},{6,7},{7,6},{8,9},{9,8},{10,11... | collective-permute-start | bytes 12296 | tf_op jit(solution)/shard_map/ppermute | solution.py:306
  13.6 6.1 %collective-permute-start.4 = (f32[272,128]{1,0:T(8,128)S(1)}, f32[272,128]{1,0:T(8,128)S(1)}, u32[]{:S(2)}, u32[]{:S(2)}) collective-permute-start(f32[272,128]{1,0:T(8,128)S(1)} %constant_dynamic-update-slice_fusion), channel_id=1, source_target_pairs={{0,8},{8,0},{16,24},{24,16},{1,9},{9,1},{17,25},{25,17},{2,10},{10... | collective-permute-start | bytes 417800 | tf_op jit(solution)/shard_map/ppermute | solution.py:306
  15.3 3.6 %collective-permute-start.3 = (f32[8,128]{1,0:T(8,128)S(1)}, f32[8,128]{1,0:T(8,128)S(1)}, u32[]{:S(2)}, u32[]{:S(2)}) collective-permute-start(f32[8,128]{1,0:T(8,128)S(1)} %add.15), channel_id=1, source_target_pairs={{0,2},{1,3},{2,0},{3,1},{4,6},{5,7},{6,4},{7,5},{8,10},{9,11},{10,... | collective-permute-start | bytes 12296 | tf_op jit(solution)/shard_map/ppermute | solution.py:306
  19.7 3.7 %collective-permute-start.5 = (f32[8,128]{1,0:T(8,128)S(1)}, f32[8,128]{1,0:T(8,128)S(1)}, u32[]{:S(2)}, u32[]{:S(2)}) collective-permute-start(f32[8,128]{1,0:T(8,128)S(1)} %add.17), channel_id=1, source_target_pairs={{0,4},{1,5},{2,6},{3,7},{4,0},{5,1},{6,2},{7,3},{8,12},{9,13},{10,... | collective-permute-start | bytes 12296 | tf_op jit(solution)/shard_map/ppermute | solution.py:306
  20.3 11.8 %collective-permute-start.8 = (f32[272,128]{1,0:T(8,128)S(1)}, f32[272,128]{1,0:T(8,128)S(1)}, u32[]{:S(2)}, u32[]{:S(2)}) collective-permute-start(f32[272,128]{1,0:T(8,128)S(1)} %add.16), channel_id=1, source_target_pairs={{0,16},{8,24},{16,0},{24,8},{1,17},{9,25},{17,1},{25,9},{2,18},{10... | collective-permute-start | bytes 417800 | tf_op jit(solution)/shard_map/ppermute | solution.py:306
  23.4 3.6 %collective-permute-start.6 = (f32[8,128]{1,0:T(8,128)S(1)}, f32[8,128]{1,0:T(8,128)S(1)}, u32[]{:S(2)}, u32[]{:S(2)}) collective-permute-start(f32[8,128]{1,0:T(8,128)S(1)} %add.18.sums_ref), channel_id=1, source_target_pairs={{0,8},{8,0},{16,24},{24,16},{1,9},{9,1},{17,25},{25,17},{2,10},{10... | collective-permute-start | bytes 12296 | tf_op jit(solution)/shard_map/ppermute | solution.py:306
  27.0 5.1 %copy-start.1 = (f32[8]{0:T(128)S(1)}, f32[8]{0:T(128)}, u32[]{:S(2)}) copy-start(f32[8]{0:T(128)} %coupling_ref.1) | copy-start | bytes 100
  27.0 5.0 %collective-permute-start.7 = (f32[8,128]{1,0:T(8,128)S(1)}, f32[8,128]{1,0:T(8,128)S(1)}, u32[]{:S(2)}, u32[]{:S(2)}) collective-permute-start(f32[8,128]{1,0:T(8,128)S(1)} %add.19), channel_id=1, source_target_pairs={{0,16},{8,24},{16,0},{24,8},{1,17},{9,25},{17,1},{25,9},{2,18},{10... | collective-permute-start | bytes 12296 | tf_op jit(solution)/shard_map/ppermute | solution.py:306

commit v7 on v6

--- a/solution.py
+++ b/solution.py
@@ -32,6 +32,11 @@
         carry = jnp.broadcast_to(value[SUBLANES - 1 :, :], value.shape)
         sums.append(value)
     return sums
+
+
+def total(pieces):
+    value = functools.reduce(jnp.add, pieces)
+    return jnp.sum(value, axis=0, keepdims=True)
 
 
 def split(value):
@@ -74,31 +79,18 @@
             target[cable] = jnp.where(lane < HALF, low, high)
 
 
-def unwrap_kernel(
-    phase_hbm, wrap_hbm, taps_ref,
-    high_ref, low_ref, totals_ref, sums_ref, weight_ref,
-    phase_ref, wrap_ref, sem,
+def increments_kernel(
+    phase_ref, wrap_hbm, taps_ref, high_ref, low_ref, totals_ref, sums_ref, weight_ref, wrap_ref, sem
 ):
-    cables, time, width = phase_hbm.shape
+    cables, time, width = phase_ref.shape
     blocks = width // LANES
     groups = time // SUBLANES
 
-    span = width // CHUNKS
-
-    def copies(chunk):
-        cable, lanes = chunk // CHUNKS, pl.ds(pl.multiple_of(chunk % CHUNKS * span, span), span)
-        return (
-            pltpu.make_async_copy(
-                phase_hbm.at[cable, :, lanes], phase_ref.at[cable, :, lanes], sem.at[0, chunk]
-            ),
-            pltpu.make_async_copy(
-                wrap_hbm.at[cable, :, lanes], wrap_ref.at[cable, :, lanes], sem.at[1, chunk]
-            ),
-        )
-
-    for chunk in range(cables * CHUNKS):
-        for copy in copies(chunk):
-            copy.start()
+    def copy(cable):
+        return pltpu.make_async_copy(wrap_hbm.at[cable], wrap_ref.at[cable], sem.at[cable])
+
+    for cable in range(cables):
+        copy(cable).start()
 
     outputs = lax.broadcasted_iota(jnp.int32, (LANES, LANES), 0)
     inputs = lax.broadcasted_iota(jnp.int32, (LANES, LANES), 1)
@@ -116,29 +108,24 @@
         for place, part in enumerate((high, high, low, low)):
             weight_ref[cable, pl.ds(place * LANES, LANES), :] = part
 
-    def chunk_step(chunk, accumulated):
-        for copy in copies(chunk):
-            copy.wait()
-        cable = chunk // CHUNKS
-        start = chunk % CHUNKS * (blocks // CHUNKS)
-
-        def block_step(index, accumulated):
-            block = start + index
+    def cable_step(cable, accumulated):
+        copy(cable).wait()
+
+        def block_step(block, accumulated):
             lanes = pl.ds(pl.multiple_of(block * LANES, LANES), LANES)
             pieces = []
             for i in range(groups):
                 rows = pl.ds(i * SUBLANES, SUBLANES)
                 turns = wrap_ref[cable, rows, lanes].astype(jnp.float32)
                 pieces.append(phase_ref[cable, rows, lanes] + two_pi * turns)
-            sums = scanned(pieces)
-            store_split(high_ref, low_ref, cable, block, sums)
-            totals_ref[pl.ds(block * cables + cable, 1), :] = sums[-1][SUBLANES - 1 :, :]
-            return tuple(a + b for a, b in zip(accumulated, sums))
-
-        return lax.fori_loop(0, blocks // CHUNKS, block_step, accumulated, unroll=4)
+            store_split(high_ref, low_ref, cable, block, pieces)
+            totals_ref[pl.ds(block * cables + cable, 1), :] = total(pieces)
+            return tuple(a + b for a, b in zip(accumulated, pieces))
+
+        return lax.fori_loop(0, blocks, block_step, accumulated, unroll=4)
 
     zeros = tuple(jnp.zeros((SUBLANES, LANES), jnp.float32) for _ in range(groups))
-    accumulated = lax.fori_loop(0, cables * CHUNKS, chunk_step, zeros)
+    accumulated = scanned(lax.fori_loop(0, cables, cable_step, zeros))
     lane = lax.broadcasted_iota(jnp.int32, (SUBLANES, LANES), 1)
     tile = jnp.zeros((SUBLANES, LANES), jnp.float32)
     for i, value in enumerate(accumulated):
@@ -155,21 +142,22 @@
     at_end = (place == 0) | (place == lax.axis_size("chan") - 1)
     for pair in range(pairs):
         inner, outer = (
-            scanned([ref[pair, pl.ds(i * SUBLANES, SUBLANES), :] for i in range(groups)])
+            [ref[pair, pl.ds(i * SUBLANES, SUBLANES), :] for i in range(groups)]
             for ref in (inner_ref, outer_ref)
         )
         outer = [jnp.where(at_end, 0.0, value) for value in outer]
         right = [jnp.where(is_even, a, b) for a, b in zip(inner, outer)]
         left = [jnp.where(is_even, b, a) for a, b in zip(inner, outer)]
-        for block, sums, moved in ((0, right, pair + pairs), (1, left, pair)):
+        for block, pieces, moved in ((0, right, pair + pairs), (1, left, pair)):
             for cable in (pair, pair + pairs):
-                placed = [pltpu.roll(v, HALF, 1) for v in sums] if cable == moved else sums
+                placed = [pltpu.roll(v, HALF, 1) for v in pieces] if cable == moved else pieces
                 store_split(high_ref, low_ref, cable, block, placed)
-                totals_ref[pl.ds(block * cables + cable, 1), :] = placed[-1][SUBLANES - 1 :, :]
+                totals_ref[pl.ds(block * cables + cable, 1), :] = total(placed)
 
 
 def filter_kernel(first, high_ref, low_ref, halo_high_ref, halo_low_ref, weight_ref, local_ref):
     _, blocks, time, _ = high_ref.shape
+    groups = time // SUBLANES
     lane = lax.broadcasted_iota(jnp.int32, (time, LANES), 1)
 
     @pl.loop(0, local_ref.shape[0])
@@ -201,7 +189,10 @@
         previous = rolled(-1)
         for block in range(blocks):
             following = rolled(block)
-            local_ref[index, block] = jnp.where(lane < HALF, previous, following)
+            value = jnp.where(lane < HALF, previous, following)
+            pieces = [value[i * SUBLANES : (i + 1) * SUBLANES] for i in range(groups)]
+            for i, piece in enumerate(scanned(pieces)):
+                local_ref[index, block, pl.ds(i * SUBLANES, SUBLANES), :] = piece
             previous = following
 
 
@@ -313,7 +304,6 @@
     population = cables * width * places
     bounds = [0, 3 * cables // 8, 5 * cables // 8, cables]
     parts = len(bounds) - 1
-    phase_step = pltpu.with_memory_space_constraint(phase_step, pltpu.HBM)
     wrap_count = pltpu.with_memory_space_constraint(wrap_count, pltpu.HBM)
     whole = pl.BlockSpec(memory_space=pltpu.VMEM)
     outside = pl.BlockSpec(memory_space=pl.ANY)
@@ -331,13 +321,13 @@
         ],
         compiler_params=pltpu.CompilerParams(vmem_limit_bytes=8 << 20),
         name="edges",
-    )(phase_step, wrap_count)
+    )(pltpu.with_memory_space_constraint(phase_step, pltpu.HBM), wrap_count)
     outer_pairs = [(i, (i + (1 if i % 2 else -1)) % places) for i in range(places)]
     outer = lax.ppermute(outer, "chan", outer_pairs)
     inner = swapped(inner, "chan", 1)
 
     high, low, totals, sums, weight = pl.pallas_call(
-        unwrap_kernel,
+        increments_kernel,
         out_shape=(
             pltpu.VMEM((cables, blocks, time, LANES), jnp.bfloat16),
             pltpu.VMEM((cables, blocks, time, LANES), jnp.bfloat16),
@@ -345,19 +335,18 @@
             pltpu.VMEM((SUBLANES, LANES), jnp.float32),
             pltpu.VMEM((cables, 4 * LANES, 2 * LANES), jnp.bfloat16),
         ),
-        in_specs=[outside, outside, whole],
+        in_specs=[whole, outside, whole],
         out_specs=[whole] * 5,
         scratch_shapes=[
-            pltpu.VMEM((cables, time, width), jnp.float32),
             pltpu.VMEM((cables, time, width), jnp.int32),
-            pltpu.SemaphoreType.DMA((2, cables * CHUNKS)),
+            pltpu.SemaphoreType.DMA((cables,)),
         ],
-        compiler_params=pltpu.CompilerParams(vmem_limit_bytes=40 << 20),
+        compiler_params=pltpu.CompilerParams(vmem_limit_bytes=16 << 20),
         cost_estimate=pl.CostEstimate(
-            flops=0, bytes_accessed=2 * phase_step.size * 4, transcendentals=0
+            flops=0, bytes_accessed=phase_step.size * 4, transcendentals=0
         ),
-        name="unwrap",
-    )(phase_step, wrap_count, filter_taps)
+        name="increments",
+    )(pltpu.with_memory_space_constraint(phase_step, pltpu.VMEM), wrap_count, filter_taps)
 
     halo_high, halo_low, halo_totals = pl.pallas_call(
         halo_kernel,

time: 36.5 us -> 33.9 us (0.929)
  Pallas kernels: 20.2 us -> 17.6 us
  waiting for transfers between devices: 2.39 us -> 1.33 us
  starting transfers between devices: 13.6 us -> 14.6 us
    pallas_call x1, Pallas kernels: 7.73 us -> 4.96 us  [shards(): pl.pallas_call(increments_kernel, out_shape=(pltpu.VMEM((cables, blocks,...]
    ppermute x8, waiting for transfers between devices: 2.39 us -> 1.33 us  [swapped(): lax.ppermute(value, axis, [(i, i ^ bit) for i in range(lax.axis_size(axis...]
    ppermute x8, starting transfers between devices: 10.1 us -> 11.1 us  [swapped(): lax.ppermute(value, axis, [(i, i ^ bit) for i in range(lax.axis_size(axis...]
  transfers between devices with their start and end apart: 9 -> 9, of which waited for: 4 -> 3; matrix products, arithmetic and copies ran while one was open for 0% -> 0% of each run, Pallas kernels for 39% -> 34%
where the time goes in v7:
time: 33.9 us; the launch traced here: 33.7 us
  Pallas kernels  17.6 us (52%)
  starting transfers between devices  14.6 us (43%)
  waiting for transfers between devices  1.33 us (4%)
    ppermute x8, starting transfers between devices, swapped(): lax.ppermute(value, axis, [(i, i ^ bit) for i in range(lax.axis_size(axis...  11.1 us
    pallas_call x3, Pallas kernels, filtered(): pl.pallas_call(functools.partial(filter_kernel, bounds[part]), out_shape=...  6.62 us
    pallas_call x1, Pallas kernels, shards(): pl.pallas_call(increments_kernel, out_shape=(pltpu.VMEM((cables, blocks,...  4.96 us
    pallas_call x1, Pallas kernels, shards(): pl.pallas_call(functools.partial(level_kernel, population), out_shape=jax...  4.27 us
    ppermute x1, starting transfers between devices, shards(): outer = lax.ppermute(outer, 'chan', outer_pairs)  3.56 us
    pallas_call x1, Pallas kernels, shards(): pl.pallas_call(edges_kernel, out_shape=[pltpu.VMEM((cables // 2, time, LA...  1.59 us
    ppermute x8, waiting for transfers between devices, swapped(): lax.ppermute(value, axis, [(i, i ^ bit) for i in range(lax.axis_size(axis...  1.33 us
  transfers between devices with their start and end apart: 9, of which 3 were waited for; matrix products, arithmetic and copies ran while one was open for 0% of the time, Pallas kernels for 34%

profile of v7, /device:TPU:0, one launch (start us, length us, event | category | flops | bytes accessed | tf_op | source)
XLA Modules:
  0.0 33.7 jit_solution(12854943582291187303)
XLA Ops:
  0.0 1.6 %edges.1 = (f32[4,64,128]{2,1,0:T(8,128)S(1)}, f32[4,64,128]{2,1,0:T(8,128)S(1)}) custom-call(f32[8,64,4096]{2,1,0:T(8,128)} %phase_hbm.1, s32[8,64,4096]{2,1,0:T(8,128)} %wrap_hbm.3), custom_call_target="tpu_custom_call" | custom-call | tf_op jit(solution)/shard_map/edges/pallas_call | solution.py:312
  1.6 0.5 %collective-permute-start = (f32[4,64,128]{2,1,0:T(8,128)S(1)}, f32[4,64,128]{2,1,0:T(8,128)S(1)}, u32[]{:S(2)}, u32[]{:S(2)}) collective-permute-start(f32[4,64,128]{2,1,0:T(8,128)S(1)} %get-tuple-element.30), channel_id=1, source_target_pairs={{0,1},{1,0},{2,3},{3,2},{4,5},{5,4},{6,7},{7,6},{8,9},{9,8},{10,11... | collective-permute-start | bytes 393224 | tf_op jit(solution)/shard_map/ppermute | solution.py:297
  2.1 3.6 %collective-permute-start.1 = (f32[4,64,128]{2,1,0:T(8,128)S(1)}, f32[4,64,128]{2,1,0:T(8,128)S(1)}, u32[]{:S(2)}, u32[]{:S(2)}) collective-permute-start(f32[4,64,128]{2,1,0:T(8,128)S(1)} %get-tuple-element.31), channel_id=1, source_target_pairs={{0,7},{1,2},{2,1},{3,4},{4,3},{5,6},{6,5},{7,0},{8,15},{9,10},{10,... | collective-permute-start | bytes 393224 | tf_op jit(solution)/shard_map/ppermute | solution.py:326
  5.7 5.0 %increments.1 = (bf16[8,32,64,128]{3,2,1,0:T(8,128)(2,1)S(1)}, bf16[8,32,64,128]{3,2,1,0:T(8,128)(2,1)S(1)}, f32[256,128]{1,0:T(8,128)S(1)}, f32[8,128]{1,0:T(8,128)S(1)}, bf16[8,512,256]{2,1,0:T(8,128)(2,1)S(1)}) custom-call(f32[8,64,4096]{2,1,0:T(8,128)S(1)} %copy-done, s32[8,64,4096]{2,1,0:T(8,128)} %wrap_hbm.3, f32[8,128]{1,0:T(8,128)S(1)} %copy-done.1), custom_call_target="tpu_custom_call" | custom-call | bytes 8388608 | tf_op jit(solution)/shard_map/increments/pallas_call | solution.py:329
  10.7 0.0 collective-permute-done.inner_ref
  10.7 0.0 collective-permute-done.1.outer_ref
  10.7 0.2 halo.1
  10.8 0.1 collective-permute-start.2
  10.9 1.6 %collective-permute-start.4 = (f32[272,128]{1,0:T(8,128)S(1)}, f32[272,128]{1,0:T(8,128)S(1)}, u32[]{:S(2)}, u32[]{:S(2)}) collective-permute-start(f32[272,128]{1,0:T(8,128)S(1)} %constant_dynamic-update-slice_fusion), channel_id=1, source_target_pairs={{0,8},{8,0},{16,24},{24,16},{1,9},{9,1},{17,25},{25,17},{2,10},{10... | collective-permute-start | bytes 417800 | tf_op jit(solution)/shard_map/ppermute | solution.py:297
  12.6 0.0 collective-permute-done.2
  12.6 1.0 %collective-permute-start.3 = (f32[8,128]{1,0:T(8,128)S(1)}, f32[8,128]{1,0:T(8,128)S(1)}, u32[]{:S(2)}, u32[]{:S(2)}) collective-permute-start(f32[8,128]{1,0:T(8,128)S(1)} %add.15), channel_id=1, source_target_pairs={{0,2},{1,3},{2,0},{3,1},{4,6},{5,7},{6,4},{7,5},{8,10},{9,11},{10,... | collective-permute-start | bytes 12296 | tf_op jit(solution)/shard_map/ppermute | solution.py:297
  13.6 2.5 %filter.3.local_refs_0_ = f32[3,32,64,128]{3,2,1,0:T(8,128)S(1)} custom-call(bf16[8,32,64,128]{3,2,1,0:T(8,128)(2,1)S(1)} %get-tuple-element.34.high_ref, bf16[8,32,64,128]{3,2,1,0:T(8,128)(2,1)S(1)} %get-tuple-element.35.low_ref, bf16[8,2,64,128]{3,2,1,0:T(8,128)(2,1)S(1)} %get-tuple-element.36.halo_high_ref, ...), custom_call_target="tpu_custom_call" | custom-call | flops 1711276032 | bytes 1048576 | tf_op jit(solution)/shard_map/filter/pallas_call | solution.py:366
  16.1 0.1 collective-permute-done.3
  16.2 0.8 %collective-permute-done.4.totals_refs_0_ = f32[272,128]{1,0:T(8,128)S(1)} collective-permute-done((f32[272,128]{1,0:T(8,128)S(1)}, f32[272,128]{1,0:T(8,128)S(1)}, u32[]{:S(2)}, u32[]{:S(2)}) %collective-permute-start.4) | collective-permute-done | bytes 139296 | tf_op jit(solution)/shard_map/ppermute | solution.py:297
  17.1 1.1 %collective-permute-start.5 = (f32[8,128]{1,0:T(8,128)S(1)}, f32[8,128]{1,0:T(8,128)S(1)}, u32[]{:S(2)}, u32[]{:S(2)}) collective-permute-start(f32[8,128]{1,0:T(8,128)S(1)} %add.17), channel_id=1, source_target_pairs={{0,4},{1,5},{2,6},{3,7},{4,0},{5,1},{6,2},{7,3},{8,12},{9,13},{10,... | collective-permute-start | bytes 12296 | tf_op jit(solution)/shard_map/ppermute | solution.py:297
  18.1 2.6 %collective-permute-start.8 = (f32[272,128]{1,0:T(8,128)S(1)}, f32[272,128]{1,0:T(8,128)S(1)}, u32[]{:S(2)}, u32[]{:S(2)}) collective-permute-start(f32[272,128]{1,0:T(8,128)S(1)} %add.16), channel_id=1, source_target_pairs={{0,16},{8,24},{16,0},{24,8},{1,17},{9,25},{17,1},{25,9},{2,18},{10... | collective-permute-start | bytes 417800 | tf_op jit(solution)/shard_map/ppermute | solution.py:297
  20.7 0.0 collective-permute-done.5
  20.7 1.6 %collective-permute-start.6 = (f32[8,128]{1,0:T(8,128)S(1)}, f32[8,128]{1,0:T(8,128)S(1)}, u32[]{:S(2)}, u32[]{:S(2)}) collective-permute-start(f32[8,128]{1,0:T(8,128)S(1)} %add.18.sums_ref), channel_id=1, source_target_pairs={{0,8},{8,0},{16,24},{24,16},{1,9},{9,1},{17,25},{25,17},{2,10},{10... | collective-permute-start | bytes 12296 | tf_op jit(solution)/shard_map/ppermute | solution.py:297
  22.3 1.7 %filter.4.local_refs_1_ = f32[2,32,64,128]{3,2,1,0:T(8,128)S(1)} custom-call(bf16[8,32,64,128]{3,2,1,0:T(8,128)(2,1)S(1)} %get-tuple-element.34.high_ref, bf16[8,32,64,128]{3,2,1,0:T(8,128)(2,1)S(1)} %get-tuple-element.35.low_ref, bf16[8,2,64,128]{3,2,1,0:T(8,128)(2,1)S(1)} %get-tuple-element.36.halo_high_ref, ...), custom_call_target="tpu_custom_call" | custom-call | flops 1140850688 | bytes 1048576 | tf_op jit(solution)/shard_map/filter/pallas_call | solution.py:366
  24.0 0.4 %collective-permute-done.6.earlier_refs_0_ = f32[8,128]{1,0:T(8,128)S(1)} collective-permute-done((f32[8,128]{1,0:T(8,128)S(1)}, f32[8,128]{1,0:T(8,128)S(1)}, u32[]{:S(2)}, u32[]{:S(2)}) %collective-permute-start.6) | collective-permute-done | bytes 4128 | tf_op jit(solution)/shard_map/ppermute | solution.py:297
  24.3 2.6 %collective-permute-start.7 = (f32[8,128]{1,0:T(8,128)S(1)}, f32[8,128]{1,0:T(8,128)S(1)}, u32[]{:S(2)}, u32[]{:S(2)}) collective-permute-start(f32[8,128]{1,0:T(8,128)S(1)} %add.19), channel_id=1, source_target_pairs={{0,16},{8,24},{16,0},{24,8},{1,17},{9,25},{17,1},{25,9},{2,18},{10... | collective-permute-start | bytes 12296 | tf_op jit(solution)/shard_map/ppermute | solution.py:297
  26.9 2.5 %filter.5.local_refs_2_ = f32[3,32,64,128]{3,2,1,0:T(8,128)S(1)} custom-call(bf16[8,32,64,128]{3,2,1,0:T(8,128)(2,1)S(1)} %get-tuple-element.34.high_ref, bf16[8,32,64,128]{3,2,1,0:T(8,128)(2,1)S(1)} %get-tuple-element.35.low_ref, bf16[8,2,64,128]{3,2,1,0:T(8,128)(2,1)S(1)} %get-tuple-element.36.halo_high_ref, ...), custom_call_target="tpu_custom_call" | custom-call | flops 1711276032 | bytes 1048576 | tf_op jit(solution)/shard_map/filter/pallas_call | solution.py:366
  29.4 0.0 collective-permute-done.7.earlier_refs_1_
  29.5 4.3 %level.1 = f32[8,64,4096]{2,1,0:T(8,128)} custom-call(f32[3,32,64,128]{3,2,1,0:T(8,128)S(1)} %filter.3.local_refs_0_, f32[2,32,64,128]{3,2,1,0:T(8,128)S(1)} %filter.4.local_refs_1_, f32[3,32,64,128]{3,2,1,0:T(8,128)S(1)} %filter.5.local_refs_2_, bf16[8,512,256]{2,1,0:T(8,128)(2,1)S(1)} %get-tuple-element.49.weight_ref, ...), custom_call_target="tpu_custom_call" | custom-call | tf_op jit(solution)/shard_map/level/pallas_call | solution.py:411
  (14 shorter events, 0.1 us)
Async XLA Ops:
  0.0 5.7 %copy-start.1 = (f32[8,128]{1,0:T(8,128)S(1)}, f32[8,128]{1,0:T(8,128)}, u32[]{:S(2)}) copy-start(f32[8,128]{1,0:T(8,128)} %taps_ref.1) | copy-start | bytes 12292
  0.0 5.7 %copy-start = (f32[8,64,4096]{2,1,0:T(8,128)S(1)}, f32[8,64,4096]{2,1,0:T(8,128)}, u32[]{:S(2)}) copy-start(f32[8,64,4096]{2,1,0:T(8,128)} %phase_hbm.1) | copy-start | bytes 25165828
  1.6 9.1 %collective-permute-start = (f32[4,64,128]{2,1,0:T(8,128)S(1)}, f32[4,64,128]{2,1,0:T(8,128)S(1)}, u32[]{:S(2)}, u32[]{:S(2)}) collective-permute-start(f32[4,64,128]{2,1,0:T(8,128)S(1)} %get-tuple-element.30), channel_id=1, source_target_pairs={{0,1},{1,0},{2,3},{3,2},{4,5},{5,4},{6,7},{7,6},{8,9},{9,8},{10,11... | collective-permute-start | bytes 393224 | tf_op jit(solution)/shard_map/ppermute | solution.py:297
  2.1 8.6 %collective-permute-start.1 = (f32[4,64,128]{2,1,0:T(8,128)S(1)}, f32[4,64,128]{2,1,0:T(8,128)S(1)}, u32[]{:S(2)}, u32[]{:S(2)}) collective-permute-start(f32[4,64,128]{2,1,0:T(8,128)S(1)} %get-tuple-element.31), channel_id=1, source_target_pairs={{0,7},{1,2},{2,1},{3,4},{4,3},{5,6},{6,5},{7,0},{8,15},{9,10},{10,... | collective-permute-start | bytes 393224 | tf_op jit(solution)/shard_map/ppermute | solution.py:326
  10.8 1.7 %collective-permute-start.2 = (f32[8,128]{1,0:T(8,128)S(1)}, f32[8,128]{1,0:T(8,128)S(1)}, u32[]{:S(2)}, u32[]{:S(2)}) collective-permute-start(f32[8,128]{1,0:T(8,128)S(1)} %get-tuple-element.33), channel_id=1, source_target_pairs={{0,1},{1,0},{2,3},{3,2},{4,5},{5,4},{6,7},{7,6},{8,9},{9,8},{10,11... | collective-permute-start | bytes 12296 | tf_op jit(solution)/shard_map/ppermute | solution.py:297
  10.9 6.1 %collective-permute-start.4 = (f32[272,128]{1,0:T(8,128)S(1)}, f32[272,128]{1,0:T(8,128)S(1)}, u32[]{:S(2)}, u32[]{:S(2)}) collective-permute-start(f32[272,128]{1,0:T(8,128)S(1)} %constant_dynamic-update-slice_fusion), channel_id=1, source_target_pairs={{0,8},{8,0},{16,24},{24,16},{1,9},{9,1},{17,25},{25,17},{2,10},{10... | collective-permute-start | bytes 417800 | tf_op jit(solution)/shard_map/ppermute | solution.py:297
  12.6 3.6 %collective-permute-start.3 = (f32[8,128]{1,0:T(8,128)S(1)}, f32[8,128]{1,0:T(8,128)S(1)}, u32[]{:S(2)}, u32[]{:S(2)}) collective-permute-start(f32[8,128]{1,0:T(8,128)S(1)} %add.15), channel_id=1, source_target_pairs={{0,2},{1,3},{2,0},{3,1},{4,6},{5,7},{6,4},{7,5},{8,10},{9,11},{10,... | collective-permute-start | bytes 12296 | tf_op jit(solution)/shard_map/ppermute | solution.py:297
  17.1 3.7 %collective-permute-start.5 = (f32[8,128]{1,0:T(8,128)S(1)}, f32[8,128]{1,0:T(8,128)S(1)}, u32[]{:S(2)}, u32[]{:S(2)}) collective-permute-start(f32[8,128]{1,0:T(8,128)S(1)} %add.17), channel_id=1, source_target_pairs={{0,4},{1,5},{2,6},{3,7},{4,0},{5,1},{6,2},{7,3},{8,12},{9,13},{10,... | collective-permute-start | bytes 12296 | tf_op jit(solution)/shard_map/ppermute | solution.py:297
  18.1 11.3 %collective-permute-start.8 = (f32[272,128]{1,0:T(8,128)S(1)}, f32[272,128]{1,0:T(8,128)S(1)}, u32[]{:S(2)}, u32[]{:S(2)}) collective-permute-start(f32[272,128]{1,0:T(8,128)S(1)} %add.16), channel_id=1, source_target_pairs={{0,16},{8,24},{16,0},{24,8},{1,17},{9,25},{17,1},{25,9},{2,18},{10... | collective-permute-start | bytes 417800 | tf_op jit(solution)/shard_map/ppermute | solution.py:297
  20.7 3.6 %collective-permute-start.6 = (f32[8,128]{1,0:T(8,128)S(1)}, f32[8,128]{1,0:T(8,128)S(1)}, u32[]{:S(2)}, u32[]{:S(2)}) collective-permute-start(f32[8,128]{1,0:T(8,128)S(1)} %add.18.sums_ref), channel_id=1, source_target_pairs={{0,8},{8,0},{16,24},{24,16},{1,9},{9,1},{17,25},{25,17},{2,10},{10... | collective-permute-start | bytes 12296 | tf_op jit(solution)/shard_map/ppermute | solution.py:297
  24.3 5.1 %copy-start.2 = (f32[8]{0:T(128)S(1)}, f32[8]{0:T(128)}, u32[]{:S(2)}) copy-start(f32[8]{0:T(128)} %coupling_ref.1) | copy-start | bytes 100
  24.3 5.1 %collective-permute-start.7 = (f32[8,128]{1,0:T(8,128)S(1)}, f32[8,128]{1,0:T(8,128)S(1)}, u32[]{:S(2)}, u32[]{:S(2)}) collective-permute-start(f32[8,128]{1,0:T(8,128)S(1)} %add.19), channel_id=1, source_target_pairs={{0,16},{8,24},{16,0},{24,8},{1,17},{9,25},{17,1},{25,9},{2,18},{10... | collective-permute-start | bytes 12296 | tf_op jit(solution)/shard_map/ppermute | solution.py:297

commit v8 on v7

--- a/solution.py
+++ b/solution.py
@@ -80,17 +80,11 @@
 
 
 def increments_kernel(
-    phase_ref, wrap_hbm, taps_ref, high_ref, low_ref, totals_ref, sums_ref, weight_ref, wrap_ref, sem
+    phase_ref, wrap_ref, taps_ref, high_ref, low_ref, totals_ref, sums_ref, weight_ref
 ):
     cables, time, width = phase_ref.shape
     blocks = width // LANES
     groups = time // SUBLANES
-
-    def copy(cable):
-        return pltpu.make_async_copy(wrap_hbm.at[cable], wrap_ref.at[cable], sem.at[cable])
-
-    for cable in range(cables):
-        copy(cable).start()
 
     outputs = lax.broadcasted_iota(jnp.int32, (LANES, LANES), 0)
     inputs = lax.broadcasted_iota(jnp.int32, (LANES, LANES), 1)
@@ -109,8 +103,6 @@
             weight_ref[cable, pl.ds(place * LANES, LANES), :] = part
 
     def cable_step(cable, accumulated):
-        copy(cable).wait()
-
         def block_step(block, accumulated):
             lanes = pl.ds(pl.multiple_of(block * LANES, LANES), LANES)
             pieces = []
@@ -304,7 +296,6 @@
     population = cables * width * places
     bounds = [0, 3 * cables // 8, 5 * cables // 8, cables]
     parts = len(bounds) - 1
-    wrap_count = pltpu.with_memory_space_constraint(wrap_count, pltpu.HBM)
     whole = pl.BlockSpec(memory_space=pltpu.VMEM)
     outside = pl.BlockSpec(memory_space=pl.ANY)
     scalars = pl.BlockSpec(memory_space=pltpu.SMEM)
@@ -321,7 +312,10 @@
         ],
         compiler_params=pltpu.CompilerParams(vmem_limit_bytes=8 << 20),
         name="edges",
-    )(pltpu.with_memory_space_constraint(phase_step, pltpu.HBM), wrap_count)
+    )(
+        pltpu.with_memory_space_constraint(phase_step, pltpu.HBM),
+        pltpu.with_memory_space_constraint(wrap_count, pltpu.HBM),
+    )
     outer_pairs = [(i, (i + (1 if i % 2 else -1)) % places) for i in range(places)]
     outer = lax.ppermute(outer, "chan", outer_pairs)
     inner = swapped(inner, "chan", 1)
@@ -335,18 +329,16 @@
             pltpu.VMEM((SUBLANES, LANES), jnp.float32),
             pltpu.VMEM((cables, 4 * LANES, 2 * LANES), jnp.bfloat16),
         ),
-        in_specs=[whole, outside, whole],
+        in_specs=[whole, whole, whole],
         out_specs=[whole] * 5,
-        scratch_shapes=[
-            pltpu.VMEM((cables, time, width), jnp.int32),
-            pltpu.SemaphoreType.DMA((cables,)),
-        ],
-        compiler_params=pltpu.CompilerParams(vmem_limit_bytes=16 << 20),
-        cost_estimate=pl.CostEstimate(
-            flops=0, bytes_accessed=phase_step.size * 4, transcendentals=0
-        ),
+        compiler_params=pltpu.CompilerParams(vmem_limit_bytes=8 << 20),
+        cost_estimate=pl.CostEstimate(flops=0, bytes_accessed=1 << 20, transcendentals=0),
         name="increments",
-    )(pltpu.with_memory_space_constraint(phase_step, pltpu.VMEM), wrap_count, filter_taps)
+    )(
+        pltpu.with_memory_space_constraint(phase_step, pltpu.VMEM),
+        pltpu.with_memory_space_constraint(wrap_count, pltpu.VMEM),
+        filter_taps,
+    )
 
     halo_high, halo_low, halo_totals = pl.pallas_call(
         halo_kernel,

time: 33.9 us -> 36.4 us (1.074)
  starting transfers between devices: 14.6 us -> 16.8 us
  local copies, waits for them, and re-layouts: 0.02 us -> 1.13 us
  waiting for transfers between devices: 1.33 us -> 0.64 us
    ppermute x8, starting transfers between devices: 11.1 us -> 13.2 us  [swapped(): lax.ppermute(value, axis, [(i, i ^ bit) for i in range(lax.axis_size(axis...]
    unnamed x7 -> x9, local copies, waits for them, and re-layouts: 0.02 us -> 1.13 us
    ppermute x8, waiting for transfers between devices: 1.33 us -> 0.63 us  [swapped(): lax.ppermute(value, axis, [(i, i ^ bit) for i in range(lax.axis_size(axis...]
  transfers between devices with their start and end apart: 9 -> 9, of which waited for: 3 -> 2; matrix products, arithmetic and copies ran while one was open for 0% -> 0% of each run, Pallas kernels for 34% -> 32%
where the time goes in v8:
time: 36.4 us; the launch traced here: 36.2 us
  Pallas kernels  17.5 us (48%)
  starting transfers between devices  16.8 us (46%)
  local copies, waits for them, and re-layouts  1.13 us (3%)
  waiting for transfers between devices  0.64 us (2%)
    ppermute x8, starting transfers between devices, swapped(): lax.ppermute(value, axis, [(i, i ^ bit) for i in range(lax.axis_size(axis...  13.2 us
    pallas_call x3, Pallas kernels, filtered(): pl.pallas_call(functools.partial(filter_kernel, bounds[part]), out_shape=...  6.62 us
    pallas_call x1, Pallas kernels, shards(): pl.pallas_call(increments_kernel, out_shape=(pltpu.VMEM((cables, blocks,...  4.91 us
    pallas_call x1, Pallas kernels, shards(): pl.pallas_call(functools.partial(level_kernel, population), out_shape=jax...  4.27 us
    ppermute x1, starting transfers between devices, shards(): outer = lax.ppermute(outer, 'chan', outer_pairs)  3.56 us
    pallas_call x1, Pallas kernels, shards(): pl.pallas_call(edges_kernel, out_shape=[pltpu.VMEM((cables // 2, time, LA...  1.59 us
    unnamed x9, local copies, waits for them, and re-layouts  1.13 us
  transfers between devices with their start and end apart: 9, of which 2 were waited for; matrix products, arithmetic and copies ran while one was open for 0% of the time, Pallas kernels for 32%

profile of v8, /device:TPU:0, one launch (start us, length us, event | category | flops | bytes accessed | tf_op | source)
XLA Modules:
  0.0 36.2 jit_solution(12922395882530600220)
XLA Ops:
  0.0 1.6 %edges.1 = (f32[4,64,128]{2,1,0:T(8,128)S(1)}, f32[4,64,128]{2,1,0:T(8,128)S(1)}) custom-call(f32[8,64,4096]{2,1,0:T(8,128)} %phase_hbm.1, s32[8,64,4096]{2,1,0:T(8,128)} %wrap_hbm.1), custom_call_target="tpu_custom_call" | custom-call | tf_op jit(solution)/shard_map/edges/pallas_call | solution.py:303
  1.6 0.5 %collective-permute-start = (f32[4,64,128]{2,1,0:T(8,128)S(1)}, f32[4,64,128]{2,1,0:T(8,128)S(1)}, u32[]{:S(2)}, u32[]{:S(2)}) collective-permute-start(f32[4,64,128]{2,1,0:T(8,128)S(1)} %get-tuple-element.30), channel_id=1, source_target_pairs={{0,1},{1,0},{2,3},{3,2},{4,5},{5,4},{6,7},{7,6},{8,9},{9,8},{10,11... | collective-permute-start | bytes 393224 | tf_op jit(solution)/shard_map/ppermute | solution.py:289
  2.1 3.6 %collective-permute-start.1 = (f32[4,64,128]{2,1,0:T(8,128)S(1)}, f32[4,64,128]{2,1,0:T(8,128)S(1)}, u32[]{:S(2)}, u32[]{:S(2)}) collective-permute-start(f32[4,64,128]{2,1,0:T(8,128)S(1)} %get-tuple-element.31), channel_id=1, source_target_pairs={{0,7},{1,2},{2,1},{3,4},{4,3},{5,6},{6,5},{7,0},{8,15},{9,10},{10,... | collective-permute-start | bytes 393224 | tf_op jit(solution)/shard_map/ppermute | solution.py:320
  5.7 0.4 %copy-done.1 = s32[8,64,4096]{2,1,0:T(8,128)S(1)} copy-done((s32[8,64,4096]{2,1,0:T(8,128)S(1)}, s32[8,64,4096]{2,1,0:T(8,128)}, u32[]{:S(2)}) %copy-start.1) | copy-done | bytes 8388632
  6.1 0.7 %copy-done.2 = f32[8,128]{1,0:T(8,128)S(1)} copy-done((f32[8,128]{1,0:T(8,128)S(1)}, f32[8,128]{1,0:T(8,128)}, u32[]{:S(2)}) %copy-start.2) | copy-done | bytes 4120
  6.8 4.9 %increments.1 = (bf16[8,32,64,128]{3,2,1,0:T(8,128)(2,1)S(1)}, bf16[8,32,64,128]{3,2,1,0:T(8,128)(2,1)S(1)}, f32[256,128]{1,0:T(8,128)S(1)}, f32[8,128]{1,0:T(8,128)S(1)}, bf16[8,512,256]{2,1,0:T(8,128)(2,1)S(1)}) custom-call(f32[8,64,4096]{2,1,0:T(8,128)S(1)} %copy-done, s32[8,64,4096]{2,1,0:T(8,128)S(1)} %copy-done.1, f32[8,128]{1,0:T(8,128)S(1)} %copy-done.2), custom_call_target="tpu_custom_call" | custom-call | bytes 1048576 | tf_op jit(solution)/shard_map/increments/pallas_call | solution.py:323
  11.7 0.0 collective-permute-done.inner_ref
  11.7 0.0 collective-permute-done.1.outer_ref
  11.7 0.2 halo.1
  11.9 0.5 %collective-permute-start.2 = (f32[8,128]{1,0:T(8,128)S(1)}, f32[8,128]{1,0:T(8,128)S(1)}, u32[]{:S(2)}, u32[]{:S(2)}) collective-permute-start(f32[8,128]{1,0:T(8,128)S(1)} %get-tuple-element.33), channel_id=1, source_target_pairs={{0,1},{1,0},{2,3},{3,2},{4,5},{5,4},{6,7},{7,6},{8,9},{9,8},{10,11... | collective-permute-start | bytes 12296 | tf_op jit(solution)/shard_map/ppermute | solution.py:289
  12.4 2.7 %collective-permute-start.4 = (f32[272,128]{1,0:T(8,128)S(1)}, f32[272,128]{1,0:T(8,128)S(1)}, u32[]{:S(2)}, u32[]{:S(2)}) collective-permute-start(f32[272,128]{1,0:T(8,128)S(1)} %constant_dynamic-update-slice_fusion), channel_id=1, source_target_pairs={{0,8},{8,0},{16,24},{24,16},{1,9},{9,1},{17,25},{25,17},{2,10},{10... | collective-permute-start | bytes 417800 | tf_op jit(solution)/shard_map/ppermute | solution.py:289
  15.1 0.0 collective-permute-done.2
  15.1 1.5 %collective-permute-start.3 = (f32[8,128]{1,0:T(8,128)S(1)}, f32[8,128]{1,0:T(8,128)S(1)}, u32[]{:S(2)}, u32[]{:S(2)}) collective-permute-start(f32[8,128]{1,0:T(8,128)S(1)} %add.15), channel_id=1, source_target_pairs={{0,2},{1,3},{2,0},{3,1},{4,6},{5,7},{6,4},{7,5},{8,10},{9,11},{10,... | collective-permute-start | bytes 12296 | tf_op jit(solution)/shard_map/ppermute | solution.py:289
  16.6 2.5 %filter.3.local_refs_0_ = f32[3,32,64,128]{3,2,1,0:T(8,128)S(1)} custom-call(bf16[8,32,64,128]{3,2,1,0:T(8,128)(2,1)S(1)} %get-tuple-element.34.high_ref, bf16[8,32,64,128]{3,2,1,0:T(8,128)(2,1)S(1)} %get-tuple-element.35.low_ref, bf16[8,2,64,128]{3,2,1,0:T(8,128)(2,1)S(1)} %get-tuple-element.36.halo_high_ref, ...), custom_call_target="tpu_custom_call" | custom-call | flops 1711276032 | bytes 1048576 | tf_op jit(solution)/shard_map/filter/pallas_call | solution.py:358
  19.1 0.3 collective-permute-done.4.totals_refs_0_
  19.4 1.8 %collective-permute-start.5 = (f32[8,128]{1,0:T(8,128)S(1)}, f32[8,128]{1,0:T(8,128)S(1)}, u32[]{:S(2)}, u32[]{:S(2)}) collective-permute-start(f32[8,128]{1,0:T(8,128)S(1)} %add.17), channel_id=1, source_target_pairs={{0,4},{1,5},{2,6},{3,7},{4,0},{5,1},{6,2},{7,3},{8,12},{9,13},{10,... | collective-permute-start | bytes 12296 | tf_op jit(solution)/shard_map/ppermute | solution.py:289
  21.1 2.6 %collective-permute-start.8 = (f32[272,128]{1,0:T(8,128)S(1)}, f32[272,128]{1,0:T(8,128)S(1)}, u32[]{:S(2)}, u32[]{:S(2)}) collective-permute-start(f32[272,128]{1,0:T(8,128)S(1)} %add.16), channel_id=1, source_target_pairs={{0,16},{8,24},{16,0},{24,8},{1,17},{9,25},{17,1},{25,9},{2,18},{10... | collective-permute-start | bytes 417800 | tf_op jit(solution)/shard_map/ppermute | solution.py:289
  23.7 1.6 %collective-permute-start.6 = (f32[8,128]{1,0:T(8,128)S(1)}, f32[8,128]{1,0:T(8,128)S(1)}, u32[]{:S(2)}, u32[]{:S(2)}) collective-permute-start(f32[8,128]{1,0:T(8,128)S(1)} %add.18.sums_ref), channel_id=1, source_target_pairs={{0,8},{8,0},{16,24},{24,16},{1,9},{9,1},{17,25},{25,17},{2,10},{10... | collective-permute-start | bytes 12296 | tf_op jit(solution)/shard_map/ppermute | solution.py:289
  25.3 1.7 %filter.4.local_refs_1_ = f32[2,32,64,128]{3,2,1,0:T(8,128)S(1)} custom-call(bf16[8,32,64,128]{3,2,1,0:T(8,128)(2,1)S(1)} %get-tuple-element.34.high_ref, bf16[8,32,64,128]{3,2,1,0:T(8,128)(2,1)S(1)} %get-tuple-element.35.low_ref, bf16[8,2,64,128]{3,2,1,0:T(8,128)(2,1)S(1)} %get-tuple-element.36.halo_high_ref, ...), custom_call_target="tpu_custom_call" | custom-call | flops 1140850688 | bytes 1048576 | tf_op jit(solution)/shard_map/filter/pallas_call | solution.py:358
  27.0 0.4 %collective-permute-done.6.earlier_refs_0_ = f32[8,128]{1,0:T(8,128)S(1)} collective-permute-done((f32[8,128]{1,0:T(8,128)S(1)}, f32[8,128]{1,0:T(8,128)S(1)}, u32[]{:S(2)}, u32[]{:S(2)}) %collective-permute-start.6) | collective-permute-done | bytes 4128 | tf_op jit(solution)/shard_map/ppermute | solution.py:289
  27.3 2.1 %collective-permute-start.7 = (f32[8,128]{1,0:T(8,128)S(1)}, f32[8,128]{1,0:T(8,128)S(1)}, u32[]{:S(2)}, u32[]{:S(2)}) collective-permute-start(f32[8,128]{1,0:T(8,128)S(1)} %add.19), channel_id=1, source_target_pairs={{0,16},{8,24},{16,0},{24,8},{1,17},{9,25},{17,1},{25,9},{2,18},{10... | collective-permute-start | bytes 12296 | tf_op jit(solution)/shard_map/ppermute | solution.py:289
  29.4 2.5 %filter.5.local_refs_2_ = f32[3,32,64,128]{3,2,1,0:T(8,128)S(1)} custom-call(bf16[8,32,64,128]{3,2,1,0:T(8,128)(2,1)S(1)} %get-tuple-element.34.high_ref, bf16[8,32,64,128]{3,2,1,0:T(8,128)(2,1)S(1)} %get-tuple-element.35.low_ref, bf16[8,2,64,128]{3,2,1,0:T(8,128)(2,1)S(1)} %get-tuple-element.36.halo_high_ref, ...), custom_call_target="tpu_custom_call" | custom-call | flops 1711276032 | bytes 1048576 | tf_op jit(solution)/shard_map/filter/pallas_call | solution.py:358
  31.9 0.0 collective-permute-done.8.totals_refs_1_
  31.9 4.3 %level.1 = f32[8,64,4096]{2,1,0:T(8,128)} custom-call(f32[3,32,64,128]{3,2,1,0:T(8,128)S(1)} %filter.3.local_refs_0_, f32[2,32,64,128]{3,2,1,0:T(8,128)S(1)} %filter.4.local_refs_1_, f32[3,32,64,128]{3,2,1,0:T(8,128)S(1)} %filter.5.local_refs_2_, bf16[8,512,256]{2,1,0:T(8,128)(2,1)S(1)} %get-tuple-element.49.weight_ref, ...), custom_call_target="tpu_custom_call" | custom-call | tf_op jit(solution)/shard_map/level/pallas_call | solution.py:403
  (16 shorter events, 0.1 us)
Async XLA Ops:
  0.0 5.7 %copy-start = (f32[8,64,4096]{2,1,0:T(8,128)S(1)}, f32[8,64,4096]{2,1,0:T(8,128)}, u32[]{:S(2)}) copy-start(f32[8,64,4096]{2,1,0:T(8,128)} %phase_hbm.1) | copy-start | bytes 25165828
  0.0 6.1 %copy-start.1 = (s32[8,64,4096]{2,1,0:T(8,128)S(1)}, s32[8,64,4096]{2,1,0:T(8,128)}, u32[]{:S(2)}) copy-start(s32[8,64,4096]{2,1,0:T(8,128)} %wrap_hbm.1) | copy-start | bytes 25165828
  1.6 10.1 %collective-permute-start = (f32[4,64,128]{2,1,0:T(8,128)S(1)}, f32[4,64,128]{2,1,0:T(8,128)S(1)}, u32[]{:S(2)}, u32[]{:S(2)}) collective-permute-start(f32[4,64,128]{2,1,0:T(8,128)S(1)} %get-tuple-element.30), channel_id=1, source_target_pairs={{0,1},{1,0},{2,3},{3,2},{4,5},{5,4},{6,7},{7,6},{8,9},{9,8},{10,11... | collective-permute-start | bytes 393224 | tf_op jit(solution)/shard_map/ppermute | solution.py:289
  2.1 9.6 %collective-permute-start.1 = (f32[4,64,128]{2,1,0:T(8,128)S(1)}, f32[4,64,128]{2,1,0:T(8,128)S(1)}, u32[]{:S(2)}, u32[]{:S(2)}) collective-permute-start(f32[4,64,128]{2,1,0:T(8,128)S(1)} %get-tuple-element.31), channel_id=1, source_target_pairs={{0,7},{1,2},{2,1},{3,4},{4,3},{5,6},{6,5},{7,0},{8,15},{9,10},{10,... | collective-permute-start | bytes 393224 | tf_op jit(solution)/shard_map/ppermute | solution.py:320
  6.1 0.7 %copy-start.2 = (f32[8,128]{1,0:T(8,128)S(1)}, f32[8,128]{1,0:T(8,128)}, u32[]{:S(2)}) copy-start(f32[8,128]{1,0:T(8,128)} %taps_ref.1) | copy-start | bytes 12292
  11.9 3.2 %collective-permute-start.2 = (f32[8,128]{1,0:T(8,128)S(1)}, f32[8,128]{1,0:T(8,128)S(1)}, u32[]{:S(2)}, u32[]{:S(2)}) collective-permute-start(f32[8,128]{1,0:T(8,128)S(1)} %get-tuple-element.33), channel_id=1, source_target_pairs={{0,1},{1,0},{2,3},{3,2},{4,5},{5,4},{6,7},{7,6},{8,9},{9,8},{10,11... | collective-permute-start | bytes 12296 | tf_op jit(solution)/shard_map/ppermute | solution.py:289
  12.4 6.9 %collective-permute-start.4 = (f32[272,128]{1,0:T(8,128)S(1)}, f32[272,128]{1,0:T(8,128)S(1)}, u32[]{:S(2)}, u32[]{:S(2)}) collective-permute-start(f32[272,128]{1,0:T(8,128)S(1)} %constant_dynamic-update-slice_fusion), channel_id=1, source_target_pairs={{0,8},{8,0},{16,24},{24,16},{1,9},{9,1},{17,25},{25,17},{2,10},{10... | collective-permute-start | bytes 417800 | tf_op jit(solution)/shard_map/ppermute | solution.py:289
  15.1 4.0 %collective-permute-start.3 = (f32[8,128]{1,0:T(8,128)S(1)}, f32[8,128]{1,0:T(8,128)S(1)}, u32[]{:S(2)}, u32[]{:S(2)}) collective-permute-start(f32[8,128]{1,0:T(8,128)S(1)} %add.15), channel_id=1, source_target_pairs={{0,2},{1,3},{2,0},{3,1},{4,6},{5,7},{6,4},{7,5},{8,10},{9,11},{10,... | collective-permute-start | bytes 12296 | tf_op jit(solution)/shard_map/ppermute | solution.py:289
  19.4 4.4 %collective-permute-start.5 = (f32[8,128]{1,0:T(8,128)S(1)}, f32[8,128]{1,0:T(8,128)S(1)}, u32[]{:S(2)}, u32[]{:S(2)}) collective-permute-start(f32[8,128]{1,0:T(8,128)S(1)} %add.17), channel_id=1, source_target_pairs={{0,4},{1,5},{2,6},{3,7},{4,0},{5,1},{6,2},{7,3},{8,12},{9,13},{10,... | collective-permute-start | bytes 12296 | tf_op jit(solution)/shard_map/ppermute | solution.py:289
  21.1 10.8 %collective-permute-start.8 = (f32[272,128]{1,0:T(8,128)S(1)}, f32[272,128]{1,0:T(8,128)S(1)}, u32[]{:S(2)}, u32[]{:S(2)}) collective-permute-start(f32[272,128]{1,0:T(8,128)S(1)} %add.16), channel_id=1, source_target_pairs={{0,16},{8,24},{16,0},{24,8},{1,17},{9,25},{17,1},{25,9},{2,18},{10... | collective-permute-start | bytes 417800 | tf_op jit(solution)/shard_map/ppermute | solution.py:289
  23.7 3.6 %collective-permute-start.6 = (f32[8,128]{1,0:T(8,128)S(1)}, f32[8,128]{1,0:T(8,128)S(1)}, u32[]{:S(2)}, u32[]{:S(2)}) collective-permute-start(f32[8,128]{1,0:T(8,128)S(1)} %add.18.sums_ref), channel_id=1, source_target_pairs={{0,8},{8,0},{16,24},{24,16},{1,9},{9,1},{17,25},{25,17},{2,10},{10... | collective-permute-start | bytes 12296 | tf_op jit(solution)/shard_map/ppermute | solution.py:289
  27.3 4.6 %copy-start.3 = (f32[8]{0:T(128)S(1)}, f32[8]{0:T(128)}, u32[]{:S(2)}) copy-start(f32[8]{0:T(128)} %coupling_ref.1) | copy-start | bytes 100
  27.3 4.6 %collective-permute-start.7 = (f32[8,128]{1,0:T(8,128)S(1)}, f32[8,128]{1,0:T(8,128)S(1)}, u32[]{:S(2)}, u32[]{:S(2)}) collective-permute-start(f32[8,128]{1,0:T(8,128)S(1)} %add.19), channel_id=1, source_target_pairs={{0,16},{8,24},{16,0},{24,8},{1,17},{9,25},{17,1},{25,9},{2,18},{10... | collective-permute-start | bytes 12296 | tf_op jit(solution)/shard_map/ppermute | solution.py:289

commit v9 on v7

--- a/solution.py
+++ b/solution.py
@@ -12,7 +12,7 @@
 LANES = 128
 HALF = LANES // 2
 SUBLANES = 8
-CHUNKS = 2
+CHUNKS = 4
 
 
 def shifted_down(value, amount):
@@ -79,6 +79,17 @@
             target[cable] = jnp.where(lane < HALF, low, high)
 
 
+def backwards(value):
+    lane = lax.broadcasted_iota(jnp.int32, value.shape, 1)
+    bit = 1
+    while bit < LANES:
+        value = jnp.where(
+            (lane & bit) == 0, pltpu.roll(value, LANES - bit, 1), pltpu.roll(value, bit, 1)
+        )
+        bit *= 2
+    return value
+
+
 def increments_kernel(
     phase_ref, wrap_hbm, taps_ref, high_ref, low_ref, totals_ref, sums_ref, weight_ref, wrap_ref, sem
 ):
@@ -92,21 +103,19 @@
     for cable in range(cables):
         copy(cable).start()
 
-    outputs = lax.broadcasted_iota(jnp.int32, (LANES, LANES), 0)
-    inputs = lax.broadcasted_iota(jnp.int32, (LANES, LANES), 1)
-    centre = (lax.broadcasted_iota(jnp.int32, (1, LANES), 1) == HALF).astype(jnp.float32)
-
-    @pl.loop(0, cables)
-    def _(cable):
-        row = (centre - taps_ref[pl.ds(cable, 1), :]) * (1.0 / (4.0 * two_pi))
-        circulant = pltpu.roll(
-            jnp.broadcast_to(row, (LANES, LANES)), 0, 1, stride=1, stride_axis=0
-        )
-        first = jnp.where(inputs >= outputs, circulant, 0.0).T
-        second = jnp.where(inputs < outputs, circulant, 0.0).T
-        high, low = split(jnp.concatenate([first, second], axis=1))
-        for place, part in enumerate((high, high, low, low)):
-            weight_ref[cable, pl.ds(place * LANES, LANES), :] = part
+    lane = lax.broadcasted_iota(jnp.int32, taps_ref.shape, 1)
+    taps = jnp.where(lane == HALF, 1.0, 0.0) - taps_ref[...]
+    reversed_taps = pltpu.roll(backwards(taps * (1.0 / (4.0 * two_pi))), 1, 1)
+    inputs = lax.broadcasted_iota(jnp.int32, (LANES, LANES), 0)
+    outputs = lax.broadcasted_iota(jnp.int32, (LANES, LANES), 1)
+    for cable in range(cables):
+        row = jnp.broadcast_to(reversed_taps[cable : cable + 1, :], (LANES, LANES))
+        circulant = pltpu.roll(row, 0, 1, stride=1, stride_axis=0)
+        for column, mask in enumerate((inputs >= outputs, inputs < outputs)):
+            high, low = split(jnp.where(mask, circulant, 0.0))
+            for place, part in enumerate((high, high, low, low)):
+                rows, lanes = pl.ds(place * LANES, LANES), pl.ds(column * LANES, LANES)
+                weight_ref[cable, rows, lanes] = part
 
     def cable_step(cable, accumulated):
         copy(cable).wait()
@@ -302,7 +311,7 @@
     blocks = width // LANES
     steps, places = lax.axis_size("tm"), lax.axis_size("chan")
     population = cables * width * places
-    bounds = [0, 3 * cables // 8, 5 * cables // 8, cables]
+    bounds = [0, cables // 2, 3 * cables // 4, cables]
     parts = len(bounds) - 1
     wrap_count = pltpu.with_memory_space_constraint(wrap_count, pltpu.HBM)
     whole = pl.BlockSpec(memory_space=pltpu.VMEM)

time: 33.9 us -> 34.3 us (1.012)
  Pallas kernels: 17.6 us -> 18.2 us
  starting transfers between devices: 14.6 us -> 14.2 us
    pallas_call x1, Pallas kernels: 4.96 us -> 5.42 us  [shards(): pl.pallas_call(increments_kernel, out_shape=(pltpu.VMEM((cables, blocks,...]
    ppermute x8, starting transfers between devices: 11.1 us -> 10.6 us  [swapped(): lax.ppermute(value, axis, [(i, i ^ bit) for i in range(lax.axis_size(axis...]
  transfers between devices with their start and end apart: 9 -> 9, of which waited for: 3 -> 3; matrix products, arithmetic and copies ran while one was open for 0% -> 0% of each run, Pallas kernels for 34% -> 35%
where the time goes in v9:
time: 34.3 us; the launch traced here: 34.2 us
  Pallas kernels  18.2 us (53%)
  starting transfers between devices  14.2 us (41%)
  waiting for transfers between devices  1.57 us (5%)
    ppermute x8, starting transfers between devices, swapped(): lax.ppermute(value, axis, [(i, i ^ bit) for i in range(lax.axis_size(axis...  10.6 us
    pallas_call x3, Pallas kernels, filtered(): pl.pallas_call(functools.partial(filter_kernel, bounds[part]), out_shape=...  6.62 us
    pallas_call x1, Pallas kernels, shards(): pl.pallas_call(increments_kernel, out_shape=(pltpu.VMEM((cables, blocks,...  5.42 us
    pallas_call x1, Pallas kernels, shards(): pl.pallas_call(functools.partial(level_kernel, population), out_shape=jax...  4.44 us
    ppermute x1, starting transfers between devices, shards(): outer = lax.ppermute(outer, 'chan', outer_pairs)  3.56 us
    pallas_call x1, Pallas kernels, shards(): pl.pallas_call(edges_kernel, out_shape=[pltpu.VMEM((cables // 2, time, LA...  1.59 us
    ppermute x8, waiting for transfers between devices, swapped(): lax.ppermute(value, axis, [(i, i ^ bit) for i in range(lax.axis_size(axis...  1.57 us
  transfers between devices with their start and end apart: 9, of which 3 were waited for; matrix products, arithmetic and copies ran while one was open for 0% of the time, Pallas kernels for 35%

profile of v9, /device:TPU:0, one launch (start us, length us, event | category | flops | bytes accessed | tf_op | source)
XLA Modules:
  0.0 34.2 jit_solution(1390626153447066705)
XLA Ops:
  0.0 1.6 %edges.1 = (f32[4,64,128]{2,1,0:T(8,128)S(1)}, f32[4,64,128]{2,1,0:T(8,128)S(1)}) custom-call(f32[8,64,4096]{2,1,0:T(8,128)} %phase_hbm.1, s32[8,64,4096]{2,1,0:T(8,128)} %wrap_hbm.3), custom_call_target="tpu_custom_call" | custom-call | tf_op jit(solution)/shard_map/edges/pallas_call | solution.py:321
  1.6 0.5 %collective-permute-start = (f32[4,64,128]{2,1,0:T(8,128)S(1)}, f32[4,64,128]{2,1,0:T(8,128)S(1)}, u32[]{:S(2)}, u32[]{:S(2)}) collective-permute-start(f32[4,64,128]{2,1,0:T(8,128)S(1)} %get-tuple-element.30), channel_id=1, source_target_pairs={{0,1},{1,0},{2,3},{3,2},{4,5},{5,4},{6,7},{7,6},{8,9},{9,8},{10,11... | collective-permute-start | bytes 393224 | tf_op jit(solution)/shard_map/ppermute | solution.py:306
  2.1 3.6 %collective-permute-start.1 = (f32[4,64,128]{2,1,0:T(8,128)S(1)}, f32[4,64,128]{2,1,0:T(8,128)S(1)}, u32[]{:S(2)}, u32[]{:S(2)}) collective-permute-start(f32[4,64,128]{2,1,0:T(8,128)S(1)} %get-tuple-element.31), channel_id=1, source_target_pairs={{0,7},{1,2},{2,1},{3,4},{4,3},{5,6},{6,5},{7,0},{8,15},{9,10},{10,... | collective-permute-start | bytes 393224 | tf_op jit(solution)/shard_map/ppermute | solution.py:335
  5.7 5.4 %increments.1 = (bf16[8,32,64,128]{3,2,1,0:T(8,128)(2,1)S(1)}, bf16[8,32,64,128]{3,2,1,0:T(8,128)(2,1)S(1)}, f32[256,128]{1,0:T(8,128)S(1)}, f32[8,128]{1,0:T(8,128)S(1)}, bf16[8,512,256]{2,1,0:T(8,128)(2,1)S(1)}) custom-call(f32[8,64,4096]{2,1,0:T(8,128)S(1)} %copy-done, s32[8,64,4096]{2,1,0:T(8,128)} %wrap_hbm.3, f32[8,128]{1,0:T(8,128)S(1)} %copy-done.1), custom_call_target="tpu_custom_call" | custom-call | bytes 8388608 | tf_op jit(solution)/shard_map/increments/pallas_call | solution.py:338
  11.1 0.0 collective-permute-done.inner_ref
  11.1 0.0 collective-permute-done.1.outer_ref
  11.1 0.2 halo.1
  11.3 0.1 collective-permute-start.2
  11.4 1.6 %collective-permute-start.4 = (f32[272,128]{1,0:T(8,128)S(1)}, f32[272,128]{1,0:T(8,128)S(1)}, u32[]{:S(2)}, u32[]{:S(2)}) collective-permute-start(f32[272,128]{1,0:T(8,128)S(1)} %constant_dynamic-update-slice_fusion), channel_id=1, source_target_pairs={{0,8},{8,0},{16,24},{24,16},{1,9},{9,1},{17,25},{25,17},{2,10},{10... | collective-permute-start | bytes 417800 | tf_op jit(solution)/shard_map/ppermute | solution.py:306
  13.0 0.0 collective-permute-done.2
  13.0 1.0 %collective-permute-start.3 = (f32[8,128]{1,0:T(8,128)S(1)}, f32[8,128]{1,0:T(8,128)S(1)}, u32[]{:S(2)}, u32[]{:S(2)}) collective-permute-start(f32[8,128]{1,0:T(8,128)S(1)} %add.15), channel_id=1, source_target_pairs={{0,2},{1,3},{2,0},{3,1},{4,6},{5,7},{6,4},{7,5},{8,10},{9,11},{10,... | collective-permute-start | bytes 12296 | tf_op jit(solution)/shard_map/ppermute | solution.py:306
  14.0 3.3 %filter.3.local_refs_0_ = f32[4,32,64,128]{3,2,1,0:T(8,128)S(1)} custom-call(bf16[8,32,64,128]{3,2,1,0:T(8,128)(2,1)S(1)} %get-tuple-element.34.high_ref, bf16[8,32,64,128]{3,2,1,0:T(8,128)(2,1)S(1)} %get-tuple-element.35.low_ref, bf16[8,2,64,128]{3,2,1,0:T(8,128)(2,1)S(1)} %get-tuple-element.36.halo_high_ref, ...), custom_call_target="tpu_custom_call" | custom-call | flops 2281701376 | bytes 1048576 | tf_op jit(solution)/shard_map/filter/pallas_call | solution.py:375
  17.3 0.0 collective-permute-done.3
  17.4 0.1 collective-permute-done.4.totals_refs_0_
  17.5 1.5 %collective-permute-start.5 = (f32[8,128]{1,0:T(8,128)S(1)}, f32[8,128]{1,0:T(8,128)S(1)}, u32[]{:S(2)}, u32[]{:S(2)}) collective-permute-start(f32[8,128]{1,0:T(8,128)S(1)} %add.17), channel_id=1, source_target_pairs={{0,4},{1,5},{2,6},{3,7},{4,0},{5,1},{6,2},{7,3},{8,12},{9,13},{10,... | collective-permute-start | bytes 12296 | tf_op jit(solution)/shard_map/ppermute | solution.py:306
  19.0 2.6 %collective-permute-start.8 = (f32[272,128]{1,0:T(8,128)S(1)}, f32[272,128]{1,0:T(8,128)S(1)}, u32[]{:S(2)}, u32[]{:S(2)}) collective-permute-start(f32[272,128]{1,0:T(8,128)S(1)} %add.16), channel_id=1, source_target_pairs={{0,16},{8,24},{16,0},{24,8},{1,17},{9,25},{17,1},{25,9},{2,18},{10... | collective-permute-start | bytes 417800 | tf_op jit(solution)/shard_map/ppermute | solution.py:306
  21.6 0.0 collective-permute-done.5
  21.6 1.2 %collective-permute-start.6 = (f32[8,128]{1,0:T(8,128)S(1)}, f32[8,128]{1,0:T(8,128)S(1)}, u32[]{:S(2)}, u32[]{:S(2)}) collective-permute-start(f32[8,128]{1,0:T(8,128)S(1)} %add.18.sums_ref), channel_id=1, source_target_pairs={{0,8},{8,0},{16,24},{24,16},{1,9},{9,1},{17,25},{25,17},{2,10},{10... | collective-permute-start | bytes 12296 | tf_op jit(solution)/shard_map/ppermute | solution.py:306
  22.8 1.7 %filter.4.local_refs_1_ = f32[2,32,64,128]{3,2,1,0:T(8,128)S(1)} custom-call(bf16[8,32,64,128]{3,2,1,0:T(8,128)(2,1)S(1)} %get-tuple-element.34.high_ref, bf16[8,32,64,128]{3,2,1,0:T(8,128)(2,1)S(1)} %get-tuple-element.35.low_ref, bf16[8,2,64,128]{3,2,1,0:T(8,128)(2,1)S(1)} %get-tuple-element.36.halo_high_ref, ...), custom_call_target="tpu_custom_call" | custom-call | flops 1140850688 | bytes 1048576 | tf_op jit(solution)/shard_map/filter/pallas_call | solution.py:375
  24.4 0.8 %collective-permute-done.6.earlier_refs_0_ = f32[8,128]{1,0:T(8,128)S(1)} collective-permute-done((f32[8,128]{1,0:T(8,128)S(1)}, f32[8,128]{1,0:T(8,128)S(1)}, u32[]{:S(2)}, u32[]{:S(2)}) %collective-permute-start.6) | collective-permute-done | bytes 4128 | tf_op jit(solution)/shard_map/ppermute | solution.py:306
  25.2 2.2 %collective-permute-start.7 = (f32[8,128]{1,0:T(8,128)S(1)}, f32[8,128]{1,0:T(8,128)S(1)}, u32[]{:S(2)}, u32[]{:S(2)}) collective-permute-start(f32[8,128]{1,0:T(8,128)S(1)} %add.19), channel_id=1, source_target_pairs={{0,16},{8,24},{16,0},{24,8},{1,17},{9,25},{17,1},{25,9},{2,18},{10... | collective-permute-start | bytes 12296 | tf_op jit(solution)/shard_map/ppermute | solution.py:306
  27.4 1.7 %filter.5.local_refs_2_ = f32[2,32,64,128]{3,2,1,0:T(8,128)S(1)} custom-call(bf16[8,32,64,128]{3,2,1,0:T(8,128)(2,1)S(1)} %get-tuple-element.34.high_ref, bf16[8,32,64,128]{3,2,1,0:T(8,128)(2,1)S(1)} %get-tuple-element.35.low_ref, bf16[8,2,64,128]{3,2,1,0:T(8,128)(2,1)S(1)} %get-tuple-element.36.halo_high_ref, ...), custom_call_target="tpu_custom_call" | custom-call | flops 1140850688 | bytes 1048576 | tf_op jit(solution)/shard_map/filter/pallas_call | solution.py:375
  29.1 0.7 %collective-permute-done.7.earlier_refs_1_ = f32[8,128]{1,0:T(8,128)S(1)} collective-permute-done((f32[8,128]{1,0:T(8,128)S(1)}, f32[8,128]{1,0:T(8,128)S(1)}, u32[]{:S(2)}, u32[]{:S(2)}) %collective-permute-start.7) | collective-permute-done | bytes 4128 | tf_op jit(solution)/shard_map/ppermute | solution.py:306
  29.7 4.4 %level.1 = f32[8,64,4096]{2,1,0:T(8,128)} custom-call(f32[4,32,64,128]{3,2,1,0:T(8,128)S(1)} %filter.3.local_refs_0_, f32[2,32,64,128]{3,2,1,0:T(8,128)S(1)} %filter.4.local_refs_1_, f32[2,32,64,128]{3,2,1,0:T(8,128)S(1)} %filter.5.local_refs_2_, bf16[8,512,256]{2,1,0:T(8,128)(2,1)S(1)} %get-tuple-element.49.weight_ref, ...), custom_call_target="tpu_custom_call" | custom-call | tf_op jit(solution)/shard_map/level/pallas_call | solution.py:420
  (14 shorter events, 0.1 us)
Async XLA Ops:
  0.0 5.7 %copy-start.1 = (f32[8,128]{1,0:T(8,128)S(1)}, f32[8,128]{1,0:T(8,128)}, u32[]{:S(2)}) copy-start(f32[8,128]{1,0:T(8,128)} %taps_ref.1) | copy-start | bytes 12292
  0.0 5.7 %copy-start = (f32[8,64,4096]{2,1,0:T(8,128)S(1)}, f32[8,64,4096]{2,1,0:T(8,128)}, u32[]{:S(2)}) copy-start(f32[8,64,4096]{2,1,0:T(8,128)} %phase_hbm.1) | copy-start | bytes 25165828
  1.6 9.5 %collective-permute-start = (f32[4,64,128]{2,1,0:T(8,128)S(1)}, f32[4,64,128]{2,1,0:T(8,128)S(1)}, u32[]{:S(2)}, u32[]{:S(2)}) collective-permute-start(f32[4,64,128]{2,1,0:T(8,128)S(1)} %get-tuple-element.30), channel_id=1, source_target_pairs={{0,1},{1,0},{2,3},{3,2},{4,5},{5,4},{6,7},{7,6},{8,9},{9,8},{10,11... | collective-permute-start | bytes 393224 | tf_op jit(solution)/shard_map/ppermute | solution.py:306
  2.1 9.0 %collective-permute-start.1 = (f32[4,64,128]{2,1,0:T(8,128)S(1)}, f32[4,64,128]{2,1,0:T(8,128)S(1)}, u32[]{:S(2)}, u32[]{:S(2)}) collective-permute-start(f32[4,64,128]{2,1,0:T(8,128)S(1)} %get-tuple-element.31), channel_id=1, source_target_pairs={{0,7},{1,2},{2,1},{3,4},{4,3},{5,6},{6,5},{7,0},{8,15},{9,10},{10,... | collective-permute-start | bytes 393224 | tf_op jit(solution)/shard_map/ppermute | solution.py:335
  11.3 1.7 %collective-permute-start.2 = (f32[8,128]{1,0:T(8,128)S(1)}, f32[8,128]{1,0:T(8,128)S(1)}, u32[]{:S(2)}, u32[]{:S(2)}) collective-permute-start(f32[8,128]{1,0:T(8,128)S(1)} %get-tuple-element.33), channel_id=1, source_target_pairs={{0,1},{1,0},{2,3},{3,2},{4,5},{5,4},{6,7},{7,6},{8,9},{9,8},{10,11... | collective-permute-start | bytes 12296 | tf_op jit(solution)/shard_map/ppermute | solution.py:306
  11.4 6.1 %collective-permute-start.4 = (f32[272,128]{1,0:T(8,128)S(1)}, f32[272,128]{1,0:T(8,128)S(1)}, u32[]{:S(2)}, u32[]{:S(2)}) collective-permute-start(f32[272,128]{1,0:T(8,128)S(1)} %constant_dynamic-update-slice_fusion), channel_id=1, source_target_pairs={{0,8},{8,0},{16,24},{24,16},{1,9},{9,1},{17,25},{25,17},{2,10},{10... | collective-permute-start | bytes 417800 | tf_op jit(solution)/shard_map/ppermute | solution.py:306
  13.0 4.3 %collective-permute-start.3 = (f32[8,128]{1,0:T(8,128)S(1)}, f32[8,128]{1,0:T(8,128)S(1)}, u32[]{:S(2)}, u32[]{:S(2)}) collective-permute-start(f32[8,128]{1,0:T(8,128)S(1)} %add.15), channel_id=1, source_target_pairs={{0,2},{1,3},{2,0},{3,1},{4,6},{5,7},{6,4},{7,5},{8,10},{9,11},{10,... | collective-permute-start | bytes 12296 | tf_op jit(solution)/shard_map/ppermute | solution.py:306
  17.5 4.1 %collective-permute-start.5 = (f32[8,128]{1,0:T(8,128)S(1)}, f32[8,128]{1,0:T(8,128)S(1)}, u32[]{:S(2)}, u32[]{:S(2)}) collective-permute-start(f32[8,128]{1,0:T(8,128)S(1)} %add.17), channel_id=1, source_target_pairs={{0,4},{1,5},{2,6},{3,7},{4,0},{5,1},{6,2},{7,3},{8,12},{9,13},{10,... | collective-permute-start | bytes 12296 | tf_op jit(solution)/shard_map/ppermute | solution.py:306
  19.0 10.7 %collective-permute-start.8 = (f32[272,128]{1,0:T(8,128)S(1)}, f32[272,128]{1,0:T(8,128)S(1)}, u32[]{:S(2)}, u32[]{:S(2)}) collective-permute-start(f32[272,128]{1,0:T(8,128)S(1)} %add.16), channel_id=1, source_target_pairs={{0,16},{8,24},{16,0},{24,8},{1,17},{9,25},{17,1},{25,9},{2,18},{10... | collective-permute-start | bytes 417800 | tf_op jit(solution)/shard_map/ppermute | solution.py:306
  21.6 3.6 %collective-permute-start.6 = (f32[8,128]{1,0:T(8,128)S(1)}, f32[8,128]{1,0:T(8,128)S(1)}, u32[]{:S(2)}, u32[]{:S(2)}) collective-permute-start(f32[8,128]{1,0:T(8,128)S(1)} %add.18.sums_ref), channel_id=1, source_target_pairs={{0,8},{8,0},{16,24},{24,16},{1,9},{9,1},{17,25},{25,17},{2,10},{10... | collective-permute-start | bytes 12296 | tf_op jit(solution)/shard_map/ppermute | solution.py:306
  25.2 4.5 %copy-start.2 = (f32[8]{0:T(128)S(1)}, f32[8]{0:T(128)}, u32[]{:S(2)}) copy-start(f32[8]{0:T(128)} %coupling_ref.1) | copy-start | bytes 100
  25.2 4.5 %collective-permute-start.7 = (f32[8,128]{1,0:T(8,128)S(1)}, f32[8,128]{1,0:T(8,128)S(1)}, u32[]{:S(2)}, u32[]{:S(2)}) collective-permute-start(f32[8,128]{1,0:T(8,128)S(1)} %add.19), channel_id=1, source_target_pairs={{0,16},{8,24},{16,0},{24,8},{1,17},{9,25},{17,1},{25,9},{2,18},{10... | collective-permute-start | bytes 12296 | tf_op jit(solution)/shard_map/ppermute | solution.py:306

commit v10 on v9

--- a/solution.py
+++ b/solution.py
@@ -12,7 +12,7 @@
 LANES = 128
 HALF = LANES // 2
 SUBLANES = 8
-CHUNKS = 4
+CHUNKS = 2
 
 
 def shifted_down(value, amount):
@@ -91,7 +91,8 @@
 
 
 def increments_kernel(
-    phase_ref, wrap_hbm, taps_ref, high_ref, low_ref, totals_ref, sums_ref, weight_ref, wrap_ref, sem
+    phase_ref, wrap_hbm, taps_ref, high_ref, low_ref, totals_ref, sums_ref, weight_ref, wrap_ref,
+    reversed_ref, sem,
 ):
     cables, time, width = phase_ref.shape
     blocks = width // LANES
@@ -105,11 +106,13 @@
 
     lane = lax.broadcasted_iota(jnp.int32, taps_ref.shape, 1)
     taps = jnp.where(lane == HALF, 1.0, 0.0) - taps_ref[...]
-    reversed_taps = pltpu.roll(backwards(taps * (1.0 / (4.0 * two_pi))), 1, 1)
+    reversed_ref[...] = pltpu.roll(backwards(taps * (1.0 / (4.0 * two_pi))), 1, 1)
     inputs = lax.broadcasted_iota(jnp.int32, (LANES, LANES), 0)
     outputs = lax.broadcasted_iota(jnp.int32, (LANES, LANES), 1)
-    for cable in range(cables):
-        row = jnp.broadcast_to(reversed_taps[cable : cable + 1, :], (LANES, LANES))
+
+    @pl.loop(0, cables)
+    def _(cable):
+        row = jnp.broadcast_to(reversed_ref[pl.ds(cable, 1), :], (LANES, LANES))
         circulant = pltpu.roll(row, 0, 1, stride=1, stride_axis=0)
         for column, mask in enumerate((inputs >= outputs, inputs < outputs)):
             high, low = split(jnp.where(mask, circulant, 0.0))
@@ -131,7 +134,7 @@
             totals_ref[pl.ds(block * cables + cable, 1), :] = total(pieces)
             return tuple(a + b for a, b in zip(accumulated, pieces))
 
-        return lax.fori_loop(0, blocks, block_step, accumulated, unroll=4)
+        return lax.fori_loop(0, blocks, block_step, accumulated, unroll=16)
 
     zeros = tuple(jnp.zeros((SUBLANES, LANES), jnp.float32) for _ in range(groups))
     accumulated = scanned(lax.fori_loop(0, cables, cable_step, zeros))
@@ -331,7 +334,8 @@
         compiler_params=pltpu.CompilerParams(vmem_limit_bytes=8 << 20),
         name="edges",
     )(pltpu.with_memory_space_constraint(phase_step, pltpu.HBM), wrap_count)
-    outer_pairs = [(i, (i + (1 if i % 2 else -1)) % places) for i in range(places)]
+    last = places - 1
+    outer_pairs = [(0, 0), (last, last)] + [(i, i + (1 if i % 2 else -1)) for i in range(1, last)]
     outer = lax.ppermute(outer, "chan", outer_pairs)
     inner = swapped(inner, "chan", 1)
 
@@ -348,6 +352,7 @@
         out_specs=[whole] * 5,
         scratch_shapes=[
             pltpu.VMEM((cables, time, width), jnp.int32),
+            pltpu.VMEM(filter_taps.shape, jnp.float32),
             pltpu.SemaphoreType.DMA((cables,)),
         ],
         compiler_params=pltpu.CompilerParams(vmem_limit_bytes=16 << 20),

time: 34.3 us -> 34.8 us (1.015)
  starting transfers between devices: 14.2 us -> 15.9 us
  Pallas kernels: 18.2 us -> 16.8 us
  local copies, waits for them, and re-layouts: 0.02 us -> 0.83 us
  waiting for transfers between devices: 1.57 us -> 0.88 us
    ppermute x8, starting transfers between devices: 10.6 us -> 15.1 us  [swapped(): lax.ppermute(value, axis, [(i, i ^ bit) for i in range(lax.axis_size(axis...]
    ppermute x1, starting transfers between devices: 3.56 us -> 0.79 us  [shards(): outer = lax.ppermute(outer, 'chan', outer_pairs)]
    pallas_call x1, Pallas kernels: 5.42 us -> 4.21 us  [shards(): pl.pallas_call(increments_kernel, out_shape=(pltpu.VMEM((cables, blocks,...]
    unnamed x7, local copies, waits for them, and re-layouts: 0.02 us -> 0.82 us
    ppermute x8, waiting for transfers between devices: 1.57 us -> 0.88 us  [swapped(): lax.ppermute(value, axis, [(i, i ^ bit) for i in range(lax.axis_size(axis...]
  transfers between devices with their start and end apart: 9 -> 9, of which waited for: 3 -> 3; matrix products, arithmetic and copies ran while one was open for 0% -> 0% of each run, Pallas kernels for 35% -> 31%
where the time goes in v10:
time: 34.8 us; the launch traced here: 34.6 us
  Pallas kernels  16.8 us (48%)
  starting transfers between devices  15.9 us (46%)
  waiting for transfers between devices  0.88 us (3%)
  local copies, waits for them, and re-layouts  0.83 us (2%)
    ppermute x8, starting transfers between devices, swapped(): lax.ppermute(value, axis, [(i, i ^ bit) for i in range(lax.axis_size(axis...  15.1 us
    pallas_call x3, Pallas kernels, filtered(): pl.pallas_call(functools.partial(filter_kernel, bounds[part]), out_shape=...  6.63 us
    pallas_call x1, Pallas kernels, shards(): pl.pallas_call(functools.partial(level_kernel, population), out_shape=jax...  4.27 us
    pallas_call x1, Pallas kernels, shards(): pl.pallas_call(increments_kernel, out_shape=(pltpu.VMEM((cables, blocks,...  4.21 us
    pallas_call x1, Pallas kernels, shards(): pl.pallas_call(edges_kernel, out_shape=[pltpu.VMEM((cables // 2, time, LA...  1.59 us
    ppermute x8, waiting for transfers between devices, swapped(): lax.ppermute(value, axis, [(i, i ^ bit) for i in range(lax.axis_size(axis...  0.88 us
    unnamed x7, local copies, waits for them, and re-layouts  0.82 us
    ppermute x1, starting transfers between devices, shards(): outer = lax.ppermute(outer, 'chan', outer_pairs)  0.79 us
  transfers between devices with their start and end apart: 9, of which 3 were waited for; matrix products, arithmetic and copies ran while one was open for 0% of the time, Pallas kernels for 31%

profile of v10, /device:TPU:0, one launch (start us, length us, event | category | flops | bytes accessed | tf_op | source)
XLA Modules:
  0.0 34.6 jit_solution(12918912282914203598)
XLA Ops:
  0.0 1.6 %edges.1 = (f32[4,64,128]{2,1,0:T(8,128)S(1)}, f32[4,64,128]{2,1,0:T(8,128)S(1)}) custom-call(f32[8,64,4096]{2,1,0:T(8,128)} %phase_hbm.1, s32[8,64,4096]{2,1,0:T(8,128)} %wrap_hbm.3), custom_call_target="tpu_custom_call" | custom-call | tf_op jit(solution)/shard_map/edges/pallas_call | solution.py:324
  1.6 0.5 %collective-permute-start = (f32[4,64,128]{2,1,0:T(8,128)S(1)}, f32[4,64,128]{2,1,0:T(8,128)S(1)}, u32[]{:S(2)}, u32[]{:S(2)}) collective-permute-start(f32[4,64,128]{2,1,0:T(8,128)S(1)} %get-tuple-element.30), channel_id=1, source_target_pairs={{0,1},{1,0},{2,3},{3,2},{4,5},{5,4},{6,7},{7,6},{8,9},{9,8},{10,11... | collective-permute-start | bytes 393224 | tf_op jit(solution)/shard_map/ppermute | solution.py:309
  2.1 0.8 %collective-permute-start.1 = (f32[4,64,128]{2,1,0:T(8,128)S(1)}, f32[4,64,128]{2,1,0:T(8,128)S(1)}, u32[]{:S(2)}, u32[]{:S(2)}) collective-permute-start(f32[4,64,128]{2,1,0:T(8,128)S(1)} %get-tuple-element.31), channel_id=1, source_target_pairs={{0,0},{7,7},{1,2},{2,1},{3,4},{4,3},{5,6},{6,5},{8,8},{15,15},{9,1... | collective-permute-start | bytes 393224 | tf_op jit(solution)/shard_map/ppermute | solution.py:339
  2.9 0.8 %copy-done = f32[8,64,4096]{2,1,0:T(8,128)S(1)} copy-done((f32[8,64,4096]{2,1,0:T(8,128)S(1)}, f32[8,64,4096]{2,1,0:T(8,128)}, u32[]{:S(2)}) %copy-start) | copy-done | bytes 8388632
  3.7 4.2 %increments.1 = (bf16[8,32,64,128]{3,2,1,0:T(8,128)(2,1)S(1)}, bf16[8,32,64,128]{3,2,1,0:T(8,128)(2,1)S(1)}, f32[256,128]{1,0:T(8,128)S(1)}, f32[8,128]{1,0:T(8,128)S(1)}, bf16[8,512,256]{2,1,0:T(8,128)(2,1)S(1)}) custom-call(f32[8,64,4096]{2,1,0:T(8,128)S(1)} %copy-done, s32[8,64,4096]{2,1,0:T(8,128)} %wrap_hbm.3, f32[8,128]{1,0:T(8,128)S(1)} %copy-done.1), custom_call_target="tpu_custom_call" | custom-call | bytes 8388608 | tf_op jit(solution)/shard_map/increments/pallas_call | solution.py:342
  8.0 0.0 collective-permute-done.inner_ref
  8.0 0.0 collective-permute-done.1.outer_ref
  8.0 0.2 halo.1
  8.1 3.3 %collective-permute-start.2 = (f32[8,128]{1,0:T(8,128)S(1)}, f32[8,128]{1,0:T(8,128)S(1)}, u32[]{:S(2)}, u32[]{:S(2)}) collective-permute-start(f32[8,128]{1,0:T(8,128)S(1)} %get-tuple-element.33), channel_id=1, source_target_pairs={{0,1},{1,0},{2,3},{3,2},{4,5},{5,4},{6,7},{7,6},{8,9},{9,8},{10,11... | collective-permute-start | bytes 12296 | tf_op jit(solution)/shard_map/ppermute | solution.py:309
  11.4 1.6 %collective-permute-start.4 = (f32[272,128]{1,0:T(8,128)S(1)}, f32[272,128]{1,0:T(8,128)S(1)}, u32[]{:S(2)}, u32[]{:S(2)}) collective-permute-start(f32[272,128]{1,0:T(8,128)S(1)} %constant_dynamic-update-slice_fusion), channel_id=1, source_target_pairs={{0,8},{8,0},{16,24},{24,16},{1,9},{9,1},{17,25},{25,17},{2,10},{10... | collective-permute-start | bytes 417800 | tf_op jit(solution)/shard_map/ppermute | solution.py:309
  13.0 0.0 collective-permute-done.2
  13.0 2.1 %collective-permute-start.3 = (f32[8,128]{1,0:T(8,128)S(1)}, f32[8,128]{1,0:T(8,128)S(1)}, u32[]{:S(2)}, u32[]{:S(2)}) collective-permute-start(f32[8,128]{1,0:T(8,128)S(1)} %add.15), channel_id=1, source_target_pairs={{0,2},{1,3},{2,0},{3,1},{4,6},{5,7},{6,4},{7,5},{8,10},{9,11},{10,... | collective-permute-start | bytes 12296 | tf_op jit(solution)/shard_map/ppermute | solution.py:309
  15.2 3.3 %filter.3.local_refs_0_ = f32[4,32,64,128]{3,2,1,0:T(8,128)S(1)} custom-call(bf16[8,32,64,128]{3,2,1,0:T(8,128)(2,1)S(1)} %get-tuple-element.34.high_ref, bf16[8,32,64,128]{3,2,1,0:T(8,128)(2,1)S(1)} %get-tuple-element.35.low_ref, bf16[8,2,64,128]{3,2,1,0:T(8,128)(2,1)S(1)} %get-tuple-element.36.halo_high_ref, ...), custom_call_target="tpu_custom_call" | custom-call | flops 2281701376 | bytes 1048576 | tf_op jit(solution)/shard_map/filter/pallas_call | solution.py:380
  18.5 0.0 collective-permute-done.4.totals_refs_0_
  18.5 0.8 %collective-permute-start.5 = (f32[8,128]{1,0:T(8,128)S(1)}, f32[8,128]{1,0:T(8,128)S(1)}, u32[]{:S(2)}, u32[]{:S(2)}) collective-permute-start(f32[8,128]{1,0:T(8,128)S(1)} %add.17), channel_id=1, source_target_pairs={{0,4},{1,5},{2,6},{3,7},{4,0},{5,1},{6,2},{7,3},{8,12},{9,13},{10,... | collective-permute-start | bytes 12296 | tf_op jit(solution)/shard_map/ppermute | solution.py:309
  19.3 2.8 %collective-permute-start.8 = (f32[272,128]{1,0:T(8,128)S(1)}, f32[272,128]{1,0:T(8,128)S(1)}, u32[]{:S(2)}, u32[]{:S(2)}) collective-permute-start(f32[272,128]{1,0:T(8,128)S(1)} %add.16), channel_id=1, source_target_pairs={{0,16},{8,24},{16,0},{24,8},{1,17},{9,25},{17,1},{25,9},{2,18},{10... | collective-permute-start | bytes 417800 | tf_op jit(solution)/shard_map/ppermute | solution.py:309
  22.1 0.1 collective-permute-done.5
  22.2 1.5 %collective-permute-start.6 = (f32[8,128]{1,0:T(8,128)S(1)}, f32[8,128]{1,0:T(8,128)S(1)}, u32[]{:S(2)}, u32[]{:S(2)}) collective-permute-start(f32[8,128]{1,0:T(8,128)S(1)} %add.18.sums_ref), channel_id=1, source_target_pairs={{0,8},{8,0},{16,24},{24,16},{1,9},{9,1},{17,25},{25,17},{2,10},{10... | collective-permute-start | bytes 12296 | tf_op jit(solution)/shard_map/ppermute | solution.py:309
  23.7 1.7 %filter.4.local_refs_1_ = f32[2,32,64,128]{3,2,1,0:T(8,128)S(1)} custom-call(bf16[8,32,64,128]{3,2,1,0:T(8,128)(2,1)S(1)} %get-tuple-element.34.high_ref, bf16[8,32,64,128]{3,2,1,0:T(8,128)(2,1)S(1)} %get-tuple-element.35.low_ref, bf16[8,2,64,128]{3,2,1,0:T(8,128)(2,1)S(1)} %get-tuple-element.36.halo_high_ref, ...), custom_call_target="tpu_custom_call" | custom-call | flops 1140850688 | bytes 1048576 | tf_op jit(solution)/shard_map/filter/pallas_call | solution.py:380
  25.3 0.5 %collective-permute-done.6.earlier_refs_0_ = f32[8,128]{1,0:T(8,128)S(1)} collective-permute-done((f32[8,128]{1,0:T(8,128)S(1)}, f32[8,128]{1,0:T(8,128)S(1)}, u32[]{:S(2)}, u32[]{:S(2)}) %collective-permute-start.6) | collective-permute-done | bytes 4128 | tf_op jit(solution)/shard_map/ppermute | solution.py:309
  25.8 2.6 %collective-permute-start.7 = (f32[8,128]{1,0:T(8,128)S(1)}, f32[8,128]{1,0:T(8,128)S(1)}, u32[]{:S(2)}, u32[]{:S(2)}) collective-permute-start(f32[8,128]{1,0:T(8,128)S(1)} %add.19), channel_id=1, source_target_pairs={{0,16},{8,24},{16,0},{24,8},{1,17},{9,25},{17,1},{25,9},{2,18},{10... | collective-permute-start | bytes 12296 | tf_op jit(solution)/shard_map/ppermute | solution.py:309
  28.4 1.7 %filter.5.local_refs_2_ = f32[2,32,64,128]{3,2,1,0:T(8,128)S(1)} custom-call(bf16[8,32,64,128]{3,2,1,0:T(8,128)(2,1)S(1)} %get-tuple-element.34.high_ref, bf16[8,32,64,128]{3,2,1,0:T(8,128)(2,1)S(1)} %get-tuple-element.35.low_ref, bf16[8,2,64,128]{3,2,1,0:T(8,128)(2,1)S(1)} %get-tuple-element.36.halo_high_ref, ...), custom_call_target="tpu_custom_call" | custom-call | flops 1140850688 | bytes 1048576 | tf_op jit(solution)/shard_map/filter/pallas_call | solution.py:380
  30.1 0.3 collective-permute-done.7.earlier_refs_1_
  30.3 4.3 %level.1 = f32[8,64,4096]{2,1,0:T(8,128)} custom-call(f32[4,32,64,128]{3,2,1,0:T(8,128)S(1)} %filter.3.local_refs_0_, f32[2,32,64,128]{3,2,1,0:T(8,128)S(1)} %filter.4.local_refs_1_, f32[2,32,64,128]{3,2,1,0:T(8,128)S(1)} %filter.5.local_refs_2_, bf16[8,512,256]{2,1,0:T(8,128)(2,1)S(1)} %get-tuple-element.49.weight_ref, ...), custom_call_target="tpu_custom_call" | custom-call | tf_op jit(solution)/shard_map/level/pallas_call | solution.py:425
  (14 shorter events, 0.1 us)
Async XLA Ops:
  0.0 2.9 %copy-start.1 = (f32[8,128]{1,0:T(8,128)S(1)}, f32[8,128]{1,0:T(8,128)}, u32[]{:S(2)}) copy-start(f32[8,128]{1,0:T(8,128)} %taps_ref.1) | copy-start | bytes 12292
  0.0 3.7 %copy-start = (f32[8,64,4096]{2,1,0:T(8,128)S(1)}, f32[8,64,4096]{2,1,0:T(8,128)}, u32[]{:S(2)}) copy-start(f32[8,64,4096]{2,1,0:T(8,128)} %phase_hbm.1) | copy-start | bytes 25165828
  1.6 6.4 %collective-permute-start = (f32[4,64,128]{2,1,0:T(8,128)S(1)}, f32[4,64,128]{2,1,0:T(8,128)S(1)}, u32[]{:S(2)}, u32[]{:S(2)}) collective-permute-start(f32[4,64,128]{2,1,0:T(8,128)S(1)} %get-tuple-element.30), channel_id=1, source_target_pairs={{0,1},{1,0},{2,3},{3,2},{4,5},{5,4},{6,7},{7,6},{8,9},{9,8},{10,11... | collective-permute-start | bytes 393224 | tf_op jit(solution)/shard_map/ppermute | solution.py:309
  2.1 5.9 %collective-permute-start.1 = (f32[4,64,128]{2,1,0:T(8,128)S(1)}, f32[4,64,128]{2,1,0:T(8,128)S(1)}, u32[]{:S(2)}, u32[]{:S(2)}) collective-permute-start(f32[4,64,128]{2,1,0:T(8,128)S(1)} %get-tuple-element.31), channel_id=1, source_target_pairs={{0,0},{7,7},{1,2},{2,1},{3,4},{4,3},{5,6},{6,5},{8,8},{15,15},{9,1... | collective-permute-start | bytes 393224 | tf_op jit(solution)/shard_map/ppermute | solution.py:339
  8.1 4.9 %collective-permute-start.2 = (f32[8,128]{1,0:T(8,128)S(1)}, f32[8,128]{1,0:T(8,128)S(1)}, u32[]{:S(2)}, u32[]{:S(2)}) collective-permute-start(f32[8,128]{1,0:T(8,128)S(1)} %get-tuple-element.33), channel_id=1, source_target_pairs={{0,1},{1,0},{2,3},{3,2},{4,5},{5,4},{6,7},{7,6},{8,9},{9,8},{10,11... | collective-permute-start | bytes 12296 | tf_op jit(solution)/shard_map/ppermute | solution.py:309
  11.4 7.1 %collective-permute-start.4 = (f32[272,128]{1,0:T(8,128)S(1)}, f32[272,128]{1,0:T(8,128)S(1)}, u32[]{:S(2)}, u32[]{:S(2)}) collective-permute-start(f32[272,128]{1,0:T(8,128)S(1)} %constant_dynamic-update-slice_fusion), channel_id=1, source_target_pairs={{0,8},{8,0},{16,24},{24,16},{1,9},{9,1},{17,25},{25,17},{2,10},{10... | collective-permute-start | bytes 417800 | tf_op jit(solution)/shard_map/ppermute | solution.py:309
  13.0 5.5 %collective-permute-start.3 = (f32[8,128]{1,0:T(8,128)S(1)}, f32[8,128]{1,0:T(8,128)S(1)}, u32[]{:S(2)}, u32[]{:S(2)}) collective-permute-start(f32[8,128]{1,0:T(8,128)S(1)} %add.15), channel_id=1, source_target_pairs={{0,2},{1,3},{2,0},{3,1},{4,6},{5,7},{6,4},{7,5},{8,10},{9,11},{10,... | collective-permute-start | bytes 12296 | tf_op jit(solution)/shard_map/ppermute | solution.py:309
  18.5 3.7 %collective-permute-start.5 = (f32[8,128]{1,0:T(8,128)S(1)}, f32[8,128]{1,0:T(8,128)S(1)}, u32[]{:S(2)}, u32[]{:S(2)}) collective-permute-start(f32[8,128]{1,0:T(8,128)S(1)} %add.17), channel_id=1, source_target_pairs={{0,4},{1,5},{2,6},{3,7},{4,0},{5,1},{6,2},{7,3},{8,12},{9,13},{10,... | collective-permute-start | bytes 12296 | tf_op jit(solution)/shard_map/ppermute | solution.py:309
  19.3 11.0 %collective-permute-start.8 = (f32[272,128]{1,0:T(8,128)S(1)}, f32[272,128]{1,0:T(8,128)S(1)}, u32[]{:S(2)}, u32[]{:S(2)}) collective-permute-start(f32[272,128]{1,0:T(8,128)S(1)} %add.16), channel_id=1, source_target_pairs={{0,16},{8,24},{16,0},{24,8},{1,17},{9,25},{17,1},{25,9},{2,18},{10... | collective-permute-start | bytes 417800 | tf_op jit(solution)/shard_map/ppermute | solution.py:309
  22.2 3.6 %collective-permute-start.6 = (f32[8,128]{1,0:T(8,128)S(1)}, f32[8,128]{1,0:T(8,128)S(1)}, u32[]{:S(2)}, u32[]{:S(2)}) collective-permute-start(f32[8,128]{1,0:T(8,128)S(1)} %add.18.sums_ref), channel_id=1, source_target_pairs={{0,8},{8,0},{16,24},{24,16},{1,9},{9,1},{17,25},{25,17},{2,10},{10... | collective-permute-start | bytes 12296 | tf_op jit(solution)/shard_map/ppermute | solution.py:309
  25.8 4.5 %copy-start.2 = (f32[8]{0:T(128)S(1)}, f32[8]{0:T(128)}, u32[]{:S(2)}) copy-start(f32[8]{0:T(128)} %coupling_ref.1) | copy-start | bytes 100
  25.8 4.5 %collective-permute-start.7 = (f32[8,128]{1,0:T(8,128)S(1)}, f32[8,128]{1,0:T(8,128)S(1)}, u32[]{:S(2)}, u32[]{:S(2)}) collective-permute-start(f32[8,128]{1,0:T(8,128)S(1)} %add.19), channel_id=1, source_target_pairs={{0,16},{8,24},{16,0},{24,8},{1,17},{9,25},{17,1},{25,9},{2,18},{10... | collective-permute-start | bytes 12296 | tf_op jit(solution)/shard_map/ppermute | solution.py:309

commit v11 on v9

--- a/solution.py
+++ b/solution.py
@@ -12,7 +12,7 @@
 LANES = 128
 HALF = LANES // 2
 SUBLANES = 8
-CHUNKS = 4
+CHUNKS = 2
 
 
 def shifted_down(value, amount):
@@ -90,9 +90,16 @@
     return value
 
 
-def increments_kernel(
-    phase_ref, wrap_hbm, taps_ref, high_ref, low_ref, totals_ref, sums_ref, weight_ref, wrap_ref, sem
-):
+def increments(phase_ref, wrap_ref, cable, lanes):
+    pieces = []
+    for i in range(phase_ref.shape[1] // SUBLANES):
+        rows = pl.ds(i * SUBLANES, SUBLANES)
+        turns = wrap_ref[cable, rows, lanes].astype(jnp.float32)
+        pieces.append(phase_ref[cable, rows, lanes] + two_pi * turns)
+    return pieces
+
+
+def totals_kernel(phase_ref, wrap_hbm, totals_ref, sums_ref, wrap_ref, sem):
     cables, time, width = phase_ref.shape
     blocks = width // LANES
     groups = time // SUBLANES
@@ -103,35 +110,16 @@
     for cable in range(cables):
         copy(cable).start()
 
-    lane = lax.broadcasted_iota(jnp.int32, taps_ref.shape, 1)
-    taps = jnp.where(lane == HALF, 1.0, 0.0) - taps_ref[...]
-    reversed_taps = pltpu.roll(backwards(taps * (1.0 / (4.0 * two_pi))), 1, 1)
-    inputs = lax.broadcasted_iota(jnp.int32, (LANES, LANES), 0)
-    outputs = lax.broadcasted_iota(jnp.int32, (LANES, LANES), 1)
-    for cable in range(cables):
-        row = jnp.broadcast_to(reversed_taps[cable : cable + 1, :], (LANES, LANES))
-        circulant = pltpu.roll(row, 0, 1, stride=1, stride_axis=0)
-        for column, mask in enumerate((inputs >= outputs, inputs < outputs)):
-            high, low = split(jnp.where(mask, circulant, 0.0))
-            for place, part in enumerate((high, high, low, low)):
-                rows, lanes = pl.ds(place * LANES, LANES), pl.ds(column * LANES, LANES)
-                weight_ref[cable, rows, lanes] = part
-
     def cable_step(cable, accumulated):
         copy(cable).wait()
 
         def block_step(block, accumulated):
             lanes = pl.ds(pl.multiple_of(block * LANES, LANES), LANES)
-            pieces = []
-            for i in range(groups):
-                rows = pl.ds(i * SUBLANES, SUBLANES)
-                turns = wrap_ref[cable, rows, lanes].astype(jnp.float32)
-                pieces.append(phase_ref[cable, rows, lanes] + two_pi * turns)
-            store_split(high_ref, low_ref, cable, block, pieces)
+            pieces = increments(phase_ref, wrap_ref, cable, lanes)
             totals_ref[pl.ds(block * cables + cable, 1), :] = total(pieces)
             return tuple(a + b for a, b in zip(accumulated, pieces))
 
-        return lax.fori_loop(0, blocks, block_step, accumulated, unroll=4)
+        return lax.fori_loop(0, blocks, block_step, accumulated, unroll=16)
 
     zeros = tuple(jnp.zeros((SUBLANES, LANES), jnp.float32) for _ in range(groups))
     accumulated = scanned(lax.fori_loop(0, cables, cable_step, zeros))
@@ -139,7 +127,8 @@
     tile = jnp.zeros((SUBLANES, LANES), jnp.float32)
     for i, value in enumerate(accumulated):
         tile = jnp.where(lane == i, jnp.sum(value, axis=1, keepdims=True), tile)
-    sums_ref[...] = tile
+    for device in range(sums_ref.shape[0]):
+        sums_ref[device] = tile
 
 
 def halo_kernel(inner_ref, outer_ref, high_ref, low_ref, totals_ref):
@@ -164,20 +153,57 @@
                 totals_ref[pl.ds(block * cables + cable, 1), :] = total(placed)
 
 
-def filter_kernel(first, high_ref, low_ref, halo_high_ref, halo_low_ref, weight_ref, local_ref):
-    _, blocks, time, _ = high_ref.shape
+def filter_kernel(
+    phase_hbm, wrap_hbm, halo_high_ref, halo_low_ref, taps_ref, local_ref, weight_ref,
+    phase_ref, wrap_ref, even_high_ref, even_low_ref, odd_high_ref, odd_low_ref, reversed_ref, sem,
+):
+    cables, time, width = phase_hbm.shape
+    blocks = width // LANES
     groups = time // SUBLANES
+
+    def copies(cable):
+        return (
+            pltpu.make_async_copy(phase_hbm.at[cable], phase_ref.at[cable], sem.at[0, cable]),
+            pltpu.make_async_copy(wrap_hbm.at[cable], wrap_ref.at[cable], sem.at[1, cable]),
+        )
+
+    for cable in range(cables):
+        for copy in copies(cable):
+            copy.start()
+
+    lane = lax.broadcasted_iota(jnp.int32, taps_ref.shape, 1)
+    taps = jnp.where(lane == HALF, 1.0, 0.0) - taps_ref[...]
+    reversed_ref[...] = pltpu.roll(backwards(taps * (1.0 / (4.0 * two_pi))), 1, 1)
+    inputs = lax.broadcasted_iota(jnp.int32, (LANES, LANES), 0)
+    outputs = lax.broadcasted_iota(jnp.int32, (LANES, LANES), 1)
+
+    @pl.loop(0, cables)
+    def _(cable):
+        row = jnp.broadcast_to(reversed_ref[pl.ds(cable, 1), :], (LANES, LANES))
+        circulant = pltpu.roll(row, 0, 1, stride=1, stride_axis=0)
+        for column, mask in enumerate((inputs >= outputs, inputs < outputs)):
+            high, low = split(jnp.where(mask, circulant, 0.0))
+            for place, part in enumerate((high, high, low, low)):
+                rows, lanes = pl.ds(place * LANES, LANES), pl.ds(column * LANES, LANES)
+                weight_ref[cable, rows, lanes] = part
+
     lane = lax.broadcasted_iota(jnp.int32, (time, LANES), 1)
-
-    @pl.loop(0, local_ref.shape[0])
-    def _(index):
-        cable = first + index
+    even, odd = (even_high_ref, even_low_ref), (odd_high_ref, odd_low_ref)
+
+    def prepare(cable, parts):
+        for copy in copies(cable):
+            copy.wait()
+        for block in range(blocks):
+            pieces = increments(phase_ref, wrap_ref, cable, pl.ds(block * LANES, LANES))
+            store_split(*parts, 0, block, pieces)
+
+    def emit(cable, parts):
         high, low = (
             jnp.concatenate(
-                [main[cable].reshape(blocks * time, LANES), halo[cable].reshape(2 * time, LANES)],
+                [main[0].reshape(blocks * time, LANES), halo[cable].reshape(2 * time, LANES)],
                 axis=0,
             )
-            for main, halo in ((high_ref, halo_high_ref), (low_ref, halo_low_ref))
+            for main, halo in zip(parts, (halo_high_ref, halo_low_ref))
         )
         product = jnp.dot(
             jnp.concatenate([high, low, high, low], axis=1),
@@ -201,15 +227,29 @@
             value = jnp.where(lane < HALF, previous, following)
             pieces = [value[i * SUBLANES : (i + 1) * SUBLANES] for i in range(groups)]
             for i, piece in enumerate(scanned(pieces)):
-                local_ref[index, block, pl.ds(i * SUBLANES, SUBLANES), :] = piece
+                local_ref[cable, block, pl.ds(i * SUBLANES, SUBLANES), :] = piece
             previous = following
 
+    prepare(0, even)
+
+    @pl.loop(0, cables // 2 - 1)
+    def _(pair):
+        cable = 2 * pair
+        prepare(cable + 1, odd)
+        emit(cable, even)
+        prepare(cable + 2, even)
+        emit(cable + 1, odd)
+
+    prepare(cables - 1, odd)
+    emit(cables - 2, even)
+    emit(cables - 1, odd)
+
 
 def level_kernel(
-    population, local_refs, weight_ref, totals_refs, sums_ref, earlier_refs, coupling_ref,
+    population, local_ref, weight_ref, totals_refs, sums_ref, coupling_ref,
     out_hbm, stage_ref, offset_ref, sem,
 ):
-    _, blocks, time, _ = local_refs[0].shape
+    _, blocks, time, _ = local_ref.shape
     span = blocks * LANES // CHUNKS
     cables = out_hbm.shape[0]
     groups = time // SUBLANES
@@ -217,15 +257,17 @@
     inside_left = jnp.where(place == 0, 0.0, 1.0)
     inside_right = jnp.where(place == lax.axis_size("chan") - 1, 0.0, 1.0)
 
-    def from_earlier(refs):
-        value = jnp.zeros(refs[0].shape, jnp.float32)
-        for bit, ref in enumerate(refs):
-            value = value + jnp.where((step & (1 << bit)) != 0, ref[...], 0.0)
-        return value
-
-    offset_ref[...] = from_earlier(totals_refs)
-    earlier = from_earlier(earlier_refs)[SUBLANES - 1 :, groups - 1 : groups]
-    common = (sums_ref[...] + earlier) * (1.0 / population)
+    offset = jnp.zeros(offset_ref.shape, jnp.float32)
+    for bit, ref in enumerate(totals_refs):
+        offset = offset + jnp.where((step & (1 << bit)) != 0, ref[...], 0.0)
+    offset_ref[...] = offset
+    common = jnp.zeros((SUBLANES, LANES), jnp.float32)
+    before = jnp.zeros((SUBLANES, LANES), jnp.float32)
+    for number in range(sums_ref.shape[0]):
+        gathered = jnp.sum(sums_ref[number], axis=0)
+        common = common + jnp.where(step == number, gathered, 0.0)
+        before = before + jnp.where(step > number, gathered, 0.0)
+    common = (common + before[SUBLANES - 1 :, groups - 1 : groups]) * (1.0 / population)
     columns = [
         jnp.broadcast_to(common[:, i : i + 1], (SUBLANES, LANES)) for i in range(groups)
     ]
@@ -268,35 +310,31 @@
         )
 
     carry = filtered_offset(0)
-    first_cable = 0
-    for local_ref in local_refs:
-
-        def cable_step(index, carry, first_cable=first_cable, local_ref=local_ref):
-            cable = first_cable + index
-            following = filtered_offset(jnp.minimum(cable + 1, cables - 1))
-            bias, first, middle, last = carry
-            shifts = [coupling_ref[cable] * column for column in columns]
-            inner = [shift * middle for shift in shifts]
-            for block in range(blocks):
-                lanes = pl.ds(block * LANES, LANES)
-                added = jnp.broadcast_to(bias[block : block + 1, :], (SUBLANES, LANES))
-                if block == 0:
-                    slopes = [shift * first for shift in shifts]
-                elif block == blocks - 1:
-                    slopes = [shift * last for shift in shifts]
-                else:
-                    slopes = inner
-                for i in range(groups):
-                    rows = pl.ds(i * SUBLANES, SUBLANES)
-                    stage_ref[cable, rows, lanes] = local_ref[index, block, rows, :] + (
-                        added - slopes[i]
-                    )
-                if (block + 1) % (blocks // CHUNKS) == 0:
-                    written(cable, block // (blocks // CHUNKS)).start()
-            return following
-
-        carry = lax.fori_loop(0, local_ref.shape[0], cable_step, carry)
-        first_cable += local_ref.shape[0]
+
+    def cable_step(cable, carry):
+        following = filtered_offset(jnp.minimum(cable + 1, cables - 1))
+        bias, first, middle, last = carry
+        shifts = [coupling_ref[cable] * column for column in columns]
+        inner = [shift * middle for shift in shifts]
+        for block in range(blocks):
+            lanes = pl.ds(block * LANES, LANES)
+            added = jnp.broadcast_to(bias[block : block + 1, :], (SUBLANES, LANES))
+            if block == 0:
+                slopes = [shift * first for shift in shifts]
+            elif block == blocks - 1:
+                slopes = [shift * last for shift in shifts]
+            else:
+                slopes = inner
+            for i in range(groups):
+                rows = pl.ds(i * SUBLANES, SUBLANES)
+                stage_ref[cable, rows, lanes] = local_ref[cable, block, rows, :] + (
+                    added - slopes[i]
+                )
+            if (block + 1) % (blocks // CHUNKS) == 0:
+                written(cable, block // (blocks // CHUNKS)).start()
+        return following
+
+    lax.fori_loop(0, cables, cable_step, carry)
     for cable in range(cables):
         for chunk in range(CHUNKS):
             written(cable, chunk).wait()
@@ -311,8 +349,6 @@
     blocks = width // LANES
     steps, places = lax.axis_size("tm"), lax.axis_size("chan")
     population = cables * width * places
-    bounds = [0, cables // 2, 3 * cables // 4, cables]
-    parts = len(bounds) - 1
     wrap_count = pltpu.with_memory_space_constraint(wrap_count, pltpu.HBM)
     whole = pl.BlockSpec(memory_space=pltpu.VMEM)
     outside = pl.BlockSpec(memory_space=pl.ANY)
@@ -335,17 +371,14 @@
     outer = lax.ppermute(outer, "chan", outer_pairs)
     inner = swapped(inner, "chan", 1)
 
-    high, low, totals, sums, weight = pl.pallas_call(
-        increments_kernel,
+    totals, sums = pl.pallas_call(
+        totals_kernel,
         out_shape=(
-            pltpu.VMEM((cables, blocks, time, LANES), jnp.bfloat16),
-            pltpu.VMEM((cables, blocks, time, LANES), jnp.bfloat16),
             pltpu.VMEM((blocks * cables, LANES), jnp.float32),
-            pltpu.VMEM((SUBLANES, LANES), jnp.float32),
-            pltpu.VMEM((cables, 4 * LANES, 2 * LANES), jnp.bfloat16),
+            jax.ShapeDtypeStruct((steps * places, SUBLANES, LANES), jnp.float32),
         ),
-        in_specs=[whole, outside, whole],
-        out_specs=[whole] * 5,
+        in_specs=[whole, outside],
+        out_specs=[whole] * 2,
         scratch_shapes=[
             pltpu.VMEM((cables, time, width), jnp.int32),
             pltpu.SemaphoreType.DMA((cables,)),
@@ -354,8 +387,8 @@
         cost_estimate=pl.CostEstimate(
             flops=0, bytes_accessed=phase_step.size * 4, transcendentals=0
         ),
-        name="increments",
-    )(pltpu.with_memory_space_constraint(phase_step, pltpu.VMEM), wrap_count, filter_taps)
+        name="totals",
+    )(pltpu.with_memory_space_constraint(phase_step, pltpu.VMEM), wrap_count)
 
     halo_high, halo_low, halo_totals = pl.pallas_call(
         halo_kernel,
@@ -370,59 +403,52 @@
         name="halo",
     )(inner, outer)
 
-    def filtered(part, weight):
-        share = bounds[part + 1] - bounds[part]
-        return pl.pallas_call(
-            functools.partial(filter_kernel, bounds[part]),
-            out_shape=pltpu.VMEM((share, blocks, time, LANES), jnp.float32),
-            in_specs=[whole] * 5,
-            out_specs=whole,
-            compiler_params=pltpu.CompilerParams(vmem_limit_bytes=16 << 20),
-            cost_estimate=pl.CostEstimate(
-                flops=2 * share * (blocks + 2) * time * 8 * LANES * LANES,
-                bytes_accessed=1 << 20,
-                transcendentals=0,
-            ),
-            name="filter",
-        )(high, low, halo_high, halo_low, weight)
-
     running = jnp.concatenate([totals, halo_totals], axis=0)
     received = [swapped(running, "tm", 1)]
     sums, halo_totals = lax.optimization_barrier((sums, halo_totals))
-    rounds = [("chan", 1 << bit) for bit in range(places.bit_length() - 1)]
-    rounds += [("tm", 1 << bit) for bit in range(steps.bit_length() - 1)]
-    local, received_sums, chan_sums, ready = [], [], sums, None
-    for number, (axis, bit) in enumerate(rounds):
-        incoming = swapped(sums, axis, bit)
-        if number % 2 == 0 and number > 0 and ready is not None:
-            received.append(swapped(ready, "tm", 1 << len(received)))
-            ready = None
-        elif number > 0 and len(local) < parts:
-            tied, sums = lax.optimization_barrier((weight, sums))
-            part = filtered(len(local), tied)
-            incoming, part = lax.optimization_barrier((incoming, part))
-            local.append(part)
-        if number % 2 == 1 and 1 << len(received) < steps:
-            running = running + received[-1]
-            ready, incoming = lax.optimization_barrier((running, incoming))
-        if axis == "tm":
-            received_sums.append(incoming)
-        sums = sums + incoming
-        if axis == "chan":
-            chan_sums = sums
-    while 1 << len(received) < steps:
-        running = running + received[-1] if ready is None else ready
-        ready = None
-        received.append(swapped(running, "tm", 1 << len(received)))
-    while len(local) < parts:
-        local.append(filtered(len(local), weight))
+    gathered = lax.all_to_all(sums, ("tm", "chan"), 0, 0, tiled=True)
+    gathered = gathered.reshape(steps, places, SUBLANES, LANES)
+    for bit in range(1, steps.bit_length() - 1):
+        running = running + received[-1]
+        running, gathered = lax.optimization_barrier((running, gathered))
+        received.append(swapped(running, "tm", 1 << bit))
+    tied, gathered = lax.optimization_barrier((filter_taps, gathered))
+    local, weight = pl.pallas_call(
+        filter_kernel,
+        out_shape=(
+            pltpu.VMEM((cables, blocks, time, LANES), jnp.float32),
+            pltpu.VMEM((cables, 4 * LANES, 2 * LANES), jnp.bfloat16),
+        ),
+        in_specs=[outside] * 2 + [whole] * 3,
+        out_specs=[whole] * 2,
+        scratch_shapes=[
+            pltpu.VMEM((cables, time, width), jnp.float32),
+            pltpu.VMEM((cables, time, width), jnp.int32),
+        ]
+        + [pltpu.VMEM((1, blocks, time, LANES), jnp.bfloat16)] * 4
+        + [
+            pltpu.VMEM(filter_taps.shape, jnp.float32),
+            pltpu.SemaphoreType.DMA((2, cables)),
+        ],
+        compiler_params=pltpu.CompilerParams(vmem_limit_bytes=32 << 20),
+        cost_estimate=pl.CostEstimate(
+            flops=2 * cables * (blocks + 2) * time * 8 * LANES * LANES,
+            bytes_accessed=2 * phase_step.size * 4,
+            transcendentals=0,
+        ),
+        name="filter",
+    )(
+        pltpu.with_memory_space_constraint(phase_step, pltpu.HBM),
+        wrap_count,
+        halo_high,
+        halo_low,
+        tied,
+    )
 
     return pl.pallas_call(
         functools.partial(level_kernel, population),
         out_shape=jax.ShapeDtypeStruct(phase_step.shape, jnp.float32),
-        in_specs=[
-            [whole] * parts, whole, [whole] * len(received), whole, [whole] * len(received), scalars
-        ],
+        in_specs=[whole, whole, [whole] * len(received), whole, scalars],
         out_specs=outside,
         scratch_shapes=[
             pltpu.VMEM((cables, time, width), jnp.float32),
@@ -431,7 +457,7 @@
         ],
         compiler_params=pltpu.CompilerParams(vmem_limit_bytes=24 << 20),
         name="level",
-    )(local, weight, received, chan_sums, received_sums, coupling)
+    )(local, weight, received, gathered, coupling)
 
 
 def solution(mesh):

time: 34.3 us -> 43.7 us (1.27)
  Pallas kernels: 18.2 us -> 23.6 us
  waiting for transfers between devices: 1.57 us -> 6.39 us
  starting transfers between devices: 14.2 us -> 13.4 us
    ppermute x8 -> x3, starting transfers between devices: 10.6 us -> 4.55 us  [swapped(): lax.ppermute(value, axis, [(i, i ^ bit) for i in range(lax.axis_size(axis...]
    pallas_call x4 -> x2, Pallas kernels: 12 us -> 17.6 us  [the longest x1 13 us: shards(): pl.pallas_call(filter_kernel, out_shape=(pltpu.VMEM((cables, blocks, time...]
    all_to_all x0 -> x1, starting transfers between devices: none -> 5.34 us  [shards(): gathered = lax.all_to_all(sums, ('tm', 'chan'), 0, 0, tiled=True)]
    ppermute x8 -> x3, waiting for transfers between devices: 1.57 us -> 6.09 us  [swapped(): lax.ppermute(value, axis, [(i, i ^ bit) for i in range(lax.axis_size(axis...]
  transfers between devices with their start and end apart: 9 -> 5, of which waited for: 3 -> 2; matrix products, arithmetic and copies ran while one was open for 0% -> 0% of each run, Pallas kernels for 35% -> 40%
where the time goes in v11:
time: 43.7 us; the launch traced here: 43.5 us
  Pallas kernels  23.6 us (54%)
  starting transfers between devices  13.4 us (31%)
  waiting for transfers between devices  6.39 us (15%)
    pallas_call x1, Pallas kernels, shards(): pl.pallas_call(filter_kernel, out_shape=(pltpu.VMEM((cables, blocks, time...  13 us
    ppermute x3, waiting for transfers between devices, swapped(): lax.ppermute(value, axis, [(i, i ^ bit) for i in range(lax.axis_size(axis...  6.09 us
    all_to_all x1, starting transfers between devices, shards(): gathered = lax.all_to_all(sums, ('tm', 'chan'), 0, 0, tiled=True)  5.34 us
    ppermute x3, starting transfers between devices, swapped(): lax.ppermute(value, axis, [(i, i ^ bit) for i in range(lax.axis_size(axis...  4.55 us
    pallas_call x1, Pallas kernels, shards(): pl.pallas_call(totals_kernel, out_shape=(pltpu.VMEM((blocks * cables, LAN...  4.53 us
    pallas_call x1, Pallas kernels, shards(): pl.pallas_call(functools.partial(level_kernel, population), out_shape=jax...  4.27 us
    ppermute x1, starting transfers between devices, shards(): outer = lax.ppermute(outer, 'chan', outer_pairs)  3.56 us
    pallas_call x1, Pallas kernels, shards(): pl.pallas_call(edges_kernel, out_shape=[pltpu.VMEM((cables // 2, time, LA...  1.59 us
  transfers between devices with their start and end apart: 5, of which 2 were waited for; matrix products, arithmetic and copies ran while one was open for 0% of the time, Pallas kernels for 40%

profile of v11, /device:TPU:0, one launch (start us, length us, event | category | flops | bytes accessed | tf_op | source)
XLA Modules:
  0.0 43.5 jit_solution(16931310420242586948)
XLA Ops:
  0.0 0.0 copy-start
  0.0 1.6 %edges.1 = (f32[4,64,128]{2,1,0:T(8,128)S(1)}, f32[4,64,128]{2,1,0:T(8,128)S(1)}) custom-call(f32[8,64,4096]{2,1,0:T(8,128)} %phase_hbm.3, s32[8,64,4096]{2,1,0:T(8,128)} %wrap_hbm.5), custom_call_target="tpu_custom_call" | custom-call | tf_op jit(solution)/shard_map/edges/pallas_call | solution.py:357
  1.6 0.5 %collective-permute-start = (f32[4,64,128]{2,1,0:T(8,128)S(1)}, f32[4,64,128]{2,1,0:T(8,128)S(1)}, u32[]{:S(2)}, u32[]{:S(2)}) collective-permute-start(f32[4,64,128]{2,1,0:T(8,128)S(1)} %get-tuple-element.19), channel_id=1, source_target_pairs={{0,1},{1,0},{2,3},{3,2},{4,5},{5,4},{6,7},{7,6},{8,9},{9,8},{10,11... | collective-permute-start | bytes 393224 | tf_op jit(solution)/shard_map/ppermute | solution.py:344
  2.1 0.0 copy-start.1
  2.1 3.6 %collective-permute-start.1 = (f32[4,64,128]{2,1,0:T(8,128)S(1)}, f32[4,64,128]{2,1,0:T(8,128)S(1)}, u32[]{:S(2)}, u32[]{:S(2)}) collective-permute-start(f32[4,64,128]{2,1,0:T(8,128)S(1)} %get-tuple-element.20), channel_id=1, source_target_pairs={{0,7},{1,2},{2,1},{3,4},{4,3},{5,6},{6,5},{7,0},{8,15},{9,10},{10,... | collective-permute-start | bytes 393224 | tf_op jit(solution)/shard_map/ppermute | solution.py:371
  5.7 0.0 copy-done
  5.7 4.5 %totals.1 = (f32[256,128]{1,0:T(8,128)S(1)}, f32[32,8,128]{2,1,0:T(8,128)}) custom-call(f32[8,64,4096]{2,1,0:T(8,128)S(1)} %copy-done, s32[8,64,4096]{2,1,0:T(8,128)} %wrap_hbm.5), custom_call_target="tpu_custom_call" | custom-call | bytes 8388608 | tf_op jit(solution)/shard_map/totals/pallas_call | solution.py:374
  10.2 0.0 collective-permute-done.inner_ref
  10.2 0.0 collective-permute-done.1.outer_ref
  10.2 0.2 halo.1
  10.4 5.3 %all-to-all-start = ((f32[32,8,128]{2,1,0:T(8,128)}), f32[32,8,128]{2,1,0:T(8,128)S(1)}, u32[]{:S(2)}, u32[]{:S(2)}) async-start(f32[32,8,128]{2,1,0:T(8,128)} %get-tuple-element.26), calls=%async_computation | async-start | bytes 262144 | tf_op jit(solution)/shard_map/all_to_all | solution.py:409
  15.8 1.8 %collective-permute-start.2 = (f32[272,128]{1,0:T(8,128)S(1)}, f32[272,128]{1,0:T(8,128)S(1)}, u32[]{:S(2)}, u32[]{:S(2)}) collective-permute-start(f32[272,128]{1,0:T(8,128)S(1)} %constant_dynamic-update-slice_fusion), channel_id=1, source_target_pairs={{0,8},{8,0},{16,24},{24,16},{1,9},{9,1},{17,25},{25,17},{2,10},{10... | collective-permute-start | bytes 417800 | tf_op jit(solution)/shard_map/ppermute | solution.py:344
  17.6 6.1 %collective-permute-done.2.totals_refs_0_ = f32[272,128]{1,0:T(8,128)S(1)} collective-permute-done((f32[272,128]{1,0:T(8,128)S(1)}, f32[272,128]{1,0:T(8,128)S(1)}, u32[]{:S(2)}, u32[]{:S(2)}) %collective-permute-start.2) | collective-permute-done | bytes 139296 | tf_op jit(solution)/shard_map/ppermute | solution.py:344
  23.7 0.3 all-to-all-done
  24.0 2.2 %collective-permute-start.3 = (f32[272,128]{1,0:T(8,128)S(1)}, f32[272,128]{1,0:T(8,128)S(1)}, u32[]{:S(2)}, u32[]{:S(2)}) collective-permute-start(f32[272,128]{1,0:T(8,128)S(1)} %add.3), channel_id=1, source_target_pairs={{0,16},{8,24},{16,0},{24,8},{1,17},{9,25},{17,1},{25,9},{2,18},{10... | collective-permute-start | bytes 417800 | tf_op jit(solution)/shard_map/ppermute | solution.py:344
  26.2 0.0 copy-done.1
  26.2 0.0 copy-start.2
  26.2 13.0 %filter.1 = (f32[8,32,64,128]{3,2,1,0:T(8,128)S(1)}, bf16[8,512,256]{2,1,0:T(8,128)(2,1)S(1)}) custom-call(f32[8,64,4096]{2,1,0:T(8,128)} %phase_hbm.3, s32[8,64,4096]{2,1,0:T(8,128)} %wrap_hbm.5, bf16[8,2,64,128]{3,2,1,0:T(8,128)(2,1)S(1)} %get-tuple-element.21.halo_high_ref, bf16[8,2,64,128]{3,2,1,0:T(8,128)(2,1)S(1)} %get-tuple-element.22.halo_low_ref, ...), custom_call_target="tpu_custom_call" | custom-call | flops 4563402752 | bytes 16777216 | tf_op jit(solution)/shard_map/filter/pallas_call | solution.py:416
  39.3 0.0 collective-permute-done.3.totals_refs_1_
  39.3 0.0 copy-done.2
  39.3 4.3 %level.1 = f32[8,64,4096]{2,1,0:T(8,128)} custom-call(f32[8,32,64,128]{3,2,1,0:T(8,128)S(1)} %get-tuple-element.29.local_ref, bf16[8,512,256]{2,1,0:T(8,128)(2,1)S(1)} %get-tuple-element.30.weight_ref, f32[272,128]{1,0:T(8,128)S(1)} %collective-permute-done.2.totals_refs_0_, f32[272,128]{1,0:T(8,128)S(1)} %collective-permute-done.3.totals_refs_1_, ...), custom_call_target="tpu_custom_call" | custom-call | tf_op jit(solution)/shard_map/level/pallas_call | solution.py:448
  (3 shorter events, 0.0 us)
Async XLA Ops:
  0.0 5.7 %copy-start = (f32[8,64,4096]{2,1,0:T(8,128)S(1)}, f32[8,64,4096]{2,1,0:T(8,128)}, u32[]{:S(2)}) copy-start(f32[8,64,4096]{2,1,0:T(8,128)} %phase_hbm.3) | copy-start | bytes 25165828
  1.6 8.6 %collective-permute-start = (f32[4,64,128]{2,1,0:T(8,128)S(1)}, f32[4,64,128]{2,1,0:T(8,128)S(1)}, u32[]{:S(2)}, u32[]{:S(2)}) collective-permute-start(f32[4,64,128]{2,1,0:T(8,128)S(1)} %get-tuple-element.19), channel_id=1, source_target_pairs={{0,1},{1,0},{2,3},{3,2},{4,5},{5,4},{6,7},{7,6},{8,9},{9,8},{10,11... | collective-permute-start | bytes 393224 | tf_op jit(solution)/shard_map/ppermute | solution.py:344
  2.1 24.1 %copy-start.1 = (f32[8,128]{1,0:T(8,128)S(1)}, f32[8,128]{1,0:T(8,128)}, u32[]{:S(2)}) copy-start(f32[8,128]{1,0:T(8,128)} %taps_ref) | copy-start | bytes 12292
  2.1 8.1 %collective-permute-start.1 = (f32[4,64,128]{2,1,0:T(8,128)S(1)}, f32[4,64,128]{2,1,0:T(8,128)S(1)}, u32[]{:S(2)}, u32[]{:S(2)}) collective-permute-start(f32[4,64,128]{2,1,0:T(8,128)S(1)} %get-tuple-element.20), channel_id=1, source_target_pairs={{0,7},{1,2},{2,1},{3,4},{4,3},{5,6},{6,5},{7,0},{8,15},{9,10},{10,... | collective-permute-start | bytes 393224 | tf_op jit(solution)/shard_map/ppermute | solution.py:371
  10.4 13.6 %all-to-all-start = ((f32[32,8,128]{2,1,0:T(8,128)}), f32[32,8,128]{2,1,0:T(8,128)S(1)}, u32[]{:S(2)}, u32[]{:S(2)}) async-start(f32[32,8,128]{2,1,0:T(8,128)} %get-tuple-element.26), calls=%async_computation | async-start | bytes 262144 | tf_op jit(solution)/shard_map/all_to_all | solution.py:409
  15.8 7.9 %collective-permute-start.2 = (f32[272,128]{1,0:T(8,128)S(1)}, f32[272,128]{1,0:T(8,128)S(1)}, u32[]{:S(2)}, u32[]{:S(2)}) collective-permute-start(f32[272,128]{1,0:T(8,128)S(1)} %constant_dynamic-update-slice_fusion), channel_id=1, source_target_pairs={{0,8},{8,0},{16,24},{24,16},{1,9},{9,1},{17,25},{25,17},{2,10},{10... | collective-permute-start | bytes 417800 | tf_op jit(solution)/shard_map/ppermute | solution.py:344
  24.0 15.2 %collective-permute-start.3 = (f32[272,128]{1,0:T(8,128)S(1)}, f32[272,128]{1,0:T(8,128)S(1)}, u32[]{:S(2)}, u32[]{:S(2)}) collective-permute-start(f32[272,128]{1,0:T(8,128)S(1)} %add.3), channel_id=1, source_target_pairs={{0,16},{8,24},{16,0},{24,8},{1,17},{9,25},{17,1},{25,9},{2,18},{10... | collective-permute-start | bytes 417800 | tf_op jit(solution)/shard_map/ppermute | solution.py:344
  26.2 13.1 %copy-start.2 = (f32[8]{0:T(128)S(1)}, f32[8]{0:T(128)}, u32[]{:S(2)}) copy-start(f32[8]{0:T(128)} %coupling_ref.1) | copy-start | bytes 100

commit v12 on v10

--- a/solution.py
+++ b/solution.py
@@ -208,36 +208,21 @@
             previous = following
 
 
-def level_kernel(
-    population, local_refs, weight_ref, totals_refs, sums_ref, earlier_refs, coupling_ref,
-    out_hbm, stage_ref, offset_ref, sem,
-):
-    _, blocks, time, _ = local_refs[0].shape
-    span = blocks * LANES // CHUNKS
-    cables = out_hbm.shape[0]
-    groups = time // SUBLANES
+def bias_kernel(weight_ref, totals_refs, bias_ref, slope_ref, offset_ref):
+    cables, blocks, _ = bias_ref.shape
     step, place = lax.axis_index("tm"), lax.axis_index("chan")
     inside_left = jnp.where(place == 0, 0.0, 1.0)
     inside_right = jnp.where(place == lax.axis_size("chan") - 1, 0.0, 1.0)
-
-    def from_earlier(refs):
-        value = jnp.zeros(refs[0].shape, jnp.float32)
-        for bit, ref in enumerate(refs):
-            value = value + jnp.where((step & (1 << bit)) != 0, ref[...], 0.0)
-        return value
-
-    offset_ref[...] = from_earlier(totals_refs)
-    earlier = from_earlier(earlier_refs)[SUBLANES - 1 :, groups - 1 : groups]
-    common = (sums_ref[...] + earlier) * (1.0 / population)
-    columns = [
-        jnp.broadcast_to(common[:, i : i + 1], (SUBLANES, LANES)) for i in range(groups)
-    ]
+    offset = jnp.zeros(offset_ref.shape, jnp.float32)
+    for bit, ref in enumerate(totals_refs):
+        offset = offset + jnp.where((step & (1 << bit)) != 0, ref[...], 0.0)
+    offset_ref[...] = offset
     used = blocks + 2
     padded = -(-(used + 1) // SUBLANES) * SUBLANES
     row = lax.broadcasted_iota(jnp.int32, (padded, LANES), 0)
     lane = lax.broadcasted_iota(jnp.int32, (padded, LANES), 1)
 
-    def filtered_offset(cable):
+    def cable_step(cable, carry):
         offset = jnp.concatenate(
             [
                 offset_ref[pl.ds(cable, used, stride=cables), :],
@@ -255,50 +240,67 @@
         left = pltpu.roll(here[used - 1 : used] + there[:1], HALF, 1)
         following = pltpu.roll(here + pltpu.roll(there, padded - 1, 0), HALF, 1)
         previous = jnp.where(row == 0, left, pltpu.roll(following, 1, 0))
-        bias = jnp.where(lane < HALF, previous, following)
+        bias_ref[cable] = jnp.where(lane < HALF, previous, following)[:blocks]
         here, there = here[used : used + 1], there[used : used + 1]
         middle = pltpu.roll(here + there, HALF, 1)
         first = pltpu.roll(here * inside_left + there, HALF, 1)
         last = pltpu.roll(here + there * inside_right, HALF, 1)
-        first = jnp.where(lane[:1] < HALF, first, middle)
-        last = jnp.where(lane[:1] < HALF, middle, last)
-        return bias, first, middle, last
+        previous = jnp.where(row == 0, first, middle)
+        following = jnp.where(row == blocks - 1, last, middle)
+        slope_ref[cable] = jnp.where(lane < HALF, previous, following)[:blocks]
+        return carry
+
+    lax.fori_loop(0, cables, cable_step, 0, unroll=4)
+
+
+def level_kernel(
+    population, local_refs, bias_ref, slope_ref, sums_ref, earlier_refs, coupling_ref,
+    out_hbm, stage_ref, sem,
+):
+    _, blocks, time, _ = local_refs[0].shape
+    span = blocks // CHUNKS
+    cables = out_hbm.shape[0]
+    groups = time // SUBLANES
+    step = lax.axis_index("tm")
+    before = jnp.zeros((SUBLANES, LANES), jnp.float32)
+    for bit, ref in enumerate(earlier_refs):
+        before = before + jnp.where((step & (1 << bit)) != 0, ref[...], 0.0)
+    common = sums_ref[...] + before[SUBLANES - 1 :, groups - 1 : groups]
+    common = common * (1.0 / population)
+    columns = [
+        jnp.broadcast_to(common[:, i : i + 1], (SUBLANES, LANES)) for i in range(groups)
+    ]
 
     def written(cable, chunk):
-        lanes = pl.ds(chunk * span, span)
+        lanes = pl.ds(chunk * span * LANES, span * LANES)
         return pltpu.make_async_copy(
             stage_ref.at[cable, :, lanes], out_hbm.at[cable, :, lanes], sem.at[cable, chunk]
         )
 
-    carry = filtered_offset(0)
     first_cable = 0
     for local_ref in local_refs:
 
         def cable_step(index, carry, first_cable=first_cable, local_ref=local_ref):
             cable = first_cable + index
-            following = filtered_offset(jnp.minimum(cable + 1, cables - 1))
-            bias, first, middle, last = carry
             shifts = [coupling_ref[cable] * column for column in columns]
-            inner = [shift * middle for shift in shifts]
-            for block in range(blocks):
-                lanes = pl.ds(block * LANES, LANES)
-                added = jnp.broadcast_to(bias[block : block + 1, :], (SUBLANES, LANES))
-                if block == 0:
-                    slopes = [shift * first for shift in shifts]
-                elif block == blocks - 1:
-                    slopes = [shift * last for shift in shifts]
-                else:
-                    slopes = inner
+
+            def block_step(block, carry):
+                lanes = pl.ds(pl.multiple_of(block * LANES, LANES), LANES)
+                bias = jnp.broadcast_to(bias_ref[cable, pl.ds(block, 1), :], (SUBLANES, LANES))
+                slope = jnp.broadcast_to(slope_ref[cable, pl.ds(block, 1), :], (SUBLANES, LANES))
                 for i in range(groups):
                     rows = pl.ds(i * SUBLANES, SUBLANES)
                     stage_ref[cable, rows, lanes] = local_ref[index, block, rows, :] + (
-                        added - slopes[i]
+                        bias - shifts[i] * slope
                     )
-                if (block + 1) % (blocks // CHUNKS) == 0:
-                    written(cable, block // (blocks // CHUNKS)).start()
-            return following
-
-        carry = lax.fori_loop(0, local_ref.shape[0], cable_step, carry)
+                return carry
+
+            for chunk in range(CHUNKS):
+                lax.fori_loop(chunk * span, (chunk + 1) * span, block_step, 0, unroll=8)
+                written(cable, chunk).start()
+            return carry
+
+        lax.fori_loop(0, local_ref.shape[0], cable_step, 0)
         first_cable += local_ref.shape[0]
     for cable in range(cables):
         for chunk in range(CHUNKS):
@@ -314,7 +316,7 @@
     blocks = width // LANES
     steps, places = lax.axis_size("tm"), lax.axis_size("chan")
     population = cables * width * places
-    bounds = [0, cables // 2, 3 * cables // 4, cables]
+    bounds = [0, 3 * cables // 8, 5 * cables // 8, 7 * cables // 8, cables]
     parts = len(bounds) - 1
     wrap_count = pltpu.with_memory_space_constraint(wrap_count, pltpu.HBM)
     whole = pl.BlockSpec(memory_space=pltpu.VMEM)
@@ -334,8 +336,7 @@
         compiler_params=pltpu.CompilerParams(vmem_limit_bytes=8 << 20),
         name="edges",
     )(pltpu.with_memory_space_constraint(phase_step, pltpu.HBM), wrap_count)
-    last = places - 1
-    outer_pairs = [(0, 0), (last, last)] + [(i, i + (1 if i % 2 else -1)) for i in range(1, last)]
+    outer_pairs = [(i, (i + (1 if i % 2 else -1)) % places) for i in range(places)]
     outer = lax.ppermute(outer, "chan", outer_pairs)
     inner = swapped(inner, "chan", 1)
 
@@ -391,25 +392,39 @@
             name="filter",
         )(high, low, halo_high, halo_low, weight)
 
+    def biased(received):
+        return pl.pallas_call(
+            bias_kernel,
+            out_shape=[pltpu.VMEM((cables, blocks, LANES), jnp.float32)] * 2,
+            in_specs=[whole, [whole] * len(received)],
+            out_specs=[whole] * 2,
+            scratch_shapes=[pltpu.VMEM(received[0].shape, jnp.float32)],
+            compiler_params=pltpu.CompilerParams(vmem_limit_bytes=8 << 20),
+            cost_estimate=pl.CostEstimate(flops=0, bytes_accessed=2 << 20, transcendentals=0),
+            name="bias",
+        )(weight, received)
+
     running = jnp.concatenate([totals, halo_totals], axis=0)
     received = [swapped(running, "tm", 1)]
     sums, halo_totals = lax.optimization_barrier((sums, halo_totals))
     rounds = [("chan", 1 << bit) for bit in range(places.bit_length() - 1)]
     rounds += [("tm", 1 << bit) for bit in range(steps.bit_length() - 1)]
-    local, received_sums, chan_sums, ready = [], [], sums, None
+    local, received_sums, chan_sums, ready, rows = [], [], sums, None, None
     for number, (axis, bit) in enumerate(rounds):
         incoming = swapped(sums, axis, bit)
         if number % 2 == 0 and number > 0 and ready is not None:
             received.append(swapped(ready, "tm", 1 << len(received)))
             ready = None
-        elif number > 0 and len(local) < parts:
+        if number > 0 and len(local) < parts:
             tied, sums = lax.optimization_barrier((weight, sums))
+            if len(local) == parts - 1 and 1 << len(received) >= steps:
+                rows, tied = lax.optimization_barrier((biased(received), tied))
             part = filtered(len(local), tied)
             incoming, part = lax.optimization_barrier((incoming, part))
             local.append(part)
         if number % 2 == 1 and 1 << len(received) < steps:
-            running = running + received[-1]
-            ready, incoming = lax.optimization_barrier((running, incoming))
+            earlier, local[-1] = lax.optimization_barrier((received[-1], local[-1]))
+            ready = running = running + earlier
         if axis == "tm":
             received_sums.append(incoming)
         sums = sums + incoming
@@ -421,22 +436,20 @@
         received.append(swapped(running, "tm", 1 << len(received)))
     while len(local) < parts:
         local.append(filtered(len(local), weight))
+    bias, slope = biased(received) if rows is None else rows
 
     return pl.pallas_call(
         functools.partial(level_kernel, population),
         out_shape=jax.ShapeDtypeStruct(phase_step.shape, jnp.float32),
-        in_specs=[
-            [whole] * parts, whole, [whole] * len(received), whole, [whole] * len(received), scalars
-        ],
+        in_specs=[[whole] * parts, whole, whole, whole, [whole] * len(received_sums), scalars],
         out_specs=outside,
         scratch_shapes=[
             pltpu.VMEM((cables, time, width), jnp.float32),
-            pltpu.VMEM(((blocks + 2) * cables, LANES), jnp.float32),
             pltpu.SemaphoreType.DMA((cables, CHUNKS)),
         ],
         compiler_params=pltpu.CompilerParams(vmem_limit_bytes=24 << 20),
         name="level",
-    )(local, weight, received, chan_sums, received_sums, coupling)
+    )(local, bias, slope, chan_sums, received_sums, coupling)
 
 
 def solution(mesh):

time: 34.8 us -> 34.3 us (0.986)
  starting transfers between devices: 15.9 us -> 12.2 us
  waiting for transfers between devices: 0.88 us -> 4.06 us
  Pallas kernels: 16.8 us -> 17.6 us
  local copies, waits for them, and re-layouts: 0.83 us -> 0.03 us
    ppermute x8, starting transfers between devices: 15.1 us -> 8.69 us  [swapped(): lax.ppermute(value, axis, [(i, i ^ bit) for i in range(lax.axis_size(axis...]
    ppermute x8, waiting for transfers between devices: 0.88 us -> 4.06 us  [swapped(): lax.ppermute(value, axis, [(i, i ^ bit) for i in range(lax.axis_size(axis...]
    ppermute x1, starting transfers between devices: 0.79 us -> 3.56 us  [shards(): outer = lax.ppermute(outer, 'chan', outer_pairs)]
    unnamed x7, local copies, waits for them, and re-layouts: 0.82 us -> 0.02 us
    pallas_call x0 -> x1, Pallas kernels: none -> 0.78 us  [biased(): pl.pallas_call(bias_kernel, out_shape=[pltpu.VMEM((cables, blocks, LANES)...]
    pallas_call x3 -> x4, Pallas kernels: 6.63 us -> 6.61 us  [filtered(): pl.pallas_call(functools.partial(filter_kernel, bounds[part]), out_shape=...]
  transfers between devices with their start and end apart: 9 -> 9, of which waited for: 3 -> 3; matrix products, arithmetic and copies ran while one was open for 0% -> 0% of each run, Pallas kernels for 31% -> 34%
where the time goes in v12:
time: 34.3 us; the launch traced here: 34.1 us
  Pallas kernels  17.6 us (51%)
  starting transfers between devices  12.2 us (36%)
  waiting for transfers between devices  4.06 us (12%)
    ppermute x8, starting transfers between devices, swapped(): lax.ppermute(value, axis, [(i, i ^ bit) for i in range(lax.axis_size(axis...  8.69 us
    pallas_call x4, Pallas kernels, filtered(): pl.pallas_call(functools.partial(filter_kernel, bounds[part]), out_shape=...  6.61 us
    pallas_call x1, Pallas kernels, shards(): pl.pallas_call(functools.partial(level_kernel, population), out_shape=jax...  4.25 us
    pallas_call x1, Pallas kernels, shards(): pl.pallas_call(increments_kernel, out_shape=(pltpu.VMEM((cables, blocks,...  4.21 us
    ppermute x8, waiting for transfers between devices, swapped(): lax.ppermute(value, axis, [(i, i ^ bit) for i in range(lax.axis_size(axis...  4.06 us
    ppermute x1, starting transfers between devices, shards(): outer = lax.ppermute(outer, 'chan', outer_pairs)  3.56 us
    pallas_call x1, Pallas kernels, shards(): pl.pallas_call(edges_kernel, out_shape=[pltpu.VMEM((cables // 2, time, LA...  1.59 us
    pallas_call x1, Pallas kernels, biased(): pl.pallas_call(bias_kernel, out_shape=[pltpu.VMEM((cables, blocks, LANES)...  0.78 us
  transfers between devices with their start and end apart: 9, of which 3 were waited for; matrix products, arithmetic and copies ran while one was open for 0% of the time, Pallas kernels for 34%

profile of v12, /device:TPU:0, one launch (start us, length us, event | category | flops | bytes accessed | tf_op | source)
XLA Modules:
  0.0 34.1 jit_solution(8189800926750180885)
XLA Ops:
  0.0 1.6 %edges.1 = (f32[4,64,128]{2,1,0:T(8,128)S(1)}, f32[4,64,128]{2,1,0:T(8,128)S(1)}) custom-call(f32[8,64,4096]{2,1,0:T(8,128)} %phase_hbm.1, s32[8,64,4096]{2,1,0:T(8,128)} %wrap_hbm.3), custom_call_target="tpu_custom_call" | custom-call | tf_op jit(solution)/shard_map/edges/pallas_call | solution.py:326
  1.6 0.5 %collective-permute-start = (f32[4,64,128]{2,1,0:T(8,128)S(1)}, f32[4,64,128]{2,1,0:T(8,128)S(1)}, u32[]{:S(2)}, u32[]{:S(2)}) collective-permute-start(f32[4,64,128]{2,1,0:T(8,128)S(1)} %get-tuple-element.39), channel_id=1, source_target_pairs={{0,1},{1,0},{2,3},{3,2},{4,5},{5,4},{6,7},{7,6},{8,9},{9,8},{10,11... | collective-permute-start | bytes 393224 | tf_op jit(solution)/shard_map/ppermute | solution.py:311
  2.1 3.6 %collective-permute-start.1 = (f32[4,64,128]{2,1,0:T(8,128)S(1)}, f32[4,64,128]{2,1,0:T(8,128)S(1)}, u32[]{:S(2)}, u32[]{:S(2)}) collective-permute-start(f32[4,64,128]{2,1,0:T(8,128)S(1)} %get-tuple-element.40), channel_id=1, source_target_pairs={{0,7},{1,2},{2,1},{3,4},{4,3},{5,6},{6,5},{7,0},{8,15},{9,10},{10,... | collective-permute-start | bytes 393224 | tf_op jit(solution)/shard_map/ppermute | solution.py:340
  5.7 4.2 %increments.1 = (bf16[8,32,64,128]{3,2,1,0:T(8,128)(2,1)S(1)}, bf16[8,32,64,128]{3,2,1,0:T(8,128)(2,1)S(1)}, f32[256,128]{1,0:T(8,128)S(1)}, f32[8,128]{1,0:T(8,128)S(1)}, bf16[8,512,256]{2,1,0:T(8,128)(2,1)S(1)}) custom-call(f32[8,64,4096]{2,1,0:T(8,128)S(1)} %copy-done, s32[8,64,4096]{2,1,0:T(8,128)} %wrap_hbm.3, f32[8,128]{1,0:T(8,128)S(1)} %copy-done.1), custom_call_target="tpu_custom_call" | custom-call | bytes 8388608 | tf_op jit(solution)/shard_map/increments/pallas_call | solution.py:343
  9.9 0.2 halo.1
  10.1 0.1 collective-permute-start.3
  10.2 1.6 %collective-permute-start.2 = (f32[272,128]{1,0:T(8,128)S(1)}, f32[272,128]{1,0:T(8,128)S(1)}, u32[]{:S(2)}, u32[]{:S(2)}) collective-permute-start(f32[272,128]{1,0:T(8,128)S(1)} %constant_dynamic-update-slice_fusion), channel_id=1, source_target_pairs={{0,8},{8,0},{16,24},{24,16},{1,9},{9,1},{17,25},{25,17},{2,10},{10... | collective-permute-start | bytes 417800 | tf_op jit(solution)/shard_map/ppermute | solution.py:311
  11.8 0.0 collective-permute-done.3
  11.8 1.2 %collective-permute-start.4 = (f32[8,128]{1,0:T(8,128)S(1)}, f32[8,128]{1,0:T(8,128)S(1)}, u32[]{:S(2)}, u32[]{:S(2)}) collective-permute-start(f32[8,128]{1,0:T(8,128)S(1)} %add.15), channel_id=1, source_target_pairs={{0,2},{1,3},{2,0},{3,1},{4,6},{5,7},{6,4},{7,5},{8,10},{9,11},{10,... | collective-permute-start | bytes 12296 | tf_op jit(solution)/shard_map/ppermute | solution.py:311
  13.1 2.5 %filter.4.local_refs_0_ = f32[3,32,64,128]{3,2,1,0:T(8,128)S(1)} custom-call(bf16[8,32,64,128]{3,2,1,0:T(8,128)(2,1)S(1)} %get-tuple-element.44.high_ref, bf16[8,32,64,128]{3,2,1,0:T(8,128)(2,1)S(1)} %get-tuple-element.45.low_ref, bf16[8,2,64,128]{3,2,1,0:T(8,128)(2,1)S(1)} %get-tuple-element.46.halo_high_ref, ...), custom_call_target="tpu_custom_call" | custom-call | flops 1711276032 | bytes 1048576 | tf_op jit(solution)/shard_map/filter/pallas_call | solution.py:381
  15.5 0.0 collective-permute-done.4
  15.6 1.3 %collective-permute-start.5 = (f32[8,128]{1,0:T(8,128)S(1)}, f32[8,128]{1,0:T(8,128)S(1)}, u32[]{:S(2)}, u32[]{:S(2)}) collective-permute-start(f32[8,128]{1,0:T(8,128)S(1)} %add.16), channel_id=1, source_target_pairs={{0,4},{1,5},{2,6},{3,7},{4,0},{5,1},{6,2},{7,3},{8,12},{9,13},{10,... | collective-permute-start | bytes 12296 | tf_op jit(solution)/shard_map/ppermute | solution.py:311
  16.9 2.7 %collective-permute-start.8 = (f32[272,128]{1,0:T(8,128)S(1)}, f32[272,128]{1,0:T(8,128)S(1)}, u32[]{:S(2)}, u32[]{:S(2)}) collective-permute-start(f32[272,128]{1,0:T(8,128)S(1)} %add.19), channel_id=1, source_target_pairs={{0,16},{8,24},{16,0},{24,8},{1,17},{9,25},{17,1},{25,9},{2,18},{10... | collective-permute-start | bytes 417800 | tf_op jit(solution)/shard_map/ppermute | solution.py:311
  19.6 1.7 %filter.5.local_refs_1_ = f32[2,32,64,128]{3,2,1,0:T(8,128)S(1)} custom-call(bf16[8,32,64,128]{3,2,1,0:T(8,128)(2,1)S(1)} %get-tuple-element.44.high_ref, bf16[8,32,64,128]{3,2,1,0:T(8,128)(2,1)S(1)} %get-tuple-element.45.low_ref, bf16[8,2,64,128]{3,2,1,0:T(8,128)(2,1)S(1)} %get-tuple-element.46.halo_high_ref, ...), custom_call_target="tpu_custom_call" | custom-call | flops 1140850688 | bytes 1048576 | tf_op jit(solution)/shard_map/filter/pallas_call | solution.py:381
  21.3 1.1 %collective-permute-start.6 = (f32[8,128]{1,0:T(8,128)S(1)}, f32[8,128]{1,0:T(8,128)S(1)}, u32[]{:S(2)}, u32[]{:S(2)}) collective-permute-start(f32[8,128]{1,0:T(8,128)S(1)} %add.17.sums_ref), channel_id=1, source_target_pairs={{0,8},{8,0},{16,24},{24,16},{1,9},{9,1},{17,25},{25,17},{2,10},{10... | collective-permute-start | bytes 12296 | tf_op jit(solution)/shard_map/ppermute | solution.py:311
  22.4 1.7 %filter.6.local_refs_2_ = f32[2,32,64,128]{3,2,1,0:T(8,128)S(1)} custom-call(bf16[8,32,64,128]{3,2,1,0:T(8,128)(2,1)S(1)} %get-tuple-element.44.high_ref, bf16[8,32,64,128]{3,2,1,0:T(8,128)(2,1)S(1)} %get-tuple-element.45.low_ref, bf16[8,2,64,128]{3,2,1,0:T(8,128)(2,1)S(1)} %get-tuple-element.46.halo_high_ref, ...), custom_call_target="tpu_custom_call" | custom-call | flops 1140850688 | bytes 1048576 | tf_op jit(solution)/shard_map/filter/pallas_call | solution.py:381
  24.1 1.3 %collective-permute-done.6.earlier_refs_0_ = f32[8,128]{1,0:T(8,128)S(1)} collective-permute-done((f32[8,128]{1,0:T(8,128)S(1)}, f32[8,128]{1,0:T(8,128)S(1)}, u32[]{:S(2)}, u32[]{:S(2)}) %collective-permute-start.6) | collective-permute-done | bytes 4128 | tf_op jit(solution)/shard_map/ppermute | solution.py:311
  25.4 0.1 collective-permute-start.7
  25.5 0.7 %collective-permute-done.8.totals_refs_1_ = f32[272,128]{1,0:T(8,128)S(1)} collective-permute-done((f32[272,128]{1,0:T(8,128)S(1)}, f32[272,128]{1,0:T(8,128)S(1)}, u32[]{:S(2)}, u32[]{:S(2)}) %collective-permute-start.8) | collective-permute-done | bytes 139296 | tf_op jit(solution)/shard_map/ppermute | solution.py:311
  26.1 0.8 %bias.1 = (f32[8,32,128]{2,1,0:T(8,128)S(1)}, f32[8,32,128]{2,1,0:T(8,128)S(1)}) custom-call(bf16[8,512,256]{2,1,0:T(8,128)(2,1)S(1)} %get-tuple-element.66.weight_ref, f32[272,128]{1,0:T(8,128)S(1)} %collective-permute-done.2.totals_refs_0_, f32[272,128]{1,0:T(8,128)S(1)} %collective-permute-done.8.totals_refs_1_), custom_call_target="tpu_custom_call" | custom-call | bytes 2097152 | tf_op jit(solution)/shard_map/bias/pallas_call | solution.py:396
  26.9 0.0 copy-start.2
  26.9 0.8 %filter.7.local_refs_3_ = f32[1,32,64,128]{3,2,1,0:T(8,128)S(1)} custom-call(bf16[8,32,64,128]{3,2,1,0:T(8,128)(2,1)S(1)} %get-tuple-element.44.high_ref, bf16[8,32,64,128]{3,2,1,0:T(8,128)(2,1)S(1)} %get-tuple-element.45.low_ref, bf16[8,2,64,128]{3,2,1,0:T(8,128)(2,1)S(1)} %get-tuple-element.46.halo_high_ref, ...), custom_call_target="tpu_custom_call" | custom-call | flops 570425344 | bytes 1048576 | tf_op jit(solution)/shard_map/filter/pallas_call | solution.py:381
  27.8 2.1 %collective-permute-done.7.earlier_refs_1_ = f32[8,128]{1,0:T(8,128)S(1)} collective-permute-done((f32[8,128]{1,0:T(8,128)S(1)}, f32[8,128]{1,0:T(8,128)S(1)}, u32[]{:S(2)}, u32[]{:S(2)}) %collective-permute-start.7) | collective-permute-done | bytes 4128 | tf_op jit(solution)/shard_map/ppermute | solution.py:311
  29.9 4.2 %level.1 = f32[8,64,4096]{2,1,0:T(8,128)} custom-call(f32[3,32,64,128]{3,2,1,0:T(8,128)S(1)} %filter.4.local_refs_0_, f32[2,32,64,128]{3,2,1,0:T(8,128)S(1)} %filter.5.local_refs_1_, f32[2,32,64,128]{3,2,1,0:T(8,128)S(1)} %filter.6.local_refs_2_, f32[1,32,64,128]{3,2,1,0:T(8,128)S(1)} %filter.7.local_refs_3_, f32[8,32,128]{2,1,0:T(8,128)S(1)} %get-tuple-element.68.bias_ref, ...), custom_call_target="tpu_custom_call" | custom-call | tf_op jit(solution)/shard_map/level/pallas_call | solution.py:441
  (16 shorter events, 0.1 us)
Async XLA Ops:
  0.0 5.7 %copy-start.1 = (f32[8,128]{1,0:T(8,128)S(1)}, f32[8,128]{1,0:T(8,128)}, u32[]{:S(2)}) copy-start(f32[8,128]{1,0:T(8,128)} %taps_ref.1) | copy-start | bytes 12292
  0.0 5.7 %copy-start = (f32[8,64,4096]{2,1,0:T(8,128)S(1)}, f32[8,64,4096]{2,1,0:T(8,128)}, u32[]{:S(2)}) copy-start(f32[8,64,4096]{2,1,0:T(8,128)} %phase_hbm.1) | copy-start | bytes 25165828
  1.6 8.3 %collective-permute-start = (f32[4,64,128]{2,1,0:T(8,128)S(1)}, f32[4,64,128]{2,1,0:T(8,128)S(1)}, u32[]{:S(2)}, u32[]{:S(2)}) collective-permute-start(f32[4,64,128]{2,1,0:T(8,128)S(1)} %get-tuple-element.39), channel_id=1, source_target_pairs={{0,1},{1,0},{2,3},{3,2},{4,5},{5,4},{6,7},{7,6},{8,9},{9,8},{10,11... | collective-permute-start | bytes 393224 | tf_op jit(solution)/shard_map/ppermute | solution.py:311
  2.1 7.8 %collective-permute-start.1 = (f32[4,64,128]{2,1,0:T(8,128)S(1)}, f32[4,64,128]{2,1,0:T(8,128)S(1)}, u32[]{:S(2)}, u32[]{:S(2)}) collective-permute-start(f32[4,64,128]{2,1,0:T(8,128)S(1)} %get-tuple-element.40), channel_id=1, source_target_pairs={{0,7},{1,2},{2,1},{3,4},{4,3},{5,6},{6,5},{7,0},{8,15},{9,10},{10,... | collective-permute-start | bytes 393224 | tf_op jit(solution)/shard_map/ppermute | solution.py:340
  10.1 1.7 %collective-permute-start.3 = (f32[8,128]{1,0:T(8,128)S(1)}, f32[8,128]{1,0:T(8,128)S(1)}, u32[]{:S(2)}, u32[]{:S(2)}) collective-permute-start(f32[8,128]{1,0:T(8,128)S(1)} %get-tuple-element.43), channel_id=1, source_target_pairs={{0,1},{1,0},{2,3},{3,2},{4,5},{5,4},{6,7},{7,6},{8,9},{9,8},{10,11... | collective-permute-start | bytes 12296 | tf_op jit(solution)/shard_map/ppermute | solution.py:311
  10.2 6.7 %collective-permute-start.2 = (f32[272,128]{1,0:T(8,128)S(1)}, f32[272,128]{1,0:T(8,128)S(1)}, u32[]{:S(2)}, u32[]{:S(2)}) collective-permute-start(f32[272,128]{1,0:T(8,128)S(1)} %constant_dynamic-update-slice_fusion), channel_id=1, source_target_pairs={{0,8},{8,0},{16,24},{24,16},{1,9},{9,1},{17,25},{25,17},{2,10},{10... | collective-permute-start | bytes 417800 | tf_op jit(solution)/shard_map/ppermute | solution.py:311
  11.8 3.7 %collective-permute-start.4 = (f32[8,128]{1,0:T(8,128)S(1)}, f32[8,128]{1,0:T(8,128)S(1)}, u32[]{:S(2)}, u32[]{:S(2)}) collective-permute-start(f32[8,128]{1,0:T(8,128)S(1)} %add.15), channel_id=1, source_target_pairs={{0,2},{1,3},{2,0},{3,1},{4,6},{5,7},{6,4},{7,5},{8,10},{9,11},{10,... | collective-permute-start | bytes 12296 | tf_op jit(solution)/shard_map/ppermute | solution.py:311
  15.6 5.7 %collective-permute-start.5 = (f32[8,128]{1,0:T(8,128)S(1)}, f32[8,128]{1,0:T(8,128)S(1)}, u32[]{:S(2)}, u32[]{:S(2)}) collective-permute-start(f32[8,128]{1,0:T(8,128)S(1)} %add.16), channel_id=1, source_target_pairs={{0,4},{1,5},{2,6},{3,7},{4,0},{5,1},{6,2},{7,3},{8,12},{9,13},{10,... | collective-permute-start | bytes 12296 | tf_op jit(solution)/shard_map/ppermute | solution.py:311
  16.9 9.2 %collective-permute-start.8 = (f32[272,128]{1,0:T(8,128)S(1)}, f32[272,128]{1,0:T(8,128)S(1)}, u32[]{:S(2)}, u32[]{:S(2)}) collective-permute-start(f32[272,128]{1,0:T(8,128)S(1)} %add.19), channel_id=1, source_target_pairs={{0,16},{8,24},{16,0},{24,8},{1,17},{9,25},{17,1},{25,9},{2,18},{10... | collective-permute-start | bytes 417800 | tf_op jit(solution)/shard_map/ppermute | solution.py:311
  21.3 4.1 %collective-permute-start.6 = (f32[8,128]{1,0:T(8,128)S(1)}, f32[8,128]{1,0:T(8,128)S(1)}, u32[]{:S(2)}, u32[]{:S(2)}) collective-permute-start(f32[8,128]{1,0:T(8,128)S(1)} %add.17.sums_ref), channel_id=1, source_target_pairs={{0,8},{8,0},{16,24},{24,16},{1,9},{9,1},{17,25},{25,17},{2,10},{10... | collective-permute-start | bytes 12296 | tf_op jit(solution)/shard_map/ppermute | solution.py:311
  25.4 4.5 %collective-permute-start.7 = (f32[8,128]{1,0:T(8,128)S(1)}, f32[8,128]{1,0:T(8,128)S(1)}, u32[]{:S(2)}, u32[]{:S(2)}) collective-permute-start(f32[8,128]{1,0:T(8,128)S(1)} %add.18), channel_id=1, source_target_pairs={{0,16},{8,24},{16,0},{24,8},{1,17},{9,25},{17,1},{25,9},{2,18},{10... | collective-permute-start | bytes 12296 | tf_op jit(solution)/shard_map/ppermute | solution.py:311
  26.9 3.0 %copy-start.2 = (f32[8]{0:T(128)S(1)}, f32[8]{0:T(128)}, u32[]{:S(2)}) copy-start(f32[8]{0:T(128)} %coupling_ref.1) | copy-start | bytes 100

commit v13 on v12

--- a/solution.py
+++ b/solution.py
@@ -63,8 +63,8 @@
             copies.append(
                 pltpu.make_async_copy(source.at[:, :, lanes], target.at[side], sem.at[kind, side])
             )
-    for copy in copies:
-        copy.start()
+    for number, copy in enumerate(copies):
+        copy.start(priority=number % 2)
     for copy in copies:
         copy.wait()
     lane = lax.broadcasted_iota(jnp.int32, (time, LANES), 1)
@@ -102,7 +102,7 @@
         return pltpu.make_async_copy(wrap_hbm.at[cable], wrap_ref.at[cable], sem.at[cable])
 
     for cable in range(cables):
-        copy(cable).start()
+        copy(cable).start(priority=cable % 2)
 
     lane = lax.broadcasted_iota(jnp.int32, taps_ref.shape, 1)
     taps = jnp.where(lane == HALF, 1.0, 0.0) - taps_ref[...]
@@ -297,7 +297,7 @@
 
             for chunk in range(CHUNKS):
                 lax.fori_loop(chunk * span, (chunk + 1) * span, block_step, 0, unroll=8)
-                written(cable, chunk).start()
+                written(cable, chunk).start(priority=chunk % 2)
             return carry
 
         lax.fori_loop(0, local_ref.shape[0], cable_step, 0)
@@ -316,7 +316,7 @@
     blocks = width // LANES
     steps, places = lax.axis_size("tm"), lax.axis_size("chan")
     population = cables * width * places
-    bounds = [0, 3 * cables // 8, 5 * cables // 8, 7 * cables // 8, cables]
+    bounds = [0, 3 * cables // 8, cables // 2, 3 * cables // 4, cables]
     parts = len(bounds) - 1
     wrap_count = pltpu.with_memory_space_constraint(wrap_count, pltpu.HBM)
     whole = pl.BlockSpec(memory_space=pltpu.VMEM)

time: 34.3 us -> 34.2 us (level)
  waiting for transfers between devices: 4.06 us -> 2.72 us
  Pallas kernels: 17.6 us -> 18.4 us
  starting transfers between devices: 12.2 us -> 12.8 us
    ppermute x8, waiting for transfers between devices: 4.06 us -> 2.72 us  [swapped(): lax.ppermute(value, axis, [(i, i ^ bit) for i in range(lax.axis_size(axis...]
    pallas_call x1, Pallas kernels: 4.21 us -> 4.96 us  [shards(): pl.pallas_call(increments_kernel, out_shape=(pltpu.VMEM((cables, blocks,...]
    ppermute x8, starting transfers between devices: 8.69 us -> 9.21 us  [swapped(): lax.ppermute(value, axis, [(i, i ^ bit) for i in range(lax.axis_size(axis...]
  transfers between devices with their start and end apart: 9 -> 9, of which waited for: 3 -> 4; matrix products, arithmetic and copies ran while one was open for 0% -> 0% of each run, Pallas kernels for 34% -> 36%
where the time goes in v13:
time: 34.2 us; the launch traced here: 34 us
  Pallas kernels  18.4 us (54%)
  starting transfers between devices  12.8 us (37%)
  waiting for transfers between devices  2.72 us (8%)
    ppermute x8, starting transfers between devices, swapped(): lax.ppermute(value, axis, [(i, i ^ bit) for i in range(lax.axis_size(axis...  9.21 us
    pallas_call x4, Pallas kernels, filtered(): pl.pallas_call(functools.partial(filter_kernel, bounds[part]), out_shape=...  6.63 us
    pallas_call x1, Pallas kernels, shards(): pl.pallas_call(increments_kernel, out_shape=(pltpu.VMEM((cables, blocks,...  4.96 us
    pallas_call x1, Pallas kernels, shards(): pl.pallas_call(functools.partial(level_kernel, population), out_shape=jax...  4.25 us
    ppermute x1, starting transfers between devices, shards(): outer = lax.ppermute(outer, 'chan', outer_pairs)  3.56 us
    ppermute x8, waiting for transfers between devices, swapped(): lax.ppermute(value, axis, [(i, i ^ bit) for i in range(lax.axis_size(axis...  2.72 us
    pallas_call x1, Pallas kernels, shards(): pl.pallas_call(edges_kernel, out_shape=[pltpu.VMEM((cables // 2, time, LA...  1.59 us
    pallas_call x1, Pallas kernels, biased(): pl.pallas_call(bias_kernel, out_shape=[pltpu.VMEM((cables, blocks, LANES)...  0.78 us
  transfers between devices with their start and end apart: 9, of which 4 were waited for; matrix products, arithmetic and copies ran while one was open for 0% of the time, Pallas kernels for 36%

profile of v13, /device:TPU:0, one launch (start us, length us, event | category | flops | bytes accessed | tf_op | source)
XLA Modules:
  0.0 34.0 jit_solution(15609756232214231410)
XLA Ops:
  0.0 1.6 %edges.1 = (f32[4,64,128]{2,1,0:T(8,128)S(1)}, f32[4,64,128]{2,1,0:T(8,128)S(1)}) custom-call(f32[8,64,4096]{2,1,0:T(8,128)} %phase_hbm.1, s32[8,64,4096]{2,1,0:T(8,128)} %wrap_hbm.3), custom_call_target="tpu_custom_call" | custom-call | tf_op jit(solution)/shard_map/edges/pallas_call | solution.py:326
  1.6 0.5 %collective-permute-start = (f32[4,64,128]{2,1,0:T(8,128)S(1)}, f32[4,64,128]{2,1,0:T(8,128)S(1)}, u32[]{:S(2)}, u32[]{:S(2)}) collective-permute-start(f32[4,64,128]{2,1,0:T(8,128)S(1)} %get-tuple-element.39), channel_id=1, source_target_pairs={{0,1},{1,0},{2,3},{3,2},{4,5},{5,4},{6,7},{7,6},{8,9},{9,8},{10,11... | collective-permute-start | bytes 393224 | tf_op jit(solution)/shard_map/ppermute | solution.py:311
  2.1 3.6 %collective-permute-start.1 = (f32[4,64,128]{2,1,0:T(8,128)S(1)}, f32[4,64,128]{2,1,0:T(8,128)S(1)}, u32[]{:S(2)}, u32[]{:S(2)}) collective-permute-start(f32[4,64,128]{2,1,0:T(8,128)S(1)} %get-tuple-element.40), channel_id=1, source_target_pairs={{0,7},{1,2},{2,1},{3,4},{4,3},{5,6},{6,5},{7,0},{8,15},{9,10},{10,... | collective-permute-start | bytes 393224 | tf_op jit(solution)/shard_map/ppermute | solution.py:340
  5.7 5.0 %increments.1 = (bf16[8,32,64,128]{3,2,1,0:T(8,128)(2,1)S(1)}, bf16[8,32,64,128]{3,2,1,0:T(8,128)(2,1)S(1)}, f32[256,128]{1,0:T(8,128)S(1)}, f32[8,128]{1,0:T(8,128)S(1)}, bf16[8,512,256]{2,1,0:T(8,128)(2,1)S(1)}) custom-call(f32[8,64,4096]{2,1,0:T(8,128)S(1)} %copy-done, s32[8,64,4096]{2,1,0:T(8,128)} %wrap_hbm.3, f32[8,128]{1,0:T(8,128)S(1)} %copy-done.1), custom_call_target="tpu_custom_call" | custom-call | bytes 8388608 | tf_op jit(solution)/shard_map/increments/pallas_call | solution.py:343
  10.7 0.0 collective-permute-done.inner_ref
  10.7 0.2 halo.1
  10.8 0.1 collective-permute-start.3
  10.9 1.6 %collective-permute-start.2 = (f32[272,128]{1,0:T(8,128)S(1)}, f32[272,128]{1,0:T(8,128)S(1)}, u32[]{:S(2)}, u32[]{:S(2)}) collective-permute-start(f32[272,128]{1,0:T(8,128)S(1)} %constant_dynamic-update-slice_fusion), channel_id=1, source_target_pairs={{0,8},{8,0},{16,24},{24,16},{1,9},{9,1},{17,25},{25,17},{2,10},{10... | collective-permute-start | bytes 417800 | tf_op jit(solution)/shard_map/ppermute | solution.py:311
  12.6 1.0 %collective-permute-start.4 = (f32[8,128]{1,0:T(8,128)S(1)}, f32[8,128]{1,0:T(8,128)S(1)}, u32[]{:S(2)}, u32[]{:S(2)}) collective-permute-start(f32[8,128]{1,0:T(8,128)S(1)} %add.15), channel_id=1, source_target_pairs={{0,2},{1,3},{2,0},{3,1},{4,6},{5,7},{6,4},{7,5},{8,10},{9,11},{10,... | collective-permute-start | bytes 12296 | tf_op jit(solution)/shard_map/ppermute | solution.py:311
  13.6 2.5 %filter.4.local_refs_0_ = f32[3,32,64,128]{3,2,1,0:T(8,128)S(1)} custom-call(bf16[8,32,64,128]{3,2,1,0:T(8,128)(2,1)S(1)} %get-tuple-element.44.high_ref, bf16[8,32,64,128]{3,2,1,0:T(8,128)(2,1)S(1)} %get-tuple-element.45.low_ref, bf16[8,2,64,128]{3,2,1,0:T(8,128)(2,1)S(1)} %get-tuple-element.46.halo_high_ref, ...), custom_call_target="tpu_custom_call" | custom-call | flops 1711276032 | bytes 1048576 | tf_op jit(solution)/shard_map/filter/pallas_call | solution.py:381
  16.1 0.1 collective-permute-done.4
  16.2 1.5 %collective-permute-start.5 = (f32[8,128]{1,0:T(8,128)S(1)}, f32[8,128]{1,0:T(8,128)S(1)}, u32[]{:S(2)}, u32[]{:S(2)}) collective-permute-start(f32[8,128]{1,0:T(8,128)S(1)} %add.16), channel_id=1, source_target_pairs={{0,4},{1,5},{2,6},{3,7},{4,0},{5,1},{6,2},{7,3},{8,12},{9,13},{10,... | collective-permute-start | bytes 12296 | tf_op jit(solution)/shard_map/ppermute | solution.py:311
  17.7 2.6 %collective-permute-start.8 = (f32[272,128]{1,0:T(8,128)S(1)}, f32[272,128]{1,0:T(8,128)S(1)}, u32[]{:S(2)}, u32[]{:S(2)}) collective-permute-start(f32[272,128]{1,0:T(8,128)S(1)} %add.19), channel_id=1, source_target_pairs={{0,16},{8,24},{16,0},{24,8},{1,17},{9,25},{17,1},{25,9},{2,18},{10... | collective-permute-start | bytes 417800 | tf_op jit(solution)/shard_map/ppermute | solution.py:311
  20.3 0.8 %filter.5.local_refs_1_ = f32[1,32,64,128]{3,2,1,0:T(8,128)S(1)} custom-call(bf16[8,32,64,128]{3,2,1,0:T(8,128)(2,1)S(1)} %get-tuple-element.44.high_ref, bf16[8,32,64,128]{3,2,1,0:T(8,128)(2,1)S(1)} %get-tuple-element.45.low_ref, bf16[8,2,64,128]{3,2,1,0:T(8,128)(2,1)S(1)} %get-tuple-element.46.halo_high_ref, ...), custom_call_target="tpu_custom_call" | custom-call | flops 570425344 | bytes 1048576 | tf_op jit(solution)/shard_map/filter/pallas_call | solution.py:381
  21.2 1.1 %collective-permute-start.6 = (f32[8,128]{1,0:T(8,128)S(1)}, f32[8,128]{1,0:T(8,128)S(1)}, u32[]{:S(2)}, u32[]{:S(2)}) collective-permute-start(f32[8,128]{1,0:T(8,128)S(1)} %add.17.sums_ref), channel_id=1, source_target_pairs={{0,8},{8,0},{16,24},{24,16},{1,9},{9,1},{17,25},{25,17},{2,10},{10... | collective-permute-start | bytes 12296 | tf_op jit(solution)/shard_map/ppermute | solution.py:311
  22.3 1.7 %filter.6.local_refs_2_ = f32[2,32,64,128]{3,2,1,0:T(8,128)S(1)} custom-call(bf16[8,32,64,128]{3,2,1,0:T(8,128)(2,1)S(1)} %get-tuple-element.44.high_ref, bf16[8,32,64,128]{3,2,1,0:T(8,128)(2,1)S(1)} %get-tuple-element.45.low_ref, bf16[8,2,64,128]{3,2,1,0:T(8,128)(2,1)S(1)} %get-tuple-element.46.halo_high_ref, ...), custom_call_target="tpu_custom_call" | custom-call | flops 1140850688 | bytes 1048576 | tf_op jit(solution)/shard_map/filter/pallas_call | solution.py:381
  24.0 1.3 %collective-permute-done.6.earlier_refs_0_ = f32[8,128]{1,0:T(8,128)S(1)} collective-permute-done((f32[8,128]{1,0:T(8,128)S(1)}, f32[8,128]{1,0:T(8,128)S(1)}, u32[]{:S(2)}, u32[]{:S(2)}) %collective-permute-start.6) | collective-permute-done | bytes 4128 | tf_op jit(solution)/shard_map/ppermute | solution.py:311
  25.3 0.7 %collective-permute-start.7 = (f32[8,128]{1,0:T(8,128)S(1)}, f32[8,128]{1,0:T(8,128)S(1)}, u32[]{:S(2)}, u32[]{:S(2)}) collective-permute-start(f32[8,128]{1,0:T(8,128)S(1)} %add.18), channel_id=1, source_target_pairs={{0,16},{8,24},{16,0},{24,8},{1,17},{9,25},{17,1},{25,9},{2,18},{10... | collective-permute-start | bytes 12296 | tf_op jit(solution)/shard_map/ppermute | solution.py:311
  26.0 0.9 %collective-permute-done.8.totals_refs_1_ = f32[272,128]{1,0:T(8,128)S(1)} collective-permute-done((f32[272,128]{1,0:T(8,128)S(1)}, f32[272,128]{1,0:T(8,128)S(1)}, u32[]{:S(2)}, u32[]{:S(2)}) %collective-permute-start.8) | collective-permute-done | bytes 139296 | tf_op jit(solution)/shard_map/ppermute | solution.py:311
  26.9 0.8 %bias.1 = (f32[8,32,128]{2,1,0:T(8,128)S(1)}, f32[8,32,128]{2,1,0:T(8,128)S(1)}) custom-call(bf16[8,512,256]{2,1,0:T(8,128)(2,1)S(1)} %get-tuple-element.66.weight_ref, f32[272,128]{1,0:T(8,128)S(1)} %collective-permute-done.2.totals_refs_0_, f32[272,128]{1,0:T(8,128)S(1)} %collective-permute-done.8.totals_refs_1_), custom_call_target="tpu_custom_call" | custom-call | bytes 2097152 | tf_op jit(solution)/shard_map/bias/pallas_call | solution.py:396
  27.7 0.0 copy-start.2
  27.7 1.7 %filter.7.local_refs_3_ = f32[2,32,64,128]{3,2,1,0:T(8,128)S(1)} custom-call(bf16[8,32,64,128]{3,2,1,0:T(8,128)(2,1)S(1)} %get-tuple-element.44.high_ref, bf16[8,32,64,128]{3,2,1,0:T(8,128)(2,1)S(1)} %get-tuple-element.45.low_ref, bf16[8,2,64,128]{3,2,1,0:T(8,128)(2,1)S(1)} %get-tuple-element.46.halo_high_ref, ...), custom_call_target="tpu_custom_call" | custom-call | flops 1140850688 | bytes 1048576 | tf_op jit(solution)/shard_map/filter/pallas_call | solution.py:381
  29.4 0.4 %collective-permute-done.7.earlier_refs_1_ = f32[8,128]{1,0:T(8,128)S(1)} collective-permute-done((f32[8,128]{1,0:T(8,128)S(1)}, f32[8,128]{1,0:T(8,128)S(1)}, u32[]{:S(2)}, u32[]{:S(2)}) %collective-permute-start.7) | collective-permute-done | bytes 4128 | tf_op jit(solution)/shard_map/ppermute | solution.py:311
  29.8 4.2 %level.1 = f32[8,64,4096]{2,1,0:T(8,128)} custom-call(f32[3,32,64,128]{3,2,1,0:T(8,128)S(1)} %filter.4.local_refs_0_, f32[1,32,64,128]{3,2,1,0:T(8,128)S(1)} %filter.5.local_refs_1_, f32[2,32,64,128]{3,2,1,0:T(8,128)S(1)} %filter.6.local_refs_2_, f32[2,32,64,128]{3,2,1,0:T(8,128)S(1)} %filter.7.local_refs_3_, f32[8,32,128]{2,1,0:T(8,128)S(1)} %get-tuple-element.68.bias_ref, ...), custom_call_target="tpu_custom_call" | custom-call | tf_op jit(solution)/shard_map/level/pallas_call | solution.py:441
  (16 shorter events, 0.1 us)
Async XLA Ops:
  0.0 5.7 %copy-start.1 = (f32[8,128]{1,0:T(8,128)S(1)}, f32[8,128]{1,0:T(8,128)}, u32[]{:S(2)}) copy-start(f32[8,128]{1,0:T(8,128)} %taps_ref.1) | copy-start | bytes 12292
  0.0 5.7 %copy-start = (f32[8,64,4096]{2,1,0:T(8,128)S(1)}, f32[8,64,4096]{2,1,0:T(8,128)}, u32[]{:S(2)}) copy-start(f32[8,64,4096]{2,1,0:T(8,128)} %phase_hbm.1) | copy-start | bytes 25165828
  1.6 9.1 %collective-permute-start = (f32[4,64,128]{2,1,0:T(8,128)S(1)}, f32[4,64,128]{2,1,0:T(8,128)S(1)}, u32[]{:S(2)}, u32[]{:S(2)}) collective-permute-start(f32[4,64,128]{2,1,0:T(8,128)S(1)} %get-tuple-element.39), channel_id=1, source_target_pairs={{0,1},{1,0},{2,3},{3,2},{4,5},{5,4},{6,7},{7,6},{8,9},{9,8},{10,11... | collective-permute-start | bytes 393224 | tf_op jit(solution)/shard_map/ppermute | solution.py:311
  2.1 8.6 %collective-permute-start.1 = (f32[4,64,128]{2,1,0:T(8,128)S(1)}, f32[4,64,128]{2,1,0:T(8,128)S(1)}, u32[]{:S(2)}, u32[]{:S(2)}) collective-permute-start(f32[4,64,128]{2,1,0:T(8,128)S(1)} %get-tuple-element.40), channel_id=1, source_target_pairs={{0,7},{1,2},{2,1},{3,4},{4,3},{5,6},{6,5},{7,0},{8,15},{9,10},{10,... | collective-permute-start | bytes 393224 | tf_op jit(solution)/shard_map/ppermute | solution.py:340
  10.8 1.7 %collective-permute-start.3 = (f32[8,128]{1,0:T(8,128)S(1)}, f32[8,128]{1,0:T(8,128)S(1)}, u32[]{:S(2)}, u32[]{:S(2)}) collective-permute-start(f32[8,128]{1,0:T(8,128)S(1)} %get-tuple-element.43), channel_id=1, source_target_pairs={{0,1},{1,0},{2,3},{3,2},{4,5},{5,4},{6,7},{7,6},{8,9},{9,8},{10,11... | collective-permute-start | bytes 12296 | tf_op jit(solution)/shard_map/ppermute | solution.py:311
  10.9 6.7 %collective-permute-start.2 = (f32[272,128]{1,0:T(8,128)S(1)}, f32[272,128]{1,0:T(8,128)S(1)}, u32[]{:S(2)}, u32[]{:S(2)}) collective-permute-start(f32[272,128]{1,0:T(8,128)S(1)} %constant_dynamic-update-slice_fusion), channel_id=1, source_target_pairs={{0,8},{8,0},{16,24},{24,16},{1,9},{9,1},{17,25},{25,17},{2,10},{10... | collective-permute-start | bytes 417800 | tf_op jit(solution)/shard_map/ppermute | solution.py:311
  12.6 3.6 %collective-permute-start.4 = (f32[8,128]{1,0:T(8,128)S(1)}, f32[8,128]{1,0:T(8,128)S(1)}, u32[]{:S(2)}, u32[]{:S(2)}) collective-permute-start(f32[8,128]{1,0:T(8,128)S(1)} %add.15), channel_id=1, source_target_pairs={{0,2},{1,3},{2,0},{3,1},{4,6},{5,7},{6,4},{7,5},{8,10},{9,11},{10,... | collective-permute-start | bytes 12296 | tf_op jit(solution)/shard_map/ppermute | solution.py:311
  16.2 5.0 %collective-permute-start.5 = (f32[8,128]{1,0:T(8,128)S(1)}, f32[8,128]{1,0:T(8,128)S(1)}, u32[]{:S(2)}, u32[]{:S(2)}) collective-permute-start(f32[8,128]{1,0:T(8,128)S(1)} %add.16), channel_id=1, source_target_pairs={{0,4},{1,5},{2,6},{3,7},{4,0},{5,1},{6,2},{7,3},{8,12},{9,13},{10,... | collective-permute-start | bytes 12296 | tf_op jit(solution)/shard_map/ppermute | solution.py:311
  17.7 9.2 %collective-permute-start.8 = (f32[272,128]{1,0:T(8,128)S(1)}, f32[272,128]{1,0:T(8,128)S(1)}, u32[]{:S(2)}, u32[]{:S(2)}) collective-permute-start(f32[272,128]{1,0:T(8,128)S(1)} %add.19), channel_id=1, source_target_pairs={{0,16},{8,24},{16,0},{24,8},{1,17},{9,25},{17,1},{25,9},{2,18},{10... | collective-permute-start | bytes 417800 | tf_op jit(solution)/shard_map/ppermute | solution.py:311
  21.2 4.1 %collective-permute-start.6 = (f32[8,128]{1,0:T(8,128)S(1)}, f32[8,128]{1,0:T(8,128)S(1)}, u32[]{:S(2)}, u32[]{:S(2)}) collective-permute-start(f32[8,128]{1,0:T(8,128)S(1)} %add.17.sums_ref), channel_id=1, source_target_pairs={{0,8},{8,0},{16,24},{24,16},{1,9},{9,1},{17,25},{25,17},{2,10},{10... | collective-permute-start | bytes 12296 | tf_op jit(solution)/shard_map/ppermute | solution.py:311
  25.3 4.5 %collective-permute-start.7 = (f32[8,128]{1,0:T(8,128)S(1)}, f32[8,128]{1,0:T(8,128)S(1)}, u32[]{:S(2)}, u32[]{:S(2)}) collective-permute-start(f32[8,128]{1,0:T(8,128)S(1)} %add.18), channel_id=1, source_target_pairs={{0,16},{8,24},{16,0},{24,8},{1,17},{9,25},{17,1},{25,9},{2,18},{10... | collective-permute-start | bytes 12296 | tf_op jit(solution)/shard_map/ppermute | solution.py:311
  27.7 2.1 %copy-start.2 = (f32[8]{0:T(128)S(1)}, f32[8]{0:T(128)}, u32[]{:S(2)}) copy-start(f32[8]{0:T(128)} %coupling_ref.1) | copy-start | bytes 100

commit v14 on v10

--- a/solution.py
+++ b/solution.py
@@ -334,8 +334,7 @@
         compiler_params=pltpu.CompilerParams(vmem_limit_bytes=8 << 20),
         name="edges",
     )(pltpu.with_memory_space_constraint(phase_step, pltpu.HBM), wrap_count)
-    last = places - 1
-    outer_pairs = [(0, 0), (last, last)] + [(i, i + (1 if i % 2 else -1)) for i in range(1, last)]
+    outer_pairs = [(i, (i + (1 if i % 2 else -1)) % places) for i in range(places)]
     outer = lax.ppermute(outer, "chan", outer_pairs)
     inner = swapped(inner, "chan", 1)
 

time: 34.8 us -> 32.9 us (0.945)
  starting transfers between devices: 15.9 us -> 14.6 us
  local copies, waits for them, and re-layouts: 0.83 us -> 0.02 us
    ppermute x8, starting transfers between devices: 15.1 us -> 11 us  [swapped(): lax.ppermute(value, axis, [(i, i ^ bit) for i in range(lax.axis_size(axis...]
    ppermute x1, starting transfers between devices: 0.79 us -> 3.56 us  [shards(): outer = lax.ppermute(outer, 'chan', outer_pairs)]
    unnamed x7, local copies, waits for them, and re-layouts: 0.82 us -> 0.02 us
  transfers between devices with their start and end apart: 9 -> 9, of which waited for: 3 -> 2; matrix products, arithmetic and copies ran while one was open for 0% -> 0% of each run, Pallas kernels for 31% -> 33%
where the time goes in v14:
time: 32.9 us; the launch traced here: 32.8 us
  Pallas kernels  16.8 us (51%)
  starting transfers between devices  14.6 us (44%)
  waiting for transfers between devices  1.19 us (4%)
    ppermute x8, starting transfers between devices, swapped(): lax.ppermute(value, axis, [(i, i ^ bit) for i in range(lax.axis_size(axis...  11 us
    pallas_call x3, Pallas kernels, filtered(): pl.pallas_call(functools.partial(filter_kernel, bounds[part]), out_shape=...  6.61 us
    pallas_call x1, Pallas kernels, shards(): pl.pallas_call(functools.partial(level_kernel, population), out_shape=jax...  4.27 us
    pallas_call x1, Pallas kernels, shards(): pl.pallas_call(increments_kernel, out_shape=(pltpu.VMEM((cables, blocks,...  4.21 us
    ppermute x1, starting transfers between devices, shards(): outer = lax.ppermute(outer, 'chan', outer_pairs)  3.56 us
    pallas_call x1, Pallas kernels, shards(): pl.pallas_call(edges_kernel, out_shape=[pltpu.VMEM((cables // 2, time, LA...  1.59 us
    ppermute x8, waiting for transfers between devices, swapped(): lax.ppermute(value, axis, [(i, i ^ bit) for i in range(lax.axis_size(axis...  1.19 us
  transfers between devices with their start and end apart: 9, of which 2 were waited for; matrix products, arithmetic and copies ran while one was open for 0% of the time, Pallas kernels for 33%

profile of v14, /device:TPU:0, one launch (start us, length us, event | category | flops | bytes accessed | tf_op | source)
XLA Modules:
  0.0 32.8 jit_solution(4553427727702140488)
XLA Ops:
  0.0 1.6 %edges.1 = (f32[4,64,128]{2,1,0:T(8,128)S(1)}, f32[4,64,128]{2,1,0:T(8,128)S(1)}) custom-call(f32[8,64,4096]{2,1,0:T(8,128)} %phase_hbm.1, s32[8,64,4096]{2,1,0:T(8,128)} %wrap_hbm.3), custom_call_target="tpu_custom_call" | custom-call | tf_op jit(solution)/shard_map/edges/pallas_call | solution.py:324
  1.6 0.5 %collective-permute-start = (f32[4,64,128]{2,1,0:T(8,128)S(1)}, f32[4,64,128]{2,1,0:T(8,128)S(1)}, u32[]{:S(2)}, u32[]{:S(2)}) collective-permute-start(f32[4,64,128]{2,1,0:T(8,128)S(1)} %get-tuple-element.30), channel_id=1, source_target_pairs={{0,1},{1,0},{2,3},{3,2},{4,5},{5,4},{6,7},{7,6},{8,9},{9,8},{10,11... | collective-permute-start | bytes 393224 | tf_op jit(solution)/shard_map/ppermute | solution.py:309
  2.1 3.6 %collective-permute-start.1 = (f32[4,64,128]{2,1,0:T(8,128)S(1)}, f32[4,64,128]{2,1,0:T(8,128)S(1)}, u32[]{:S(2)}, u32[]{:S(2)}) collective-permute-start(f32[4,64,128]{2,1,0:T(8,128)S(1)} %get-tuple-element.31), channel_id=1, source_target_pairs={{0,7},{1,2},{2,1},{3,4},{4,3},{5,6},{6,5},{7,0},{8,15},{9,10},{10,... | collective-permute-start | bytes 393224 | tf_op jit(solution)/shard_map/ppermute | solution.py:338
  5.7 4.2 %increments.1 = (bf16[8,32,64,128]{3,2,1,0:T(8,128)(2,1)S(1)}, bf16[8,32,64,128]{3,2,1,0:T(8,128)(2,1)S(1)}, f32[256,128]{1,0:T(8,128)S(1)}, f32[8,128]{1,0:T(8,128)S(1)}, bf16[8,512,256]{2,1,0:T(8,128)(2,1)S(1)}) custom-call(f32[8,64,4096]{2,1,0:T(8,128)S(1)} %copy-done, s32[8,64,4096]{2,1,0:T(8,128)} %wrap_hbm.3, f32[8,128]{1,0:T(8,128)S(1)} %copy-done.1), custom_call_target="tpu_custom_call" | custom-call | bytes 8388608 | tf_op jit(solution)/shard_map/increments/pallas_call | solution.py:341
  9.9 0.0 collective-permute-done.inner_ref
  9.9 0.0 collective-permute-done.1.outer_ref
  9.9 0.2 halo.1
  10.1 0.1 collective-permute-start.2
  10.2 1.6 %collective-permute-start.4 = (f32[272,128]{1,0:T(8,128)S(1)}, f32[272,128]{1,0:T(8,128)S(1)}, u32[]{:S(2)}, u32[]{:S(2)}) collective-permute-start(f32[272,128]{1,0:T(8,128)S(1)} %constant_dynamic-update-slice_fusion), channel_id=1, source_target_pairs={{0,8},{8,0},{16,24},{24,16},{1,9},{9,1},{17,25},{25,17},{2,10},{10... | collective-permute-start | bytes 417800 | tf_op jit(solution)/shard_map/ppermute | solution.py:309
  11.8 0.0 collective-permute-done.2
  11.8 1.2 %collective-permute-start.3 = (f32[8,128]{1,0:T(8,128)S(1)}, f32[8,128]{1,0:T(8,128)S(1)}, u32[]{:S(2)}, u32[]{:S(2)}) collective-permute-start(f32[8,128]{1,0:T(8,128)S(1)} %add.15), channel_id=1, source_target_pairs={{0,2},{1,3},{2,0},{3,1},{4,6},{5,7},{6,4},{7,5},{8,10},{9,11},{10,... | collective-permute-start | bytes 12296 | tf_op jit(solution)/shard_map/ppermute | solution.py:309
  13.1 3.3 %filter.3.local_refs_0_ = f32[4,32,64,128]{3,2,1,0:T(8,128)S(1)} custom-call(bf16[8,32,64,128]{3,2,1,0:T(8,128)(2,1)S(1)} %get-tuple-element.34.high_ref, bf16[8,32,64,128]{3,2,1,0:T(8,128)(2,1)S(1)} %get-tuple-element.35.low_ref, bf16[8,2,64,128]{3,2,1,0:T(8,128)(2,1)S(1)} %get-tuple-element.36.halo_high_ref, ...), custom_call_target="tpu_custom_call" | custom-call | flops 2281701376 | bytes 1048576 | tf_op jit(solution)/shard_map/filter/pallas_call | solution.py:379
  16.4 0.0 collective-permute-done.3
  16.4 0.0 collective-permute-done.4.totals_refs_0_
  16.4 1.4 %collective-permute-start.5 = (f32[8,128]{1,0:T(8,128)S(1)}, f32[8,128]{1,0:T(8,128)S(1)}, u32[]{:S(2)}, u32[]{:S(2)}) collective-permute-start(f32[8,128]{1,0:T(8,128)S(1)} %add.17), channel_id=1, source_target_pairs={{0,4},{1,5},{2,6},{3,7},{4,0},{5,1},{6,2},{7,3},{8,12},{9,13},{10,... | collective-permute-start | bytes 12296 | tf_op jit(solution)/shard_map/ppermute | solution.py:309
  17.8 2.6 %collective-permute-start.8 = (f32[272,128]{1,0:T(8,128)S(1)}, f32[272,128]{1,0:T(8,128)S(1)}, u32[]{:S(2)}, u32[]{:S(2)}) collective-permute-start(f32[272,128]{1,0:T(8,128)S(1)} %add.16), channel_id=1, source_target_pairs={{0,16},{8,24},{16,0},{24,8},{1,17},{9,25},{17,1},{25,9},{2,18},{10... | collective-permute-start | bytes 417800 | tf_op jit(solution)/shard_map/ppermute | solution.py:309
  20.4 1.3 %collective-permute-start.6 = (f32[8,128]{1,0:T(8,128)S(1)}, f32[8,128]{1,0:T(8,128)S(1)}, u32[]{:S(2)}, u32[]{:S(2)}) collective-permute-start(f32[8,128]{1,0:T(8,128)S(1)} %add.18.sums_ref), channel_id=1, source_target_pairs={{0,8},{8,0},{16,24},{24,16},{1,9},{9,1},{17,25},{25,17},{2,10},{10... | collective-permute-start | bytes 12296 | tf_op jit(solution)/shard_map/ppermute | solution.py:309
  21.7 1.7 %filter.4.local_refs_1_ = f32[2,32,64,128]{3,2,1,0:T(8,128)S(1)} custom-call(bf16[8,32,64,128]{3,2,1,0:T(8,128)(2,1)S(1)} %get-tuple-element.34.high_ref, bf16[8,32,64,128]{3,2,1,0:T(8,128)(2,1)S(1)} %get-tuple-element.35.low_ref, bf16[8,2,64,128]{3,2,1,0:T(8,128)(2,1)S(1)} %get-tuple-element.36.halo_high_ref, ...), custom_call_target="tpu_custom_call" | custom-call | flops 1140850688 | bytes 1048576 | tf_op jit(solution)/shard_map/filter/pallas_call | solution.py:379
  23.3 0.7 %collective-permute-done.6.earlier_refs_0_ = f32[8,128]{1,0:T(8,128)S(1)} collective-permute-done((f32[8,128]{1,0:T(8,128)S(1)}, f32[8,128]{1,0:T(8,128)S(1)}, u32[]{:S(2)}, u32[]{:S(2)}) %collective-permute-start.6) | collective-permute-done | bytes 4128 | tf_op jit(solution)/shard_map/ppermute | solution.py:309
  24.0 2.3 %collective-permute-start.7 = (f32[8,128]{1,0:T(8,128)S(1)}, f32[8,128]{1,0:T(8,128)S(1)}, u32[]{:S(2)}, u32[]{:S(2)}) collective-permute-start(f32[8,128]{1,0:T(8,128)S(1)} %add.19), channel_id=1, source_target_pairs={{0,16},{8,24},{16,0},{24,8},{1,17},{9,25},{17,1},{25,9},{2,18},{10... | collective-permute-start | bytes 12296 | tf_op jit(solution)/shard_map/ppermute | solution.py:309
  26.3 1.6 %filter.5.local_refs_2_ = f32[2,32,64,128]{3,2,1,0:T(8,128)S(1)} custom-call(bf16[8,32,64,128]{3,2,1,0:T(8,128)(2,1)S(1)} %get-tuple-element.34.high_ref, bf16[8,32,64,128]{3,2,1,0:T(8,128)(2,1)S(1)} %get-tuple-element.35.low_ref, bf16[8,2,64,128]{3,2,1,0:T(8,128)(2,1)S(1)} %get-tuple-element.36.halo_high_ref, ...), custom_call_target="tpu_custom_call" | custom-call | flops 1140850688 | bytes 1048576 | tf_op jit(solution)/shard_map/filter/pallas_call | solution.py:379
  28.0 0.5 %collective-permute-done.7.earlier_refs_1_ = f32[8,128]{1,0:T(8,128)S(1)} collective-permute-done((f32[8,128]{1,0:T(8,128)S(1)}, f32[8,128]{1,0:T(8,128)S(1)}, u32[]{:S(2)}, u32[]{:S(2)}) %collective-permute-start.7) | collective-permute-done | bytes 4128 | tf_op jit(solution)/shard_map/ppermute | solution.py:309
  28.5 0.0 collective-permute-done.8.totals_refs_1_
  28.5 4.3 %level.1 = f32[8,64,4096]{2,1,0:T(8,128)} custom-call(f32[4,32,64,128]{3,2,1,0:T(8,128)S(1)} %filter.3.local_refs_0_, f32[2,32,64,128]{3,2,1,0:T(8,128)S(1)} %filter.4.local_refs_1_, f32[2,32,64,128]{3,2,1,0:T(8,128)S(1)} %filter.5.local_refs_2_, bf16[8,512,256]{2,1,0:T(8,128)(2,1)S(1)} %get-tuple-element.49.weight_ref, ...), custom_call_target="tpu_custom_call" | custom-call | tf_op jit(solution)/shard_map/level/pallas_call | solution.py:424
  (14 shorter events, 0.1 us)
Async XLA Ops:
  0.0 5.7 %copy-start.1 = (f32[8,128]{1,0:T(8,128)S(1)}, f32[8,128]{1,0:T(8,128)}, u32[]{:S(2)}) copy-start(f32[8,128]{1,0:T(8,128)} %taps_ref.1) | copy-start | bytes 12292
  0.0 5.7 %copy-start = (f32[8,64,4096]{2,1,0:T(8,128)S(1)}, f32[8,64,4096]{2,1,0:T(8,128)}, u32[]{:S(2)}) copy-start(f32[8,64,4096]{2,1,0:T(8,128)} %phase_hbm.1) | copy-start | bytes 25165828
  1.6 8.3 %collective-permute-start = (f32[4,64,128]{2,1,0:T(8,128)S(1)}, f32[4,64,128]{2,1,0:T(8,128)S(1)}, u32[]{:S(2)}, u32[]{:S(2)}) collective-permute-start(f32[4,64,128]{2,1,0:T(8,128)S(1)} %get-tuple-element.30), channel_id=1, source_target_pairs={{0,1},{1,0},{2,3},{3,2},{4,5},{5,4},{6,7},{7,6},{8,9},{9,8},{10,11... | collective-permute-start | bytes 393224 | tf_op jit(solution)/shard_map/ppermute | solution.py:309
  2.1 7.8 %collective-permute-start.1 = (f32[4,64,128]{2,1,0:T(8,128)S(1)}, f32[4,64,128]{2,1,0:T(8,128)S(1)}, u32[]{:S(2)}, u32[]{:S(2)}) collective-permute-start(f32[4,64,128]{2,1,0:T(8,128)S(1)} %get-tuple-element.31), channel_id=1, source_target_pairs={{0,7},{1,2},{2,1},{3,4},{4,3},{5,6},{6,5},{7,0},{8,15},{9,10},{10,... | collective-permute-start | bytes 393224 | tf_op jit(solution)/shard_map/ppermute | solution.py:338
  10.1 1.7 %collective-permute-start.2 = (f32[8,128]{1,0:T(8,128)S(1)}, f32[8,128]{1,0:T(8,128)S(1)}, u32[]{:S(2)}, u32[]{:S(2)}) collective-permute-start(f32[8,128]{1,0:T(8,128)S(1)} %get-tuple-element.33), channel_id=1, source_target_pairs={{0,1},{1,0},{2,3},{3,2},{4,5},{5,4},{6,7},{7,6},{8,9},{9,8},{10,11... | collective-permute-start | bytes 12296 | tf_op jit(solution)/shard_map/ppermute | solution.py:309
  10.2 6.2 %collective-permute-start.4 = (f32[272,128]{1,0:T(8,128)S(1)}, f32[272,128]{1,0:T(8,128)S(1)}, u32[]{:S(2)}, u32[]{:S(2)}) collective-permute-start(f32[272,128]{1,0:T(8,128)S(1)} %constant_dynamic-update-slice_fusion), channel_id=1, source_target_pairs={{0,8},{8,0},{16,24},{24,16},{1,9},{9,1},{17,25},{25,17},{2,10},{10... | collective-permute-start | bytes 417800 | tf_op jit(solution)/shard_map/ppermute | solution.py:309
  11.8 4.5 %collective-permute-start.3 = (f32[8,128]{1,0:T(8,128)S(1)}, f32[8,128]{1,0:T(8,128)S(1)}, u32[]{:S(2)}, u32[]{:S(2)}) collective-permute-start(f32[8,128]{1,0:T(8,128)S(1)} %add.15), channel_id=1, source_target_pairs={{0,2},{1,3},{2,0},{3,1},{4,6},{5,7},{6,4},{7,5},{8,10},{9,11},{10,... | collective-permute-start | bytes 12296 | tf_op jit(solution)/shard_map/ppermute | solution.py:309
  16.4 3.9 %collective-permute-start.5 = (f32[8,128]{1,0:T(8,128)S(1)}, f32[8,128]{1,0:T(8,128)S(1)}, u32[]{:S(2)}, u32[]{:S(2)}) collective-permute-start(f32[8,128]{1,0:T(8,128)S(1)} %add.17), channel_id=1, source_target_pairs={{0,4},{1,5},{2,6},{3,7},{4,0},{5,1},{6,2},{7,3},{8,12},{9,13},{10,... | collective-permute-start | bytes 12296 | tf_op jit(solution)/shard_map/ppermute | solution.py:309
  17.8 10.7 %collective-permute-start.8 = (f32[272,128]{1,0:T(8,128)S(1)}, f32[272,128]{1,0:T(8,128)S(1)}, u32[]{:S(2)}, u32[]{:S(2)}) collective-permute-start(f32[272,128]{1,0:T(8,128)S(1)} %add.16), channel_id=1, source_target_pairs={{0,16},{8,24},{16,0},{24,8},{1,17},{9,25},{17,1},{25,9},{2,18},{10... | collective-permute-start | bytes 417800 | tf_op jit(solution)/shard_map/ppermute | solution.py:309
  20.4 3.6 %collective-permute-start.6 = (f32[8,128]{1,0:T(8,128)S(1)}, f32[8,128]{1,0:T(8,128)S(1)}, u32[]{:S(2)}, u32[]{:S(2)}) collective-permute-start(f32[8,128]{1,0:T(8,128)S(1)} %add.18.sums_ref), channel_id=1, source_target_pairs={{0,8},{8,0},{16,24},{24,16},{1,9},{9,1},{17,25},{25,17},{2,10},{10... | collective-permute-start | bytes 12296 | tf_op jit(solution)/shard_map/ppermute | solution.py:309
  24.0 4.5 %copy-start.2 = (f32[8]{0:T(128)S(1)}, f32[8]{0:T(128)}, u32[]{:S(2)}) copy-start(f32[8]{0:T(128)} %coupling_ref.1) | copy-start | bytes 100
  24.0 4.5 %collective-permute-start.7 = (f32[8,128]{1,0:T(8,128)S(1)}, f32[8,128]{1,0:T(8,128)S(1)}, u32[]{:S(2)}, u32[]{:S(2)}) collective-permute-start(f32[8,128]{1,0:T(8,128)S(1)} %add.19), channel_id=1, source_target_pairs={{0,16},{8,24},{16,0},{24,8},{1,17},{9,25},{17,1},{25,9},{2,18},{10... | collective-permute-start | bytes 12296 | tf_op jit(solution)/shard_map/ppermute | solution.py:309

commit v15 on v14

--- a/solution.py
+++ b/solution.py
@@ -12,6 +12,7 @@
 LANES = 128
 HALF = LANES // 2
 SUBLANES = 8
+MASK_FLOPS = 570000000
 CHUNKS = 2
 
 
@@ -208,6 +209,11 @@
             previous = following
 
 
+def masked_kernel(bit, value_ref, masked_ref):
+    later = (lax.axis_index("tm") & bit) != 0
+    masked_ref[...] = jnp.where(later, value_ref[...], 0.0)
+
+
 def level_kernel(
     population, local_refs, weight_ref, totals_refs, sums_ref, earlier_refs, coupling_ref,
     out_hbm, stage_ref, offset_ref, sem,
@@ -220,14 +226,11 @@
     inside_left = jnp.where(place == 0, 0.0, 1.0)
     inside_right = jnp.where(place == lax.axis_size("chan") - 1, 0.0, 1.0)
 
-    def from_earlier(refs):
-        value = jnp.zeros(refs[0].shape, jnp.float32)
-        for bit, ref in enumerate(refs):
-            value = value + jnp.where((step & (1 << bit)) != 0, ref[...], 0.0)
-        return value
-
-    offset_ref[...] = from_earlier(totals_refs)
-    earlier = from_earlier(earlier_refs)[SUBLANES - 1 :, groups - 1 : groups]
+    earlier = jnp.zeros((SUBLANES, LANES), jnp.float32)
+    for bit, ref in enumerate(earlier_refs):
+        earlier = earlier + jnp.where((step & (1 << bit)) != 0, ref[...], 0.0)
+    offset_ref[...] = functools.reduce(jnp.add, [ref[...] for ref in totals_refs])
+    earlier = earlier[SUBLANES - 1 :, groups - 1 : groups]
     common = (sums_ref[...] + earlier) * (1.0 / population)
     columns = [
         jnp.broadcast_to(common[:, i : i + 1], (SUBLANES, LANES)) for i in range(groups)
@@ -314,7 +317,7 @@
     blocks = width // LANES
     steps, places = lax.axis_size("tm"), lax.axis_size("chan")
     population = cables * width * places
-    bounds = [0, cables // 2, 3 * cables // 4, cables]
+    bounds = [0, 3 * cables // 8, 3 * cables // 4, cables]
     parts = len(bounds) - 1
     wrap_count = pltpu.with_memory_space_constraint(wrap_count, pltpu.HBM)
     whole = pl.BlockSpec(memory_space=pltpu.VMEM)
@@ -374,6 +377,19 @@
         name="halo",
     )(inner, outer)
 
+    def from_earlier(value, number):
+        return pl.pallas_call(
+            functools.partial(masked_kernel, 1 << number),
+            out_shape=pltpu.VMEM(value.shape, value.dtype),
+            in_specs=[whole],
+            out_specs=whole,
+            compiler_params=pltpu.CompilerParams(vmem_limit_bytes=4 << 20),
+            cost_estimate=pl.CostEstimate(
+                flops=MASK_FLOPS, bytes_accessed=1 << 20, transcendentals=0
+            ),
+            name="masked",
+        )(value)
+
     def filtered(part, weight):
         share = bounds[part + 1] - bounds[part]
         return pl.pallas_call(
@@ -403,12 +419,19 @@
             ready = None
         elif number > 0 and len(local) < parts:
             tied, sums = lax.optimization_barrier((weight, sums))
+            if number == len(rounds) - 1 and 1 << len(received) >= steps:
+                received[1] = from_earlier(received[1], 1)
+                received[1], tied = lax.optimization_barrier((received[1], tied))
             part = filtered(len(local), tied)
             incoming, part = lax.optimization_barrier((incoming, part))
             local.append(part)
-        if number % 2 == 1 and 1 << len(received) < steps:
-            running = running + received[-1]
-            ready, incoming = lax.optimization_barrier((running, incoming))
+        if number == 2:
+            first, sums = lax.optimization_barrier((received[0], sums))
+            masked = from_earlier(first, 0)
+            incoming, masked = lax.optimization_barrier((incoming, masked))
+        if number == 1 and 1 << len(received) < steps:
+            earlier, local[-1] = lax.optimization_barrier((received[-1], local[-1]))
+            ready = running = running + earlier
         if axis == "tm":
             received_sums.append(incoming)
         sums = sums + incoming
@@ -420,12 +443,13 @@
         received.append(swapped(running, "tm", 1 << len(received)))
     while len(local) < parts:
         local.append(filtered(len(local), weight))
+    offsets = [masked] + received[1:]
 
     return pl.pallas_call(
         functools.partial(level_kernel, population),
         out_shape=jax.ShapeDtypeStruct(phase_step.shape, jnp.float32),
         in_specs=[
-            [whole] * parts, whole, [whole] * len(received), whole, [whole] * len(received), scalars
+            [whole] * parts, whole, [whole] * len(offsets), whole, [whole] * len(received_sums), scalars
         ],
         out_specs=outside,
         scratch_shapes=[
@@ -435,7 +459,7 @@
         ],
         compiler_params=pltpu.CompilerParams(vmem_limit_bytes=24 << 20),
         name="level",
-    )(local, weight, received, chan_sums, received_sums, coupling)
+    )(local, weight, offsets, chan_sums, received_sums, coupling)
 
 
 def solution(mesh):

time: 32.9 us -> 34.5 us (1.049)
  waiting for transfers between devices: 1.19 us -> 4.93 us
  starting transfers between devices: 14.6 us -> 12.3 us
    ppermute x8, waiting for transfers between devices: 1.19 us -> 4.92 us  [swapped(): lax.ppermute(value, axis, [(i, i ^ bit) for i in range(lax.axis_size(axis...]
    ppermute x8, starting transfers between devices: 11 us -> 8.73 us  [swapped(): lax.ppermute(value, axis, [(i, i ^ bit) for i in range(lax.axis_size(axis...]
  transfers between devices with their start and end apart: 9 -> 9, of which waited for: 2 -> 2; matrix products, arithmetic and copies ran while one was open for 0% -> 0% of each run, Pallas kernels for 33% -> 32%
where the time goes in v15:
time: 34.5 us; the launch traced here: 34.3 us
  Pallas kernels  16.9 us (49%)
  starting transfers between devices  12.3 us (36%)
  waiting for transfers between devices  4.93 us (14%)
    ppermute x8, starting transfers between devices, swapped(): lax.ppermute(value, axis, [(i, i ^ bit) for i in range(lax.axis_size(axis...  8.73 us
    pallas_call x3, Pallas kernels, filtered(): pl.pallas_call(functools.partial(filter_kernel, bounds[part]), out_shape=...  6.63 us
    ppermute x8, waiting for transfers between devices, swapped(): lax.ppermute(value, axis, [(i, i ^ bit) for i in range(lax.axis_size(axis...  4.92 us
    pallas_call x1, Pallas kernels, shards(): pl.pallas_call(functools.partial(level_kernel, population), out_shape=jax...  4.28 us
    pallas_call x1, Pallas kernels, shards(): pl.pallas_call(increments_kernel, out_shape=(pltpu.VMEM((cables, blocks,...  4.21 us
    ppermute x1, starting transfers between devices, shards(): outer = lax.ppermute(outer, 'chan', outer_pairs)  3.56 us
    pallas_call x1, Pallas kernels, shards(): pl.pallas_call(edges_kernel, out_shape=[pltpu.VMEM((cables // 2, time, LA...  1.59 us
  transfers between devices with their start and end apart: 9, of which 2 were waited for; matrix products, arithmetic and copies ran while one was open for 0% of the time, Pallas kernels for 32%

profile of v15, /device:TPU:0, one launch (start us, length us, event | category | flops | bytes accessed | tf_op | source)
XLA Modules:
  0.0 34.3 jit_solution(12589480638558606509)
XLA Ops:
  0.0 1.6 %edges.1 = (f32[4,64,128]{2,1,0:T(8,128)S(1)}, f32[4,64,128]{2,1,0:T(8,128)S(1)}) custom-call(f32[8,64,4096]{2,1,0:T(8,128)} %phase_hbm.1, s32[8,64,4096]{2,1,0:T(8,128)} %wrap_hbm.3), custom_call_target="tpu_custom_call" | custom-call | tf_op jit(solution)/shard_map/edges/pallas_call | solution.py:327
  1.6 0.5 %collective-permute-start = (f32[4,64,128]{2,1,0:T(8,128)S(1)}, f32[4,64,128]{2,1,0:T(8,128)S(1)}, u32[]{:S(2)}, u32[]{:S(2)}) collective-permute-start(f32[4,64,128]{2,1,0:T(8,128)S(1)} %get-tuple-element.36), channel_id=1, source_target_pairs={{0,1},{1,0},{2,3},{3,2},{4,5},{5,4},{6,7},{7,6},{8,9},{9,8},{10,11... | collective-permute-start | bytes 393224 | tf_op jit(solution)/shard_map/ppermute | solution.py:312
  2.1 3.6 %collective-permute-start.1 = (f32[4,64,128]{2,1,0:T(8,128)S(1)}, f32[4,64,128]{2,1,0:T(8,128)S(1)}, u32[]{:S(2)}, u32[]{:S(2)}) collective-permute-start(f32[4,64,128]{2,1,0:T(8,128)S(1)} %get-tuple-element.37), channel_id=1, source_target_pairs={{0,7},{1,2},{2,1},{3,4},{4,3},{5,6},{6,5},{7,0},{8,15},{9,10},{10,... | collective-permute-start | bytes 393224 | tf_op jit(solution)/shard_map/ppermute | solution.py:341
  5.7 4.2 %increments.1 = (bf16[8,32,64,128]{3,2,1,0:T(8,128)(2,1)S(1)}, bf16[8,32,64,128]{3,2,1,0:T(8,128)(2,1)S(1)}, f32[256,128]{1,0:T(8,128)S(1)}, f32[8,128]{1,0:T(8,128)S(1)}, bf16[8,512,256]{2,1,0:T(8,128)(2,1)S(1)}) custom-call(f32[8,64,4096]{2,1,0:T(8,128)S(1)} %copy-done, s32[8,64,4096]{2,1,0:T(8,128)} %wrap_hbm.3, f32[8,128]{1,0:T(8,128)S(1)} %copy-done.1), custom_call_target="tpu_custom_call" | custom-call | bytes 8388608 | tf_op jit(solution)/shard_map/increments/pallas_call | solution.py:344
  9.9 0.0 collective-permute-done.inner_ref
  9.9 0.2 halo.1
  10.1 0.1 collective-permute-start.3
  10.2 1.6 %collective-permute-start.2 = (f32[272,128]{1,0:T(8,128)S(1)}, f32[272,128]{1,0:T(8,128)S(1)}, u32[]{:S(2)}, u32[]{:S(2)}) collective-permute-start(f32[272,128]{1,0:T(8,128)S(1)} %constant_dynamic-update-slice_fusion), channel_id=1, source_target_pairs={{0,8},{8,0},{16,24},{24,16},{1,9},{9,1},{17,25},{25,17},{2,10},{10... | collective-permute-start | bytes 417800 | tf_op jit(solution)/shard_map/ppermute | solution.py:312
  11.8 1.2 %collective-permute-start.4 = (f32[8,128]{1,0:T(8,128)S(1)}, f32[8,128]{1,0:T(8,128)S(1)}, u32[]{:S(2)}, u32[]{:S(2)}) collective-permute-start(f32[8,128]{1,0:T(8,128)S(1)} %add.15), channel_id=1, source_target_pairs={{0,2},{1,3},{2,0},{3,1},{4,6},{5,7},{6,4},{7,5},{8,10},{9,11},{10,... | collective-permute-start | bytes 12296 | tf_op jit(solution)/shard_map/ppermute | solution.py:312
  13.1 2.5 %filter.3.local_refs_0_ = f32[3,32,64,128]{3,2,1,0:T(8,128)S(1)} custom-call(bf16[8,32,64,128]{3,2,1,0:T(8,128)(2,1)S(1)} %get-tuple-element.41.high_ref, bf16[8,32,64,128]{3,2,1,0:T(8,128)(2,1)S(1)} %get-tuple-element.42.low_ref, bf16[8,2,64,128]{3,2,1,0:T(8,128)(2,1)S(1)} %get-tuple-element.43.halo_high_ref, ...), custom_call_target="tpu_custom_call" | custom-call | flops 1711276032 | bytes 1048576 | tf_op jit(solution)/shard_map/filter/pallas_call | solution.py:395
  15.6 0.0 collective-permute-done.4
  15.6 1.3 %collective-permute-start.5 = (f32[8,128]{1,0:T(8,128)S(1)}, f32[8,128]{1,0:T(8,128)S(1)}, u32[]{:S(2)}, u32[]{:S(2)}) collective-permute-start(f32[8,128]{1,0:T(8,128)S(1)} %add.16), channel_id=1, source_target_pairs={{0,4},{1,5},{2,6},{3,7},{4,0},{5,1},{6,2},{7,3},{8,12},{9,13},{10,... | collective-permute-start | bytes 12296 | tf_op jit(solution)/shard_map/ppermute | solution.py:312
  16.9 0.0 collective-permute-done.2.value_ref
  16.9 2.3 %collective-permute-done.5 = f32[8,128]{1,0:T(8,128)S(1)} collective-permute-done((f32[8,128]{1,0:T(8,128)S(1)}, f32[8,128]{1,0:T(8,128)S(1)}, u32[]{:S(2)}, u32[]{:S(2)}) %collective-permute-start.5) | collective-permute-done | bytes 4128 | tf_op jit(solution)/shard_map/ppermute | solution.py:312
  19.3 0.9 %collective-permute-start.6 = (f32[8,128]{1,0:T(8,128)S(1)}, f32[8,128]{1,0:T(8,128)S(1)}, u32[]{:S(2)}, u32[]{:S(2)}) collective-permute-start(f32[8,128]{1,0:T(8,128)S(1)} %add.17.sums_ref), channel_id=1, source_target_pairs={{0,8},{8,0},{16,24},{24,16},{1,9},{9,1},{17,25},{25,17},{2,10},{10... | collective-permute-start | bytes 12296 | tf_op jit(solution)/shard_map/ppermute | solution.py:312
  20.2 2.7 %collective-permute-start.8 = (f32[272,128]{1,0:T(8,128)S(1)}, f32[272,128]{1,0:T(8,128)S(1)}, u32[]{:S(2)}, u32[]{:S(2)}) collective-permute-start(f32[272,128]{1,0:T(8,128)S(1)} %add.19), channel_id=1, source_target_pairs={{0,16},{8,24},{16,0},{24,8},{1,17},{9,25},{17,1},{25,9},{2,18},{10... | collective-permute-start | bytes 417800 | tf_op jit(solution)/shard_map/ppermute | solution.py:312
  22.8 2.5 %filter.4.local_refs_1_ = f32[3,32,64,128]{3,2,1,0:T(8,128)S(1)} custom-call(bf16[8,32,64,128]{3,2,1,0:T(8,128)(2,1)S(1)} %get-tuple-element.41.high_ref, bf16[8,32,64,128]{3,2,1,0:T(8,128)(2,1)S(1)} %get-tuple-element.42.low_ref, bf16[8,2,64,128]{3,2,1,0:T(8,128)(2,1)S(1)} %get-tuple-element.43.halo_high_ref, ...), custom_call_target="tpu_custom_call" | custom-call | flops 1711276032 | bytes 1048576 | tf_op jit(solution)/shard_map/filter/pallas_call | solution.py:395
  25.3 0.0 collective-permute-done.6.earlier_refs_0_
  25.3 0.4 %collective-permute-start.7 = (f32[8,128]{1,0:T(8,128)S(1)}, f32[8,128]{1,0:T(8,128)S(1)}, u32[]{:S(2)}, u32[]{:S(2)}) collective-permute-start(f32[8,128]{1,0:T(8,128)S(1)} %add.18), channel_id=1, source_target_pairs={{0,16},{8,24},{16,0},{24,8},{1,17},{9,25},{17,1},{25,9},{2,18},{10... | collective-permute-start | bytes 12296 | tf_op jit(solution)/shard_map/ppermute | solution.py:312
  25.7 2.6 %collective-permute-done.8.value_ref = f32[272,128]{1,0:T(8,128)S(1)} collective-permute-done((f32[272,128]{1,0:T(8,128)S(1)}, f32[272,128]{1,0:T(8,128)S(1)}, u32[]{:S(2)}, u32[]{:S(2)}) %collective-permute-start.8) | collective-permute-done | bytes 139296 | tf_op jit(solution)/shard_map/ppermute | solution.py:312
  28.4 0.0 copy-start.2
  28.4 1.7 %filter.5.local_refs_2_ = f32[2,32,64,128]{3,2,1,0:T(8,128)S(1)} custom-call(bf16[8,32,64,128]{3,2,1,0:T(8,128)(2,1)S(1)} %get-tuple-element.41.high_ref, bf16[8,32,64,128]{3,2,1,0:T(8,128)(2,1)S(1)} %get-tuple-element.42.low_ref, bf16[8,2,64,128]{3,2,1,0:T(8,128)(2,1)S(1)} %get-tuple-element.43.halo_high_ref, ...), custom_call_target="tpu_custom_call" | custom-call | flops 1140850688 | bytes 1048576 | tf_op jit(solution)/shard_map/filter/pallas_call | solution.py:395
  30.0 0.0 collective-permute-done.7.earlier_refs_1_
  30.1 4.3 %level.1 = f32[8,64,4096]{2,1,0:T(8,128)} custom-call(f32[3,32,64,128]{3,2,1,0:T(8,128)S(1)} %filter.3.local_refs_0_, f32[3,32,64,128]{3,2,1,0:T(8,128)S(1)} %filter.4.local_refs_1_, f32[2,32,64,128]{3,2,1,0:T(8,128)S(1)} %filter.5.local_refs_2_, bf16[8,512,256]{2,1,0:T(8,128)(2,1)S(1)} %get-tuple-element.60.weight_ref, ...), custom_call_target="tpu_custom_call" | custom-call | tf_op jit(solution)/shard_map/level/pallas_call | solution.py:448
  (16 shorter events, 0.1 us)
Async XLA Ops:
  0.0 5.7 %copy-start.1 = (f32[8,128]{1,0:T(8,128)S(1)}, f32[8,128]{1,0:T(8,128)}, u32[]{:S(2)}) copy-start(f32[8,128]{1,0:T(8,128)} %taps_ref.1) | copy-start | bytes 12292
  0.0 5.7 %copy-start = (f32[8,64,4096]{2,1,0:T(8,128)S(1)}, f32[8,64,4096]{2,1,0:T(8,128)}, u32[]{:S(2)}) copy-start(f32[8,64,4096]{2,1,0:T(8,128)} %phase_hbm.1) | copy-start | bytes 25165828
  1.6 8.3 %collective-permute-start = (f32[4,64,128]{2,1,0:T(8,128)S(1)}, f32[4,64,128]{2,1,0:T(8,128)S(1)}, u32[]{:S(2)}, u32[]{:S(2)}) collective-permute-start(f32[4,64,128]{2,1,0:T(8,128)S(1)} %get-tuple-element.36), channel_id=1, source_target_pairs={{0,1},{1,0},{2,3},{3,2},{4,5},{5,4},{6,7},{7,6},{8,9},{9,8},{10,11... | collective-permute-start | bytes 393224 | tf_op jit(solution)/shard_map/ppermute | solution.py:312
  2.1 7.8 %collective-permute-start.1 = (f32[4,64,128]{2,1,0:T(8,128)S(1)}, f32[4,64,128]{2,1,0:T(8,128)S(1)}, u32[]{:S(2)}, u32[]{:S(2)}) collective-permute-start(f32[4,64,128]{2,1,0:T(8,128)S(1)} %get-tuple-element.37), channel_id=1, source_target_pairs={{0,7},{1,2},{2,1},{3,4},{4,3},{5,6},{6,5},{7,0},{8,15},{9,10},{10,... | collective-permute-start | bytes 393224 | tf_op jit(solution)/shard_map/ppermute | solution.py:341
  10.1 1.7 %collective-permute-start.3 = (f32[8,128]{1,0:T(8,128)S(1)}, f32[8,128]{1,0:T(8,128)S(1)}, u32[]{:S(2)}, u32[]{:S(2)}) collective-permute-start(f32[8,128]{1,0:T(8,128)S(1)} %get-tuple-element.40), channel_id=1, source_target_pairs={{0,1},{1,0},{2,3},{3,2},{4,5},{5,4},{6,7},{7,6},{8,9},{9,8},{10,11... | collective-permute-start | bytes 12296 | tf_op jit(solution)/shard_map/ppermute | solution.py:312
  10.2 6.7 %collective-permute-start.2 = (f32[272,128]{1,0:T(8,128)S(1)}, f32[272,128]{1,0:T(8,128)S(1)}, u32[]{:S(2)}, u32[]{:S(2)}) collective-permute-start(f32[272,128]{1,0:T(8,128)S(1)} %constant_dynamic-update-slice_fusion), channel_id=1, source_target_pairs={{0,8},{8,0},{16,24},{24,16},{1,9},{9,1},{17,25},{25,17},{2,10},{10... | collective-permute-start | bytes 417800 | tf_op jit(solution)/shard_map/ppermute | solution.py:312
  11.8 3.7 %collective-permute-start.4 = (f32[8,128]{1,0:T(8,128)S(1)}, f32[8,128]{1,0:T(8,128)S(1)}, u32[]{:S(2)}, u32[]{:S(2)}) collective-permute-start(f32[8,128]{1,0:T(8,128)S(1)} %add.15), channel_id=1, source_target_pairs={{0,2},{1,3},{2,0},{3,1},{4,6},{5,7},{6,4},{7,5},{8,10},{9,11},{10,... | collective-permute-start | bytes 12296 | tf_op jit(solution)/shard_map/ppermute | solution.py:312
  15.6 3.7 %collective-permute-start.5 = (f32[8,128]{1,0:T(8,128)S(1)}, f32[8,128]{1,0:T(8,128)S(1)}, u32[]{:S(2)}, u32[]{:S(2)}) collective-permute-start(f32[8,128]{1,0:T(8,128)S(1)} %add.16), channel_id=1, source_target_pairs={{0,4},{1,5},{2,6},{3,7},{4,0},{5,1},{6,2},{7,3},{8,12},{9,13},{10,... | collective-permute-start | bytes 12296 | tf_op jit(solution)/shard_map/ppermute | solution.py:312
  19.3 6.1 %collective-permute-start.6 = (f32[8,128]{1,0:T(8,128)S(1)}, f32[8,128]{1,0:T(8,128)S(1)}, u32[]{:S(2)}, u32[]{:S(2)}) collective-permute-start(f32[8,128]{1,0:T(8,128)S(1)} %add.17.sums_ref), channel_id=1, source_target_pairs={{0,8},{8,0},{16,24},{24,16},{1,9},{9,1},{17,25},{25,17},{2,10},{10... | collective-permute-start | bytes 12296 | tf_op jit(solution)/shard_map/ppermute | solution.py:312
  20.2 8.2 %collective-permute-start.8 = (f32[272,128]{1,0:T(8,128)S(1)}, f32[272,128]{1,0:T(8,128)S(1)}, u32[]{:S(2)}, u32[]{:S(2)}) collective-permute-start(f32[272,128]{1,0:T(8,128)S(1)} %add.19), channel_id=1, source_target_pairs={{0,16},{8,24},{16,0},{24,8},{1,17},{9,25},{17,1},{25,9},{2,18},{10... | collective-permute-start | bytes 417800 | tf_op jit(solution)/shard_map/ppermute | solution.py:312
  25.3 4.7 %collective-permute-start.7 = (f32[8,128]{1,0:T(8,128)S(1)}, f32[8,128]{1,0:T(8,128)S(1)}, u32[]{:S(2)}, u32[]{:S(2)}) collective-permute-start(f32[8,128]{1,0:T(8,128)S(1)} %add.18), channel_id=1, source_target_pairs={{0,16},{8,24},{16,0},{24,8},{1,17},{9,25},{17,1},{25,9},{2,18},{10... | collective-permute-start | bytes 12296 | tf_op jit(solution)/shard_map/ppermute | solution.py:312
  28.4 1.7 %copy-start.2 = (f32[8]{0:T(128)S(1)}, f32[8]{0:T(128)}, u32[]{:S(2)}) copy-start(f32[8]{0:T(128)} %coupling_ref.1) | copy-start | bytes 100

commit v16 on v15

--- a/solution.py
+++ b/solution.py
@@ -317,7 +317,7 @@
     blocks = width // LANES
     steps, places = lax.axis_size("tm"), lax.axis_size("chan")
     population = cables * width * places
-    bounds = [0, 3 * cables // 8, 3 * cables // 4, cables]
+    bounds = [0, 3 * cables // 8, 5 * cables // 8, cables]
     parts = len(bounds) - 1
     wrap_count = pltpu.with_memory_space_constraint(wrap_count, pltpu.HBM)
     whole = pl.BlockSpec(memory_space=pltpu.VMEM)

time: 34.5 us -> 33.1 us (0.959)
  waiting for transfers between devices: 4.93 us -> 1.56 us
  starting transfers between devices: 12.3 us -> 14.3 us
    ppermute x8, waiting for transfers between devices: 4.92 us -> 1.56 us  [swapped(): lax.ppermute(value, axis, [(i, i ^ bit) for i in range(lax.axis_size(axis...]
    ppermute x8, starting transfers between devices: 8.73 us -> 10.7 us  [swapped(): lax.ppermute(value, axis, [(i, i ^ bit) for i in range(lax.axis_size(axis...]
  transfers between devices with their start and end apart: 9 -> 9, of which waited for: 2 -> 2; matrix products, arithmetic and copies ran while one was open for 0% -> 0% of each run, Pallas kernels for 32% -> 33%
where the time goes in v16:
time: 33.1 us; the launch traced here: 32.9 us
  Pallas kernels  16.9 us (51%)
  starting transfers between devices  14.3 us (43%)
  waiting for transfers between devices  1.56 us (5%)
    ppermute x8, starting transfers between devices, swapped(): lax.ppermute(value, axis, [(i, i ^ bit) for i in range(lax.axis_size(axis...  10.7 us
    pallas_call x3, Pallas kernels, filtered(): pl.pallas_call(functools.partial(filter_kernel, bounds[part]), out_shape=...  6.62 us
    pallas_call x1, Pallas kernels, shards(): pl.pallas_call(functools.partial(level_kernel, population), out_shape=jax...  4.28 us
    pallas_call x1, Pallas kernels, shards(): pl.pallas_call(increments_kernel, out_shape=(pltpu.VMEM((cables, blocks,...  4.21 us
    ppermute x1, starting transfers between devices, shards(): outer = lax.ppermute(outer, 'chan', outer_pairs)  3.56 us
    pallas_call x1, Pallas kernels, shards(): pl.pallas_call(edges_kernel, out_shape=[pltpu.VMEM((cables // 2, time, LA...  1.59 us
    ppermute x8, waiting for transfers between devices, swapped(): lax.ppermute(value, axis, [(i, i ^ bit) for i in range(lax.axis_size(axis...  1.56 us
  transfers between devices with their start and end apart: 9, of which 2 were waited for; matrix products, arithmetic and copies ran while one was open for 0% of the time, Pallas kernels for 33%

profile of v16, /device:TPU:0, one launch (start us, length us, event | category | flops | bytes accessed | tf_op | source)
XLA Modules:
  0.0 32.9 jit_solution(636974169865684274)
XLA Ops:
  0.0 1.6 %edges.1 = (f32[4,64,128]{2,1,0:T(8,128)S(1)}, f32[4,64,128]{2,1,0:T(8,128)S(1)}) custom-call(f32[8,64,4096]{2,1,0:T(8,128)} %phase_hbm.1, s32[8,64,4096]{2,1,0:T(8,128)} %wrap_hbm.3), custom_call_target="tpu_custom_call" | custom-call | tf_op jit(solution)/shard_map/edges/pallas_call | solution.py:327
  1.6 0.5 %collective-permute-start = (f32[4,64,128]{2,1,0:T(8,128)S(1)}, f32[4,64,128]{2,1,0:T(8,128)S(1)}, u32[]{:S(2)}, u32[]{:S(2)}) collective-permute-start(f32[4,64,128]{2,1,0:T(8,128)S(1)} %get-tuple-element.36), channel_id=1, source_target_pairs={{0,1},{1,0},{2,3},{3,2},{4,5},{5,4},{6,7},{7,6},{8,9},{9,8},{10,11... | collective-permute-start | bytes 393224 | tf_op jit(solution)/shard_map/ppermute | solution.py:312
  2.1 3.6 %collective-permute-start.1 = (f32[4,64,128]{2,1,0:T(8,128)S(1)}, f32[4,64,128]{2,1,0:T(8,128)S(1)}, u32[]{:S(2)}, u32[]{:S(2)}) collective-permute-start(f32[4,64,128]{2,1,0:T(8,128)S(1)} %get-tuple-element.37), channel_id=1, source_target_pairs={{0,7},{1,2},{2,1},{3,4},{4,3},{5,6},{6,5},{7,0},{8,15},{9,10},{10,... | collective-permute-start | bytes 393224 | tf_op jit(solution)/shard_map/ppermute | solution.py:341
  5.7 4.2 %increments.1 = (bf16[8,32,64,128]{3,2,1,0:T(8,128)(2,1)S(1)}, bf16[8,32,64,128]{3,2,1,0:T(8,128)(2,1)S(1)}, f32[256,128]{1,0:T(8,128)S(1)}, f32[8,128]{1,0:T(8,128)S(1)}, bf16[8,512,256]{2,1,0:T(8,128)(2,1)S(1)}) custom-call(f32[8,64,4096]{2,1,0:T(8,128)S(1)} %copy-done, s32[8,64,4096]{2,1,0:T(8,128)} %wrap_hbm.3, f32[8,128]{1,0:T(8,128)S(1)} %copy-done.1), custom_call_target="tpu_custom_call" | custom-call | bytes 8388608 | tf_op jit(solution)/shard_map/increments/pallas_call | solution.py:344
  9.9 0.0 collective-permute-done.inner_ref
  9.9 0.2 halo.1
  10.1 0.1 collective-permute-start.3
  10.2 1.6 %collective-permute-start.2 = (f32[272,128]{1,0:T(8,128)S(1)}, f32[272,128]{1,0:T(8,128)S(1)}, u32[]{:S(2)}, u32[]{:S(2)}) collective-permute-start(f32[272,128]{1,0:T(8,128)S(1)} %constant_dynamic-update-slice_fusion), channel_id=1, source_target_pairs={{0,8},{8,0},{16,24},{24,16},{1,9},{9,1},{17,25},{25,17},{2,10},{10... | collective-permute-start | bytes 417800 | tf_op jit(solution)/shard_map/ppermute | solution.py:312
  11.8 0.0 collective-permute-done.3
  11.8 1.2 %collective-permute-start.4 = (f32[8,128]{1,0:T(8,128)S(1)}, f32[8,128]{1,0:T(8,128)S(1)}, u32[]{:S(2)}, u32[]{:S(2)}) collective-permute-start(f32[8,128]{1,0:T(8,128)S(1)} %add.15), channel_id=1, source_target_pairs={{0,2},{1,3},{2,0},{3,1},{4,6},{5,7},{6,4},{7,5},{8,10},{9,11},{10,... | collective-permute-start | bytes 12296 | tf_op jit(solution)/shard_map/ppermute | solution.py:312
  13.1 2.5 %filter.3.local_refs_0_ = f32[3,32,64,128]{3,2,1,0:T(8,128)S(1)} custom-call(bf16[8,32,64,128]{3,2,1,0:T(8,128)(2,1)S(1)} %get-tuple-element.41.high_ref, bf16[8,32,64,128]{3,2,1,0:T(8,128)(2,1)S(1)} %get-tuple-element.42.low_ref, bf16[8,2,64,128]{3,2,1,0:T(8,128)(2,1)S(1)} %get-tuple-element.43.halo_high_ref, ...), custom_call_target="tpu_custom_call" | custom-call | flops 1711276032 | bytes 1048576 | tf_op jit(solution)/shard_map/filter/pallas_call | solution.py:395
  15.6 1.3 %collective-permute-start.5 = (f32[8,128]{1,0:T(8,128)S(1)}, f32[8,128]{1,0:T(8,128)S(1)}, u32[]{:S(2)}, u32[]{:S(2)}) collective-permute-start(f32[8,128]{1,0:T(8,128)S(1)} %add.16), channel_id=1, source_target_pairs={{0,4},{1,5},{2,6},{3,7},{4,0},{5,1},{6,2},{7,3},{8,12},{9,13},{10,... | collective-permute-start | bytes 12296 | tf_op jit(solution)/shard_map/ppermute | solution.py:312
  16.9 0.0 collective-permute-done.2.value_ref
  16.9 2.7 %collective-permute-start.8 = (f32[272,128]{1,0:T(8,128)S(1)}, f32[272,128]{1,0:T(8,128)S(1)}, u32[]{:S(2)}, u32[]{:S(2)}) collective-permute-start(f32[272,128]{1,0:T(8,128)S(1)} %add.19), channel_id=1, source_target_pairs={{0,16},{8,24},{16,0},{24,8},{1,17},{9,25},{17,1},{25,9},{2,18},{10... | collective-permute-start | bytes 417800 | tf_op jit(solution)/shard_map/ppermute | solution.py:312
  19.6 0.0 collective-permute-done.5
  19.7 1.1 %collective-permute-start.6 = (f32[8,128]{1,0:T(8,128)S(1)}, f32[8,128]{1,0:T(8,128)S(1)}, u32[]{:S(2)}, u32[]{:S(2)}) collective-permute-start(f32[8,128]{1,0:T(8,128)S(1)} %add.17.sums_ref), channel_id=1, source_target_pairs={{0,8},{8,0},{16,24},{24,16},{1,9},{9,1},{17,25},{25,17},{2,10},{10... | collective-permute-start | bytes 12296 | tf_op jit(solution)/shard_map/ppermute | solution.py:312
  20.8 1.6 %filter.4.local_refs_1_ = f32[2,32,64,128]{3,2,1,0:T(8,128)S(1)} custom-call(bf16[8,32,64,128]{3,2,1,0:T(8,128)(2,1)S(1)} %get-tuple-element.41.high_ref, bf16[8,32,64,128]{3,2,1,0:T(8,128)(2,1)S(1)} %get-tuple-element.42.low_ref, bf16[8,2,64,128]{3,2,1,0:T(8,128)(2,1)S(1)} %get-tuple-element.43.halo_high_ref, ...), custom_call_target="tpu_custom_call" | custom-call | flops 1140850688 | bytes 1048576 | tf_op jit(solution)/shard_map/filter/pallas_call | solution.py:395
  22.4 0.9 %collective-permute-done.6.earlier_refs_0_ = f32[8,128]{1,0:T(8,128)S(1)} collective-permute-done((f32[8,128]{1,0:T(8,128)S(1)}, f32[8,128]{1,0:T(8,128)S(1)}, u32[]{:S(2)}, u32[]{:S(2)}) %collective-permute-start.6) | collective-permute-done | bytes 4128 | tf_op jit(solution)/shard_map/ppermute | solution.py:312
  23.3 2.1 %collective-permute-start.7 = (f32[8,128]{1,0:T(8,128)S(1)}, f32[8,128]{1,0:T(8,128)S(1)}, u32[]{:S(2)}, u32[]{:S(2)}) collective-permute-start(f32[8,128]{1,0:T(8,128)S(1)} %add.18), channel_id=1, source_target_pairs={{0,16},{8,24},{16,0},{24,8},{1,17},{9,25},{17,1},{25,9},{2,18},{10... | collective-permute-start | bytes 12296 | tf_op jit(solution)/shard_map/ppermute | solution.py:312
  25.5 0.7 %collective-permute-done.8.value_ref = f32[272,128]{1,0:T(8,128)S(1)} collective-permute-done((f32[272,128]{1,0:T(8,128)S(1)}, f32[272,128]{1,0:T(8,128)S(1)}, u32[]{:S(2)}, u32[]{:S(2)}) %collective-permute-start.8) | collective-permute-done | bytes 139296 | tf_op jit(solution)/shard_map/ppermute | solution.py:312
  26.1 0.0 copy-start.2
  26.1 2.5 %filter.5.local_refs_2_ = f32[3,32,64,128]{3,2,1,0:T(8,128)S(1)} custom-call(bf16[8,32,64,128]{3,2,1,0:T(8,128)(2,1)S(1)} %get-tuple-element.41.high_ref, bf16[8,32,64,128]{3,2,1,0:T(8,128)(2,1)S(1)} %get-tuple-element.42.low_ref, bf16[8,2,64,128]{3,2,1,0:T(8,128)(2,1)S(1)} %get-tuple-element.43.halo_high_ref, ...), custom_call_target="tpu_custom_call" | custom-call | flops 1711276032 | bytes 1048576 | tf_op jit(solution)/shard_map/filter/pallas_call | solution.py:395
  28.6 0.0 collective-permute-done.7.earlier_refs_1_
  28.7 4.3 %level.1 = f32[8,64,4096]{2,1,0:T(8,128)} custom-call(f32[3,32,64,128]{3,2,1,0:T(8,128)S(1)} %filter.3.local_refs_0_, f32[2,32,64,128]{3,2,1,0:T(8,128)S(1)} %filter.4.local_refs_1_, f32[3,32,64,128]{3,2,1,0:T(8,128)S(1)} %filter.5.local_refs_2_, bf16[8,512,256]{2,1,0:T(8,128)(2,1)S(1)} %get-tuple-element.60.weight_ref, ...), custom_call_target="tpu_custom_call" | custom-call | tf_op jit(solution)/shard_map/level/pallas_call | solution.py:448
  (16 shorter events, 0.1 us)
Async XLA Ops:
  0.0 5.7 %copy-start.1 = (f32[8,128]{1,0:T(8,128)S(1)}, f32[8,128]{1,0:T(8,128)}, u32[]{:S(2)}) copy-start(f32[8,128]{1,0:T(8,128)} %taps_ref.1) | copy-start | bytes 12292
  0.0 5.7 %copy-start = (f32[8,64,4096]{2,1,0:T(8,128)S(1)}, f32[8,64,4096]{2,1,0:T(8,128)}, u32[]{:S(2)}) copy-start(f32[8,64,4096]{2,1,0:T(8,128)} %phase_hbm.1) | copy-start | bytes 25165828
  1.6 8.3 %collective-permute-start = (f32[4,64,128]{2,1,0:T(8,128)S(1)}, f32[4,64,128]{2,1,0:T(8,128)S(1)}, u32[]{:S(2)}, u32[]{:S(2)}) collective-permute-start(f32[4,64,128]{2,1,0:T(8,128)S(1)} %get-tuple-element.36), channel_id=1, source_target_pairs={{0,1},{1,0},{2,3},{3,2},{4,5},{5,4},{6,7},{7,6},{8,9},{9,8},{10,11... | collective-permute-start | bytes 393224 | tf_op jit(solution)/shard_map/ppermute | solution.py:312
  2.1 7.8 %collective-permute-start.1 = (f32[4,64,128]{2,1,0:T(8,128)S(1)}, f32[4,64,128]{2,1,0:T(8,128)S(1)}, u32[]{:S(2)}, u32[]{:S(2)}) collective-permute-start(f32[4,64,128]{2,1,0:T(8,128)S(1)} %get-tuple-element.37), channel_id=1, source_target_pairs={{0,7},{1,2},{2,1},{3,4},{4,3},{5,6},{6,5},{7,0},{8,15},{9,10},{10,... | collective-permute-start | bytes 393224 | tf_op jit(solution)/shard_map/ppermute | solution.py:341
  10.1 1.7 %collective-permute-start.3 = (f32[8,128]{1,0:T(8,128)S(1)}, f32[8,128]{1,0:T(8,128)S(1)}, u32[]{:S(2)}, u32[]{:S(2)}) collective-permute-start(f32[8,128]{1,0:T(8,128)S(1)} %get-tuple-element.40), channel_id=1, source_target_pairs={{0,1},{1,0},{2,3},{3,2},{4,5},{5,4},{6,7},{7,6},{8,9},{9,8},{10,11... | collective-permute-start | bytes 12296 | tf_op jit(solution)/shard_map/ppermute | solution.py:312
  10.2 6.7 %collective-permute-start.2 = (f32[272,128]{1,0:T(8,128)S(1)}, f32[272,128]{1,0:T(8,128)S(1)}, u32[]{:S(2)}, u32[]{:S(2)}) collective-permute-start(f32[272,128]{1,0:T(8,128)S(1)} %constant_dynamic-update-slice_fusion), channel_id=1, source_target_pairs={{0,8},{8,0},{16,24},{24,16},{1,9},{9,1},{17,25},{25,17},{2,10},{10... | collective-permute-start | bytes 417800 | tf_op jit(solution)/shard_map/ppermute | solution.py:312
  11.8 3.7 %collective-permute-start.4 = (f32[8,128]{1,0:T(8,128)S(1)}, f32[8,128]{1,0:T(8,128)S(1)}, u32[]{:S(2)}, u32[]{:S(2)}) collective-permute-start(f32[8,128]{1,0:T(8,128)S(1)} %add.15), channel_id=1, source_target_pairs={{0,2},{1,3},{2,0},{3,1},{4,6},{5,7},{6,4},{7,5},{8,10},{9,11},{10,... | collective-permute-start | bytes 12296 | tf_op jit(solution)/shard_map/ppermute | solution.py:312
  15.6 4.1 %collective-permute-start.5 = (f32[8,128]{1,0:T(8,128)S(1)}, f32[8,128]{1,0:T(8,128)S(1)}, u32[]{:S(2)}, u32[]{:S(2)}) collective-permute-start(f32[8,128]{1,0:T(8,128)S(1)} %add.16), channel_id=1, source_target_pairs={{0,4},{1,5},{2,6},{3,7},{4,0},{5,1},{6,2},{7,3},{8,12},{9,13},{10,... | collective-permute-start | bytes 12296 | tf_op jit(solution)/shard_map/ppermute | solution.py:312
  16.9 9.2 %collective-permute-start.8 = (f32[272,128]{1,0:T(8,128)S(1)}, f32[272,128]{1,0:T(8,128)S(1)}, u32[]{:S(2)}, u32[]{:S(2)}) collective-permute-start(f32[272,128]{1,0:T(8,128)S(1)} %add.19), channel_id=1, source_target_pairs={{0,16},{8,24},{16,0},{24,8},{1,17},{9,25},{17,1},{25,9},{2,18},{10... | collective-permute-start | bytes 417800 | tf_op jit(solution)/shard_map/ppermute | solution.py:312
  19.7 3.7 %collective-permute-start.6 = (f32[8,128]{1,0:T(8,128)S(1)}, f32[8,128]{1,0:T(8,128)S(1)}, u32[]{:S(2)}, u32[]{:S(2)}) collective-permute-start(f32[8,128]{1,0:T(8,128)S(1)} %add.17.sums_ref), channel_id=1, source_target_pairs={{0,8},{8,0},{16,24},{24,16},{1,9},{9,1},{17,25},{25,17},{2,10},{10... | collective-permute-start | bytes 12296 | tf_op jit(solution)/shard_map/ppermute | solution.py:312
  23.3 5.3 %collective-permute-start.7 = (f32[8,128]{1,0:T(8,128)S(1)}, f32[8,128]{1,0:T(8,128)S(1)}, u32[]{:S(2)}, u32[]{:S(2)}) collective-permute-start(f32[8,128]{1,0:T(8,128)S(1)} %add.18), channel_id=1, source_target_pairs={{0,16},{8,24},{16,0},{24,8},{1,17},{9,25},{17,1},{25,9},{2,18},{10... | collective-permute-start | bytes 12296 | tf_op jit(solution)/shard_map/ppermute | solution.py:312
  26.1 2.5 %copy-start.2 = (f32[8]{0:T(128)S(1)}, f32[8]{0:T(128)}, u32[]{:S(2)}) copy-start(f32[8]{0:T(128)} %coupling_ref.1) | copy-start | bytes 100

commit v17 on v15

--- a/solution.py
+++ b/solution.py
@@ -209,8 +209,8 @@
             previous = following
 
 
-def masked_kernel(bit, value_ref, masked_ref):
-    later = (lax.axis_index("tm") & bit) != 0
+def masked_kernel(value_ref, masked_ref):
+    later = (lax.axis_index("tm") & 1) != 0
     masked_ref[...] = jnp.where(later, value_ref[...], 0.0)
 
 
@@ -229,7 +229,10 @@
     earlier = jnp.zeros((SUBLANES, LANES), jnp.float32)
     for bit, ref in enumerate(earlier_refs):
         earlier = earlier + jnp.where((step & (1 << bit)) != 0, ref[...], 0.0)
-    offset_ref[...] = functools.reduce(jnp.add, [ref[...] for ref in totals_refs])
+    offset = totals_refs[0][...]
+    for bit, ref in enumerate(totals_refs[1:], 1):
+        offset = offset + jnp.where((step & (1 << bit)) != 0, ref[...], 0.0)
+    offset_ref[...] = offset
     earlier = earlier[SUBLANES - 1 :, groups - 1 : groups]
     common = (sums_ref[...] + earlier) * (1.0 / population)
     columns = [
@@ -318,6 +321,7 @@
     steps, places = lax.axis_size("tm"), lax.axis_size("chan")
     population = cables * width * places
     bounds = [0, 3 * cables // 8, 3 * cables // 4, cables]
+    weighed = (3, 1, 1)
     parts = len(bounds) - 1
     wrap_count = pltpu.with_memory_space_constraint(wrap_count, pltpu.HBM)
     whole = pl.BlockSpec(memory_space=pltpu.VMEM)
@@ -377,9 +381,9 @@
         name="halo",
     )(inner, outer)
 
-    def from_earlier(value, number):
+    def from_earlier(value):
         return pl.pallas_call(
-            functools.partial(masked_kernel, 1 << number),
+            masked_kernel,
             out_shape=pltpu.VMEM(value.shape, value.dtype),
             in_specs=[whole],
             out_specs=whole,
@@ -399,7 +403,7 @@
             out_specs=whole,
             compiler_params=pltpu.CompilerParams(vmem_limit_bytes=16 << 20),
             cost_estimate=pl.CostEstimate(
-                flops=2 * share * (blocks + 2) * time * 8 * LANES * LANES,
+                flops=weighed[part] * (cables * (blocks + 2) * time * 2 * LANES * LANES),
                 bytes_accessed=1 << 20,
                 transcendentals=0,
             ),
@@ -419,15 +423,12 @@
             ready = None
         elif number > 0 and len(local) < parts:
             tied, sums = lax.optimization_barrier((weight, sums))
-            if number == len(rounds) - 1 and 1 << len(received) >= steps:
-                received[1] = from_earlier(received[1], 1)
-                received[1], tied = lax.optimization_barrier((received[1], tied))
             part = filtered(len(local), tied)
             incoming, part = lax.optimization_barrier((incoming, part))
             local.append(part)
         if number == 2:
             first, sums = lax.optimization_barrier((received[0], sums))
-            masked = from_earlier(first, 0)
+            masked = from_earlier(first)
             incoming, masked = lax.optimization_barrier((incoming, masked))
         if number == 1 and 1 << len(received) < steps:
             earlier, local[-1] = lax.optimization_barrier((received[-1], local[-1]))

time: 34.5 us -> 32.3 us (0.936)
  waiting for transfers between devices: 4.93 us -> 0.83 us
  starting transfers between devices: 12.3 us -> 14.3 us
    ppermute x8, waiting for transfers between devices: 4.92 us -> 0.83 us  [swapped(): lax.ppermute(value, axis, [(i, i ^ bit) for i in range(lax.axis_size(axis...]
    ppermute x8, starting transfers between devices: 8.73 us -> 10.7 us  [swapped(): lax.ppermute(value, axis, [(i, i ^ bit) for i in range(lax.axis_size(axis...]
  transfers between devices with their start and end apart: 9 -> 9, of which waited for: 2 -> 2; matrix products, arithmetic and copies ran while one was open for 0% -> 0% of each run, Pallas kernels for 32% -> 34%
where the time goes in v17:
time: 32.3 us; the launch traced here: 32.1 us
  Pallas kernels  16.9 us (52%)
  starting transfers between devices  14.3 us (44%)
  waiting for transfers between devices  0.83 us (3%)
    ppermute x8, starting transfers between devices, swapped(): lax.ppermute(value, axis, [(i, i ^ bit) for i in range(lax.axis_size(axis...  10.7 us
    pallas_call x3, Pallas kernels, filtered(): pl.pallas_call(functools.partial(filter_kernel, bounds[part]), out_shape=...  6.6 us
    pallas_call x1, Pallas kernels, shards(): pl.pallas_call(functools.partial(level_kernel, population), out_shape=jax...  4.28 us
    pallas_call x1, Pallas kernels, shards(): pl.pallas_call(increments_kernel, out_shape=(pltpu.VMEM((cables, blocks,...  4.21 us
    ppermute x1, starting transfers between devices, shards(): outer = lax.ppermute(outer, 'chan', outer_pairs)  3.56 us
    pallas_call x1, Pallas kernels, shards(): pl.pallas_call(edges_kernel, out_shape=[pltpu.VMEM((cables // 2, time, LA...  1.59 us
    ppermute x8, waiting for transfers between devices, swapped(): lax.ppermute(value, axis, [(i, i ^ bit) for i in range(lax.axis_size(axis...  0.83 us
  transfers between devices with their start and end apart: 9, of which 2 were waited for; matrix products, arithmetic and copies ran while one was open for 0% of the time, Pallas kernels for 34%

profile of v17, /device:TPU:0, one launch (start us, length us, event | category | flops | bytes accessed | tf_op | source)
XLA Modules:
  0.0 32.1 jit_solution(7801107051444883684)
XLA Ops:
  0.0 1.6 %edges.1 = (f32[4,64,128]{2,1,0:T(8,128)S(1)}, f32[4,64,128]{2,1,0:T(8,128)S(1)}) custom-call(f32[8,64,4096]{2,1,0:T(8,128)} %phase_hbm.1, s32[8,64,4096]{2,1,0:T(8,128)} %wrap_hbm.3), custom_call_target="tpu_custom_call" | custom-call | tf_op jit(solution)/shard_map/edges/pallas_call | solution.py:331
  1.6 0.5 %collective-permute-start = (f32[4,64,128]{2,1,0:T(8,128)S(1)}, f32[4,64,128]{2,1,0:T(8,128)S(1)}, u32[]{:S(2)}, u32[]{:S(2)}) collective-permute-start(f32[4,64,128]{2,1,0:T(8,128)S(1)} %get-tuple-element.34), channel_id=1, source_target_pairs={{0,1},{1,0},{2,3},{3,2},{4,5},{5,4},{6,7},{7,6},{8,9},{9,8},{10,11... | collective-permute-start | bytes 393224 | tf_op jit(solution)/shard_map/ppermute | solution.py:315
  2.1 3.6 %collective-permute-start.1 = (f32[4,64,128]{2,1,0:T(8,128)S(1)}, f32[4,64,128]{2,1,0:T(8,128)S(1)}, u32[]{:S(2)}, u32[]{:S(2)}) collective-permute-start(f32[4,64,128]{2,1,0:T(8,128)S(1)} %get-tuple-element.35), channel_id=1, source_target_pairs={{0,7},{1,2},{2,1},{3,4},{4,3},{5,6},{6,5},{7,0},{8,15},{9,10},{10,... | collective-permute-start | bytes 393224 | tf_op jit(solution)/shard_map/ppermute | solution.py:345
  5.7 4.2 %increments.1 = (bf16[8,32,64,128]{3,2,1,0:T(8,128)(2,1)S(1)}, bf16[8,32,64,128]{3,2,1,0:T(8,128)(2,1)S(1)}, f32[256,128]{1,0:T(8,128)S(1)}, f32[8,128]{1,0:T(8,128)S(1)}, bf16[8,512,256]{2,1,0:T(8,128)(2,1)S(1)}) custom-call(f32[8,64,4096]{2,1,0:T(8,128)S(1)} %copy-done, s32[8,64,4096]{2,1,0:T(8,128)} %wrap_hbm.3, f32[8,128]{1,0:T(8,128)S(1)} %copy-done.1), custom_call_target="tpu_custom_call" | custom-call | bytes 8388608 | tf_op jit(solution)/shard_map/increments/pallas_call | solution.py:348
  9.9 0.0 collective-permute-done.inner_ref
  9.9 0.0 collective-permute-done.1.outer_ref
  9.9 0.2 halo.1
  10.1 0.1 collective-permute-start.3
  10.2 1.6 %collective-permute-start.2 = (f32[272,128]{1,0:T(8,128)S(1)}, f32[272,128]{1,0:T(8,128)S(1)}, u32[]{:S(2)}, u32[]{:S(2)}) collective-permute-start(f32[272,128]{1,0:T(8,128)S(1)} %constant_dynamic-update-slice_fusion), channel_id=1, source_target_pairs={{0,8},{8,0},{16,24},{24,16},{1,9},{9,1},{17,25},{25,17},{2,10},{10... | collective-permute-start | bytes 417800 | tf_op jit(solution)/shard_map/ppermute | solution.py:315
  11.8 0.0 collective-permute-done.3
  11.8 1.2 %collective-permute-start.4 = (f32[8,128]{1,0:T(8,128)S(1)}, f32[8,128]{1,0:T(8,128)S(1)}, u32[]{:S(2)}, u32[]{:S(2)}) collective-permute-start(f32[8,128]{1,0:T(8,128)S(1)} %add.15), channel_id=1, source_target_pairs={{0,2},{1,3},{2,0},{3,1},{4,6},{5,7},{6,4},{7,5},{8,10},{9,11},{10,... | collective-permute-start | bytes 12296 | tf_op jit(solution)/shard_map/ppermute | solution.py:315
  13.1 2.5 %filter.3.local_refs_0_ = f32[3,32,64,128]{3,2,1,0:T(8,128)S(1)} custom-call(bf16[8,32,64,128]{3,2,1,0:T(8,128)(2,1)S(1)} %get-tuple-element.39.high_ref, bf16[8,32,64,128]{3,2,1,0:T(8,128)(2,1)S(1)} %get-tuple-element.40.low_ref, bf16[8,2,64,128]{3,2,1,0:T(8,128)(2,1)S(1)} %get-tuple-element.41.halo_high_ref, ...), custom_call_target="tpu_custom_call" | custom-call | flops 1711276032 | bytes 1048576 | tf_op jit(solution)/shard_map/filter/pallas_call | solution.py:399
  15.6 0.0 collective-permute-done.4
  15.6 1.3 %collective-permute-start.5 = (f32[8,128]{1,0:T(8,128)S(1)}, f32[8,128]{1,0:T(8,128)S(1)}, u32[]{:S(2)}, u32[]{:S(2)}) collective-permute-start(f32[8,128]{1,0:T(8,128)S(1)} %add.16), channel_id=1, source_target_pairs={{0,4},{1,5},{2,6},{3,7},{4,0},{5,1},{6,2},{7,3},{8,12},{9,13},{10,... | collective-permute-start | bytes 12296 | tf_op jit(solution)/shard_map/ppermute | solution.py:315
  16.9 0.0 collective-permute-done.2.value_ref
  16.9 2.7 %collective-permute-start.8 = (f32[272,128]{1,0:T(8,128)S(1)}, f32[272,128]{1,0:T(8,128)S(1)}, u32[]{:S(2)}, u32[]{:S(2)}) collective-permute-start(f32[272,128]{1,0:T(8,128)S(1)} %add.19), channel_id=1, source_target_pairs={{0,16},{8,24},{16,0},{24,8},{1,17},{9,25},{17,1},{25,9},{2,18},{10... | collective-permute-start | bytes 417800 | tf_op jit(solution)/shard_map/ppermute | solution.py:315
  19.6 0.0 collective-permute-done.5
  19.7 1.1 %collective-permute-start.6 = (f32[8,128]{1,0:T(8,128)S(1)}, f32[8,128]{1,0:T(8,128)S(1)}, u32[]{:S(2)}, u32[]{:S(2)}) collective-permute-start(f32[8,128]{1,0:T(8,128)S(1)} %add.17.sums_ref), channel_id=1, source_target_pairs={{0,8},{8,0},{16,24},{24,16},{1,9},{9,1},{17,25},{25,17},{2,10},{10... | collective-permute-start | bytes 12296 | tf_op jit(solution)/shard_map/ppermute | solution.py:315
  20.8 2.5 %filter.4.local_refs_1_ = f32[3,32,64,128]{3,2,1,0:T(8,128)S(1)} custom-call(bf16[8,32,64,128]{3,2,1,0:T(8,128)(2,1)S(1)} %get-tuple-element.39.high_ref, bf16[8,32,64,128]{3,2,1,0:T(8,128)(2,1)S(1)} %get-tuple-element.40.low_ref, bf16[8,2,64,128]{3,2,1,0:T(8,128)(2,1)S(1)} %get-tuple-element.41.halo_high_ref, ...), custom_call_target="tpu_custom_call" | custom-call | flops 570425344 | bytes 1048576 | tf_op jit(solution)/shard_map/filter/pallas_call | solution.py:399
  23.3 0.1 collective-permute-done.6.earlier_refs_0_
  23.3 2.1 %collective-permute-start.7 = (f32[8,128]{1,0:T(8,128)S(1)}, f32[8,128]{1,0:T(8,128)S(1)}, u32[]{:S(2)}, u32[]{:S(2)}) collective-permute-start(f32[8,128]{1,0:T(8,128)S(1)} %add.18), channel_id=1, source_target_pairs={{0,16},{8,24},{16,0},{24,8},{1,17},{9,25},{17,1},{25,9},{2,18},{10... | collective-permute-start | bytes 12296 | tf_op jit(solution)/shard_map/ppermute | solution.py:315
  25.5 1.6 %filter.5.local_refs_2_ = f32[2,32,64,128]{3,2,1,0:T(8,128)S(1)} custom-call(bf16[8,32,64,128]{3,2,1,0:T(8,128)(2,1)S(1)} %get-tuple-element.39.high_ref, bf16[8,32,64,128]{3,2,1,0:T(8,128)(2,1)S(1)} %get-tuple-element.40.low_ref, bf16[8,2,64,128]{3,2,1,0:T(8,128)(2,1)S(1)} %get-tuple-element.41.halo_high_ref, ...), custom_call_target="tpu_custom_call" | custom-call | flops 570425344 | bytes 1048576 | tf_op jit(solution)/shard_map/filter/pallas_call | solution.py:399
  27.1 0.7 %collective-permute-done.7.earlier_refs_1_ = f32[8,128]{1,0:T(8,128)S(1)} collective-permute-done((f32[8,128]{1,0:T(8,128)S(1)}, f32[8,128]{1,0:T(8,128)S(1)}, u32[]{:S(2)}, u32[]{:S(2)}) %collective-permute-start.7) | collective-permute-done | bytes 4128 | tf_op jit(solution)/shard_map/ppermute | solution.py:315
  27.9 4.3 %level.1 = f32[8,64,4096]{2,1,0:T(8,128)} custom-call(f32[3,32,64,128]{3,2,1,0:T(8,128)S(1)} %filter.3.local_refs_0_, f32[3,32,64,128]{3,2,1,0:T(8,128)S(1)} %filter.4.local_refs_1_, f32[2,32,64,128]{3,2,1,0:T(8,128)S(1)} %filter.5.local_refs_2_, bf16[8,512,256]{2,1,0:T(8,128)(2,1)S(1)} %get-tuple-element.56.weight_ref, ...), custom_call_target="tpu_custom_call" | custom-call | tf_op jit(solution)/shard_map/level/pallas_call | solution.py:449
  (15 shorter events, 0.1 us)
Async XLA Ops:
  0.0 5.7 %copy-start.1 = (f32[8,128]{1,0:T(8,128)S(1)}, f32[8,128]{1,0:T(8,128)}, u32[]{:S(2)}) copy-start(f32[8,128]{1,0:T(8,128)} %taps_ref.1) | copy-start | bytes 12292
  0.0 5.7 %copy-start = (f32[8,64,4096]{2,1,0:T(8,128)S(1)}, f32[8,64,4096]{2,1,0:T(8,128)}, u32[]{:S(2)}) copy-start(f32[8,64,4096]{2,1,0:T(8,128)} %phase_hbm.1) | copy-start | bytes 25165828
  1.6 8.3 %collective-permute-start = (f32[4,64,128]{2,1,0:T(8,128)S(1)}, f32[4,64,128]{2,1,0:T(8,128)S(1)}, u32[]{:S(2)}, u32[]{:S(2)}) collective-permute-start(f32[4,64,128]{2,1,0:T(8,128)S(1)} %get-tuple-element.34), channel_id=1, source_target_pairs={{0,1},{1,0},{2,3},{3,2},{4,5},{5,4},{6,7},{7,6},{8,9},{9,8},{10,11... | collective-permute-start | bytes 393224 | tf_op jit(solution)/shard_map/ppermute | solution.py:315
  2.1 7.8 %collective-permute-start.1 = (f32[4,64,128]{2,1,0:T(8,128)S(1)}, f32[4,64,128]{2,1,0:T(8,128)S(1)}, u32[]{:S(2)}, u32[]{:S(2)}) collective-permute-start(f32[4,64,128]{2,1,0:T(8,128)S(1)} %get-tuple-element.35), channel_id=1, source_target_pairs={{0,7},{1,2},{2,1},{3,4},{4,3},{5,6},{6,5},{7,0},{8,15},{9,10},{10,... | collective-permute-start | bytes 393224 | tf_op jit(solution)/shard_map/ppermute | solution.py:345
  10.1 1.7 %collective-permute-start.3 = (f32[8,128]{1,0:T(8,128)S(1)}, f32[8,128]{1,0:T(8,128)S(1)}, u32[]{:S(2)}, u32[]{:S(2)}) collective-permute-start(f32[8,128]{1,0:T(8,128)S(1)} %get-tuple-element.38), channel_id=1, source_target_pairs={{0,1},{1,0},{2,3},{3,2},{4,5},{5,4},{6,7},{7,6},{8,9},{9,8},{10,11... | collective-permute-start | bytes 12296 | tf_op jit(solution)/shard_map/ppermute | solution.py:315
  10.2 6.7 %collective-permute-start.2 = (f32[272,128]{1,0:T(8,128)S(1)}, f32[272,128]{1,0:T(8,128)S(1)}, u32[]{:S(2)}, u32[]{:S(2)}) collective-permute-start(f32[272,128]{1,0:T(8,128)S(1)} %constant_dynamic-update-slice_fusion), channel_id=1, source_target_pairs={{0,8},{8,0},{16,24},{24,16},{1,9},{9,1},{17,25},{25,17},{2,10},{10... | collective-permute-start | bytes 417800 | tf_op jit(solution)/shard_map/ppermute | solution.py:315
  11.8 3.7 %collective-permute-start.4 = (f32[8,128]{1,0:T(8,128)S(1)}, f32[8,128]{1,0:T(8,128)S(1)}, u32[]{:S(2)}, u32[]{:S(2)}) collective-permute-start(f32[8,128]{1,0:T(8,128)S(1)} %add.15), channel_id=1, source_target_pairs={{0,2},{1,3},{2,0},{3,1},{4,6},{5,7},{6,4},{7,5},{8,10},{9,11},{10,... | collective-permute-start | bytes 12296 | tf_op jit(solution)/shard_map/ppermute | solution.py:315
  15.6 4.1 %collective-permute-start.5 = (f32[8,128]{1,0:T(8,128)S(1)}, f32[8,128]{1,0:T(8,128)S(1)}, u32[]{:S(2)}, u32[]{:S(2)}) collective-permute-start(f32[8,128]{1,0:T(8,128)S(1)} %add.16), channel_id=1, source_target_pairs={{0,4},{1,5},{2,6},{3,7},{4,0},{5,1},{6,2},{7,3},{8,12},{9,13},{10,... | collective-permute-start | bytes 12296 | tf_op jit(solution)/shard_map/ppermute | solution.py:315
  16.9 10.9 %collective-permute-start.8 = (f32[272,128]{1,0:T(8,128)S(1)}, f32[272,128]{1,0:T(8,128)S(1)}, u32[]{:S(2)}, u32[]{:S(2)}) collective-permute-start(f32[272,128]{1,0:T(8,128)S(1)} %add.19), channel_id=1, source_target_pairs={{0,16},{8,24},{16,0},{24,8},{1,17},{9,25},{17,1},{25,9},{2,18},{10... | collective-permute-start | bytes 417800 | tf_op jit(solution)/shard_map/ppermute | solution.py:315
  19.7 3.7 %collective-permute-start.6 = (f32[8,128]{1,0:T(8,128)S(1)}, f32[8,128]{1,0:T(8,128)S(1)}, u32[]{:S(2)}, u32[]{:S(2)}) collective-permute-start(f32[8,128]{1,0:T(8,128)S(1)} %add.17.sums_ref), channel_id=1, source_target_pairs={{0,8},{8,0},{16,24},{24,16},{1,9},{9,1},{17,25},{25,17},{2,10},{10... | collective-permute-start | bytes 12296 | tf_op jit(solution)/shard_map/ppermute | solution.py:315
  23.3 4.5 %copy-start.2 = (f32[8]{0:T(128)S(1)}, f32[8]{0:T(128)}, u32[]{:S(2)}) copy-start(f32[8]{0:T(128)} %coupling_ref.1) | copy-start | bytes 100
  23.3 4.5 %collective-permute-start.7 = (f32[8,128]{1,0:T(8,128)S(1)}, f32[8,128]{1,0:T(8,128)S(1)}, u32[]{:S(2)}, u32[]{:S(2)}) collective-permute-start(f32[8,128]{1,0:T(8,128)S(1)} %add.18), channel_id=1, source_target_pairs={{0,16},{8,24},{16,0},{24,8},{1,17},{9,25},{17,1},{25,9},{2,18},{10... | collective-permute-start | bytes 12296 | tf_op jit(solution)/shard_map/ppermute | solution.py:315

commit v18 on v17

--- a/solution.py
+++ b/solution.py
@@ -146,7 +146,7 @@
     sums_ref[...] = tile
 
 
-def halo_kernel(inner_ref, outer_ref, high_ref, low_ref, totals_ref):
+def halo_kernel(outer_ref, inner_ref, high_ref, low_ref, totals_ref):
     pairs, time, _ = inner_ref.shape
     cables = 2 * pairs
     groups = time // SUBLANES
@@ -379,7 +379,7 @@
         out_specs=[whole] * 3,
         compiler_params=pltpu.CompilerParams(vmem_limit_bytes=8 << 20),
         name="halo",
-    )(inner, outer)
+    )(outer, inner)
 
     def from_earlier(value):
         return pl.pallas_call(

time: 32.3 us -> 32.3 us (level)
  no operation moved by 1% of the time
where the time goes in v18:
time: 32.3 us; the launch traced here: 32.1 us
  Pallas kernels  16.9 us (52%)
  starting transfers between devices  14.1 us (44%)
  waiting for transfers between devices  1 us (3%)
    ppermute x8, starting transfers between devices, swapped(): lax.ppermute(value, axis, [(i, i ^ bit) for i in range(lax.axis_size(axis...  10.7 us
    pallas_call x3, Pallas kernels, filtered(): pl.pallas_call(functools.partial(filter_kernel, bounds[part]), out_shape=...  6.61 us
    pallas_call x1, Pallas kernels, shards(): pl.pallas_call(functools.partial(level_kernel, population), out_shape=jax...  4.28 us
    pallas_call x1, Pallas kernels, shards(): pl.pallas_call(increments_kernel, out_shape=(pltpu.VMEM((cables, blocks,...  4.21 us
    ppermute x1, starting transfers between devices, shards(): outer = lax.ppermute(outer, 'chan', outer_pairs)  3.4 us
    pallas_call x1, Pallas kernels, shards(): pl.pallas_call(edges_kernel, out_shape=[pltpu.VMEM((cables // 2, time, LA...  1.59 us
    ppermute x8, waiting for transfers between devices, swapped(): lax.ppermute(value, axis, [(i, i ^ bit) for i in range(lax.axis_size(axis...  1 us
  transfers between devices with their start and end apart: 9, of which 2 were waited for; matrix products, arithmetic and copies ran while one was open for 0% of the time, Pallas kernels for 34%

profile of v18, /device:TPU:0, one launch (start us, length us, event | category | flops | bytes accessed | tf_op | source)
XLA Modules:
  0.0 32.1 jit_solution(5715681795582428445)
XLA Ops:
  0.0 1.6 %edges.1 = (f32[4,64,128]{2,1,0:T(8,128)S(1)}, f32[4,64,128]{2,1,0:T(8,128)S(1)}) custom-call(f32[8,64,4096]{2,1,0:T(8,128)} %phase_hbm.1, s32[8,64,4096]{2,1,0:T(8,128)} %wrap_hbm.3), custom_call_target="tpu_custom_call" | custom-call | tf_op jit(solution)/shard_map/edges/pallas_call | solution.py:331
  1.6 3.4 %collective-permute-start = (f32[4,64,128]{2,1,0:T(8,128)S(1)}, f32[4,64,128]{2,1,0:T(8,128)S(1)}, u32[]{:S(2)}, u32[]{:S(2)}) collective-permute-start(f32[4,64,128]{2,1,0:T(8,128)S(1)} %get-tuple-element.34), channel_id=1, source_target_pairs={{0,7},{1,2},{2,1},{3,4},{4,3},{5,6},{6,5},{7,0},{8,15},{9,10},{10,... | collective-permute-start | bytes 393224 | tf_op jit(solution)/shard_map/ppermute | solution.py:345
  5.0 0.0 collective-permute-start.1
  5.0 4.2 %increments.1 = (bf16[8,32,64,128]{3,2,1,0:T(8,128)(2,1)S(1)}, bf16[8,32,64,128]{3,2,1,0:T(8,128)(2,1)S(1)}, f32[256,128]{1,0:T(8,128)S(1)}, f32[8,128]{1,0:T(8,128)S(1)}, bf16[8,512,256]{2,1,0:T(8,128)(2,1)S(1)}) custom-call(f32[8,64,4096]{2,1,0:T(8,128)S(1)} %copy-done, s32[8,64,4096]{2,1,0:T(8,128)} %wrap_hbm.3, f32[8,128]{1,0:T(8,128)S(1)} %copy-done.1), custom_call_target="tpu_custom_call" | custom-call | bytes 8388608 | tf_op jit(solution)/shard_map/increments/pallas_call | solution.py:348
  9.2 0.0 collective-permute-done.outer_ref
  9.3 0.0 collective-permute-done.1.inner_ref
  9.3 0.2 halo.1
  9.4 0.6 %collective-permute-start.3 = (f32[8,128]{1,0:T(8,128)S(1)}, f32[8,128]{1,0:T(8,128)S(1)}, u32[]{:S(2)}, u32[]{:S(2)}) collective-permute-start(f32[8,128]{1,0:T(8,128)S(1)} %get-tuple-element.38), channel_id=1, source_target_pairs={{0,1},{1,0},{2,3},{3,2},{4,5},{5,4},{6,7},{7,6},{8,9},{9,8},{10,11... | collective-permute-start | bytes 12296 | tf_op jit(solution)/shard_map/ppermute | solution.py:315
  10.0 1.6 %collective-permute-start.2 = (f32[272,128]{1,0:T(8,128)S(1)}, f32[272,128]{1,0:T(8,128)S(1)}, u32[]{:S(2)}, u32[]{:S(2)}) collective-permute-start(f32[272,128]{1,0:T(8,128)S(1)} %constant_dynamic-update-slice_fusion), channel_id=1, source_target_pairs={{0,8},{8,0},{16,24},{24,16},{1,9},{9,1},{17,25},{25,17},{2,10},{10... | collective-permute-start | bytes 417800 | tf_op jit(solution)/shard_map/ppermute | solution.py:315
  11.6 0.0 collective-permute-done.3
  11.6 1.3 %collective-permute-start.4 = (f32[8,128]{1,0:T(8,128)S(1)}, f32[8,128]{1,0:T(8,128)S(1)}, u32[]{:S(2)}, u32[]{:S(2)}) collective-permute-start(f32[8,128]{1,0:T(8,128)S(1)} %add.15), channel_id=1, source_target_pairs={{0,2},{1,3},{2,0},{3,1},{4,6},{5,7},{6,4},{7,5},{8,10},{9,11},{10,... | collective-permute-start | bytes 12296 | tf_op jit(solution)/shard_map/ppermute | solution.py:315
  12.9 2.5 %filter.3.local_refs_0_ = f32[3,32,64,128]{3,2,1,0:T(8,128)S(1)} custom-call(bf16[8,32,64,128]{3,2,1,0:T(8,128)(2,1)S(1)} %get-tuple-element.39.high_ref, bf16[8,32,64,128]{3,2,1,0:T(8,128)(2,1)S(1)} %get-tuple-element.40.low_ref, bf16[8,2,64,128]{3,2,1,0:T(8,128)(2,1)S(1)} %get-tuple-element.41.halo_high_ref, ...), custom_call_target="tpu_custom_call" | custom-call | flops 1711276032 | bytes 1048576 | tf_op jit(solution)/shard_map/filter/pallas_call | solution.py:399
  15.4 0.0 collective-permute-done.4
  15.4 1.5 %collective-permute-start.5 = (f32[8,128]{1,0:T(8,128)S(1)}, f32[8,128]{1,0:T(8,128)S(1)}, u32[]{:S(2)}, u32[]{:S(2)}) collective-permute-start(f32[8,128]{1,0:T(8,128)S(1)} %add.16), channel_id=1, source_target_pairs={{0,4},{1,5},{2,6},{3,7},{4,0},{5,1},{6,2},{7,3},{8,12},{9,13},{10,... | collective-permute-start | bytes 12296 | tf_op jit(solution)/shard_map/ppermute | solution.py:315
  16.9 0.0 collective-permute-done.2.value_ref
  16.9 2.7 %collective-permute-start.8 = (f32[272,128]{1,0:T(8,128)S(1)}, f32[272,128]{1,0:T(8,128)S(1)}, u32[]{:S(2)}, u32[]{:S(2)}) collective-permute-start(f32[272,128]{1,0:T(8,128)S(1)} %add.19), channel_id=1, source_target_pairs={{0,16},{8,24},{16,0},{24,8},{1,17},{9,25},{17,1},{25,9},{2,18},{10... | collective-permute-start | bytes 417800 | tf_op jit(solution)/shard_map/ppermute | solution.py:315
  19.7 1.1 %collective-permute-start.6 = (f32[8,128]{1,0:T(8,128)S(1)}, f32[8,128]{1,0:T(8,128)S(1)}, u32[]{:S(2)}, u32[]{:S(2)}) collective-permute-start(f32[8,128]{1,0:T(8,128)S(1)} %add.17.sums_ref), channel_id=1, source_target_pairs={{0,8},{8,0},{16,24},{24,16},{1,9},{9,1},{17,25},{25,17},{2,10},{10... | collective-permute-start | bytes 12296 | tf_op jit(solution)/shard_map/ppermute | solution.py:315
  20.8 2.5 %filter.4.local_refs_1_ = f32[3,32,64,128]{3,2,1,0:T(8,128)S(1)} custom-call(bf16[8,32,64,128]{3,2,1,0:T(8,128)(2,1)S(1)} %get-tuple-element.39.high_ref, bf16[8,32,64,128]{3,2,1,0:T(8,128)(2,1)S(1)} %get-tuple-element.40.low_ref, bf16[8,2,64,128]{3,2,1,0:T(8,128)(2,1)S(1)} %get-tuple-element.41.halo_high_ref, ...), custom_call_target="tpu_custom_call" | custom-call | flops 570425344 | bytes 1048576 | tf_op jit(solution)/shard_map/filter/pallas_call | solution.py:399
  23.3 0.1 collective-permute-done.6.earlier_refs_0_
  23.3 2.0 %collective-permute-start.7 = (f32[8,128]{1,0:T(8,128)S(1)}, f32[8,128]{1,0:T(8,128)S(1)}, u32[]{:S(2)}, u32[]{:S(2)}) collective-permute-start(f32[8,128]{1,0:T(8,128)S(1)} %add.18), channel_id=1, source_target_pairs={{0,16},{8,24},{16,0},{24,8},{1,17},{9,25},{17,1},{25,9},{2,18},{10... | collective-permute-start | bytes 12296 | tf_op jit(solution)/shard_map/ppermute | solution.py:315
  25.3 1.6 %filter.5.local_refs_2_ = f32[2,32,64,128]{3,2,1,0:T(8,128)S(1)} custom-call(bf16[8,32,64,128]{3,2,1,0:T(8,128)(2,1)S(1)} %get-tuple-element.39.high_ref, bf16[8,32,64,128]{3,2,1,0:T(8,128)(2,1)S(1)} %get-tuple-element.40.low_ref, bf16[8,2,64,128]{3,2,1,0:T(8,128)(2,1)S(1)} %get-tuple-element.41.halo_high_ref, ...), custom_call_target="tpu_custom_call" | custom-call | flops 570425344 | bytes 1048576 | tf_op jit(solution)/shard_map/filter/pallas_call | solution.py:399
  26.9 0.9 %collective-permute-done.7.earlier_refs_1_ = f32[8,128]{1,0:T(8,128)S(1)} collective-permute-done((f32[8,128]{1,0:T(8,128)S(1)}, f32[8,128]{1,0:T(8,128)S(1)}, u32[]{:S(2)}, u32[]{:S(2)}) %collective-permute-start.7) | collective-permute-done | bytes 4128 | tf_op jit(solution)/shard_map/ppermute | solution.py:315
  27.9 0.0 collective-permute-done.8.totals_refs_1_
  27.9 4.3 %level.1 = f32[8,64,4096]{2,1,0:T(8,128)} custom-call(f32[3,32,64,128]{3,2,1,0:T(8,128)S(1)} %filter.3.local_refs_0_, f32[3,32,64,128]{3,2,1,0:T(8,128)S(1)} %filter.4.local_refs_1_, f32[2,32,64,128]{3,2,1,0:T(8,128)S(1)} %filter.5.local_refs_2_, bf16[8,512,256]{2,1,0:T(8,128)(2,1)S(1)} %get-tuple-element.56.weight_ref, ...), custom_call_target="tpu_custom_call" | custom-call | tf_op jit(solution)/shard_map/level/pallas_call | solution.py:449
  (15 shorter events, 0.1 us)
Async XLA Ops:
  0.0 5.0 %copy-start.1 = (f32[8,128]{1,0:T(8,128)S(1)}, f32[8,128]{1,0:T(8,128)}, u32[]{:S(2)}) copy-start(f32[8,128]{1,0:T(8,128)} %taps_ref.1) | copy-start | bytes 12292
  0.0 5.0 %copy-start = (f32[8,64,4096]{2,1,0:T(8,128)S(1)}, f32[8,64,4096]{2,1,0:T(8,128)}, u32[]{:S(2)}) copy-start(f32[8,64,4096]{2,1,0:T(8,128)} %phase_hbm.1) | copy-start | bytes 25165828
  1.6 7.7 %collective-permute-start = (f32[4,64,128]{2,1,0:T(8,128)S(1)}, f32[4,64,128]{2,1,0:T(8,128)S(1)}, u32[]{:S(2)}, u32[]{:S(2)}) collective-permute-start(f32[4,64,128]{2,1,0:T(8,128)S(1)} %get-tuple-element.34), channel_id=1, source_target_pairs={{0,7},{1,2},{2,1},{3,4},{4,3},{5,6},{6,5},{7,0},{8,15},{9,10},{10,... | collective-permute-start | bytes 393224 | tf_op jit(solution)/shard_map/ppermute | solution.py:345
  5.0 4.3 %collective-permute-start.1 = (f32[4,64,128]{2,1,0:T(8,128)S(1)}, f32[4,64,128]{2,1,0:T(8,128)S(1)}, u32[]{:S(2)}, u32[]{:S(2)}) collective-permute-start(f32[4,64,128]{2,1,0:T(8,128)S(1)} %get-tuple-element.35), channel_id=1, source_target_pairs={{0,1},{1,0},{2,3},{3,2},{4,5},{5,4},{6,7},{7,6},{8,9},{9,8},{10,11... | collective-permute-start | bytes 393224 | tf_op jit(solution)/shard_map/ppermute | solution.py:315
  9.4 2.2 %collective-permute-start.3 = (f32[8,128]{1,0:T(8,128)S(1)}, f32[8,128]{1,0:T(8,128)S(1)}, u32[]{:S(2)}, u32[]{:S(2)}) collective-permute-start(f32[8,128]{1,0:T(8,128)S(1)} %get-tuple-element.38), channel_id=1, source_target_pairs={{0,1},{1,0},{2,3},{3,2},{4,5},{5,4},{6,7},{7,6},{8,9},{9,8},{10,11... | collective-permute-start | bytes 12296 | tf_op jit(solution)/shard_map/ppermute | solution.py:315
  10.0 6.9 %collective-permute-start.2 = (f32[272,128]{1,0:T(8,128)S(1)}, f32[272,128]{1,0:T(8,128)S(1)}, u32[]{:S(2)}, u32[]{:S(2)}) collective-permute-start(f32[272,128]{1,0:T(8,128)S(1)} %constant_dynamic-update-slice_fusion), channel_id=1, source_target_pairs={{0,8},{8,0},{16,24},{24,16},{1,9},{9,1},{17,25},{25,17},{2,10},{10... | collective-permute-start | bytes 417800 | tf_op jit(solution)/shard_map/ppermute | solution.py:315
  11.6 3.8 %collective-permute-start.4 = (f32[8,128]{1,0:T(8,128)S(1)}, f32[8,128]{1,0:T(8,128)S(1)}, u32[]{:S(2)}, u32[]{:S(2)}) collective-permute-start(f32[8,128]{1,0:T(8,128)S(1)} %add.15), channel_id=1, source_target_pairs={{0,2},{1,3},{2,0},{3,1},{4,6},{5,7},{6,4},{7,5},{8,10},{9,11},{10,... | collective-permute-start | bytes 12296 | tf_op jit(solution)/shard_map/ppermute | solution.py:315
  15.4 4.2 %collective-permute-start.5 = (f32[8,128]{1,0:T(8,128)S(1)}, f32[8,128]{1,0:T(8,128)S(1)}, u32[]{:S(2)}, u32[]{:S(2)}) collective-permute-start(f32[8,128]{1,0:T(8,128)S(1)} %add.16), channel_id=1, source_target_pairs={{0,4},{1,5},{2,6},{3,7},{4,0},{5,1},{6,2},{7,3},{8,12},{9,13},{10,... | collective-permute-start | bytes 12296 | tf_op jit(solution)/shard_map/ppermute | solution.py:315
  16.9 10.9 %collective-permute-start.8 = (f32[272,128]{1,0:T(8,128)S(1)}, f32[272,128]{1,0:T(8,128)S(1)}, u32[]{:S(2)}, u32[]{:S(2)}) collective-permute-start(f32[272,128]{1,0:T(8,128)S(1)} %add.19), channel_id=1, source_target_pairs={{0,16},{8,24},{16,0},{24,8},{1,17},{9,25},{17,1},{25,9},{2,18},{10... | collective-permute-start | bytes 417800 | tf_op jit(solution)/shard_map/ppermute | solution.py:315
  19.7 3.7 %collective-permute-start.6 = (f32[8,128]{1,0:T(8,128)S(1)}, f32[8,128]{1,0:T(8,128)S(1)}, u32[]{:S(2)}, u32[]{:S(2)}) collective-permute-start(f32[8,128]{1,0:T(8,128)S(1)} %add.17.sums_ref), channel_id=1, source_target_pairs={{0,8},{8,0},{16,24},{24,16},{1,9},{9,1},{17,25},{25,17},{2,10},{10... | collective-permute-start | bytes 12296 | tf_op jit(solution)/shard_map/ppermute | solution.py:315
  23.3 4.5 %copy-start.2 = (f32[8]{0:T(128)S(1)}, f32[8]{0:T(128)}, u32[]{:S(2)}) copy-start(f32[8]{0:T(128)} %coupling_ref.1) | copy-start | bytes 100
  23.3 4.5 %collective-permute-start.7 = (f32[8,128]{1,0:T(8,128)S(1)}, f32[8,128]{1,0:T(8,128)S(1)}, u32[]{:S(2)}, u32[]{:S(2)}) collective-permute-start(f32[8,128]{1,0:T(8,128)S(1)} %add.18), channel_id=1, source_target_pairs={{0,16},{8,24},{16,0},{24,8},{1,17},{9,25},{17,1},{25,9},{2,18},{10... | collective-permute-start | bytes 12296 | tf_op jit(solution)/shard_map/ppermute | solution.py:315

commit v19 on v18

--- a/solution.py
+++ b/solution.py
@@ -232,7 +232,7 @@
     offset = totals_refs[0][...]
     for bit, ref in enumerate(totals_refs[1:], 1):
         offset = offset + jnp.where((step & (1 << bit)) != 0, ref[...], 0.0)
-    offset_ref[...] = offset
+    offset_ref[pl.ds(0, offset.shape[0]), :] = offset
     earlier = earlier[SUBLANES - 1 :, groups - 1 : groups]
     common = (sums_ref[...] + earlier) * (1.0 / population)
     columns = [
@@ -455,7 +455,7 @@
         out_specs=outside,
         scratch_shapes=[
             pltpu.VMEM((cables, time, width), jnp.float32),
-            pltpu.VMEM(((blocks + 2) * cables, LANES), jnp.float32),
+            pltpu.VMEM((-(-(blocks + 2) // SUBLANES) * SUBLANES * cables, LANES), jnp.float32),
             pltpu.SemaphoreType.DMA((cables, CHUNKS)),
         ],
         compiler_params=pltpu.CompilerParams(vmem_limit_bytes=24 << 20),

time: 32.3 us -> 32.3 us (level)
  no operation moved by 1% of the time
where the time goes in v19:
time: 32.3 us; the launch traced here: 32.1 us
  Pallas kernels  16.9 us (52%)
  starting transfers between devices  14.1 us (44%)
  waiting for transfers between devices  1 us (3%)
    ppermute x8, starting transfers between devices, swapped(): lax.ppermute(value, axis, [(i, i ^ bit) for i in range(lax.axis_size(axis...  10.7 us
    pallas_call x3, Pallas kernels, filtered(): pl.pallas_call(functools.partial(filter_kernel, bounds[part]), out_shape=...  6.61 us
    pallas_call x1, Pallas kernels, shards(): pl.pallas_call(functools.partial(level_kernel, population), out_shape=jax...  4.28 us
    pallas_call x1, Pallas kernels, shards(): pl.pallas_call(increments_kernel, out_shape=(pltpu.VMEM((cables, blocks,...  4.21 us
    ppermute x1, starting transfers between devices, shards(): outer = lax.ppermute(outer, 'chan', outer_pairs)  3.4 us
    pallas_call x1, Pallas kernels, shards(): pl.pallas_call(edges_kernel, out_shape=[pltpu.VMEM((cables // 2, time, LA...  1.59 us
    ppermute x8, waiting for transfers between devices, swapped(): lax.ppermute(value, axis, [(i, i ^ bit) for i in range(lax.axis_size(axis...  1 us
  transfers between devices with their start and end apart: 9, of which 2 were waited for; matrix products, arithmetic and copies ran while one was open for 0% of the time, Pallas kernels for 34%

profile of v19, /device:TPU:0, one launch (start us, length us, event | category | flops | bytes accessed | tf_op | source)
XLA Modules:
  0.0 32.1 jit_solution(14696881247331460278)
XLA Ops:
  0.0 1.6 %edges.1 = (f32[4,64,128]{2,1,0:T(8,128)S(1)}, f32[4,64,128]{2,1,0:T(8,128)S(1)}) custom-call(f32[8,64,4096]{2,1,0:T(8,128)} %phase_hbm.1, s32[8,64,4096]{2,1,0:T(8,128)} %wrap_hbm.3), custom_call_target="tpu_custom_call" | custom-call | tf_op jit(solution)/shard_map/edges/pallas_call | solution.py:331
  1.6 3.4 %collective-permute-start = (f32[4,64,128]{2,1,0:T(8,128)S(1)}, f32[4,64,128]{2,1,0:T(8,128)S(1)}, u32[]{:S(2)}, u32[]{:S(2)}) collective-permute-start(f32[4,64,128]{2,1,0:T(8,128)S(1)} %get-tuple-element.34), channel_id=1, source_target_pairs={{0,7},{1,2},{2,1},{3,4},{4,3},{5,6},{6,5},{7,0},{8,15},{9,10},{10,... | collective-permute-start | bytes 393224 | tf_op jit(solution)/shard_map/ppermute | solution.py:345
  5.0 0.0 collective-permute-start.1
  5.0 4.2 %increments.1 = (bf16[8,32,64,128]{3,2,1,0:T(8,128)(2,1)S(1)}, bf16[8,32,64,128]{3,2,1,0:T(8,128)(2,1)S(1)}, f32[256,128]{1,0:T(8,128)S(1)}, f32[8,128]{1,0:T(8,128)S(1)}, bf16[8,512,256]{2,1,0:T(8,128)(2,1)S(1)}) custom-call(f32[8,64,4096]{2,1,0:T(8,128)S(1)} %copy-done, s32[8,64,4096]{2,1,0:T(8,128)} %wrap_hbm.3, f32[8,128]{1,0:T(8,128)S(1)} %copy-done.1), custom_call_target="tpu_custom_call" | custom-call | bytes 8388608 | tf_op jit(solution)/shard_map/increments/pallas_call | solution.py:348
  9.2 0.0 collective-permute-done.outer_ref
  9.3 0.0 collective-permute-done.1.inner_ref
  9.3 0.2 halo.1
  9.4 0.6 %collective-permute-start.3 = (f32[8,128]{1,0:T(8,128)S(1)}, f32[8,128]{1,0:T(8,128)S(1)}, u32[]{:S(2)}, u32[]{:S(2)}) collective-permute-start(f32[8,128]{1,0:T(8,128)S(1)} %get-tuple-element.38), channel_id=1, source_target_pairs={{0,1},{1,0},{2,3},{3,2},{4,5},{5,4},{6,7},{7,6},{8,9},{9,8},{10,11... | collective-permute-start | bytes 12296 | tf_op jit(solution)/shard_map/ppermute | solution.py:315
  10.0 1.6 %collective-permute-start.2 = (f32[272,128]{1,0:T(8,128)S(1)}, f32[272,128]{1,0:T(8,128)S(1)}, u32[]{:S(2)}, u32[]{:S(2)}) collective-permute-start(f32[272,128]{1,0:T(8,128)S(1)} %constant_dynamic-update-slice_fusion), channel_id=1, source_target_pairs={{0,8},{8,0},{16,24},{24,16},{1,9},{9,1},{17,25},{25,17},{2,10},{10... | collective-permute-start | bytes 417800 | tf_op jit(solution)/shard_map/ppermute | solution.py:315
  11.6 0.0 collective-permute-done.3
  11.6 1.3 %collective-permute-start.4 = (f32[8,128]{1,0:T(8,128)S(1)}, f32[8,128]{1,0:T(8,128)S(1)}, u32[]{:S(2)}, u32[]{:S(2)}) collective-permute-start(f32[8,128]{1,0:T(8,128)S(1)} %add.15), channel_id=1, source_target_pairs={{0,2},{1,3},{2,0},{3,1},{4,6},{5,7},{6,4},{7,5},{8,10},{9,11},{10,... | collective-permute-start | bytes 12296 | tf_op jit(solution)/shard_map/ppermute | solution.py:315
  12.9 2.5 %filter.3.local_refs_0_ = f32[3,32,64,128]{3,2,1,0:T(8,128)S(1)} custom-call(bf16[8,32,64,128]{3,2,1,0:T(8,128)(2,1)S(1)} %get-tuple-element.39.high_ref, bf16[8,32,64,128]{3,2,1,0:T(8,128)(2,1)S(1)} %get-tuple-element.40.low_ref, bf16[8,2,64,128]{3,2,1,0:T(8,128)(2,1)S(1)} %get-tuple-element.41.halo_high_ref, ...), custom_call_target="tpu_custom_call" | custom-call | flops 1711276032 | bytes 1048576 | tf_op jit(solution)/shard_map/filter/pallas_call | solution.py:399
  15.4 0.0 collective-permute-done.4
  15.4 1.5 %collective-permute-start.5 = (f32[8,128]{1,0:T(8,128)S(1)}, f32[8,128]{1,0:T(8,128)S(1)}, u32[]{:S(2)}, u32[]{:S(2)}) collective-permute-start(f32[8,128]{1,0:T(8,128)S(1)} %add.16), channel_id=1, source_target_pairs={{0,4},{1,5},{2,6},{3,7},{4,0},{5,1},{6,2},{7,3},{8,12},{9,13},{10,... | collective-permute-start | bytes 12296 | tf_op jit(solution)/shard_map/ppermute | solution.py:315
  16.9 0.0 collective-permute-done.2.value_ref
  16.9 2.7 %collective-permute-start.8 = (f32[272,128]{1,0:T(8,128)S(1)}, f32[272,128]{1,0:T(8,128)S(1)}, u32[]{:S(2)}, u32[]{:S(2)}) collective-permute-start(f32[272,128]{1,0:T(8,128)S(1)} %add.19), channel_id=1, source_target_pairs={{0,16},{8,24},{16,0},{24,8},{1,17},{9,25},{17,1},{25,9},{2,18},{10... | collective-permute-start | bytes 417800 | tf_op jit(solution)/shard_map/ppermute | solution.py:315
  19.7 1.1 %collective-permute-start.6 = (f32[8,128]{1,0:T(8,128)S(1)}, f32[8,128]{1,0:T(8,128)S(1)}, u32[]{:S(2)}, u32[]{:S(2)}) collective-permute-start(f32[8,128]{1,0:T(8,128)S(1)} %add.17.sums_ref), channel_id=1, source_target_pairs={{0,8},{8,0},{16,24},{24,16},{1,9},{9,1},{17,25},{25,17},{2,10},{10... | collective-permute-start | bytes 12296 | tf_op jit(solution)/shard_map/ppermute | solution.py:315
  20.8 2.5 %filter.4.local_refs_1_ = f32[3,32,64,128]{3,2,1,0:T(8,128)S(1)} custom-call(bf16[8,32,64,128]{3,2,1,0:T(8,128)(2,1)S(1)} %get-tuple-element.39.high_ref, bf16[8,32,64,128]{3,2,1,0:T(8,128)(2,1)S(1)} %get-tuple-element.40.low_ref, bf16[8,2,64,128]{3,2,1,0:T(8,128)(2,1)S(1)} %get-tuple-element.41.halo_high_ref, ...), custom_call_target="tpu_custom_call" | custom-call | flops 570425344 | bytes 1048576 | tf_op jit(solution)/shard_map/filter/pallas_call | solution.py:399
  23.3 0.1 collective-permute-done.6.earlier_refs_0_
  23.3 2.0 %collective-permute-start.7 = (f32[8,128]{1,0:T(8,128)S(1)}, f32[8,128]{1,0:T(8,128)S(1)}, u32[]{:S(2)}, u32[]{:S(2)}) collective-permute-start(f32[8,128]{1,0:T(8,128)S(1)} %add.18), channel_id=1, source_target_pairs={{0,16},{8,24},{16,0},{24,8},{1,17},{9,25},{17,1},{25,9},{2,18},{10... | collective-permute-start | bytes 12296 | tf_op jit(solution)/shard_map/ppermute | solution.py:315
  25.3 1.6 %filter.5.local_refs_2_ = f32[2,32,64,128]{3,2,1,0:T(8,128)S(1)} custom-call(bf16[8,32,64,128]{3,2,1,0:T(8,128)(2,1)S(1)} %get-tuple-element.39.high_ref, bf16[8,32,64,128]{3,2,1,0:T(8,128)(2,1)S(1)} %get-tuple-element.40.low_ref, bf16[8,2,64,128]{3,2,1,0:T(8,128)(2,1)S(1)} %get-tuple-element.41.halo_high_ref, ...), custom_call_target="tpu_custom_call" | custom-call | flops 570425344 | bytes 1048576 | tf_op jit(solution)/shard_map/filter/pallas_call | solution.py:399
  26.9 0.9 %collective-permute-done.7.earlier_refs_1_ = f32[8,128]{1,0:T(8,128)S(1)} collective-permute-done((f32[8,128]{1,0:T(8,128)S(1)}, f32[8,128]{1,0:T(8,128)S(1)}, u32[]{:S(2)}, u32[]{:S(2)}) %collective-permute-start.7) | collective-permute-done | bytes 4128 | tf_op jit(solution)/shard_map/ppermute | solution.py:315
  27.9 0.0 collective-permute-done.8.totals_refs_1_
  27.9 4.3 %level.1 = f32[8,64,4096]{2,1,0:T(8,128)} custom-call(f32[3,32,64,128]{3,2,1,0:T(8,128)S(1)} %filter.3.local_refs_0_, f32[3,32,64,128]{3,2,1,0:T(8,128)S(1)} %filter.4.local_refs_1_, f32[2,32,64,128]{3,2,1,0:T(8,128)S(1)} %filter.5.local_refs_2_, bf16[8,512,256]{2,1,0:T(8,128)(2,1)S(1)} %get-tuple-element.56.weight_ref, ...), custom_call_target="tpu_custom_call" | custom-call | tf_op jit(solution)/shard_map/level/pallas_call | solution.py:449
  (15 shorter events, 0.1 us)
Async XLA Ops:
  0.0 5.0 %copy-start.1 = (f32[8,128]{1,0:T(8,128)S(1)}, f32[8,128]{1,0:T(8,128)}, u32[]{:S(2)}) copy-start(f32[8,128]{1,0:T(8,128)} %taps_ref.1) | copy-start | bytes 12292
  0.0 5.0 %copy-start = (f32[8,64,4096]{2,1,0:T(8,128)S(1)}, f32[8,64,4096]{2,1,0:T(8,128)}, u32[]{:S(2)}) copy-start(f32[8,64,4096]{2,1,0:T(8,128)} %phase_hbm.1) | copy-start | bytes 25165828
  1.6 7.7 %collective-permute-start = (f32[4,64,128]{2,1,0:T(8,128)S(1)}, f32[4,64,128]{2,1,0:T(8,128)S(1)}, u32[]{:S(2)}, u32[]{:S(2)}) collective-permute-start(f32[4,64,128]{2,1,0:T(8,128)S(1)} %get-tuple-element.34), channel_id=1, source_target_pairs={{0,7},{1,2},{2,1},{3,4},{4,3},{5,6},{6,5},{7,0},{8,15},{9,10},{10,... | collective-permute-start | bytes 393224 | tf_op jit(solution)/shard_map/ppermute | solution.py:345
  5.0 4.3 %collective-permute-start.1 = (f32[4,64,128]{2,1,0:T(8,128)S(1)}, f32[4,64,128]{2,1,0:T(8,128)S(1)}, u32[]{:S(2)}, u32[]{:S(2)}) collective-permute-start(f32[4,64,128]{2,1,0:T(8,128)S(1)} %get-tuple-element.35), channel_id=1, source_target_pairs={{0,1},{1,0},{2,3},{3,2},{4,5},{5,4},{6,7},{7,6},{8,9},{9,8},{10,11... | collective-permute-start | bytes 393224 | tf_op jit(solution)/shard_map/ppermute | solution.py:315
  9.4 2.2 %collective-permute-start.3 = (f32[8,128]{1,0:T(8,128)S(1)}, f32[8,128]{1,0:T(8,128)S(1)}, u32[]{:S(2)}, u32[]{:S(2)}) collective-permute-start(f32[8,128]{1,0:T(8,128)S(1)} %get-tuple-element.38), channel_id=1, source_target_pairs={{0,1},{1,0},{2,3},{3,2},{4,5},{5,4},{6,7},{7,6},{8,9},{9,8},{10,11... | collective-permute-start | bytes 12296 | tf_op jit(solution)/shard_map/ppermute | solution.py:315
  10.0 6.9 %collective-permute-start.2 = (f32[272,128]{1,0:T(8,128)S(1)}, f32[272,128]{1,0:T(8,128)S(1)}, u32[]{:S(2)}, u32[]{:S(2)}) collective-permute-start(f32[272,128]{1,0:T(8,128)S(1)} %constant_dynamic-update-slice_fusion), channel_id=1, source_target_pairs={{0,8},{8,0},{16,24},{24,16},{1,9},{9,1},{17,25},{25,17},{2,10},{10... | collective-permute-start | bytes 417800 | tf_op jit(solution)/shard_map/ppermute | solution.py:315
  11.6 3.8 %collective-permute-start.4 = (f32[8,128]{1,0:T(8,128)S(1)}, f32[8,128]{1,0:T(8,128)S(1)}, u32[]{:S(2)}, u32[]{:S(2)}) collective-permute-start(f32[8,128]{1,0:T(8,128)S(1)} %add.15), channel_id=1, source_target_pairs={{0,2},{1,3},{2,0},{3,1},{4,6},{5,7},{6,4},{7,5},{8,10},{9,11},{10,... | collective-permute-start | bytes 12296 | tf_op jit(solution)/shard_map/ppermute | solution.py:315
  15.4 4.2 %collective-permute-start.5 = (f32[8,128]{1,0:T(8,128)S(1)}, f32[8,128]{1,0:T(8,128)S(1)}, u32[]{:S(2)}, u32[]{:S(2)}) collective-permute-start(f32[8,128]{1,0:T(8,128)S(1)} %add.16), channel_id=1, source_target_pairs={{0,4},{1,5},{2,6},{3,7},{4,0},{5,1},{6,2},{7,3},{8,12},{9,13},{10,... | collective-permute-start | bytes 12296 | tf_op jit(solution)/shard_map/ppermute | solution.py:315
  16.9 10.9 %collective-permute-start.8 = (f32[272,128]{1,0:T(8,128)S(1)}, f32[272,128]{1,0:T(8,128)S(1)}, u32[]{:S(2)}, u32[]{:S(2)}) collective-permute-start(f32[272,128]{1,0:T(8,128)S(1)} %add.19), channel_id=1, source_target_pairs={{0,16},{8,24},{16,0},{24,8},{1,17},{9,25},{17,1},{25,9},{2,18},{10... | collective-permute-start | bytes 417800 | tf_op jit(solution)/shard_map/ppermute | solution.py:315
  19.7 3.7 %collective-permute-start.6 = (f32[8,128]{1,0:T(8,128)S(1)}, f32[8,128]{1,0:T(8,128)S(1)}, u32[]{:S(2)}, u32[]{:S(2)}) collective-permute-start(f32[8,128]{1,0:T(8,128)S(1)} %add.17.sums_ref), channel_id=1, source_target_pairs={{0,8},{8,0},{16,24},{24,16},{1,9},{9,1},{17,25},{25,17},{2,10},{10... | collective-permute-start | bytes 12296 | tf_op jit(solution)/shard_map/ppermute | solution.py:315
  23.3 4.5 %copy-start.2 = (f32[8]{0:T(128)S(1)}, f32[8]{0:T(128)}, u32[]{:S(2)}) copy-start(f32[8]{0:T(128)} %coupling_ref.1) | copy-start | bytes 100
  23.3 4.5 %collective-permute-start.7 = (f32[8,128]{1,0:T(8,128)S(1)}, f32[8,128]{1,0:T(8,128)S(1)}, u32[]{:S(2)}, u32[]{:S(2)}) collective-permute-start(f32[8,128]{1,0:T(8,128)S(1)} %add.18), channel_id=1, source_target_pairs={{0,16},{8,24},{16,0},{24,8},{1,17},{9,25},{17,1},{25,9},{2,18},{10... | collective-permute-start | bytes 12296 | tf_op jit(solution)/shard_map/ppermute | solution.py:315
